TPU v7x, 32 devices: a whole 2x2x4 slice. The times are simulated.
32 devices in a mesh: parts: 2 (over x), dp: 2 (over core), mp: 8 (over z, y).
Axes of the slice: x: 2, y: 2, z: 4, core: 2. Of those that a mesh axis runs over, the one named last changes fastest.
Arguments:
- hidden_in: bfloat16 [32, 5120], P(('parts', 'dp')), parts along dimension 0, may hold values from -6 to 6
- norm_gain: float32 [5120], replicated, may hold values from 0.1 to 1.9
- w_query: bfloat16 [5120, 8192], P(None, 'mp'), may hold values from -1 to 1
- w_key_value: bfloat16 [5120, 2048], P(None, 'mp'), may hold values from -1 to 1
- w_output: bfloat16 [8192, 5120], P('mp'), may hold values from -0.25 to 0.25
- cache_keys: bfloat16 [32, 512, 1024], P(('parts', 'dp'), 'mp'), parts along dimension 0, may hold values from -200 to 200
- cache_values: bfloat16 [32, 512, 1024], P(('parts', 'dp'), 'mp'), parts along dimension 0, may hold values from -6 to 6
- cache_lengths: int32 [32], P('parts'), parts along dimension 0, may hold values from 64 to 512
- remaining_steps: int32 [32], P('parts'), parts along dimension 0, may hold values from 1 to 4
- move_from: int32 [4], P('parts'), parts along dimension 0, may hold values from 0 to 7, as said below
- move_to: int32 [4], P('parts'), parts along dimension 0, may hold values from 0 to 7, as said below
Outputs:
- hidden_out: bfloat16 [32, 5120], P(('parts', 'dp')), parts along dimension 0
- new_kv: bfloat16 [4, 32, 2048], P(None, ('parts', 'dp'), 'mp'), parts along dimension 1
There are 2 independent parts, one for each index of `parts`. A program takes and returns all parts, laid end to end along the dimension named above; an argument that names none is the same for every part. Nothing has to cross between parts.
Inputs may be any that keep to these rules, and one draw needn't show every extreme that they name: `move_from`: 2 distinct slots. `move_to`: 2 distinct slots.
All inputs are finite; a program needn't handle non-finite values.
Results may differ from a plain program's by a relative error of at most 0.018.
Values may be sent and summed in bfloat16 or wider, within the bound.
No kernel may reach another device: no remote copies, remote signals or barrier semaphores. Data moves between devices by JAX's collectives and lax.ppermute only.
A program may use at most 128 MiB of HBM per device.

v0:
```python
import math

import jax
import jax.numpy as jnp
from jax import lax
from jax.sharding import PartitionSpec as P

HD = 128
STEPS = 4


rope_base = 1000000.0
norm_eps = 1e-06


def partner(block, axis, stride):
    count = lax.axis_size(axis)
    route = []
    for low in range(count):
        high = low | 1 << stride
        if high != low and high < count:
            route += [(low, high), (high, low)]
    return lax.ppermute(block, axis, route)


def root_norm(values):
    return values * lax.rsqrt(jnp.mean(values * values, axis=-1, keepdims=True) + norm_eps)


def rotate(values, positions):
    half_width = values.shape[-1] // 2
    frequency = rope_base ** (-jnp.arange(half_width).astype(jnp.float32) * 2.0 / values.shape[-1])
    angles = positions.astype(jnp.float32)[:, None] * frequency[None, :]
    cosine = jnp.cos(angles)[:, None, :]
    sine_part = jnp.sin(angles)[:, None, :]
    first_half = values[..., :half_width]
    second_half = values[..., half_width:]
    return jnp.concatenate(
        [
            first_half * cosine - second_half * sine_part,
            second_half * cosine + first_half * sine_part,
        ],
        axis=-1,
    )


def combine_blocks(pieces):
    numer_parts, max_parts, den_parts = pieces
    top_block = jnp.max(max_parts, axis=0)
    factors = jnp.exp(max_parts - top_block[None])
    head_width = numer_parts.shape[2] // max_parts.shape[2]
    shaped = numer_parts.reshape(
        numer_parts.shape[0], numer_parts.shape[1], max_parts.shape[2], head_width
    )
    summed = jnp.sum(factors[..., None] * shaped, axis=0)
    return (top_block, summed.reshape(summed.shape[0], -1), jnp.sum(factors * den_parts, axis=0))


def per_device(
    hidden_in,
    norm_gain,
    w_query,
    w_key_value,
    w_output,
    cache_keys,
    cache_values,
    cache_lengths,
    remaining_steps,
    move_from,
    move_to,
):
    seq_count = hidden_in.shape[0]
    model_size = lax.axis_size("mp")
    model_index = lax.axis_index("mp")
    group_index = lax.axis_index("dp")
    head_dim = HD
    heads_here = w_query.shape[1] // head_dim
    kv_width = cache_keys.shape[2]
    kv_heads = kv_width // head_dim
    group_size = heads_here * model_size // kv_heads
    block_len = cache_keys.shape[1]
    col_width = w_key_value.shape[1]
    total_seqs = cache_lengths.shape[0]
    new_order = jnp.arange(total_seqs)
    new_order = new_order.at[move_from].set(move_to + seq_count)
    new_order = new_order.at[move_to + seq_count].set(move_from)
    own_slots = jnp.where(group_index == 0, move_from, move_to)
    arrived = partner(
        (cache_keys[own_slots], cache_values[own_slots], hidden_in[own_slots]), "dp", 0
    )
    cache_keys = cache_keys.at[own_slots].set(arrived[0])
    cache_values = cache_values.at[own_slots].set(arrived[1])
    hidden = hidden_in.at[own_slots].set(arrived[2])
    lengths_all = cache_lengths[new_order]
    remain_all = remaining_steps[new_order]
    lengths = lax.dynamic_slice_in_dim(lengths_all, group_index * seq_count, seq_count)
    remaining = lax.dynamic_slice_in_dim(remain_all, group_index * seq_count, seq_count)
    score_scale = 1.0 / math.sqrt(head_dim)
    positions_here = model_index * block_len + jnp.arange(block_len)
    valid_mask = positions_here[None, :] < lengths[:, None]
    live_mask = valid_mask[:, None, None, :]
    keys_view = cache_keys.reshape(seq_count, block_len, kv_heads, head_dim)
    values_view = cache_values.reshape(seq_count, block_len, kv_heads, head_dim)
    kv_index = (model_index * heads_here + jnp.arange(heads_here)) // group_size
    fresh_keys = jnp.zeros((seq_count, STEPS, kv_heads, head_dim), jnp.bfloat16)
    fresh_values = jnp.zeros((seq_count, STEPS, kv_heads, head_dim), jnp.bfloat16)
    kv_outputs = []
    for step_index in range(STEPS):
        active = remaining > step_index
        step_pos = lengths + step_index
        hidden_float = hidden.astype(jnp.float32)
        normed = (root_norm(hidden_float) * norm_gain).astype(jnp.bfloat16)
        projected = jnp.dot(normed, w_query, preferred_element_type=jnp.float32).reshape(
            seq_count, heads_here, head_dim
        )
        queries = rotate(root_norm(projected), step_pos).astype(jnp.bfloat16)
        raw_part = jnp.dot(normed, w_key_value, preferred_element_type=jnp.float32).astype(
            jnp.bfloat16
        )
        raw_full = lax.all_gather(raw_part, "mp", axis=1, tiled=True)
        key_part = raw_full[:, :kv_width].astype(jnp.float32).reshape(seq_count, kv_heads, head_dim)
        new_keys = rotate(root_norm(key_part), step_pos).astype(jnp.bfloat16)
        new_values = raw_full[:, kv_width:].reshape(seq_count, kv_heads, head_dim)
        active_mask = active[:, None, None]
        new_keys = jnp.where(active_mask, new_keys, jnp.zeros_like(new_keys))
        new_values = jnp.where(active_mask, new_values, jnp.zeros_like(new_values))
        fresh_keys = fresh_keys.at[:, step_index].set(new_keys)
        fresh_values = fresh_values.at[:, step_index].set(new_values)
        kv_both = jnp.concatenate(
            [new_keys.reshape(seq_count, kv_width), new_values.reshape(seq_count, kv_width)],
            axis=-1,
        )
        kv_outputs.append(lax.dynamic_slice_in_dim(kv_both, model_index * col_width, col_width, 1))
        query_all = lax.all_gather(
            queries.reshape(seq_count, heads_here * head_dim), "mp", axis=1, tiled=True
        )
        grouped = query_all.reshape(seq_count, kv_heads, group_size, head_dim)
        scores = (
            jnp.einsum("skgd,spkd->skgp", grouped, keys_view, preferred_element_type=jnp.float32)
            * score_scale
        )
        local_max = jnp.max(jnp.where(live_mask, scores, -1e30), axis=-1)
        weights = jnp.where(live_mask, jnp.exp(scores - local_max[..., None]), 0.0).astype(
            jnp.bfloat16
        )
        numerator = jnp.einsum(
            "skgp,spkd->skgd", weights, values_view, preferred_element_type=jnp.float32
        )
        denominator = jnp.sum(weights.astype(jnp.float32), axis=-1)
        merged_max, merged_num, merged_den = combine_blocks(
            (
                lax.all_to_all(
                    numerator.reshape(1, seq_count, -1),
                    "mp",
                    split_axis=2,
                    concat_axis=0,
                    tiled=True,
                ),
                lax.all_to_all(
                    local_max.reshape(1, seq_count, -1),
                    "mp",
                    split_axis=2,
                    concat_axis=0,
                    tiled=True,
                ),
                lax.all_to_all(
                    denominator.reshape(1, seq_count, -1),
                    "mp",
                    split_axis=2,
                    concat_axis=0,
                    tiled=True,
                ),
            )
        )
        chosen_keys = jnp.take(fresh_keys, kv_index, axis=2)
        chosen_values = jnp.take(fresh_values, kv_index, axis=2)
        fresh_scores = (
            jnp.einsum("shd,sthd->sht", queries, chosen_keys, preferred_element_type=jnp.float32)
            * score_scale
        )
        fresh_live = (jnp.arange(STEPS) <= step_index)[None, None, :]
        fresh_max = jnp.max(jnp.where(fresh_live, fresh_scores, -1e30), axis=-1)
        fresh_weights = jnp.where(
            fresh_live, jnp.exp(fresh_scores - fresh_max[..., None]), 0.0
        ).astype(jnp.bfloat16)
        fresh_num = jnp.einsum(
            "sht,sthd->shd", fresh_weights, chosen_values, preferred_element_type=jnp.float32
        )
        fresh_den = jnp.sum(fresh_weights.astype(jnp.float32), axis=-1)
        top_score = jnp.maximum(merged_max, fresh_max)
        old_scale = jnp.exp(merged_max - top_score)
        new_scale = jnp.exp(fresh_max - top_score)
        weighted = (
            old_scale[..., None] * merged_num.reshape(seq_count, heads_here, head_dim)
            + new_scale[..., None] * fresh_num
        )
        mass_sum = old_scale * merged_den + new_scale * fresh_den
        attended = (
            (weighted / mass_sum[..., None])
            .reshape(seq_count, heads_here * head_dim)
            .astype(jnp.bfloat16)
        )
        summed = lax.psum(jnp.dot(attended, w_output, preferred_element_type=jnp.float32), "mp")
        hidden = jnp.where(active[:, None], hidden_float + summed, hidden_float).astype(
            jnp.bfloat16
        )
    kv_local = jnp.stack(kv_outputs)
    return (hidden, kv_local)


def solution(mesh):
    placed = (
        P(("parts", "dp"), None),
        P(),
        P(None, "mp"),
        P(None, "mp"),
        P("mp", None),
        P(("parts", "dp"), "mp", None),
        P(("parts", "dp"), "mp", None),
        P("parts"),
        P("parts"),
        P("parts"),
        P("parts"),
    )
    return jax.shard_map(
        per_device,
        mesh=mesh,
        in_specs=placed,
        out_specs=(P(("parts", "dp"), None), P(None, ("parts", "dp"), "mp")),
        check_vma=False,
    )
```

profile of v0, /device:TPU:0, one launch (start us, length us, event | category | flops | bytes accessed | tf_op | source)
XLA Modules:
  0.0 1001.3 jit_solution(14922851031313512605)
XLA Ops:
  14.0 2.5 gather_fusion.3
  16.6 2.5 gather_fusion.4
  26.6 5.6 multiply_reduce_fusion.11
  32.7 31.8 %all_gather.25 = bf16[8,2048]{1,0:T(8,128)(2,1)S(1)} all-gather(bf16[8,256]{1,0:T(8,128)(2,1)S(1)} %convolution_convert_fusion.3), channel_id=1, replica_groups=mesh['parts'=2,'dp'=2,'mp'=8] {'mp'}, dimensions={1}, use_global_device_ids=true | all-gather | bytes 36864 | tf_op jit(solution)/shard_map/all_gather | solution.py:120
  66.1 30.5 %all_gather.24 = bf16[8,8192]{1,0:T(8,128)(2,1)S(1)} all-gather(bf16[8,1024]{1,0:T(8,128)(2,1)S(1)} %fusion.132), channel_id=1, replica_groups=mesh['parts'=2,'dp'=2,'mp'=8] {'mp'}, dimensions={1}, use_global_device_ids=true | all-gather | bytes 147456 | tf_op jit(solution)/shard_map/all_gather | solution.py:134
  102.0 5.6 all-to-all-start.2
  114.9 4.3 all-to-all-start
  120.9 2.6 copy.201
  124.0 38.4 %reduce.32 = f32[8192,8]{1,0:T(8,128)} reduce(f32[8192,1,8]{2,1,0:T(1,128)} %bitcast.350, f32[]{:T(128)} %broadcast.893), dimensions={1}, to_apply=%bitcast.274.reduce_sub_computation | reduce | bytes 524292
  162.4 4.5 reshape.1260
  166.9 6.0 all-to-all-start.1
  175.7 5.5 all-to-all-done.1
  181.2 2.9 reduce.33
  184.1 10.6 %reshape.1261 = f32[8192,1,8]{2,1,0:T(1,128)} reshape(f32[8,8192]{1,0:T(8,128)} %reduce.33) | data formatting | bytes 524288
  194.7 2.7 fusion.3
  197.4 6.1 fusion.133
  204.3 67.1 %all-reduce.7.cloned.1.call-done = f32[8,5120]{1,0:T(8,128)} async-done(((f32[8,5120]{1,0:T(8,128)}), f32[8,5120]{1,0:T(8,128)}) %all-reduce.7.cloned.1.call-update) | async-done | bytes 163856 | tf_op jit(solution)/shard_map/psum | solution.py:203
  273.1 5.7 multiply_reduce_fusion.9
  279.2 30.5 %all_gather.26 = bf16[8,8192]{1,0:T(8,128)(2,1)S(1)} all-gather(bf16[8,1024]{1,0:T(8,128)(2,1)S(1)} %fusion.130), channel_id=1, replica_groups=mesh['parts'=2,'dp'=2,'mp'=8] {'mp'}, dimensions={1}, use_global_device_ids=true | all-gather | bytes 147456 | tf_op jit(solution)/shard_map/all_gather | solution.py:134
  311.2 30.4 %all_gather.27 = bf16[8,2048]{1,0:T(8,128)(2,1)S(1)} all-gather(bf16[8,256]{1,0:T(8,128)(2,1)S(1)} %convolution_convert_fusion.2), channel_id=1, replica_groups=mesh['parts'=2,'dp'=2,'mp'=8] {'mp'}, dimensions={1}, use_global_device_ids=true | all-gather | bytes 36864 | tf_op jit(solution)/shard_map/all_gather | solution.py:120
  343.2 4.3 all-to-all-start.5
  349.6 4.7 all-to-all-done.5
  354.3 15.7 %all-to-all-start.3 = ((f32[1,8,64]{1,0,2:T(1,128)}), f32[1,8,64]{1,0,2:T(1,128)S(1)}, u32[]{:S(2)}, u32[]{:S(2)}) async-start(f32[1,8,64]{1,0,2:T(1,128)} %bitcast.33), calls=%async_computation.3 | async-start | bytes 65536 | tf_op jit(solution)/shard_map/all_to_all | solution.py:159
  370.1 2.6 copy.203
  372.7 38.4 %reduce.34 = f32[8192,8]{1,0:T(8,128)} reduce(f32[8192,1,8]{2,1,0:T(1,128)} %bitcast.355, f32[]{:T(128)} %broadcast.893), dimensions={1}, to_apply=%bitcast.276.reduce_sub_computation | reduce | bytes 524292
  411.0 4.4 reshape.1262
  416.2 5.8 all-to-all-start.4
  423.3 7.0 all-to-all-done.4
  430.3 2.9 reduce.35
  433.2 10.6 %reshape.1263 = f32[8192,1,8]{2,1,0:T(1,128)} reshape(f32[8,8192]{1,0:T(8,128)} %reduce.35) | data formatting | bytes 524288
  443.8 2.7 fusion.2
  446.6 6.1 fusion.134
  453.5 67.2 %all-reduce.9.cloned.1.call-done = f32[8,5120]{1,0:T(8,128)} async-done(((f32[8,5120]{1,0:T(8,128)}), f32[8,5120]{1,0:T(8,128)}) %all-reduce.9.cloned.1.call-update) | async-done | bytes 163856 | tf_op jit(solution)/shard_map/psum | solution.py:203
  522.3 5.7 multiply_reduce_fusion.7
  528.4 30.5 %all_gather.28 = bf16[8,8192]{1,0:T(8,128)(2,1)S(1)} all-gather(bf16[8,1024]{1,0:T(8,128)(2,1)S(1)} %fusion.128), channel_id=1, replica_groups=mesh['parts'=2,'dp'=2,'mp'=8] {'mp'}, dimensions={1}, use_global_device_ids=true | all-gather | bytes 147456 | tf_op jit(solution)/shard_map/all_gather | solution.py:134
  560.4 30.4 %all_gather.29 = bf16[8,2048]{1,0:T(8,128)(2,1)S(1)} all-gather(bf16[8,256]{1,0:T(8,128)(2,1)S(1)} %convolution_convert_fusion.1), channel_id=1, replica_groups=mesh['parts'=2,'dp'=2,'mp'=8] {'mp'}, dimensions={1}, use_global_device_ids=true | all-gather | bytes 36864 | tf_op jit(solution)/shard_map/all_gather | solution.py:120
  591.8 4.3 all-to-all-start.8
  598.1 4.7 all-to-all-done.8
  603.4 3.7 all-to-all-start.6
  607.2 2.6 copy.205
  609.8 38.4 %reduce.36 = f32[8192,8]{1,0:T(8,128)} reduce(f32[8192,1,8]{2,1,0:T(1,128)} %bitcast.356, f32[]{:T(128)} %broadcast.893), dimensions={1}, to_apply=%bitcast.278.reduce_sub_computation | reduce | bytes 524292
  648.2 4.4 reshape.1264
  653.4 6.0 all-to-all-start.7
  660.7 7.0 all-to-all-done.7
  667.7 2.9 reduce.37
  670.6 10.6 %reshape.1265 = f32[8192,1,8]{2,1,0:T(1,128)} reshape(f32[8,8192]{1,0:T(8,128)} %reduce.37) | data formatting | bytes 524288
  681.2 2.7 fusion.1
  684.0 6.1 fusion.135
  690.9 67.1 %all-reduce.11.cloned.1.call-done = f32[8,5120]{1,0:T(8,128)} async-done(((f32[8,5120]{1,0:T(8,128)}), f32[8,5120]{1,0:T(8,128)}) %all-reduce.11.cloned.1.call-update) | async-done | bytes 163856 | tf_op jit(solution)/shard_map/psum | solution.py:203
  759.6 5.7 multiply_reduce_fusion.5
  765.7 30.5 %all_gather.30 = bf16[8,8192]{1,0:T(8,128)(2,1)S(1)} all-gather(bf16[8,1024]{1,0:T(8,128)(2,1)S(1)} %fusion.126), channel_id=1, replica_groups=mesh['parts'=2,'dp'=2,'mp'=8] {'mp'}, dimensions={1}, use_global_device_ids=true | all-gather | bytes 147456 | tf_op jit(solution)/shard_map/all_gather | solution.py:134
  797.7 30.4 %all_gather.31 = bf16[8,2048]{1,0:T(8,128)(2,1)S(1)} all-gather(bf16[8,256]{1,0:T(8,128)(2,1)S(1)} %convolution_convert_fusion), channel_id=1, replica_groups=mesh['parts'=2,'dp'=2,'mp'=8] {'mp'}, dimensions={1}, use_global_device_ids=true | all-gather | bytes 36864 | tf_op jit(solution)/shard_map/all_gather | solution.py:120
  829.1 4.3 all-to-all-start.11
  836.1 4.0 all-to-all-done.11
  840.1 3.5 all-to-all-start.9
  843.7 2.6 copy.207
  846.3 38.4 %reduce.38 = f32[8192,8]{1,0:T(8,128)} reduce(f32[8192,1,8]{2,1,0:T(1,128)} %bitcast.357, f32[]{:T(128)} %broadcast.893), dimensions={1}, to_apply=%bitcast.280.reduce_sub_computation | reduce | bytes 524292
  884.6 4.4 reshape.1266
  889.8 6.0 all-to-all-start.10
  896.6 7.5 all-to-all-done.10
  906.4 9.6 reshape.1267
  916.0 2.7 fusion
  918.8 6.1 fusion.136
  925.7 67.2 %all-reduce.13.cloned.1.call-done = f32[8,5120]{1,0:T(8,128)} async-done(((f32[8,5120]{1,0:T(8,128)}), f32[8,5120]{1,0:T(8,128)}) %all-reduce.13.cloned.1.call-update) | async-done | bytes 163856 | tf_op jit(solution)/shard_map/psum | solution.py:203
  (279 shorter events, 68.2 us)
Async XLA Ops:
  7.2 25.0 %copy-start = (bf16[5120,256]{1,0:T(8,128)(2,1)S(1)}, bf16[5120,256]{1,0:T(8,128)(2,1)}, u32[]{:S(2)}) copy-start(bf16[5120,256]{1,0:T(8,128)(2,1)} %param.32) | copy-start | bytes 7864324
  7.2 14.6 %copy-start.1 = (s32[16]{0:T(128)S(1)}, s32[16]{0:T(128)}, u32[]{:S(2)}) copy-start(s32[16]{0:T(128)} %param.36) | copy-start | bytes 196
  7.2 15.4 %copy-start.2 = (s32[16]{0:T(128)S(1)}, s32[16]{0:T(128)}, u32[]{:S(2)}) copy-start(s32[16]{0:T(128)} %param.37) | copy-start | bytes 196
  7.2 5.7 copy-start.35
  7.2 5.7 copy-start.39
  8.3 18.3 %copy-start.9 = (f32[5120]{0:T(1024)S(1)}, f32[5120]{0:T(1024)}, u32[]{:S(2)}) copy-start(f32[5120]{0:T(1024)} %param.30) | copy-start | bytes 61444
  13.5 12.2 %collective-permute-start = (bf16[2,5120]{1,0:T(2,128)(2,1)S(1)}, bf16[2,5120]{1,0:T(2,128)(2,1)S(1)}, u32[]{:S(2)}, u32[]{:S(2)}) collective-permute-start(bf16[2,5120]{1,0:T(2,128)(2,1)S(1)} %gather_fusion.1), channel_id=1, source_target_pairs={{0,8},{8,0},{1,9},{9,1},{2,10},{10,2},{3,11},{11,3},{4,12},{12,4},... | collective-permute-start | bytes 61448 | tf_op jit(solution)/shard_map/ppermute | solution.py:23
  16.5 80.2 %collective-permute-start.1 = (bf16[2,64,1024]{2,1,0:T(8,128)(2,1)}, bf16[2,64,1024]{2,1,0:T(8,128)(2,1)}, u32[]{:S(2)}, u32[]{:S(2)}) collective-permute-start(bf16[2,64,1024]{2,1,0:T(8,128)(2,1)} %gather_fusion.3), channel_id=1, source_target_pairs={{0,8},{8,0},{1,9},{9,1},{2,10},{10,2},{3,11},{11,3},{4,12},{12,4},... | collective-permute-start | bytes 786440 | tf_op jit(solution)/shard_map/ppermute | solution.py:23
  19.1 91.2 %collective-permute-start.2 = (bf16[2,64,1024]{2,1,0:T(8,128)(2,1)}, bf16[2,64,1024]{2,1,0:T(8,128)(2,1)}, u32[]{:S(2)}, u32[]{:S(2)}) collective-permute-start(bf16[2,64,1024]{2,1,0:T(8,128)(2,1)} %gather_fusion.4), channel_id=1, source_target_pairs={{0,8},{8,0},{1,9},{9,1},{2,10},{10,2},{3,11},{11,3},{4,12},{12,4},... | collective-permute-start | bytes 786440 | tf_op jit(solution)/shard_map/ppermute | solution.py:23
  23.9 635.5 %copy-start.16 = (pred[8]{0:T(512)(128)(4,1)}, pred[8]{0:T(512)(128)(4,1)S(1)}, u32[]{:S(2)}) copy-start(pred[8]{0:T(512)(128)(4,1)S(1)} %get-tuple-element.209) | copy-start | bytes 28
  24.5 40.5 %copy-start.33 = (pred[8]{0:T(512)(128)(4,1)}, pred[8]{0:T(512)(128)(4,1)S(1)}, u32[]{:S(2)}) copy-start(pred[8]{0:T(512)(128)(4,1)S(1)} %get-tuple-element.181) | copy-start | bytes 28
  24.5 83.9 %copy-start.22 = (s32[1024]{0:T(1024)}, s32[1024]{0:T(1024)S(1)}, u32[]{:S(2)}) copy-start(s32[1024]{0:T(1024)S(1)} %pad_clamp_fusion) | copy-start | bytes 12292
  25.2 253.7 %copy-start.20 = (f32[8,64]{1,0:T(8,128)}, f32[8,64]{1,0:T(8,128)S(1)}, u32[]{:S(2)}) copy-start(f32[8,64]{1,0:T(8,128)S(1)} %get-tuple-element.171) | copy-start | bytes 6148
  25.2 253.7 %copy-start.21 = (f32[8,64]{1,0:T(8,128)}, f32[8,64]{1,0:T(8,128)S(1)}, u32[]{:S(2)}) copy-start(f32[8,64]{1,0:T(8,128)S(1)} %get-tuple-element.172) | copy-start | bytes 6148
  102.0 12.3 %all-to-all-start.2 = ((f32[1,8,64]{1,0,2:T(1,128)}), f32[1,8,64]{1,0,2:T(1,128)S(1)}, u32[]{:S(2)}, u32[]{:S(2)}) async-start(f32[1,8,64]{1,0,2:T(1,128)} %bitcast.26), calls=%async_computation.2 | async-start | bytes 65536 | tf_op jit(solution)/shard_map/all_to_all | solution.py:166
  114.3 0.6 copy-start.12
  114.9 52.0 %all-to-all-start = ((f32[1,8,64]{1,0,2:T(1,128)}), f32[1,8,64]{1,0,2:T(1,128)S(1)}, u32[]{:S(2)}, u32[]{:S(2)}) async-start(f32[1,8,64]{1,0,2:T(1,128)} %bitcast.6), calls=%async_computation | async-start | bytes 65536 | tf_op jit(solution)/shard_map/all_to_all | solution.py:159
  162.4 10.8 %copy-start.10 = (bf16[8,8,4,128]{3,1,2,0:T(8,128)(2,1)S(1)}, bf16[8,8,4,128]{3,1,2,0:T(8,128)(2,1)}, u32[]{:S(2)}) copy-start(bf16[8,8,4,128]{3,1,2,0:T(8,128)(2,1)} %gather_fusion.6) | copy-start | bytes 196612
  162.4 11.0 %copy-start.26 = (f32[8,8]{1,0:T(8,128)S(1)}, f32[8,8]{1,0:T(8,128)}, u32[]{:S(2)}) copy-start(f32[8,8]{1,0:T(8,128)} %get-tuple-element.135) | copy-start | bytes 772
  166.9 14.3 %all-to-all-start.1 = ((f32[8,1,8192]{2,1,0:T(1,128)}), f32[8,1,8192]{2,1,0:T(1,128)}, u32[]{:S(2)}, u32[]{:S(2)}) async-start(f32[8,1,8192]{2,1,0:T(1,128)} %reshape.1260), calls=%async_computation.1 | async-start | bytes 524288 | tf_op jit(solution)/shard_map/all_to_all | solution.py:152
  172.9 98.6 %all-reduce.7.cloned.1.call-start = ((), (), s32[]{:S(2)}) async-start(), calls=%async_computation.12 | async-start | bytes 327680 | tf_op jit(solution)/shard_map/psum | solution.py:203
  197.4 6.2 copy-start.34
  273.1 36.6 %copy-start.3 = (bf16[8,64,1024]{2,1,0:T(8,128)(2,1)S(1)}, bf16[8,64,1024]{2,1,0:T(8,128)(2,1)}, u32[]{:S(2)}) copy-start(bf16[8,64,1024]{2,1,0:T(8,128)(2,1)} %scatter_fusion.3) | copy-start | bytes 3145732
  273.1 37.6 %copy-start.6 = (bf16[8,64,1024]{2,1,0:T(8,128)(2,1)S(1)}, bf16[8,64,1024]{2,1,0:T(8,128)(2,1)}, u32[]{:S(2)}) copy-start(bf16[8,64,1024]{2,1,0:T(8,128)(2,1)} %scatter_fusion.4) | copy-start | bytes 3145732
  278.8 68.8 %copy-start.31 = (pred[8]{0:T(512)(128)(4,1)S(1)}, pred[8]{0:T(512)(128)(4,1)}, u32[]{:S(2)}) copy-start(pred[8]{0:T(512)(128)(4,1)} %get-tuple-element.180) | copy-start | bytes 28
  278.8 70.0 %copy-start.38 = (pred[4]{0:T(512)(128)(4,1)S(1)}, pred[4]{0:T(512)(128)(4,1)}, u32[]{:S(2)}) copy-start(pred[4]{0:T(512)(128)(4,1)} %iota_compare_fusion.2) | copy-start | bytes 16
  343.2 11.0 %all-to-all-start.5 = ((f32[1,8,64]{1,0,2:T(1,128)}), f32[1,8,64]{1,0,2:T(1,128)S(1)}, u32[]{:S(2)}, u32[]{:S(2)}) async-start(f32[1,8,64]{1,0,2:T(1,128)} %bitcast.53), calls=%async_computation.5 | async-start | bytes 65536 | tf_op jit(solution)/shard_map/all_to_all | solution.py:166
  354.3 56.8 %copy-start.13 = (f32[1,8,64]{1,0,2:T(1,128)}, f32[1,8,64]{1,0,2:T(1,128)S(1)}, u32[]{:S(2)}) copy-start(f32[1,8,64]{1,0,2:T(1,128)S(1)} %all-to-all-done.5) | copy-start | bytes 6148
  354.3 62.0 %all-to-all-start.3 = ((f32[1,8,64]{1,0,2:T(1,128)}), f32[1,8,64]{1,0,2:T(1,128)S(1)}, u32[]{:S(2)}, u32[]{:S(2)}) async-start(f32[1,8,64]{1,0,2:T(1,128)} %bitcast.33), calls=%async_computation.3 | async-start | bytes 65536 | tf_op jit(solution)/shard_map/all_to_all | solution.py:159
  416.2 14.1 %all-to-all-start.4 = ((f32[8,1,8192]{2,1,0:T(1,128)}), f32[8,1,8192]{2,1,0:T(1,128)}, u32[]{:S(2)}, u32[]{:S(2)}) async-start(f32[8,1,8192]{2,1,0:T(1,128)} %reshape.1262), calls=%async_computation.4 | async-start | bytes 524288 | tf_op jit(solution)/shard_map/all_to_all | solution.py:152
  422.0 98.7 %all-reduce.9.cloned.1.call-start = ((), (), s32[]{:S(2)}) async-start(), calls=%async_computation.13 | async-start | bytes 327680 | tf_op jit(solution)/shard_map/psum | solution.py:203
  446.6 6.2 copy-start.32
  522.3 5.8 copy-start.18
  522.3 5.8 copy-start.19
  522.3 36.6 %copy-start.4 = (bf16[8,64,1024]{2,1,0:T(8,128)(2,1)S(1)}, bf16[8,64,1024]{2,1,0:T(8,128)(2,1)}, u32[]{:S(2)}) copy-start(bf16[8,64,1024]{2,1,0:T(8,128)(2,1)} %scatter_fusion.3) | copy-start | bytes 3145732
  522.3 37.6 %copy-start.7 = (bf16[8,64,1024]{2,1,0:T(8,128)(2,1)S(1)}, bf16[8,64,1024]{2,1,0:T(8,128)(2,1)}, u32[]{:S(2)}) copy-start(bf16[8,64,1024]{2,1,0:T(8,128)(2,1)} %scatter_fusion.4) | copy-start | bytes 3145732
  528.0 68.1 %copy-start.29 = (pred[8]{0:T(512)(128)(4,1)S(1)}, pred[8]{0:T(512)(128)(4,1)}, u32[]{:S(2)}) copy-start(pred[8]{0:T(512)(128)(4,1)} %get-tuple-element.179) | copy-start | bytes 28
  528.0 69.3 %copy-start.37 = (pred[4]{0:T(512)(128)(4,1)S(1)}, pred[4]{0:T(512)(128)(4,1)}, u32[]{:S(2)}) copy-start(pred[4]{0:T(512)(128)(4,1)} %iota_compare_fusion.1) | copy-start | bytes 16
  591.8 11.0 %all-to-all-start.8 = ((f32[1,8,64]{1,0,2:T(1,128)}), f32[1,8,64]{1,0,2:T(1,128)S(1)}, u32[]{:S(2)}, u32[]{:S(2)}) async-start(f32[1,8,64]{1,0,2:T(1,128)} %bitcast.80), calls=%async_computation.8 | async-start | bytes 65536 | tf_op jit(solution)/shard_map/all_to_all | solution.py:166
  602.8 0.6 copy-start.11
  603.4 50.0 %all-to-all-start.6 = ((f32[1,8,64]{1,0,2:T(1,128)}), f32[1,8,64]{1,0,2:T(1,128)S(1)}, u32[]{:S(2)}, u32[]{:S(2)}) async-start(f32[1,8,64]{1,0,2:T(1,128)} %bitcast.60), calls=%async_computation.6 | async-start | bytes 65536 | tf_op jit(solution)/shard_map/all_to_all | solution.py:159
  653.4 14.3 %all-to-all-start.7 = ((f32[8,1,8192]{2,1,0:T(1,128)}), f32[8,1,8192]{2,1,0:T(1,128)}, u32[]{:S(2)}, u32[]{:S(2)}) async-start(f32[8,1,8192]{2,1,0:T(1,128)} %reshape.1264), calls=%async_computation.7 | async-start | bytes 524288 | tf_op jit(solution)/shard_map/all_to_all | solution.py:152
  659.4 98.6 %all-reduce.11.cloned.1.call-start = ((), (), s32[]{:S(2)}) async-start(), calls=%async_computation.14 | async-start | bytes 327680 | tf_op jit(solution)/shard_map/psum | solution.py:203
  684.0 6.2 copy-start.30
  759.6 36.6 %copy-start.5 = (bf16[8,64,1024]{2,1,0:T(8,128)(2,1)S(1)}, bf16[8,64,1024]{2,1,0:T(8,128)(2,1)}, u32[]{:S(2)}) copy-start(bf16[8,64,1024]{2,1,0:T(8,128)(2,1)} %scatter_fusion.3) | copy-start | bytes 3145732
  759.6 37.6 %copy-start.8 = (bf16[8,64,1024]{2,1,0:T(8,128)(2,1)S(1)}, bf16[8,64,1024]{2,1,0:T(8,128)(2,1)}, u32[]{:S(2)}) copy-start(bf16[8,64,1024]{2,1,0:T(8,128)(2,1)} %scatter_fusion.4) | copy-start | bytes 3145732
  765.3 68.1 %copy-start.27 = (pred[8]{0:T(512)(128)(4,1)S(1)}, pred[8]{0:T(512)(128)(4,1)}, u32[]{:S(2)}) copy-start(pred[8]{0:T(512)(128)(4,1)} %get-tuple-element.106) | copy-start | bytes 28
  765.3 69.6 %copy-start.17 = (pred[8]{0:T(512)(128)(4,1)S(1)}, pred[8]{0:T(512)(128)(4,1)}, u32[]{:S(2)}) copy-start(pred[8]{0:T(512)(128)(4,1)} %copy-done.16) | copy-start | bytes 28
  765.3 70.0 %copy-start.36 = (pred[4]{0:T(512)(128)(4,1)S(1)}, pred[4]{0:T(512)(128)(4,1)}, u32[]{:S(2)}) copy-start(pred[4]{0:T(512)(128)(4,1)} %iota_compare_fusion) | copy-start | bytes 16
  829.1 11.0 %all-to-all-start.11 = ((f32[1,8,64]{1,0,2:T(1,128)}), f32[1,8,64]{1,0,2:T(1,128)S(1)}, u32[]{:S(2)}, u32[]{:S(2)}) async-start(f32[1,8,64]{1,0,2:T(1,128)} %bitcast.107), calls=%async_computation.11 | async-start | bytes 65536 | tf_op jit(solution)/shard_map/all_to_all | solution.py:166
  840.1 49.8 %all-to-all-start.9 = ((f32[1,8,64]{1,0,2:T(1,128)}), f32[1,8,64]{1,0,2:T(1,128)S(1)}, u32[]{:S(2)}, u32[]{:S(2)}) async-start(f32[1,8,64]{1,0,2:T(1,128)} %bitcast.87), calls=%async_computation.9 | async-start | bytes 65536 | tf_op jit(solution)/shard_map/all_to_all | solution.py:159
  889.8 14.3 %all-to-all-start.10 = ((f32[8,1,8192]{2,1,0:T(1,128)}), f32[8,1,8192]{2,1,0:T(1,128)}, u32[]{:S(2)}, u32[]{:S(2)}) async-start(f32[8,1,8192]{2,1,0:T(1,128)} %reshape.1266), calls=%async_computation.10 | async-start | bytes 524288 | tf_op jit(solution)/shard_map/all_to_all | solution.py:152
  895.8 97.1 %all-reduce.13.cloned.1.call-start = ((), (), s32[]{:S(2)}) async-start(), calls=%async_computation.15 | async-start | bytes 327680 | tf_op jit(solution)/shard_map/psum | solution.py:203
  918.8 6.2 copy-start.14
  918.8 6.2 copy-start.15
  918.8 6.3 copy-start.23
  918.8 6.3 copy-start.24
  918.8 6.3 copy-start.25
  918.8 74.1 %copy-start.28 = (pred[8]{0:T(512)(128)(4,1)S(1)}, pred[8]{0:T(512)(128)(4,1)}, u32[]{:S(2)}) copy-start(pred[8]{0:T(512)(128)(4,1)} %get-tuple-element.106) | copy-start | bytes 28
Sparse Core Ops, SparseCore 0:
  203.7 67.6 all-reduce.6
  452.9 67.7 all-reduce.8
  690.3 67.6 all-reduce.10
  925.1 67.7 all-reduce.12
where the time goes:
time: 1010 us; the launch traced here: 1000 us
  waiting for transfers between devices  311 us (31%)
  blocking collectives  245 us (24%)
  other arithmetic  197 us (20%)
  local copies, waits for them, and re-layouts  105 us (10%)
  starting transfers between devices  71.3 us (7%)
  matrix products  57.1 us (6%)
  between operations  14.9 us (1%)
    psum x4, waiting for transfers between devices, per_device(): lax.psum(jnp.dot(attended, w_output, preferred_element_type=jnp.float32),...  269 us
    unnamed x8, other arithmetic  154 us
    all_gather x4, blocking collectives, per_device(): raw_full = lax.all_gather(raw_part, 'mp', axis=1, tiled=True)  123 us
    all_gather x4, blocking collectives, per_device(): lax.all_gather(queries.reshape(seq_count, heads_here * head_dim), 'mp', a...  122 us
    unnamed x96, local copies, waits for them, and re-layouts  67 us
    all_to_all x4, starting transfers between devices, per_device(): lax.all_to_all(local_max.reshape(1, seq_count, -1), 'mp', split_axis=2, c...  27.3 us
    all_to_all x4, waiting for transfers between devices, per_device(): lax.all_to_all(numerator.reshape(1, seq_count, -1), 'mp', split_axis=2, c...  27 us
    dot_general x4, matrix products, per_device(): jnp.dot(attended, w_output, preferred_element_type=jnp.float32)  24.6 us
  transfers between devices with their start and end apart: 19, of which 12 were waited for; matrix products, arithmetic and copies ran while one was open for 23% of the time, Pallas kernels for 0%

commit v1 on v0

v1 whole, which is shorter than its diff:
```python
import functools
import math

import jax
import jax.numpy as jnp
from jax import lax
from jax.experimental import pallas as pl
from jax.experimental.pallas import tpu as pltpu
from jax.sharding import PartitionSpec as P

HD = 128
STEPS = 4
KERNEL_VMEM = 18 * 2**20


rope_base = 1000000.0
norm_eps = 1e-06

in_vmem = pl.BlockSpec(memory_space=pltpu.VMEM)
in_smem = pl.BlockSpec(memory_space=pltpu.SMEM)
in_place = pl.BlockSpec(memory_space=pl.ANY)


def exchange(block, axis, mask):
    count = lax.axis_size(axis)
    return lax.ppermute(block, axis, [(low, low ^ mask) for low in range(count)])


def root_norm(values):
    return values * lax.rsqrt(jnp.mean(values * values, axis=-1, keepdims=True) + norm_eps)


def turn(values, cosine, sine):
    return values * cosine + pltpu.roll(values, values.shape[-1] // 2, 1) * sine


def pack_kernel(index_ref, keys_ref, values_ref, *rest):
    outs, sems = rest[:-1], rest[-1]
    me = index_ref[0]
    copies = []
    for step, out in enumerate(outs):
        head = pl.multiple_of((me ^ step) * HD, HD)
        for which, source in enumerate((keys_ref, values_ref)):
            copies.append(
                pltpu.make_async_copy(
                    source.at[:, :, pl.ds(head, HD)], out.at[which], sems.at[2 * step + which]
                )
            )
    for copy in copies:
        copy.start()
    for copy in copies:
        copy.wait()


def norm_kernel(has_update, *refs):
    if has_update:
        hidden_ref, first_ref, second_ref, active_before_ref, *refs = refs
    else:
        hidden_ref, *refs = refs
    gain_ref, w_ref, hidden_out, normed_out, raw_out = refs
    hidden = hidden_ref[...].astype(jnp.float32)
    if has_update:
        update = first_ref[...].astype(jnp.float32) + second_ref[...].astype(jnp.float32)
        keep = active_before_ref[:, :1] > 0.0
        hidden = jnp.where(keep, hidden + update, hidden).astype(jnp.bfloat16)
        hidden_out[...] = hidden
        hidden = hidden.astype(jnp.float32)
    else:
        hidden_out[...] = hidden_ref[...]
    normed = (root_norm(hidden) * gain_ref[...]).astype(jnp.bfloat16)
    normed_out[...] = normed
    raw_out[...] = jnp.dot(normed, w_ref[...], preferred_element_type=jnp.float32).astype(
        jnp.bfloat16
    )


def key_kernel(index_ref, raw_ref, cos_ref, sin_ref, active_ref, both_out, a_out, b_out):
    is_key = index_ref[1] == 1
    live = active_ref[...] > 0.0
    done = []
    for head in range(2):
        raw = raw_ref[:, head * HD : (head + 1) * HD].astype(jnp.float32)
        turned = turn(root_norm(raw), cos_ref[...], sin_ref[...])
        chosen = jnp.where(is_key, turned, raw)
        done.append(jnp.where(live, chosen, 0.0).astype(jnp.bfloat16))
        both_out[:, head * HD : (head + 1) * HD] = done[head]
    a_out[...] = jnp.where(is_key, done[0], done[1])
    b_out[...] = jnp.where(is_key, done[1], done[0])


def query_kernel(
    block_count,
    lengths_ref,
    normed_ref,
    w_ref,
    cos_ref,
    sin_ref,
    places_ref,
    *rest,
):
    caches, rest = rest[:block_count], rest[block_count:]
    query_out, num_out, max_out, den_out = rest
    seq_count = normed_ref.shape[0]
    heads = w_ref.shape[1] // HD
    projected = jnp.dot(normed_ref[...], w_ref[...], preferred_element_type=jnp.float32)
    for head in range(heads):
        piece = projected[:, head * HD : (head + 1) * HD]
        turned = turn(root_norm(piece), cos_ref[...], sin_ref[...])
        query_out[head] = turned.astype(jnp.bfloat16).astype(jnp.float32)
    places = places_ref[...]

    def rows(which, seq):
        return jnp.concatenate(
            [ref[which, seq] if ref.ndim == 4 else ref[:, which, seq].reshape(-1, HD) for ref in caches],
            axis=0,
        )

    for seq in range(seq_count):
        query = query_out[:, seq, :].astype(jnp.bfloat16)
        scores = lax.dot_general(
            query, rows(0, seq), (((1,), (1,)), ((), ())), preferred_element_type=jnp.float32
        ) * (1.0 / math.sqrt(HD))
        valid = places < lengths_ref[seq]
        top = jnp.max(jnp.where(valid, scores, -1e30), axis=-1, keepdims=True)
        weights = jnp.where(valid, jnp.exp(scores - top), 0.0).astype(jnp.bfloat16)
        mass = jnp.sum(weights.astype(jnp.float32), axis=-1, keepdims=True)
        num_out[:, seq, :] = jnp.dot(weights, rows(1, seq), preferred_element_type=jnp.float32)
        max_out[:, seq, :] = jnp.broadcast_to(top, (heads, HD))
        den_out[:, seq, :] = jnp.broadcast_to(mass, (heads, HD))


def output_kernel(fresh_count, query_ref, num_ref, max_ref, den_ref, w_ref, *rest):
    fresh, out_ref = rest[:-1], rest[-1]
    heads = query_ref.shape[0]
    keys = [ref[...].astype(jnp.float32) for ref in fresh[:fresh_count]]
    values = [ref[...].astype(jnp.float32) for ref in fresh[fresh_count:]]
    attended = []
    for head in range(heads):
        query = query_ref[head]
        scores = [
            jnp.sum(query * key, axis=-1, keepdims=True) * (1.0 / math.sqrt(HD)) for key in keys
        ]
        top_old = max_ref[head]
        top = functools.reduce(jnp.maximum, scores, top_old)
        scale = jnp.exp(top_old - top)
        num = scale * num_ref[head]
        den = scale * den_ref[head]
        for score, value in zip(scores, values):
            weight = jnp.exp(score - top).astype(jnp.bfloat16).astype(jnp.float32)
            num = num + weight * value
            den = den + weight
        attended.append((num / den).astype(jnp.bfloat16))
    out_ref[...] = jnp.dot(
        jnp.concatenate(attended, axis=1), w_ref[...], preferred_element_type=jnp.float32
    ).astype(jnp.bfloat16)


def sum_rounds(part, axis):
    masks = [1 << bit for bit in range(lax.axis_size(axis).bit_length() - 1)]
    rounds = [masks[at : at + 2] for at in range(0, len(masks), 2)]
    if len(rounds[-1]) == 2:
        rounds = rounds[:-1] + [rounds[-1][:1], rounds[-1][1:]]
    for masks_now in rounds[:-1]:
        if len(masks_now) == 1:
            total = part.astype(jnp.float32) + exchange(part, axis, masks_now[0]).astype(jnp.float32)
        else:
            low, high = masks_now
            near = exchange(part, axis, low)
            far = exchange(part, axis, high)
            both = exchange(part, axis, low | high)
            total = (part.astype(jnp.float32) + near.astype(jnp.float32)) + (
                far.astype(jnp.float32) + both.astype(jnp.float32)
            )
        part = total.astype(jnp.bfloat16)
    return part, exchange(part, axis, rounds[-1][0])


def trade(own, other, slots_here, slots_there, axis):
    rows = jnp.arange(own.shape[axis])
    hits = slots_here[None, :] == rows[:, None]
    picks = jnp.any(
        hits[:, :, None] & (slots_there[None, :, None] == rows[None, None, :]), axis=1
    ).astype(own.dtype)
    moved = jnp.tensordot(picks, other, axes=((1,), (axis,)), preferred_element_type=jnp.float32)
    moved = jnp.moveaxis(moved, 0, axis).astype(own.dtype)
    shape = [1] * own.ndim
    shape[axis] = -1
    return jnp.where(jnp.any(hits, axis=1).reshape(shape), moved, own)


def per_device(
    hidden_in,
    norm_gain,
    w_query,
    w_key_value,
    w_output,
    cache_keys,
    cache_values,
    cache_lengths,
    remaining_steps,
    move_from,
    move_to,
):
    bf16, f32 = jnp.bfloat16, jnp.float32
    seq_count, width = hidden_in.shape
    model_size = lax.axis_size("mp")
    model_index = lax.axis_index("mp")
    group_index = lax.axis_index("dp")
    heads_here = w_query.shape[1] // HD
    kv_width = cache_keys.shape[2]
    kv_heads = kv_width // HD
    block_len = cache_keys.shape[1]
    col_width = w_key_value.shape[1]
    one_head_each = model_size == kv_heads and col_width == 2 * HD

    lengths = lax.dynamic_slice_in_dim(cache_lengths, group_index * seq_count, seq_count)
    remaining = lax.dynamic_slice_in_dim(remaining_steps, group_index * seq_count, seq_count)
    own_head = model_index * kv_heads // model_size
    flags = jnp.stack([model_index, (model_index < model_size // 2).astype(jnp.int32)])

    if one_head_each:
        shape = jax.ShapeDtypeStruct((2, seq_count, block_len, HD), bf16)
        packed = pl.pallas_call(
            pack_kernel,
            out_shape=[shape] * model_size,
            in_specs=[in_smem, in_place, in_place],
            out_specs=[in_place] * model_size,
            scratch_shapes=[pltpu.SemaphoreType.DMA((2 * model_size,))],
        )(flags, cache_keys, cache_values)
        order = sorted(range(1, model_size), key=lambda mask: mask < model_size // 2)
        blocks = {0: packed[0]}
        for mask in order:
            blocks[mask] = exchange(packed[mask], "mp", mask)
        caches = [blocks[mask] for mask in range(model_size)]
        block_index = jnp.stack([model_index ^ mask for mask in range(model_size)])
    else:
        both = jnp.stack([cache_keys, cache_values]).reshape(
            2, seq_count, block_len, kv_heads, HD
        )
        to_all = jnp.repeat(jnp.moveaxis(both, 3, 0), model_size // kv_heads, axis=0)
        caches = [lax.all_to_all(to_all, "mp", 0, 0, tiled=True)]
        block_index = jnp.arange(model_size)
    places = (block_index[:, None] * block_len + jnp.arange(block_len)[None, :]).reshape(1, -1)

    half = HD // 2
    frequency = rope_base ** (-jnp.arange(half).astype(f32) * 2.0 / HD)
    cosines, sines, actives = [], [], []
    for step_index in range(STEPS):
        angles = (lengths + step_index).astype(f32)[:, None] * frequency[None, :]
        cosines.append(jnp.concatenate([jnp.cos(angles)] * 2, axis=1))
        sine = jnp.sin(angles)
        sines.append(jnp.concatenate([-sine, sine], axis=1))
        actives.append(
            jnp.broadcast_to((remaining > step_index).astype(f32)[:, None], (seq_count, HD))
        )

    gain = norm_gain.reshape(1, width)
    hidden = hidden_in
    terms = ()
    fresh_keys, fresh_values, kv_outputs = [], [], []
    row_f32 = jax.ShapeDtypeStruct((heads_here, seq_count, HD), f32)
    row_bf16 = jax.ShapeDtypeStruct((seq_count, width), bf16)
    for step_index in range(STEPS):
        hidden, normed, raw = pl.pallas_call(
            functools.partial(norm_kernel, step_index > 0),
            out_shape=[row_bf16, row_bf16, jax.ShapeDtypeStruct((seq_count, col_width), bf16)],
            in_specs=[in_vmem] * (6 if step_index > 0 else 3),
            out_specs=[in_vmem] * 3,
            compiler_params=pltpu.CompilerParams(vmem_limit_bytes=KERNEL_VMEM),
        )(
            hidden,
            *terms,
            *([actives[step_index - 1]] if step_index > 0 else []),
            gain,
            w_key_value,
        )
        if one_head_each:
            head_row = jax.ShapeDtypeStruct((seq_count, HD), bf16)
            both, sent_a, sent_b = pl.pallas_call(
                key_kernel,
                out_shape=[jax.ShapeDtypeStruct((seq_count, col_width), bf16), head_row, head_row],
                in_specs=[in_smem] + [in_vmem] * 4,
                out_specs=[in_vmem] * 3,
            )(flags, raw, cosines[step_index], sines[step_index], actives[step_index])
            kv_outputs.append(both)
            pairs = model_size // 2
            got_a = lax.ppermute(
                sent_a,
                "mp",
                [(low, 2 * low) for low in range(pairs)]
                + [(pairs + low, 2 * low + 1) for low in range(pairs)],
            )
            got_b = lax.ppermute(
                sent_b,
                "mp",
                [(low, 2 * low + 1) for low in range(pairs)]
                + [(pairs + low, 2 * low) for low in range(pairs)],
            )
            even = model_index % 2 == 0
            new_key = jnp.where(even, got_a, got_b)
            new_value = jnp.where(even, got_b, got_a)
        else:
            raw_full = lax.all_gather(raw, "mp", axis=1, tiled=True)
            key_part = raw_full[:, :kv_width].astype(f32).reshape(seq_count, kv_heads, HD)
            key_part = root_norm(key_part)
            swapped = jnp.concatenate([key_part[..., half:], key_part[..., :half]], axis=-1)
            new_keys = (
                key_part * cosines[step_index][:, None, :] + swapped * sines[step_index][:, None, :]
            ).astype(bf16)
            new_values = raw_full[:, kv_width:].reshape(seq_count, kv_heads, HD)
            live = (remaining > step_index)[:, None, None]
            new_kv = jnp.where(live, jnp.concatenate([new_keys, new_values], axis=1), 0)
            kv_outputs.append(
                lax.dynamic_slice_in_dim(
                    new_kv.reshape(seq_count, 2 * kv_width), model_index * col_width, col_width, 1
                )
            )
            new_key = lax.dynamic_index_in_dim(new_kv, own_head, 1, False)
            new_value = lax.dynamic_index_in_dim(new_kv, kv_heads + own_head, 1, False)
        fresh_keys.append(new_key)
        fresh_values.append(new_value)
        queries, num, top, den = pl.pallas_call(
            functools.partial(query_kernel, len(caches)),
            out_shape=[row_f32] * 4,
            in_specs=[in_smem] + [in_vmem] * (5 + len(caches)),
            out_specs=[in_vmem] * 4,
            cost_estimate=pl.CostEstimate(
                flops=2 * seq_count * width * heads_here * HD,
                bytes_accessed=2 * width * heads_here * HD,
                transcendentals=0,
            ),
            compiler_params=pltpu.CompilerParams(vmem_limit_bytes=KERNEL_VMEM),
        )(lengths, normed, w_query, cosines[step_index], sines[step_index], places, *caches)
        part = pl.pallas_call(
            functools.partial(output_kernel, step_index + 1),
            out_shape=row_bf16,
            in_specs=[in_vmem] * (5 + 2 * (step_index + 1)),
            out_specs=in_vmem,
            compiler_params=pltpu.CompilerParams(vmem_limit_bytes=KERNEL_VMEM),
        )(queries, num, top, den, w_output, *fresh_keys, *fresh_values)
        terms = sum_rounds(part, "mp")
    update = terms[0].astype(f32) + terms[1].astype(f32)
    hidden_float = hidden.astype(f32)
    hidden = jnp.where(
        (remaining > STEPS - 1)[:, None], hidden_float + update, hidden_float
    ).astype(bf16)
    kv_local = jnp.stack(kv_outputs)

    slots_here = jnp.where(group_index == 0, move_from, move_to)
    slots_there = jnp.where(group_index == 0, move_to, move_from)
    other_kv = exchange(kv_local, "dp", 1)
    other_hidden = exchange(hidden, "dp", 1)
    return (
        trade(hidden, other_hidden, slots_here, slots_there, 0),
        trade(kv_local, other_kv, slots_here, slots_there, 1),
    )


def solution(mesh):
    placed = (
        P(("parts", "dp"), None),
        P(),
        P(None, "mp"),
        P(None, "mp"),
        P("mp", None),
        P(("parts", "dp"), "mp", None),
        P(("parts", "dp"), "mp", None),
        P("parts"),
        P("parts"),
        P("parts"),
        P("parts"),
    )
    return jax.shard_map(
        per_device,
        mesh=mesh,
        in_specs=placed,
        out_specs=(P(("parts", "dp"), None), P(None, ("parts", "dp"), "mp")),
        check_vma=False,
    )
```

time: 1010 us -> 297 us (0.29)
  waiting for transfers between devices: 311 us -> 53.9 us
  blocking collectives: 245 us -> 0 us
  other arithmetic: 197 us -> 9.38 us
  Pallas kernels: 0 us -> 97 us
  matrix products: 57.1 us -> 1.52 us
  local copies, waits for them, and re-layouts: 105 us -> 66.7 us
  between operations: 14.9 us -> 1.05 us
    psum x4 -> x0, waiting for transfers between devices: 269 us -> none  [per_device(): lax.psum(jnp.dot(attended, w_output, preferred_element_type=jnp.float32),...]
    all_gather x8 -> x0, blocking collectives: 245 us -> none  [the longest x4 123 us: per_device(): raw_full = lax.all_gather(raw_part, 'mp', axis=1, tiled=True)]
    unnamed x8 -> x0, other arithmetic: 154 us -> none
    pallas_call x0 -> x17, Pallas kernels: none -> 97 us  [the longest x1 65.4 us: per_device(): pl.pallas_call(pack_kernel, out_shape=[shape] * model_size, in_specs=[in_...]
    all_to_all x12 -> x0, starting transfers between devices: 69.6 us -> none  [the longest x4 27.3 us: per_device(): lax.all_to_all(local_max.reshape(1, seq_count, -1), 'mp', split_axis=2, c...]
    ppermute x3 -> x33, starting transfers between devices: 1.03 us -> 65.3 us  [the longest x25 44.8 us: exchange(): lax.ppermute(block, axis, [(low, low ^ mask) for low in range(count)])]
    dot_general x24 -> x2, matrix products: 57.1 us -> 1.52 us  [trade(): jnp.tensordot(picks, other, axes=((1,), (axis,)), preferred_element_type=...]
    ppermute x3 -> x33, waiting for transfers between devices: 0.01 us -> 53.9 us  [the longest x25 53.8 us: exchange(): lax.ppermute(block, axis, [(low, low ^ mask) for low in range(count)])]
  transfers between devices with their start and end apart: 19 -> 33, of which waited for: 12 -> 18; matrix products, arithmetic and copies ran while one was open for 23% -> 3% of each run, Pallas kernels for 0% -> 5%
where the time goes in v1:
time: 297 us; the launch traced here: 295 us
  Pallas kernels  97 us (33%)
  local copies, waits for them, and re-layouts  66.7 us (22%)
  starting transfers between devices  65.3 us (22%)
  waiting for transfers between devices  53.9 us (18%)
  other arithmetic  9.38 us (3%)
    pallas_call x1, Pallas kernels, per_device(): pl.pallas_call(pack_kernel, out_shape=[shape] * model_size, in_specs=[in_...  65.4 us
    unnamed x160, local copies, waits for them, and re-layouts  63.9 us
    ppermute x25, waiting for transfers between devices, exchange(): lax.ppermute(block, axis, [(low, low ^ mask) for low in range(count)])  53.8 us
    ppermute x25, starting transfers between devices, exchange(): lax.ppermute(block, axis, [(low, low ^ mask) for low in range(count)])  44.8 us
    pallas_call x4, Pallas kernels, per_device(): pl.pallas_call(functools.partial(query_kernel, len(caches)), out_shape=[r...  16.7 us
    ppermute x4, starting transfers between devices, per_device(): lax.ppermute(sent_b, 'mp', [(low, 2 * low + 1) for low in range(pairs)] +...  15.2 us
    pallas_call x4, Pallas kernels, per_device(): pl.pallas_call(key_kernel, out_shape=[jax.ShapeDtypeStruct((seq_count, co...  6.24 us
    pallas_call x4, Pallas kernels, per_device(): pl.pallas_call(functools.partial(output_kernel, step_index + 1), out_shap...  6.17 us
  transfers between devices with their start and end apart: 33, of which 18 were waited for; matrix products, arithmetic and copies ran while one was open for 3% of the time, Pallas kernels for 5%

profile of v1, /device:TPU:0, one launch (start us, length us, event | category | flops | bytes accessed | tf_op | source)
XLA Modules:
  0.0 294.8 jit_solution(5075674744307217315)
XLA Ops:
  1.3 65.4 %shard_map.123 = (bf16[2,8,64,128]{3,2,1,0:T(8,128)(2,1)}, bf16[2,8,64,128]{3,2,1,0:T(8,128)(2,1)}, bf16[2,8,64,128]{3,2,1,0:T(8,128)(2,1)}, bf16[2,8,64,128]{3,...) custom-call(s32[2]{0:T(128)} %pad_add_fusion.index_ref, ...), custom_call_target="tpu_custom_call" | custom-call | tf_op jit(solution)/shard_map/pallas_call | solution.py:223
  66.7 3.0 %collective-permute-start = (bf16[2,8,64,128]{3,2,1,0:T(8,128)(2,1)}, bf16[2,8,64,128]{3,2,1,0:T(8,128)(2,1)S(1)}, u32[]{:S(2)}, u32[]{:S(2)}) collective-permute-start(bf16[2,8,64,128]{3,2,1,0:T(8,128)(2,1)} %get-tuple-element.53), channel_id=1, source_target_pairs={{0,1},{1,0},{2,3},{3,2},{4,5},{5,4},{6,7},{7,6},{8,9},{9,8},{10,11... | collective-permute-start | bytes 786440 | tf_op jit(solution)/shard_map/ppermute | solution.py:26
  69.8 1.6 collective-permute-start.1
  72.1 1.2 broadcast_compare_fusion
  75.3 1.7 copy-done.8
  80.5 1.6 shard_map.125
  82.1 1.3 collective-permute-start.7
  83.4 4.0 %collective-permute-start.8 = (bf16[8,128]{1,0:T(8,128)(2,1)}, bf16[8,128]{1,0:T(8,128)(2,1)S(1)}, u32[]{:S(2)}, u32[]{:S(2)}) collective-permute-start(bf16[8,128]{1,0:T(8,128)(2,1)} %get-tuple-element.66), channel_id=1, source_target_pairs={{0,1},{1,3},{2,5},{3,7},{4,0},{5,2},{6,4},{7,6},{8,9},{9,11},{10,1... | collective-permute-start | bytes 6152 | tf_op jit(solution)/shard_map/ppermute | solution.py:293
  87.5 3.2 %collective-permute-start.3 = (bf16[2,8,64,128]{3,2,1,0:T(8,128)(2,1)}, bf16[2,8,64,128]{3,2,1,0:T(8,128)(2,1)S(1)}, u32[]{:S(2)}, u32[]{:S(2)}) collective-permute-start(bf16[2,8,64,128]{3,2,1,0:T(8,128)(2,1)} %get-tuple-element.56), channel_id=1, source_target_pairs={{0,4},{1,5},{2,6},{3,7},{4,0},{5,1},{6,2},{7,3},{8,12},{9,13},{10,... | collective-permute-start | bytes 786440 | tf_op jit(solution)/shard_map/ppermute | solution.py:26
  90.7 3.1 %collective-permute-start.4 = (bf16[2,8,64,128]{3,2,1,0:T(8,128)(2,1)}, bf16[2,8,64,128]{3,2,1,0:T(8,128)(2,1)S(1)}, u32[]{:S(2)}, u32[]{:S(2)}) collective-permute-start(bf16[2,8,64,128]{3,2,1,0:T(8,128)(2,1)} %get-tuple-element.57), channel_id=1, source_target_pairs={{0,5},{1,4},{2,7},{3,6},{4,1},{5,0},{6,3},{7,2},{8,13},{9,12},{10,... | collective-permute-start | bytes 786440 | tf_op jit(solution)/shard_map/ppermute | solution.py:26
  93.8 1.8 collective-permute-start.5
  95.7 1.8 collective-permute-start.6
  98.3 22.3 %collective-permute-done.3.rest_4_ = bf16[2,8,64,128]{3,2,1,0:T(8,128)(2,1)S(1)} collective-permute-done((bf16[2,8,64,128]{3,2,1,0:T(8,128)(2,1)}, bf16[2,8,64,128]{3,2,1,0:T(8,128)(2,1)S(1)}, u32[]{:S(2)}, u32[]{:S(2)}) %collective-permute-start.3) | collective-permute-done | bytes 262176 | tf_op jit(solution)/shard_map/ppermute | solution.py:26
  121.3 4.7 %collective-permute-done.4.rest_5_ = bf16[2,8,64,128]{3,2,1,0:T(8,128)(2,1)S(1)} collective-permute-done((bf16[2,8,64,128]{3,2,1,0:T(8,128)(2,1)}, bf16[2,8,64,128]{3,2,1,0:T(8,128)(2,1)S(1)}, u32[]{:S(2)}, u32[]{:S(2)}) %collective-permute-start.4) | collective-permute-done | bytes 262176 | tf_op jit(solution)/shard_map/ppermute | solution.py:26
  128.1 4.0 %copy-done = bf16[5120,1024]{1,0:T(8,128)(2,1)S(1)} copy-done((bf16[5120,1024]{1,0:T(8,128)(2,1)S(1)}, bf16[5120,1024]{1,0:T(8,128)(2,1)}, u32[]{:S(2)}) %copy-start) | copy-done | bytes 10485784
  132.1 0.9 copy-done.10
  133.0 0.9 copy-done.13
  134.9 0.9 copy-done.23
  139.2 4.2 %shard_map.124 = (f32[8,8,128]{2,1,0:T(8,128)S(1)}, f32[8,8,128]{2,1,0:T(8,128)S(1)}, f32[8,8,128]{2,1,0:T(8,128)S(1)}, f32[8,8,128]{2,1,0:T(8,128)S(1)}) custom-call(s32[8]{0:T(128)S(1)} %get-tuple-element.101.lengths_ref, bf16[8,5120]{1,0:T(8,128)(2,1)S(1)} %get-tuple-element.51.normed_ref, bf16[5120,1024]{1,0:T(8,128)(2,1)S(1)} %copy-done, ...), custom_call_target="tpu_custom_call" | custom-call | flops 83886080 | bytes 10485760 | tf_op jit(solution)/shard_map/pallas_call | solution.py:322
  143.4 1.5 shard_map.126
  144.9 10.3 %collective-permute-start.10 = (bf16[8,5120]{1,0:T(8,128)(2,1)S(1)}, bf16[8,5120]{1,0:T(8,128)(2,1)S(1)}, u32[]{:S(2)}, u32[]{:S(2)}) collective-permute-start(bf16[8,5120]{1,0:T(8,128)(2,1)S(1)} %shard_map.126), channel_id=1, source_target_pairs={{0,2},{1,3},{2,0},{3,1},{4,6},{5,7},{6,4},{7,5},{8,10},{9,11},{10,... | collective-permute-start | bytes 245768 | tf_op jit(solution)/shard_map/ppermute | solution.py:26
  155.2 1.5 collective-permute-start.9
  157.3 1.2 collective-permute-done.10
  158.5 2.2 collective-permute-done.11
  161.1 1.9 collective-permute-start.12
  163.7 4.3 %collective-permute-done.12.refs_2_ = bf16[8,5120]{1,0:T(8,128)(2,1)S(1)} collective-permute-done((bf16[8,5120]{1,0:T(8,128)(2,1)S(1)}, bf16[8,5120]{1,0:T(8,128)(2,1)S(1)}, u32[]{:S(2)}, u32[]{:S(2)}) %collective-permute-start.12) | collective-permute-done | bytes 81952 | tf_op jit(solution)/shard_map/ppermute | solution.py:26
  169.9 1.6 shard_map.129
  171.5 1.3 collective-permute-start.13
  172.8 1.9 collective-permute-start.14
  174.7 4.0 %copy-done.1 = bf16[5120,1024]{1,0:T(8,128)(2,1)S(1)} copy-done((bf16[5120,1024]{1,0:T(8,128)(2,1)S(1)}, bf16[5120,1024]{1,0:T(8,128)(2,1)}, u32[]{:S(2)}) %copy-start.1) | copy-done | bytes 10485784
  184.8 4.2 %shard_map.128 = (f32[8,8,128]{2,1,0:T(8,128)S(1)}, f32[8,8,128]{2,1,0:T(8,128)S(1)}, f32[8,8,128]{2,1,0:T(8,128)S(1)}, f32[8,8,128]{2,1,0:T(8,128)S(1)}) custom-call(s32[8]{0:T(128)S(1)} %get-tuple-element.101.lengths_ref, bf16[8,5120]{1,0:T(8,128)(2,1)S(1)} %get-tuple-element.68.normed_ref, bf16[5120,1024]{1,0:T(8,128)(2,1)S(1)} %copy-done.1, ...), custom_call_target="tpu_custom_call" | custom-call | flops 83886080 | bytes 10485760 | tf_op jit(solution)/shard_map/pallas_call | solution.py:322
  189.0 4.0 %copy-done.5 = bf16[1024,5120]{1,0:T(8,128)(2,1)S(1)} copy-done((bf16[1024,5120]{1,0:T(8,128)(2,1)S(1)}, bf16[1024,5120]{1,0:T(8,128)(2,1)}, u32[]{:S(2)}) %copy-start.5) | copy-done | bytes 10485784
  193.0 1.5 shard_map.130
  194.5 2.3 collective-permute-start.15
  196.8 1.5 collective-permute-start.17
  198.3 1.1 fusion.10
  199.4 1.8 collective-permute-done.16
  202.2 2.6 collective-permute-start.18
  205.5 2.1 collective-permute-done.18.refs_2_
  210.1 1.6 shard_map.133
  211.7 1.3 collective-permute-start.19
  213.0 5.1 %collective-permute-start.20 = (bf16[8,128]{1,0:T(8,128)(2,1)}, bf16[8,128]{1,0:T(8,128)(2,1)S(1)}, u32[]{:S(2)}, u32[]{:S(2)}) collective-permute-start(bf16[8,128]{1,0:T(8,128)(2,1)} %get-tuple-element.84), channel_id=1, source_target_pairs={{0,1},{1,3},{2,5},{3,7},{4,0},{5,2},{6,4},{7,6},{8,9},{9,11},{10,1... | collective-permute-start | bytes 6152 | tf_op jit(solution)/shard_map/ppermute | solution.py:293
  218.1 4.0 %copy-done.2 = bf16[5120,1024]{1,0:T(8,128)(2,1)S(1)} copy-done((bf16[5120,1024]{1,0:T(8,128)(2,1)S(1)}, bf16[5120,1024]{1,0:T(8,128)(2,1)}, u32[]{:S(2)}) %copy-start.2) | copy-done | bytes 10485784
  228.2 4.2 %shard_map.132 = (f32[8,8,128]{2,1,0:T(8,128)S(1)}, f32[8,8,128]{2,1,0:T(8,128)S(1)}, f32[8,8,128]{2,1,0:T(8,128)S(1)}, f32[8,8,128]{2,1,0:T(8,128)S(1)}) custom-call(s32[8]{0:T(128)S(1)} %get-tuple-element.101.lengths_ref, bf16[8,5120]{1,0:T(8,128)(2,1)S(1)} %get-tuple-element.77.normed_ref, bf16[5120,1024]{1,0:T(8,128)(2,1)S(1)} %copy-done.2, ...), custom_call_target="tpu_custom_call" | custom-call | flops 83886080 | bytes 10485760 | tf_op jit(solution)/shard_map/pallas_call | solution.py:322
  232.5 4.0 %copy-done.6 = bf16[1024,5120]{1,0:T(8,128)(2,1)S(1)} copy-done((bf16[1024,5120]{1,0:T(8,128)(2,1)S(1)}, bf16[1024,5120]{1,0:T(8,128)(2,1)}, u32[]{:S(2)}) %copy-start.6) | copy-done | bytes 10485784
  236.4 1.5 shard_map.134
  238.0 2.1 collective-permute-start.21
  240.1 1.5 collective-permute-start.23
  242.5 2.0 collective-permute-done.22
  245.5 1.1 collective-permute-start.24
  247.3 3.6 %collective-permute-done.24.refs_2_ = bf16[8,5120]{1,0:T(8,128)(2,1)S(1)} collective-permute-done((bf16[8,5120]{1,0:T(8,128)(2,1)S(1)}, bf16[8,5120]{1,0:T(8,128)(2,1)S(1)}, u32[]{:S(2)}, u32[]{:S(2)}) %collective-permute-start.24) | collective-permute-done | bytes 81952 | tf_op jit(solution)/shard_map/ppermute | solution.py:26
  253.4 1.6 shard_map.137
  255.0 1.3 collective-permute-start.25
  256.3 4.1 %collective-permute-start.26 = (bf16[8,128]{1,0:T(8,128)(2,1)}, bf16[8,128]{1,0:T(8,128)(2,1)S(1)}, u32[]{:S(2)}, u32[]{:S(2)}) collective-permute-start(bf16[8,128]{1,0:T(8,128)(2,1)} %get-tuple-element.93), channel_id=1, source_target_pairs={{0,1},{1,3},{2,5},{3,7},{4,0},{5,2},{6,4},{7,6},{8,9},{9,11},{10,1... | collective-permute-start | bytes 6152 | tf_op jit(solution)/shard_map/ppermute | solution.py:293
  260.4 4.0 %copy-done.3 = bf16[5120,1024]{1,0:T(8,128)(2,1)S(1)} copy-done((bf16[5120,1024]{1,0:T(8,128)(2,1)S(1)}, bf16[5120,1024]{1,0:T(8,128)(2,1)}, u32[]{:S(2)}) %copy-start.3) | copy-done | bytes 10485784
  270.6 4.2 %shard_map.136 = (f32[8,8,128]{2,1,0:T(8,128)S(1)}, f32[8,8,128]{2,1,0:T(8,128)S(1)}, f32[8,8,128]{2,1,0:T(8,128)S(1)}, f32[8,8,128]{2,1,0:T(8,128)S(1)}) custom-call(s32[8]{0:T(128)S(1)} %get-tuple-element.101.lengths_ref, bf16[8,5120]{1,0:T(8,128)(2,1)S(1)} %get-tuple-element.86.normed_ref, bf16[5120,1024]{1,0:T(8,128)(2,1)S(1)} %copy-done.3, ...), custom_call_target="tpu_custom_call" | custom-call | flops 83886080 | bytes 10485760 | tf_op jit(solution)/shard_map/pallas_call | solution.py:322
  274.8 4.0 %copy-done.7 = bf16[1024,5120]{1,0:T(8,128)(2,1)S(1)} copy-done((bf16[1024,5120]{1,0:T(8,128)(2,1)S(1)}, bf16[1024,5120]{1,0:T(8,128)(2,1)}, u32[]{:S(2)}) %copy-start.7) | copy-done | bytes 10485784
  278.8 1.6 shard_map.138
  280.3 1.3 collective-permute-start.27
  281.6 2.2 collective-permute-start.29
  284.8 1.3 collective-permute-done.28
  286.1 1.1 collective-permute-done.29
  287.2 1.9 collective-permute-start.30
  289.2 3.4 %collective-permute-done.30 = bf16[8,5120]{1,0:T(8,128)(2,1)S(1)} collective-permute-done((bf16[8,5120]{1,0:T(8,128)(2,1)S(1)}, bf16[8,5120]{1,0:T(8,128)(2,1)S(1)}, u32[]{:S(2)}, u32[]{:S(2)}) %collective-permute-start.30) | collective-permute-done | bytes 81952 | tf_op jit(solution)/shard_map/ppermute | solution.py:26
  (214 shorter events, 49.5 us)
Async XLA Ops:
  66.7 27.1 %collective-permute-start = (bf16[2,8,64,128]{3,2,1,0:T(8,128)(2,1)}, bf16[2,8,64,128]{3,2,1,0:T(8,128)(2,1)S(1)}, u32[]{:S(2)}, u32[]{:S(2)}) collective-permute-start(bf16[2,8,64,128]{3,2,1,0:T(8,128)(2,1)} %get-tuple-element.53), channel_id=1, source_target_pairs={{0,1},{1,0},{2,3},{3,2},{4,5},{5,4},{6,7},{7,6},{8,9},{9,8},{10,11... | collective-permute-start | bytes 786440 | tf_op jit(solution)/shard_map/ppermute | solution.py:26
  69.8 25.9 %collective-permute-start.1 = (bf16[2,8,64,128]{3,2,1,0:T(8,128)(2,1)}, bf16[2,8,64,128]{3,2,1,0:T(8,128)(2,1)S(1)}, u32[]{:S(2)}, u32[]{:S(2)}) collective-permute-start(bf16[2,8,64,128]{3,2,1,0:T(8,128)(2,1)} %get-tuple-element.54), channel_id=1, source_target_pairs={{0,2},{1,3},{2,0},{3,1},{4,6},{5,7},{6,4},{7,5},{8,10},{9,11},{10,... | collective-permute-start | bytes 786440 | tf_op jit(solution)/shard_map/ppermute | solution.py:26
  71.4 26.3 %collective-permute-start.2 = (bf16[2,8,64,128]{3,2,1,0:T(8,128)(2,1)}, bf16[2,8,64,128]{3,2,1,0:T(8,128)(2,1)S(1)}, u32[]{:S(2)}, u32[]{:S(2)}) collective-permute-start(bf16[2,8,64,128]{3,2,1,0:T(8,128)(2,1)} %get-tuple-element.55), channel_id=1, source_target_pairs={{0,3},{1,2},{2,1},{3,0},{4,7},{5,6},{6,5},{7,4},{8,11},{9,10},{10,... | collective-permute-start | bytes 786440 | tf_op jit(solution)/shard_map/ppermute | solution.py:26
  82.1 5.5 %collective-permute-start.7 = (bf16[8,128]{1,0:T(8,128)(2,1)}, bf16[8,128]{1,0:T(8,128)(2,1)S(1)}, u32[]{:S(2)}, u32[]{:S(2)}) collective-permute-start(bf16[8,128]{1,0:T(8,128)(2,1)} %get-tuple-element.65), channel_id=1, source_target_pairs={{0,0},{1,2},{2,4},{3,6},{4,1},{5,3},{6,5},{7,7},{8,8},{9,10},{10,1... | collective-permute-start | bytes 6152 | tf_op jit(solution)/shard_map/ppermute | solution.py:287
  83.4 7.3 %collective-permute-start.8 = (bf16[8,128]{1,0:T(8,128)(2,1)}, bf16[8,128]{1,0:T(8,128)(2,1)S(1)}, u32[]{:S(2)}, u32[]{:S(2)}) collective-permute-start(bf16[8,128]{1,0:T(8,128)(2,1)} %get-tuple-element.66), channel_id=1, source_target_pairs={{0,1},{1,3},{2,5},{3,7},{4,0},{5,2},{6,4},{7,6},{8,9},{9,11},{10,1... | collective-permute-start | bytes 6152 | tf_op jit(solution)/shard_map/ppermute | solution.py:293
  87.5 33.1 %collective-permute-start.3 = (bf16[2,8,64,128]{3,2,1,0:T(8,128)(2,1)}, bf16[2,8,64,128]{3,2,1,0:T(8,128)(2,1)S(1)}, u32[]{:S(2)}, u32[]{:S(2)}) collective-permute-start(bf16[2,8,64,128]{3,2,1,0:T(8,128)(2,1)} %get-tuple-element.56), channel_id=1, source_target_pairs={{0,4},{1,5},{2,6},{3,7},{4,0},{5,1},{6,2},{7,3},{8,12},{9,13},{10,... | collective-permute-start | bytes 786440 | tf_op jit(solution)/shard_map/ppermute | solution.py:26
  90.7 35.3 %collective-permute-start.4 = (bf16[2,8,64,128]{3,2,1,0:T(8,128)(2,1)}, bf16[2,8,64,128]{3,2,1,0:T(8,128)(2,1)S(1)}, u32[]{:S(2)}, u32[]{:S(2)}) collective-permute-start(bf16[2,8,64,128]{3,2,1,0:T(8,128)(2,1)} %get-tuple-element.57), channel_id=1, source_target_pairs={{0,5},{1,4},{2,7},{3,6},{4,1},{5,0},{6,3},{7,2},{8,13},{9,12},{10,... | collective-permute-start | bytes 786440 | tf_op jit(solution)/shard_map/ppermute | solution.py:26
  93.8 32.9 %collective-permute-start.5 = (bf16[2,8,64,128]{3,2,1,0:T(8,128)(2,1)}, bf16[2,8,64,128]{3,2,1,0:T(8,128)(2,1)S(1)}, u32[]{:S(2)}, u32[]{:S(2)}) collective-permute-start(bf16[2,8,64,128]{3,2,1,0:T(8,128)(2,1)} %get-tuple-element.58), channel_id=1, source_target_pairs={{0,6},{1,7},{2,4},{3,5},{4,2},{5,3},{6,0},{7,1},{8,14},{9,15},{10,... | collective-permute-start | bytes 786440 | tf_op jit(solution)/shard_map/ppermute | solution.py:26
  95.7 31.8 %collective-permute-start.6 = (bf16[2,8,64,128]{3,2,1,0:T(8,128)(2,1)}, bf16[2,8,64,128]{3,2,1,0:T(8,128)(2,1)S(1)}, u32[]{:S(2)}, u32[]{:S(2)}) collective-permute-start(bf16[2,8,64,128]{3,2,1,0:T(8,128)(2,1)} %get-tuple-element.59), channel_id=1, source_target_pairs={{0,7},{1,6},{2,5},{3,4},{4,3},{5,2},{6,1},{7,0},{8,15},{9,14},{10,... | collective-permute-start | bytes 786440 | tf_op jit(solution)/shard_map/ppermute | solution.py:26
  139.1 4.3 %copy-start.4 = (bf16[1024,5120]{1,0:T(8,128)(2,1)S(1)}, bf16[1024,5120]{1,0:T(8,128)(2,1)}, u32[]{:S(2)}) copy-start(bf16[1024,5120]{1,0:T(8,128)(2,1)} %w_ref.15) | copy-start | bytes 31457284
  139.1 17.6 %copy-start.74 = (s32[2]{0:T(128)S(1)}, s32[2]{0:T(128)}, u32[]{:S(2)}) copy-start(s32[2]{0:T(128)} %param.20) | copy-start | bytes 28
  139.1 17.6 %copy-start.75 = (s32[2]{0:T(128)S(1)}, s32[2]{0:T(128)}, u32[]{:S(2)}) copy-start(s32[2]{0:T(128)} %param.21) | copy-start | bytes 28
  139.1 23.9 %copy-start.64 = (f32[8,64]{1,0:T(8,128)S(1)}, f32[8,64]{1,0:T(8,128)}, u32[]{:S(2)}) copy-start(f32[8,64]{1,0:T(8,128)} %get-tuple-element.135) | copy-start | bytes 6148
  139.2 28.8 %copy-start.9 = (bf16[5120,256]{1,0:T(8,128)(2,1)S(1)}, bf16[5120,256]{1,0:T(8,128)(2,1)}, u32[]{:S(2)}) copy-start(bf16[5120,256]{1,0:T(8,128)(2,1)} %refs_5_.5) | copy-start | bytes 7864324
  139.2 28.8 %copy-start.38 = (f32[5120]{0:T(1024)S(1)}, f32[5120]{0:T(1024)}, u32[]{:S(2)}) copy-start(f32[5120]{0:T(1024)} %param.12) | copy-start | bytes 61444
  139.2 28.8 %copy-start.40 = (bf16[8,5120]{1,0:T(8,128)(2,1)S(1)}, bf16[8,5120]{1,0:T(8,128)(2,1)}, u32[]{:S(2)}) copy-start(bf16[8,5120]{1,0:T(8,128)(2,1)} %copy-done.39) | copy-start | bytes 245764
  139.2 28.8 %copy-start.56 = (f32[8,128]{1,0:T(8,128)S(1)}, f32[8,128]{1,0:T(8,128)}, u32[]{:S(2)}) copy-start(f32[8,128]{1,0:T(8,128)} %broadcast_in_dim.25.active_ref.refs_3_) | copy-start | bytes 12292
  139.2 30.0 %copy-start.72 = (f32[8]{0:T(128)S(1)}, f32[8]{0:T(128)}, u32[]{:S(2)}) copy-start(f32[8]{0:T(128)} %get-tuple-element.128) | copy-start | bytes 100
  139.2 35.5 %copy-start.11 = (bf16[2,8,64,128]{3,2,1,0:T(8,128)(2,1)S(1)}, bf16[2,8,64,128]{3,2,1,0:T(8,128)(2,1)}, u32[]{:S(2)}) copy-start(bf16[2,8,64,128]{3,2,1,0:T(8,128)(2,1)} %get-tuple-element.52.rest_0_) | copy-start | bytes 786436
  144.9 13.5 %collective-permute-start.10 = (bf16[8,5120]{1,0:T(8,128)(2,1)S(1)}, bf16[8,5120]{1,0:T(8,128)(2,1)S(1)}, u32[]{:S(2)}, u32[]{:S(2)}) collective-permute-start(bf16[8,5120]{1,0:T(8,128)(2,1)S(1)} %shard_map.126), channel_id=1, source_target_pairs={{0,2},{1,3},{2,0},{3,1},{4,6},{5,7},{6,4},{7,5},{8,10},{9,11},{10,... | collective-permute-start | bytes 245768 | tf_op jit(solution)/shard_map/ppermute | solution.py:26
  155.2 5.4 %collective-permute-start.11 = (bf16[8,5120]{1,0:T(8,128)(2,1)S(1)}, bf16[8,5120]{1,0:T(8,128)(2,1)S(1)}, u32[]{:S(2)}, u32[]{:S(2)}) collective-permute-start(bf16[8,5120]{1,0:T(8,128)(2,1)S(1)} %shard_map.126), channel_id=1, source_target_pairs={{0,3},{1,2},{2,1},{3,0},{4,7},{5,6},{6,5},{7,4},{8,11},{9,10},{10,... | collective-permute-start | bytes 245768 | tf_op jit(solution)/shard_map/ppermute | solution.py:26
  155.2 5.9 %collective-permute-start.9 = (bf16[8,5120]{1,0:T(8,128)(2,1)S(1)}, bf16[8,5120]{1,0:T(8,128)(2,1)S(1)}, u32[]{:S(2)}, u32[]{:S(2)}) collective-permute-start(bf16[8,5120]{1,0:T(8,128)(2,1)S(1)} %shard_map.126), channel_id=1, source_target_pairs={{0,1},{1,0},{2,3},{3,2},{4,5},{5,4},{6,7},{7,6},{8,9},{9,8},{10,11... | collective-permute-start | bytes 245768 | tf_op jit(solution)/shard_map/ppermute | solution.py:26
  161.1 6.8 %collective-permute-start.12 = (bf16[8,5120]{1,0:T(8,128)(2,1)S(1)}, bf16[8,5120]{1,0:T(8,128)(2,1)S(1)}, u32[]{:S(2)}, u32[]{:S(2)}) collective-permute-start(bf16[8,5120]{1,0:T(8,128)(2,1)S(1)} %add_convert_fusion.3.refs_1_), channel_id=1, source_target_pairs={{0,4},{1,5},{2,6},{3,7},{4,0},{5,1},{6,2},{7,3},{8,12},{9,13},{10,... | collective-permute-start | bytes 245768 | tf_op jit(solution)/shard_map/ppermute | solution.py:26
  171.5 17.5 %collective-permute-start.13 = (bf16[8,128]{1,0:T(8,128)(2,1)}, bf16[8,128]{1,0:T(8,128)(2,1)S(1)}, u32[]{:S(2)}, u32[]{:S(2)}) collective-permute-start(bf16[8,128]{1,0:T(8,128)(2,1)} %get-tuple-element.74), channel_id=1, source_target_pairs={{0,0},{1,2},{2,4},{3,6},{4,1},{5,3},{6,5},{7,7},{8,8},{9,10},{10,1... | collective-permute-start | bytes 6152 | tf_op jit(solution)/shard_map/ppermute | solution.py:287
  172.8 16.2 %collective-permute-start.14 = (bf16[8,128]{1,0:T(8,128)(2,1)}, bf16[8,128]{1,0:T(8,128)(2,1)S(1)}, u32[]{:S(2)}, u32[]{:S(2)}) collective-permute-start(bf16[8,128]{1,0:T(8,128)(2,1)} %get-tuple-element.75), channel_id=1, source_target_pairs={{0,1},{1,3},{2,5},{3,7},{4,0},{5,2},{6,4},{7,6},{8,9},{9,11},{10,1... | collective-permute-start | bytes 6152 | tf_op jit(solution)/shard_map/ppermute | solution.py:293
  184.8 13.5 %copy-start.77 = (s32[2]{0:T(128)S(1)}, s32[2]{0:T(128)}, u32[]{:S(2)}) copy-start(s32[2]{0:T(128)} %get-tuple-element.110) | copy-start | bytes 28
  184.8 20.1 %copy-start.63 = (f32[8,64]{1,0:T(8,128)S(1)}, f32[8,64]{1,0:T(8,128)}, u32[]{:S(2)}) copy-start(f32[8,64]{1,0:T(8,128)} %get-tuple-element.132) | copy-start | bytes 6148
  184.8 22.8 %copy-start.42 = (bf16[8,5120]{1,0:T(8,128)(2,1)S(1)}, bf16[8,5120]{1,0:T(8,128)(2,1)}, u32[]{:S(2)}) copy-start(bf16[8,5120]{1,0:T(8,128)(2,1)} %copy-done.41) | copy-start | bytes 245764
  184.8 22.8 %copy-start.57 = (f32[8,128]{1,0:T(8,128)S(1)}, f32[8,128]{1,0:T(8,128)}, u32[]{:S(2)}) copy-start(f32[8,128]{1,0:T(8,128)} %broadcast_in_dim.26.active_ref.refs_3_) | copy-start | bytes 12292
  184.8 24.7 %copy-start.71 = (f32[8]{0:T(128)S(1)}, f32[8]{0:T(128)}, u32[]{:S(2)}) copy-start(f32[8]{0:T(128)} %get-tuple-element.127) | copy-start | bytes 100
  189.0 4.0 %copy-start.5 = (bf16[1024,5120]{1,0:T(8,128)(2,1)S(1)}, bf16[1024,5120]{1,0:T(8,128)(2,1)}, u32[]{:S(2)}) copy-start(bf16[1024,5120]{1,0:T(8,128)(2,1)} %w_ref.15) | copy-start | bytes 31457284
  194.5 4.9 %collective-permute-start.15 = (bf16[8,5120]{1,0:T(8,128)(2,1)S(1)}, bf16[8,5120]{1,0:T(8,128)(2,1)S(1)}, u32[]{:S(2)}, u32[]{:S(2)}) collective-permute-start(bf16[8,5120]{1,0:T(8,128)(2,1)S(1)} %shard_map.130), channel_id=1, source_target_pairs={{0,1},{1,0},{2,3},{3,2},{4,5},{5,4},{6,7},{7,6},{8,9},{9,8},{10,11... | collective-permute-start | bytes 245768 | tf_op jit(solution)/shard_map/ppermute | solution.py:26
  196.8 4.4 %collective-permute-start.16 = (bf16[8,5120]{1,0:T(8,128)(2,1)S(1)}, bf16[8,5120]{1,0:T(8,128)(2,1)S(1)}, u32[]{:S(2)}, u32[]{:S(2)}) collective-permute-start(bf16[8,5120]{1,0:T(8,128)(2,1)S(1)} %shard_map.130), channel_id=1, source_target_pairs={{0,2},{1,3},{2,0},{3,1},{4,6},{5,7},{6,4},{7,5},{8,10},{9,11},{10,... | collective-permute-start | bytes 245768 | tf_op jit(solution)/shard_map/ppermute | solution.py:26
  196.8 5.3 %collective-permute-start.17 = (bf16[8,5120]{1,0:T(8,128)(2,1)S(1)}, bf16[8,5120]{1,0:T(8,128)(2,1)S(1)}, u32[]{:S(2)}, u32[]{:S(2)}) collective-permute-start(bf16[8,5120]{1,0:T(8,128)(2,1)S(1)} %shard_map.130), channel_id=1, source_target_pairs={{0,3},{1,2},{2,1},{3,0},{4,7},{5,6},{6,5},{7,4},{8,11},{9,10},{10,... | collective-permute-start | bytes 245768 | tf_op jit(solution)/shard_map/ppermute | solution.py:26
  202.2 5.4 %collective-permute-start.18 = (bf16[8,5120]{1,0:T(8,128)(2,1)S(1)}, bf16[8,5120]{1,0:T(8,128)(2,1)S(1)}, u32[]{:S(2)}, u32[]{:S(2)}) collective-permute-start(bf16[8,5120]{1,0:T(8,128)(2,1)S(1)} %add_convert_fusion.2.refs_1_), channel_id=1, source_target_pairs={{0,4},{1,5},{2,6},{3,7},{4,0},{5,1},{6,2},{7,3},{8,12},{9,13},{10,... | collective-permute-start | bytes 245768 | tf_op jit(solution)/shard_map/ppermute | solution.py:26
  211.7 20.7 %collective-permute-start.19 = (bf16[8,128]{1,0:T(8,128)(2,1)}, bf16[8,128]{1,0:T(8,128)(2,1)S(1)}, u32[]{:S(2)}, u32[]{:S(2)}) collective-permute-start(bf16[8,128]{1,0:T(8,128)(2,1)} %get-tuple-element.83), channel_id=1, source_target_pairs={{0,0},{1,2},{2,4},{3,6},{4,1},{5,3},{6,5},{7,7},{8,8},{9,10},{10,1... | collective-permute-start | bytes 6152 | tf_op jit(solution)/shard_map/ppermute | solution.py:287
  213.0 19.4 %collective-permute-start.20 = (bf16[8,128]{1,0:T(8,128)(2,1)}, bf16[8,128]{1,0:T(8,128)(2,1)S(1)}, u32[]{:S(2)}, u32[]{:S(2)}) collective-permute-start(bf16[8,128]{1,0:T(8,128)(2,1)} %get-tuple-element.84), channel_id=1, source_target_pairs={{0,1},{1,3},{2,5},{3,7},{4,0},{5,2},{6,4},{7,6},{8,9},{9,11},{10,1... | collective-permute-start | bytes 6152 | tf_op jit(solution)/shard_map/ppermute | solution.py:293
  228.2 13.3 %copy-start.76 = (s32[2]{0:T(128)S(1)}, s32[2]{0:T(128)}, u32[]{:S(2)}) copy-start(s32[2]{0:T(128)} %get-tuple-element.111) | copy-start | bytes 28
  228.2 22.7 %copy-start.44 = (bf16[8,5120]{1,0:T(8,128)(2,1)S(1)}, bf16[8,5120]{1,0:T(8,128)(2,1)}, u32[]{:S(2)}) copy-start(bf16[8,5120]{1,0:T(8,128)(2,1)} %copy-done.43) | copy-start | bytes 245764
  228.2 22.7 %copy-start.58 = (f32[8,128]{1,0:T(8,128)S(1)}, f32[8,128]{1,0:T(8,128)}, u32[]{:S(2)}) copy-start(f32[8,128]{1,0:T(8,128)} %broadcast_in_dim.27.active_ref.refs_3_) | copy-start | bytes 12292
  228.2 24.5 %copy-start.70 = (f32[8]{0:T(128)S(1)}, f32[8]{0:T(128)}, u32[]{:S(2)}) copy-start(f32[8]{0:T(128)} %get-tuple-element.126) | copy-start | bytes 100
  232.5 4.0 %copy-start.6 = (bf16[1024,5120]{1,0:T(8,128)(2,1)S(1)}, bf16[1024,5120]{1,0:T(8,128)(2,1)}, u32[]{:S(2)}) copy-start(bf16[1024,5120]{1,0:T(8,128)(2,1)} %w_ref.15) | copy-start | bytes 31457284
  238.0 4.5 %collective-permute-start.21 = (bf16[8,5120]{1,0:T(8,128)(2,1)S(1)}, bf16[8,5120]{1,0:T(8,128)(2,1)S(1)}, u32[]{:S(2)}, u32[]{:S(2)}) collective-permute-start(bf16[8,5120]{1,0:T(8,128)(2,1)S(1)} %shard_map.134), channel_id=1, source_target_pairs={{0,1},{1,0},{2,3},{3,2},{4,5},{5,4},{6,7},{7,6},{8,9},{9,8},{10,11... | collective-permute-start | bytes 245768 | tf_op jit(solution)/shard_map/ppermute | solution.py:26
  240.1 4.4 %collective-permute-start.22 = (bf16[8,5120]{1,0:T(8,128)(2,1)S(1)}, bf16[8,5120]{1,0:T(8,128)(2,1)S(1)}, u32[]{:S(2)}, u32[]{:S(2)}) collective-permute-start(bf16[8,5120]{1,0:T(8,128)(2,1)S(1)} %shard_map.134), channel_id=1, source_target_pairs={{0,2},{1,3},{2,0},{3,1},{4,6},{5,7},{6,4},{7,5},{8,10},{9,11},{10,... | collective-permute-start | bytes 245768 | tf_op jit(solution)/shard_map/ppermute | solution.py:26
  240.1 5.3 %collective-permute-start.23 = (bf16[8,5120]{1,0:T(8,128)(2,1)S(1)}, bf16[8,5120]{1,0:T(8,128)(2,1)S(1)}, u32[]{:S(2)}, u32[]{:S(2)}) collective-permute-start(bf16[8,5120]{1,0:T(8,128)(2,1)S(1)} %shard_map.134), channel_id=1, source_target_pairs={{0,3},{1,2},{2,1},{3,0},{4,7},{5,6},{6,5},{7,4},{8,11},{9,10},{10,... | collective-permute-start | bytes 245768 | tf_op jit(solution)/shard_map/ppermute | solution.py:26
  245.5 5.4 %collective-permute-start.24 = (bf16[8,5120]{1,0:T(8,128)(2,1)S(1)}, bf16[8,5120]{1,0:T(8,128)(2,1)S(1)}, u32[]{:S(2)}, u32[]{:S(2)}) collective-permute-start(bf16[8,5120]{1,0:T(8,128)(2,1)S(1)} %add_convert_fusion.1.refs_1_), channel_id=1, source_target_pairs={{0,4},{1,5},{2,6},{3,7},{4,0},{5,1},{6,2},{7,3},{8,12},{9,13},{10,... | collective-permute-start | bytes 245768 | tf_op jit(solution)/shard_map/ppermute | solution.py:26
  255.0 19.8 %collective-permute-start.25 = (bf16[8,128]{1,0:T(8,128)(2,1)}, bf16[8,128]{1,0:T(8,128)(2,1)S(1)}, u32[]{:S(2)}, u32[]{:S(2)}) collective-permute-start(bf16[8,128]{1,0:T(8,128)(2,1)} %get-tuple-element.92), channel_id=1, source_target_pairs={{0,0},{1,2},{2,4},{3,6},{4,1},{5,3},{6,5},{7,7},{8,8},{9,10},{10,1... | collective-permute-start | bytes 6152 | tf_op jit(solution)/shard_map/ppermute | solution.py:287
  256.3 18.5 %collective-permute-start.26 = (bf16[8,128]{1,0:T(8,128)(2,1)}, bf16[8,128]{1,0:T(8,128)(2,1)S(1)}, u32[]{:S(2)}, u32[]{:S(2)}) collective-permute-start(bf16[8,128]{1,0:T(8,128)(2,1)} %get-tuple-element.93), channel_id=1, source_target_pairs={{0,1},{1,3},{2,5},{3,7},{4,0},{5,2},{6,4},{7,6},{8,9},{9,11},{10,1... | collective-permute-start | bytes 6152 | tf_op jit(solution)/shard_map/ppermute | solution.py:293
  270.5 13.3 %copy-start.78 = (pred[8,2]{0,1:T(4,128)(4,1)S(1)}, pred[8,2]{0,1:T(4,128)(4,1)}, u32[]{:S(2)}) copy-start(pred[8,2]{0,1:T(4,128)(4,1)} %get-tuple-element.125) | copy-start | bytes 52
  270.5 13.3 %copy-start.79 = (pred[2,8]{1,0:T(4,128)(4,1)S(1)}, pred[2,8]{1,0:T(4,128)(4,1)}, u32[]{:S(2)}) copy-start(pred[2,8]{1,0:T(4,128)(4,1)} %iota_compare_fusion) | copy-start | bytes 52
  270.5 18.5 %copy-start.65 = (bf16[8,256]{1,0:T(8,128)(2,1)S(1)}, bf16[8,256]{1,0:T(8,128)(2,1)}, u32[]{:S(2)}) copy-start(bf16[8,256]{1,0:T(8,128)(2,1)} %get-tuple-element.94) | copy-start | bytes 12292
  270.5 18.5 %copy-start.66 = (bf16[8,256]{1,0:T(8,128)(2,1)S(1)}, bf16[8,256]{1,0:T(8,128)(2,1)}, u32[]{:S(2)}) copy-start(bf16[8,256]{1,0:T(8,128)(2,1)} %get-tuple-element.95) | copy-start | bytes 12292
  270.5 18.5 %copy-start.67 = (bf16[8,256]{1,0:T(8,128)(2,1)S(1)}, bf16[8,256]{1,0:T(8,128)(2,1)}, u32[]{:S(2)}) copy-start(bf16[8,256]{1,0:T(8,128)(2,1)} %get-tuple-element.96) | copy-start | bytes 12292
  270.5 18.5 %copy-start.68 = (bf16[8,256]{1,0:T(8,128)(2,1)S(1)}, bf16[8,256]{1,0:T(8,128)(2,1)}, u32[]{:S(2)}) copy-start(bf16[8,256]{1,0:T(8,128)(2,1)} %get-tuple-element.97) | copy-start | bytes 12292
  270.6 22.0 %copy-start.46 = (bf16[8,5120]{1,0:T(8,128)(2,1)S(1)}, bf16[8,5120]{1,0:T(8,128)(2,1)}, u32[]{:S(2)}) copy-start(bf16[8,5120]{1,0:T(8,128)(2,1)} %copy-done.45) | copy-start | bytes 245764
  270.6 22.0 %copy-start.69 = (pred[8]{0:T(512)(128)(4,1)S(1)}, pred[8]{0:T(512)(128)(4,1)}, u32[]{:S(2)}) copy-start(pred[8]{0:T(512)(128)(4,1)} %get-tuple-element.98) | copy-start | bytes 28
  270.6 22.2 %copy-start.73 = (pred[8]{0:T(512)(128)(4,1)S(1)}, pred[8]{0:T(512)(128)(4,1)}, u32[]{:S(2)}) copy-start(pred[8]{0:T(512)(128)(4,1)} %get-tuple-element.124) | copy-start | bytes 28
  274.8 4.0 %copy-start.7 = (bf16[1024,5120]{1,0:T(8,128)(2,1)S(1)}, bf16[1024,5120]{1,0:T(8,128)(2,1)}, u32[]{:S(2)}) copy-start(bf16[1024,5120]{1,0:T(8,128)(2,1)} %w_ref.15) | copy-start | bytes 31457284
  280.3 4.4 %collective-permute-start.27 = (bf16[8,5120]{1,0:T(8,128)(2,1)S(1)}, bf16[8,5120]{1,0:T(8,128)(2,1)S(1)}, u32[]{:S(2)}, u32[]{:S(2)}) collective-permute-start(bf16[8,5120]{1,0:T(8,128)(2,1)S(1)} %shard_map.138), channel_id=1, source_target_pairs={{0,1},{1,0},{2,3},{3,2},{4,5},{5,4},{6,7},{7,6},{8,9},{9,8},{10,11... | collective-permute-start | bytes 245768 | tf_op jit(solution)/shard_map/ppermute | solution.py:26
  281.6 4.4 %collective-permute-start.28 = (bf16[8,5120]{1,0:T(8,128)(2,1)S(1)}, bf16[8,5120]{1,0:T(8,128)(2,1)S(1)}, u32[]{:S(2)}, u32[]{:S(2)}) collective-permute-start(bf16[8,5120]{1,0:T(8,128)(2,1)S(1)} %shard_map.138), channel_id=1, source_target_pairs={{0,2},{1,3},{2,0},{3,1},{4,6},{5,7},{6,4},{7,5},{8,10},{9,11},{10,... | collective-permute-start | bytes 245768 | tf_op jit(solution)/shard_map/ppermute | solution.py:26
  281.6 5.5 %collective-permute-start.29 = (bf16[8,5120]{1,0:T(8,128)(2,1)S(1)}, bf16[8,5120]{1,0:T(8,128)(2,1)S(1)}, u32[]{:S(2)}, u32[]{:S(2)}) collective-permute-start(bf16[8,5120]{1,0:T(8,128)(2,1)S(1)} %shard_map.138), channel_id=1, source_target_pairs={{0,3},{1,2},{2,1},{3,0},{4,7},{5,6},{6,5},{7,4},{8,11},{9,10},{10,... | collective-permute-start | bytes 245768 | tf_op jit(solution)/shard_map/ppermute | solution.py:26
  287.2 5.4 %collective-permute-start.30 = (bf16[8,5120]{1,0:T(8,128)(2,1)S(1)}, bf16[8,5120]{1,0:T(8,128)(2,1)S(1)}, u32[]{:S(2)}, u32[]{:S(2)}) collective-permute-start(bf16[8,5120]{1,0:T(8,128)(2,1)S(1)} %add_convert_fusion), channel_id=1, source_target_pairs={{0,4},{1,5},{2,6},{3,7},{4,0},{5,1},{6,2},{7,3},{8,12},{9,13},{10,... | collective-permute-start | bytes 245768 | tf_op jit(solution)/shard_map/ppermute | solution.py:26
  289.1 3.7 %collective-permute-start.32 = (bf16[4,8,256]{2,1,0:T(8,128)(2,1)S(1)}, bf16[4,8,256]{2,1,0:T(8,128)(2,1)S(1)}, u32[]{:S(2)}, u32[]{:S(2)}) collective-permute-start(bf16[4,8,256]{2,1,0:T(8,128)(2,1)S(1)} %pad_maximum_fusion), channel_id=1, source_target_pairs={{0,8},{8,0},{1,9},{9,1},{2,10},{10,2},{3,11},{11,3},{4,12},{12,4},... | collective-permute-start | bytes 49160 | tf_op jit(solution)/shard_map/ppermute | solution.py:26
  292.7 1.3 collective-permute-start.31
  (49 other events, 53.3 us)

commit v2 on v1

v2 whole, which is shorter than its diff:
```python
import functools
import math

import jax
import jax.numpy as jnp
from jax import lax
from jax.experimental import pallas as pl
from jax.experimental.pallas import tpu as pltpu
from jax.sharding import PartitionSpec as P

HD = 128
STEPS = 4
KERNEL_VMEM = 18 * 2**20
SMALL_VMEM = 6 * 2**20


rope_base = 1000000.0
norm_eps = 1e-06

in_vmem = pl.BlockSpec(memory_space=pltpu.VMEM)
in_smem = pl.BlockSpec(memory_space=pltpu.SMEM)


def exchange(block, axis, mask):
    count = lax.axis_size(axis)
    return lax.ppermute(block, axis, [(low, low ^ mask) for low in range(count)])


def root_norm(values):
    return values * lax.rsqrt(jnp.mean(values * values, axis=-1, keepdims=True) + norm_eps)


def turn(values, cosine, sine):
    return values * cosine + pltpu.roll(values, values.shape[-1] // 2, 1) * sine


def pack_kernel(masks, index_ref, keys_ref, values_ref, *outs):
    me = index_ref[0]
    for mask, out in zip(masks, outs):
        head = pl.multiple_of((me ^ mask) * HD, HD)
        out[0] = keys_ref[:, :, pl.ds(head, HD)]
        out[1] = values_ref[:, :, pl.ds(head, HD)]


def norm_kernel(step, split_heads, index_ref, tables_ref, remaining_ref, gain_ref, w_ref, *refs):
    if step > 0:
        hidden_ref, first_ref, second_ref, *refs = refs
    else:
        hidden_ref, *refs = refs
    hidden = hidden_ref[...].astype(jnp.float32)
    if step > 0:
        hidden_out, *refs = refs
        update = first_ref[...].astype(jnp.float32) + second_ref[...].astype(jnp.float32)
        keep = remaining_ref[:, :1] > step - 1
        hidden = jnp.where(keep, hidden + update, hidden).astype(jnp.bfloat16)
        hidden_out[...] = hidden
        hidden = hidden.astype(jnp.float32)
    normed = (root_norm(hidden) * gain_ref[...]).astype(jnp.bfloat16)
    normed_out, raw_out, *refs = refs
    normed_out[...] = normed
    raw = jnp.dot(normed, w_ref[...], preferred_element_type=jnp.float32).astype(jnp.bfloat16)
    if not split_heads:
        raw_out[...] = raw
        return
    is_key = index_ref[1] == 1
    live = remaining_ref[...] > step
    done = []
    for head in range(2):
        piece = raw[:, head * HD : (head + 1) * HD].astype(jnp.float32)
        turned = turn(root_norm(piece), tables_ref[step, 0], tables_ref[step, 1])
        chosen = jnp.where(is_key, turned, piece)
        done.append(jnp.where(live, chosen, 0.0))
        raw_out[:, head * HD : (head + 1) * HD] = done[head].astype(jnp.bfloat16)
    a_out, b_out = refs
    a_out[...] = jnp.where(is_key, done[0], done[1]).astype(jnp.bfloat16)
    b_out[...] = jnp.where(is_key, done[1], done[0]).astype(jnp.bfloat16)


def query_kernel(step, masks, index_ref, lengths_ref, tables_ref, normed_ref, w_ref, *rest):
    caches, rest = rest[: len(masks)], rest[len(masks) :]
    query_out, num_out, max_out, den_out = rest
    caches = [cache for _, cache in sorted(zip(masks, caches), key=lambda pair: pair[0])]
    seq_count = normed_ref.shape[0]
    heads = w_ref.shape[1] // HD
    projected = jnp.dot(normed_ref[...], w_ref[...], preferred_element_type=jnp.float32)
    for head in range(heads):
        piece = projected[:, head * HD : (head + 1) * HD]
        turned = turn(root_norm(piece), tables_ref[step, 0], tables_ref[step, 1])
        query_out[head] = turned.astype(jnp.bfloat16).astype(jnp.float32)

    def rows(which, seq):
        return jnp.concatenate(
            [
                ref[which, seq] if ref.ndim == 4 else ref[:, which, seq].reshape(-1, HD)
                for ref in caches
            ],
            axis=0,
        )

    scores = [
        lax.dot_general(
            query_out[:, seq, :].astype(jnp.bfloat16),
            rows(0, seq),
            (((1,), (1,)), ((), ())),
            preferred_element_type=jnp.float32,
        )
        * (1.0 / math.sqrt(HD))
        for seq in range(seq_count)
    ]
    places = lax.broadcasted_iota(jnp.int32, scores[0].shape, 1) ^ index_ref[3]
    valids = [places < lengths_ref[seq] for seq in range(seq_count)]
    tops = [
        jnp.max(jnp.where(valid, score, -1e30), axis=-1, keepdims=True)
        for valid, score in zip(valids, scores)
    ]
    weights = [
        jnp.where(valid, jnp.exp(score - top), 0.0).astype(jnp.bfloat16)
        for valid, score, top in zip(valids, scores, tops)
    ]
    for seq in range(seq_count):
        num_out[:, seq, :] = jnp.dot(
            weights[seq], rows(1, seq), preferred_element_type=jnp.float32
        )
        mass = jnp.sum(weights[seq].astype(jnp.float32), axis=-1, keepdims=True)
        max_out[:, seq, :] = jnp.broadcast_to(tops[seq], (heads, HD))
        den_out[:, seq, :] = jnp.broadcast_to(mass, (heads, HD))


def output_kernel(index_ref, query_ref, num_ref, max_ref, den_ref, w_ref, *rest):
    fresh, out_ref = rest[:-1], rest[-1]
    heads = query_ref.shape[0]
    key_first = index_ref[2] == 1
    keys, values = [], []
    for one_ref, other_ref in zip(fresh[0::2], fresh[1::2]):
        one, other = one_ref[...].astype(jnp.float32), other_ref[...].astype(jnp.float32)
        keys.append(jnp.where(key_first, one, other))
        values.append(jnp.where(key_first, other, one))
    attended = []
    for head in range(heads):
        query = query_ref[head]
        scores = [
            jnp.sum(query * key, axis=-1, keepdims=True) * (1.0 / math.sqrt(HD)) for key in keys
        ]
        top_old = max_ref[head]
        top = functools.reduce(jnp.maximum, scores, top_old)
        scale = jnp.exp(top_old - top)
        num = scale * num_ref[head]
        den = scale * den_ref[head]
        for score, value in zip(scores, values):
            weight = jnp.exp(score - top).astype(jnp.bfloat16).astype(jnp.float32)
            num = num + weight * value
            den = den + weight
        attended.append((num / den).astype(jnp.bfloat16))
    out_ref[...] = jnp.dot(
        jnp.concatenate(attended, axis=1), w_ref[...], preferred_element_type=jnp.float32
    ).astype(jnp.bfloat16)


def sum_rounds(part, axis):
    masks = [1 << bit for bit in range(lax.axis_size(axis).bit_length() - 1)]
    rounds = [masks[at : at + 2] for at in range(0, len(masks), 2)]
    if len(rounds[-1]) == 2:
        rounds = rounds[:-1] + [rounds[-1][:1], rounds[-1][1:]]
    for masks_now in rounds[:-1]:
        if len(masks_now) == 1:
            total = part.astype(jnp.float32) + exchange(part, axis, masks_now[0]).astype(jnp.float32)
        else:
            low, high = masks_now
            near = exchange(part, axis, low)
            far = exchange(part, axis, high)
            both = exchange(part, axis, low | high)
            total = (part.astype(jnp.float32) + near.astype(jnp.float32)) + (
                far.astype(jnp.float32) + both.astype(jnp.float32)
            )
        part = total.astype(jnp.bfloat16)
    return part, exchange(part, axis, rounds[-1][0])


def trade(own, other, slots_here, slots_there, axis):
    rows = jnp.arange(own.shape[axis])
    hits = slots_here[None, :] == rows[:, None]
    picks = jnp.any(
        hits[:, :, None] & (slots_there[None, :, None] == rows[None, None, :]), axis=1
    ).astype(own.dtype)
    moved = jnp.tensordot(picks, other, axes=((1,), (axis,)), preferred_element_type=jnp.float32)
    moved = jnp.moveaxis(moved, 0, axis).astype(own.dtype)
    shape = [1] * own.ndim
    shape[axis] = -1
    return jnp.where(jnp.any(hits, axis=1).reshape(shape), moved, own)


def per_device(
    hidden_in,
    norm_gain,
    w_query,
    w_key_value,
    w_output,
    cache_keys,
    cache_values,
    cache_lengths,
    remaining_steps,
    move_from,
    move_to,
):
    bf16, f32 = jnp.bfloat16, jnp.float32
    seq_count, width = hidden_in.shape
    model_size = lax.axis_size("mp")
    model_index = lax.axis_index("mp")
    group_index = lax.axis_index("dp")
    heads_here = w_query.shape[1] // HD
    kv_width = cache_keys.shape[2]
    kv_heads = kv_width // HD
    block_len = cache_keys.shape[1]
    col_width = w_key_value.shape[1]
    one_head_each = model_size == kv_heads and col_width == 2 * HD

    lengths = lax.dynamic_slice_in_dim(cache_lengths, group_index * seq_count, seq_count)
    remaining = lax.dynamic_slice_in_dim(remaining_steps, group_index * seq_count, seq_count)
    own_head = model_index * kv_heads // model_size
    flags = jnp.stack(
        [
            model_index,
            (model_index < model_size // 2).astype(jnp.int32),
            (model_index % 2 == 0).astype(jnp.int32) if one_head_each else jnp.int32(1),
            model_index * block_len if one_head_each else jnp.int32(0),
        ]
    )

    if one_head_each:
        half_size = model_size // 2
        across = list(range(half_size, model_size))
        masks = across[:2] + list(range(1, half_size)) + across[2:] + [0]
        shape = jax.ShapeDtypeStruct((2, seq_count, block_len, HD), bf16)
        packed = pl.pallas_call(
            functools.partial(pack_kernel, masks),
            out_shape=[shape] * model_size,
            in_specs=[in_smem, in_vmem, in_vmem],
            out_specs=[in_vmem] * model_size,
            compiler_params=pltpu.CompilerParams(vmem_limit_bytes=SMALL_VMEM),
        )(flags, cache_keys, cache_values)
        caches = [
            block if mask == 0 else exchange(block, "mp", mask)
            for mask, block in zip(masks, packed)
        ]
    else:
        masks = [0]
        both = jnp.stack([cache_keys, cache_values]).reshape(
            2, seq_count, block_len, kv_heads, HD
        )
        to_all = jnp.repeat(jnp.moveaxis(both, 3, 0), model_size // kv_heads, axis=0)
        caches = [lax.all_to_all(to_all, "mp", 0, 0, tiled=True)]

    half = HD // 2
    frequency = rope_base ** (-jnp.arange(half).astype(f32) * 2.0 / HD)
    positions = lengths[None, :] + jnp.arange(STEPS)[:, None]
    angles = positions.astype(f32)[:, :, None] * frequency[None, None, :]
    cosine, sine = jnp.cos(angles), jnp.sin(angles)
    tables = jnp.stack(
        [
            jnp.concatenate([cosine, cosine], axis=-1),
            jnp.concatenate([-sine, sine], axis=-1),
        ],
        axis=1,
    )
    remaining_rows = jnp.broadcast_to(remaining[:, None], (seq_count, HD))

    gain = norm_gain.reshape(1, width)
    hidden = hidden_in
    terms = ()
    fresh, kv_outputs = [], []
    row_f32 = jax.ShapeDtypeStruct((heads_here, seq_count, HD), f32)
    row_bf16 = jax.ShapeDtypeStruct((seq_count, width), bf16)
    head_row = jax.ShapeDtypeStruct((seq_count, HD), bf16)
    for step in range(STEPS):
        outs = [row_bf16, jax.ShapeDtypeStruct((seq_count, col_width), bf16)]
        outs = [row_bf16] * (step > 0) + outs + [head_row] * (2 * one_head_each)
        made = pl.pallas_call(
            functools.partial(norm_kernel, step, one_head_each),
            out_shape=outs,
            in_specs=[in_smem] + [in_vmem] * (5 + len(terms)),
            out_specs=[in_vmem] * len(outs),
            compiler_params=pltpu.CompilerParams(vmem_limit_bytes=SMALL_VMEM),
        )(flags, tables, remaining_rows, gain, w_key_value, hidden, *terms)
        if step > 0:
            hidden, *made = made
        normed, raw, *sent = made
        if one_head_each:
            kv_outputs.append(raw)
            pairs = model_size // 2
            to_even = [(low, 2 * low) for low in range(pairs)]
            to_odd = [(low, 2 * low + 1) for low in range(pairs)]
            fresh.append(
                lax.ppermute(sent[0], "mp", to_even + [(pairs + a, b) for a, b in to_odd])
            )
            fresh.append(
                lax.ppermute(sent[1], "mp", to_odd + [(pairs + a, b) for a, b in to_even])
            )
        else:
            raw_full = lax.all_gather(raw, "mp", axis=1, tiled=True)
            key_part = raw_full[:, :kv_width].astype(f32).reshape(seq_count, kv_heads, HD)
            key_part = root_norm(key_part)
            swapped = jnp.concatenate([key_part[..., half:], key_part[..., :half]], axis=-1)
            new_keys = (
                key_part * tables[step, 0][:, None, :] + swapped * tables[step, 1][:, None, :]
            ).astype(bf16)
            new_values = raw_full[:, kv_width:].reshape(seq_count, kv_heads, HD)
            live = (remaining > step)[:, None, None]
            new_kv = jnp.where(live, jnp.concatenate([new_keys, new_values], axis=1), 0)
            kv_outputs.append(
                lax.dynamic_slice_in_dim(
                    new_kv.reshape(seq_count, 2 * kv_width), model_index * col_width, col_width, 1
                )
            )
            fresh.append(lax.dynamic_index_in_dim(new_kv, own_head, 1, False))
            fresh.append(lax.dynamic_index_in_dim(new_kv, kv_heads + own_head, 1, False))
        attention = pl.pallas_call(
            functools.partial(query_kernel, step, masks),
            out_shape=[row_f32] * 4,
            in_specs=[in_smem] * 2 + [in_vmem] * (3 + len(caches)),
            out_specs=[in_vmem] * 4,
            cost_estimate=pl.CostEstimate(
                flops=2 * seq_count * width * heads_here * HD,
                bytes_accessed=2 * width * heads_here * HD,
                transcendentals=0,
            ),
            compiler_params=pltpu.CompilerParams(vmem_limit_bytes=KERNEL_VMEM),
        )(flags, lengths, tables, normed, w_query, *caches)
        part = pl.pallas_call(
            output_kernel,
            out_shape=row_bf16,
            in_specs=[in_smem] + [in_vmem] * (5 + len(fresh)),
            out_specs=in_vmem,
            compiler_params=pltpu.CompilerParams(vmem_limit_bytes=KERNEL_VMEM),
        )(flags, *attention, w_output, *fresh)
        terms = sum_rounds(part, "mp")
    update = terms[0].astype(f32) + terms[1].astype(f32)
    hidden_float = hidden.astype(f32)
    hidden = jnp.where(
        (remaining > STEPS - 1)[:, None], hidden_float + update, hidden_float
    ).astype(bf16)
    kv_local = jnp.stack(kv_outputs)

    slots_here = jnp.where(group_index == 0, move_from, move_to)
    slots_there = jnp.where(group_index == 0, move_to, move_from)
    other_kv = exchange(kv_local, "dp", 1)
    other_hidden = exchange(hidden, "dp", 1)
    return (
        trade(hidden, other_hidden, slots_here, slots_there, 0),
        trade(kv_local, other_kv, slots_here, slots_there, 1),
    )


def solution(mesh):
    placed = (
        P(("parts", "dp"), None),
        P(),
        P(None, "mp"),
        P(None, "mp"),
        P("mp", None),
        P(("parts", "dp"), "mp", None),
        P(("parts", "dp"), "mp", None),
        P("parts"),
        P("parts"),
        P("parts"),
        P("parts"),
    )
    return jax.shard_map(
        per_device,
        mesh=mesh,
        in_specs=placed,
        out_specs=(P(("parts", "dp"), None), P(None, ("parts", "dp"), "mp")),
        check_vma=False,
    )
```

time: 297 us -> 179 us (0.60)
  Pallas kernels: 97 us -> 25.7 us
  local copies, waits for them, and re-layouts: 66.7 us -> 36.4 us
  starting transfers between devices: 65.3 us -> 58.6 us
  other arithmetic: 9.38 us -> 3.7 us
    pallas_call x17 -> x13, Pallas kernels: 97 us -> 25.7 us  [the longest x4 11 us: per_device(): pl.pallas_call(functools.partial(query_kernel, step, masks), out_shape=[r...]
    unnamed x160 -> x110, local copies, waits for them, and re-layouts: 63.9 us -> 35.6 us
    ppermute x25, waiting for transfers between devices: 53.8 us -> 49.2 us  [exchange(): lax.ppermute(block, axis, [(low, low ^ mask) for low in range(count)])]
    ppermute x8, starting transfers between devices: 20.5 us -> 16.8 us  [the longest x4 14.2 us: per_device(): lax.ppermute(sent[1], 'mp', to_odd + [(pairs + a, b) for a, b in to_even])]
    ppermute x25, starting transfers between devices: 44.8 us -> 41.8 us  [exchange(): lax.ppermute(block, axis, [(low, low ^ mask) for low in range(count)])]
  transfers between devices with their start and end apart: 33 -> 33, of which waited for: 18 -> 21; matrix products, arithmetic and copies ran while one was open for 3% -> 2% of each run, Pallas kernels for 5% -> 7%
where the time goes in v2:
time: 179 us; the launch traced here: 178 us
  starting transfers between devices  58.6 us (33%)
  waiting for transfers between devices  51.1 us (29%)
  local copies, waits for them, and re-layouts  36.4 us (20%)
  Pallas kernels  25.7 us (14%)
  other arithmetic  3.7 us (2%)
    ppermute x25, waiting for transfers between devices, exchange(): lax.ppermute(block, axis, [(low, low ^ mask) for low in range(count)])  49.2 us
    ppermute x25, starting transfers between devices, exchange(): lax.ppermute(block, axis, [(low, low ^ mask) for low in range(count)])  41.8 us
    unnamed x110, local copies, waits for them, and re-layouts  35.6 us
    ppermute x4, starting transfers between devices, per_device(): lax.ppermute(sent[1], 'mp', to_odd + [(pairs + a, b) for a, b in to_even])  14.2 us
    pallas_call x4, Pallas kernels, per_device(): pl.pallas_call(functools.partial(query_kernel, step, masks), out_shape=[r...  11 us
    pallas_call x4, Pallas kernels, per_device(): pl.pallas_call(output_kernel, out_shape=row_bf16, in_specs=[in_smem] + [i...  8.36 us
    pallas_call x4, Pallas kernels, per_device(): pl.pallas_call(functools.partial(norm_kernel, step, one_head_each), out_s...  5.2 us
  transfers between devices with their start and end apart: 33, of which 21 were waited for; matrix products, arithmetic and copies ran while one was open for 2% of the time, Pallas kernels for 7%

profile of v2, /device:TPU:0, one launch (start us, length us, event | category | flops | bytes accessed | tf_op | source)
XLA Modules:
  0.0 178.1 jit_solution(156346018148196206)
XLA Ops:
  0.7 1.2 copy-done.21
  2.0 1.2 copy-done.22
  3.2 1.1 shard_map.123
  4.3 4.1 %collective-permute-start = (bf16[2,8,64,128]{3,2,1,0:T(8,128)(2,1)S(1)}, bf16[2,8,64,128]{3,2,1,0:T(8,128)(2,1)S(1)}, u32[]{:S(2)}, u32[]{:S(2)}) collective-permute-start(bf16[2,8,64,128]{3,2,1,0:T(8,128)(2,1)S(1)} %get-tuple-element.46), channel_id=1, source_target_pairs={{0,4},{1,5},{2,6},{3,7},{4,0},{5,1},{6,2},{7,3},{8,12},{9,13},{10,... | collective-permute-start | bytes 786440 | tf_op jit(solution)/shard_map/ppermute | solution.py:26
  8.4 1.3 collective-permute-start.1
  9.9 1.8 %collective-permute-start.3 = (bf16[2,8,64,128]{3,2,1,0:T(8,128)(2,1)S(1)}, bf16[2,8,64,128]{3,2,1,0:T(8,128)(2,1)S(1)}, u32[]{:S(2)}, u32[]{:S(2)}) collective-permute-start(bf16[2,8,64,128]{3,2,1,0:T(8,128)(2,1)S(1)} %get-tuple-element.49), channel_id=1, source_target_pairs={{0,2},{1,3},{2,0},{3,1},{4,6},{5,7},{6,4},{7,5},{8,10},{9,11},{10,... | collective-permute-start | bytes 786440 | tf_op jit(solution)/shard_map/ppermute | solution.py:26
  11.7 1.4 collective-permute-start.4
  14.0 12.8 %collective-permute-done.rest_0_ = bf16[2,8,64,128]{3,2,1,0:T(8,128)(2,1)S(1)} collective-permute-done((bf16[2,8,64,128]{3,2,1,0:T(8,128)(2,1)S(1)}, bf16[2,8,64,128]{3,2,1,0:T(8,128)(2,1)S(1)}, u32[]{:S(2)}, u32[]{:S(2)}) %collective-permute-start) | collective-permute-done | bytes 262176 | tf_op jit(solution)/shard_map/ppermute | solution.py:26
  26.8 2.8 %collective-permute-start.5 = (bf16[2,8,64,128]{3,2,1,0:T(8,128)(2,1)S(1)}, bf16[2,8,64,128]{3,2,1,0:T(8,128)(2,1)S(1)}, u32[]{:S(2)}, u32[]{:S(2)}) collective-permute-start(bf16[2,8,64,128]{3,2,1,0:T(8,128)(2,1)S(1)} %get-tuple-element.51), channel_id=1, source_target_pairs={{0,6},{1,7},{2,4},{3,5},{4,2},{5,3},{6,0},{7,1},{8,14},{9,15},{10,... | collective-permute-start | bytes 786440 | tf_op jit(solution)/shard_map/ppermute | solution.py:26
  29.6 5.2 %collective-permute-done.1.rest_1_ = bf16[2,8,64,128]{3,2,1,0:T(8,128)(2,1)S(1)} collective-permute-done((bf16[2,8,64,128]{3,2,1,0:T(8,128)(2,1)S(1)}, bf16[2,8,64,128]{3,2,1,0:T(8,128)(2,1)S(1)}, u32[]{:S(2)}, u32[]{:S(2)}) %collective-permute-start.1) | collective-permute-done | bytes 262176 | tf_op jit(solution)/shard_map/ppermute | solution.py:26
  34.8 2.4 %collective-permute-start.6 = (bf16[2,8,64,128]{3,2,1,0:T(8,128)(2,1)S(1)}, bf16[2,8,64,128]{3,2,1,0:T(8,128)(2,1)S(1)}, u32[]{:S(2)}, u32[]{:S(2)}) collective-permute-start(bf16[2,8,64,128]{3,2,1,0:T(8,128)(2,1)S(1)} %get-tuple-element.52), channel_id=1, source_target_pairs={{0,7},{1,6},{2,5},{3,4},{4,3},{5,2},{6,1},{7,0},{8,15},{9,14},{10,... | collective-permute-start | bytes 786440 | tf_op jit(solution)/shard_map/ppermute | solution.py:26
  37.3 1.2 broadcast_compare_fusion
  38.7 1.7 copy-done.4
  42.0 1.2 shard_map.122
  46.0 2.8 %collective-permute-start.8 = (bf16[8,128]{1,0:T(8,128)(2,1)S(1)}, bf16[8,128]{1,0:T(8,128)(2,1)S(1)}, u32[]{:S(2)}, u32[]{:S(2)}) collective-permute-start(bf16[8,128]{1,0:T(8,128)(2,1)S(1)} %get-tuple-element.59), channel_id=1, source_target_pairs={{0,1},{1,3},{2,5},{3,7},{4,0},{5,2},{6,4},{7,6},{8,9},{9,11},{10,1... | collective-permute-start | bytes 6152 | tf_op jit(solution)/shard_map/ppermute | solution.py:296
  49.5 4.2 %copy-done = bf16[5120,1024]{1,0:T(8,128)(2,1)S(1)} copy-done((bf16[5120,1024]{1,0:T(8,128)(2,1)S(1)}, bf16[5120,1024]{1,0:T(8,128)(2,1)}, u32[]{:S(2)}) %copy-start) | copy-done | bytes 10485784
  53.6 0.9 copy-done.7
  54.6 0.9 copy-done.12
  55.5 0.9 copy-done.15
  56.5 2.8 %shard_map.124 = (f32[8,8,128]{2,1,0:T(8,128)S(1)}, f32[8,8,128]{2,1,0:T(8,128)S(1)}, f32[8,8,128]{2,1,0:T(8,128)S(1)}, f32[8,8,128]{2,1,0:T(8,128)S(1)}) custom-call(s32[4]{0:T(128)S(1)} %pad_add_fusion.index_ref, s32[8]{0:T(128)S(1)} %dynamic_slice.7.lengths_ref, f32[4,2,8,128]{3,2,1,0:T(8,128)S(1)} %pad_maximum_fusion.tables_ref, ...), custom_call_target="tpu_custom_call" | custom-call | flops 83886080 | bytes 10485760 | tf_op jit(solution)/shard_map/pallas_call | solution.py:316
  59.3 4.4 %copy-done.2 = bf16[1024,5120]{1,0:T(8,128)(2,1)S(1)} copy-done((bf16[1024,5120]{1,0:T(8,128)(2,1)S(1)}, bf16[1024,5120]{1,0:T(8,128)(2,1)}, u32[]{:S(2)}) %copy-start.2) | copy-done | bytes 10485784
  63.8 2.1 %shard_map.125 = bf16[8,5120]{1,0:T(8,128)(2,1)S(1)} custom-call(s32[4]{0:T(128)S(1)} %pad_add_fusion.index_ref, f32[8,8,128]{2,1,0:T(8,128)S(1)} %get-tuple-element.54.query_ref, f32[8,8,128]{2,1,0:T(8,128)S(1)} %get-tuple-element.55.num_ref, f32[8,8,128]{2,1,0:T(8,128)S(1)} %get-tuple-element.56.max_ref, f32[8,8,128]{2,1,0:T(8,128)S(1)} %get-tuple-element.57.den_ref, ...), custom_call_target="tpu_custom_call" | custom-call | tf_op jit(solution)/shard_map/pallas_call | solution.py:328
  65.8 6.1 %collective-permute-start.10 = (bf16[8,5120]{1,0:T(8,128)(2,1)S(1)}, bf16[8,5120]{1,0:T(8,128)(2,1)S(1)}, u32[]{:S(2)}, u32[]{:S(2)}) collective-permute-start(bf16[8,5120]{1,0:T(8,128)(2,1)S(1)} %shard_map.125), channel_id=1, source_target_pairs={{0,2},{1,3},{2,0},{3,1},{4,6},{5,7},{6,4},{7,5},{8,10},{9,11},{10,... | collective-permute-start | bytes 245768 | tf_op jit(solution)/shard_map/ppermute | solution.py:26
  72.1 1.3 collective-permute-start.9
  73.5 1.0 collective-permute-done.10
  74.4 3.0 %collective-permute-done.11 = bf16[8,5120]{1,0:T(8,128)(2,1)S(1)} collective-permute-done((bf16[8,5120]{1,0:T(8,128)(2,1)S(1)}, bf16[8,5120]{1,0:T(8,128)(2,1)S(1)}, u32[]{:S(2)}, u32[]{:S(2)}) %collective-permute-start.11) | collective-permute-done | bytes 81952 | tf_op jit(solution)/shard_map/ppermute | solution.py:26
  77.9 3.5 %collective-permute-start.12 = (bf16[8,5120]{1,0:T(8,128)(2,1)S(1)}, bf16[8,5120]{1,0:T(8,128)(2,1)S(1)}, u32[]{:S(2)}, u32[]{:S(2)}) collective-permute-start(bf16[8,5120]{1,0:T(8,128)(2,1)S(1)} %add_convert_fusion.3.refs_1_), channel_id=1, source_target_pairs={{0,4},{1,5},{2,6},{3,7},{4,0},{5,1},{6,2},{7,3},{8,12},{9,13},{10,... | collective-permute-start | bytes 245768 | tf_op jit(solution)/shard_map/ppermute | solution.py:26
  81.3 3.7 %collective-permute-done.12.refs_2_ = bf16[8,5120]{1,0:T(8,128)(2,1)S(1)} collective-permute-done((bf16[8,5120]{1,0:T(8,128)(2,1)S(1)}, bf16[8,5120]{1,0:T(8,128)(2,1)S(1)}, u32[]{:S(2)}, u32[]{:S(2)}) %collective-permute-start.12) | collective-permute-done | bytes 81952 | tf_op jit(solution)/shard_map/ppermute | solution.py:26
  85.0 1.3 shard_map.126
  88.2 2.7 %collective-permute-start.14 = (bf16[8,128]{1,0:T(8,128)(2,1)S(1)}, bf16[8,128]{1,0:T(8,128)(2,1)S(1)}, u32[]{:S(2)}, u32[]{:S(2)}) collective-permute-start(bf16[8,128]{1,0:T(8,128)(2,1)S(1)} %get-tuple-element.67), channel_id=1, source_target_pairs={{0,1},{1,3},{2,5},{3,7},{4,0},{5,2},{6,4},{7,6},{8,9},{9,11},{10,1... | collective-permute-start | bytes 6152 | tf_op jit(solution)/shard_map/ppermute | solution.py:296
  91.0 2.8 %shard_map.127 = (f32[8,8,128]{2,1,0:T(8,128)S(1)}, f32[8,8,128]{2,1,0:T(8,128)S(1)}, f32[8,8,128]{2,1,0:T(8,128)S(1)}, f32[8,8,128]{2,1,0:T(8,128)S(1)}) custom-call(s32[4]{0:T(128)S(1)} %pad_add_fusion.index_ref, s32[8]{0:T(128)S(1)} %dynamic_slice.7.lengths_ref, f32[4,2,8,128]{3,2,1,0:T(8,128)S(1)} %pad_maximum_fusion.tables_ref, ...), custom_call_target="tpu_custom_call" | custom-call | flops 83886080 | bytes 10485760 | tf_op jit(solution)/shard_map/pallas_call | solution.py:316
  93.8 1.1 collective-permute-done.14.rest_3_
  94.9 2.1 %shard_map.128 = bf16[8,5120]{1,0:T(8,128)(2,1)S(1)} custom-call(s32[4]{0:T(128)S(1)} %pad_add_fusion.index_ref, f32[8,8,128]{2,1,0:T(8,128)S(1)} %get-tuple-element.62.query_ref, f32[8,8,128]{2,1,0:T(8,128)S(1)} %get-tuple-element.63.num_ref, f32[8,8,128]{2,1,0:T(8,128)S(1)} %get-tuple-element.64.max_ref, f32[8,8,128]{2,1,0:T(8,128)S(1)} %get-tuple-element.65.den_ref, ...), custom_call_target="tpu_custom_call" | custom-call | tf_op jit(solution)/shard_map/pallas_call | solution.py:328
  97.0 1.4 collective-permute-start.15
  99.1 1.4 collective-permute-start.17
  100.5 1.5 collective-permute-done.15
  102.0 1.0 collective-permute-done.16
  103.0 1.6 collective-permute-done.17
  104.5 1.0 add_convert_fusion.2.refs_1_
  105.5 2.2 %collective-permute-start.18 = (bf16[8,5120]{1,0:T(8,128)(2,1)S(1)}, bf16[8,5120]{1,0:T(8,128)(2,1)S(1)}, u32[]{:S(2)}, u32[]{:S(2)}) collective-permute-start(bf16[8,5120]{1,0:T(8,128)(2,1)S(1)} %add_convert_fusion.2.refs_1_), channel_id=1, source_target_pairs={{0,4},{1,5},{2,6},{3,7},{4,0},{5,1},{6,2},{7,3},{8,12},{9,13},{10,... | collective-permute-start | bytes 245768 | tf_op jit(solution)/shard_map/ppermute | solution.py:26
  108.4 2.5 %collective-permute-done.18.refs_2_ = bf16[8,5120]{1,0:T(8,128)(2,1)S(1)} collective-permute-done((bf16[8,5120]{1,0:T(8,128)(2,1)S(1)}, bf16[8,5120]{1,0:T(8,128)(2,1)S(1)}, u32[]{:S(2)}, u32[]{:S(2)}) %collective-permute-start.18) | collective-permute-done | bytes 81952 | tf_op jit(solution)/shard_map/ppermute | solution.py:26
  111.9 1.3 shard_map.129
  113.8 4.4 %collective-permute-start.20 = (bf16[8,128]{1,0:T(8,128)(2,1)S(1)}, bf16[8,128]{1,0:T(8,128)(2,1)S(1)}, u32[]{:S(2)}, u32[]{:S(2)}) collective-permute-start(bf16[8,128]{1,0:T(8,128)(2,1)S(1)} %get-tuple-element.75), channel_id=1, source_target_pairs={{0,1},{1,3},{2,5},{3,7},{4,0},{5,2},{6,4},{7,6},{8,9},{9,11},{10,1... | collective-permute-start | bytes 6152 | tf_op jit(solution)/shard_map/ppermute | solution.py:296
  118.2 4.0 %copy-done.1 = bf16[5120,1024]{1,0:T(8,128)(2,1)S(1)} copy-done((bf16[5120,1024]{1,0:T(8,128)(2,1)S(1)}, bf16[5120,1024]{1,0:T(8,128)(2,1)}, u32[]{:S(2)}) %copy-start.1) | copy-done | bytes 10485784
  122.2 0.9 copy-done.9
  123.1 0.9 copy-done.13
  125.0 0.9 copy-done.18
  127.6 2.8 %shard_map.130 = (f32[8,8,128]{2,1,0:T(8,128)S(1)}, f32[8,8,128]{2,1,0:T(8,128)S(1)}, f32[8,8,128]{2,1,0:T(8,128)S(1)}, f32[8,8,128]{2,1,0:T(8,128)S(1)}) custom-call(s32[4]{0:T(128)S(1)} %pad_add_fusion.index_ref, s32[8]{0:T(128)S(1)} %copy-done.36, f32[4,2,8,128]{3,2,1,0:T(8,128)S(1)} %pad_maximum_fusion.tables_ref, ...), custom_call_target="tpu_custom_call" | custom-call | flops 83886080 | bytes 10485760 | tf_op jit(solution)/shard_map/pallas_call | solution.py:316
  130.5 4.0 %copy-done.3 = bf16[1024,5120]{1,0:T(8,128)(2,1)S(1)} copy-done((bf16[1024,5120]{1,0:T(8,128)(2,1)S(1)}, bf16[1024,5120]{1,0:T(8,128)(2,1)}, u32[]{:S(2)}) %copy-start.3) | copy-done | bytes 10485784
  134.4 2.1 %shard_map.131 = bf16[8,5120]{1,0:T(8,128)(2,1)S(1)} custom-call(s32[4]{0:T(128)S(1)} %pad_add_fusion.index_ref, f32[8,8,128]{2,1,0:T(8,128)S(1)} %get-tuple-element.70.query_ref, f32[8,8,128]{2,1,0:T(8,128)S(1)} %get-tuple-element.71.num_ref, f32[8,8,128]{2,1,0:T(8,128)S(1)} %get-tuple-element.72.max_ref, f32[8,8,128]{2,1,0:T(8,128)S(1)} %get-tuple-element.73.den_ref, ...), custom_call_target="tpu_custom_call" | custom-call | tf_op jit(solution)/shard_map/pallas_call | solution.py:328
  136.5 1.3 collective-permute-start.21
  137.9 2.2 %collective-permute-start.23 = (bf16[8,5120]{1,0:T(8,128)(2,1)S(1)}, bf16[8,5120]{1,0:T(8,128)(2,1)S(1)}, u32[]{:S(2)}, u32[]{:S(2)}) collective-permute-start(bf16[8,5120]{1,0:T(8,128)(2,1)S(1)} %shard_map.131), channel_id=1, source_target_pairs={{0,3},{1,2},{2,1},{3,0},{4,7},{5,6},{6,5},{7,4},{8,11},{9,10},{10,... | collective-permute-start | bytes 245768 | tf_op jit(solution)/shard_map/ppermute | solution.py:26
  141.0 2.2 %collective-permute-done.22 = bf16[8,5120]{1,0:T(8,128)(2,1)S(1)} collective-permute-done((bf16[8,5120]{1,0:T(8,128)(2,1)S(1)}, bf16[8,5120]{1,0:T(8,128)(2,1)S(1)}, u32[]{:S(2)}, u32[]{:S(2)}) %collective-permute-start.22) | collective-permute-done | bytes 81952 | tf_op jit(solution)/shard_map/ppermute | solution.py:26
  143.7 2.4 %collective-permute-start.24 = (bf16[8,5120]{1,0:T(8,128)(2,1)S(1)}, bf16[8,5120]{1,0:T(8,128)(2,1)S(1)}, u32[]{:S(2)}, u32[]{:S(2)}) collective-permute-start(bf16[8,5120]{1,0:T(8,128)(2,1)S(1)} %add_convert_fusion.1.refs_1_), channel_id=1, source_target_pairs={{0,4},{1,5},{2,6},{3,7},{4,0},{5,1},{6,2},{7,3},{8,12},{9,13},{10,... | collective-permute-start | bytes 245768 | tf_op jit(solution)/shard_map/ppermute | solution.py:26
  146.2 2.9 %collective-permute-done.24.refs_2_ = bf16[8,5120]{1,0:T(8,128)(2,1)S(1)} collective-permute-done((bf16[8,5120]{1,0:T(8,128)(2,1)S(1)}, bf16[8,5120]{1,0:T(8,128)(2,1)S(1)}, u32[]{:S(2)}, u32[]{:S(2)}) %collective-permute-start.24) | collective-permute-done | bytes 81952 | tf_op jit(solution)/shard_map/ppermute | solution.py:26
  149.1 1.3 shard_map.132
  151.1 4.3 %collective-permute-start.26 = (bf16[8,128]{1,0:T(8,128)(2,1)S(1)}, bf16[8,128]{1,0:T(8,128)(2,1)S(1)}, u32[]{:S(2)}, u32[]{:S(2)}) collective-permute-start(bf16[8,128]{1,0:T(8,128)(2,1)S(1)} %get-tuple-element.83), channel_id=1, source_target_pairs={{0,1},{1,3},{2,5},{3,7},{4,0},{5,2},{6,4},{7,6},{8,9},{9,11},{10,1... | collective-permute-start | bytes 6152 | tf_op jit(solution)/shard_map/ppermute | solution.py:296
  155.5 2.8 %shard_map.133 = (f32[8,8,128]{2,1,0:T(8,128)S(1)}, f32[8,8,128]{2,1,0:T(8,128)S(1)}, f32[8,8,128]{2,1,0:T(8,128)S(1)}, f32[8,8,128]{2,1,0:T(8,128)S(1)}) custom-call(s32[4]{0:T(128)S(1)} %pad_add_fusion.index_ref, s32[8]{0:T(128)S(1)} %copy-done.37, f32[4,2,8,128]{3,2,1,0:T(8,128)S(1)} %pad_maximum_fusion.tables_ref, ...), custom_call_target="tpu_custom_call" | custom-call | flops 83886080 | bytes 10485760 | tf_op jit(solution)/shard_map/pallas_call | solution.py:316
  159.1 2.1 %shard_map.134 = bf16[8,5120]{1,0:T(8,128)(2,1)S(1)} custom-call(s32[4]{0:T(128)S(1)} %pad_add_fusion.index_ref, f32[8,8,128]{2,1,0:T(8,128)S(1)} %get-tuple-element.78.query_ref, f32[8,8,128]{2,1,0:T(8,128)S(1)} %get-tuple-element.79.num_ref, f32[8,8,128]{2,1,0:T(8,128)S(1)} %get-tuple-element.80.max_ref, f32[8,8,128]{2,1,0:T(8,128)S(1)} %get-tuple-element.81.den_ref, ...), custom_call_target="tpu_custom_call" | custom-call | tf_op jit(solution)/shard_map/pallas_call | solution.py:328
  161.2 2.4 %collective-permute-start.27 = (bf16[8,5120]{1,0:T(8,128)(2,1)S(1)}, bf16[8,5120]{1,0:T(8,128)(2,1)S(1)}, u32[]{:S(2)}, u32[]{:S(2)}) collective-permute-start(bf16[8,5120]{1,0:T(8,128)(2,1)S(1)} %shard_map.134), channel_id=1, source_target_pairs={{0,1},{1,0},{2,3},{3,2},{4,5},{5,4},{6,7},{7,6},{8,9},{9,8},{10,11... | collective-permute-start | bytes 245768 | tf_op jit(solution)/shard_map/ppermute | solution.py:26
  165.9 2.0 %collective-permute-done.28 = bf16[8,5120]{1,0:T(8,128)(2,1)S(1)} collective-permute-done((bf16[8,5120]{1,0:T(8,128)(2,1)S(1)}, bf16[8,5120]{1,0:T(8,128)(2,1)S(1)}, u32[]{:S(2)}, u32[]{:S(2)}) %collective-permute-start.28) | collective-permute-done | bytes 81952 | tf_op jit(solution)/shard_map/ppermute | solution.py:26
  168.0 1.6 collective-permute-done.29
  169.6 1.0 collective-permute-start.30
  170.7 5.2 %collective-permute-done.30 = bf16[8,5120]{1,0:T(8,128)(2,1)S(1)} collective-permute-done((bf16[8,5120]{1,0:T(8,128)(2,1)S(1)}, bf16[8,5120]{1,0:T(8,128)(2,1)S(1)}, u32[]{:S(2)}, u32[]{:S(2)}) %collective-permute-start.30) | collective-permute-done | bytes 81952 | tf_op jit(solution)/shard_map/ppermute | solution.py:26
  (150 shorter events, 22.2 us)
Async XLA Ops:
  4.3 22.6 %collective-permute-start = (bf16[2,8,64,128]{3,2,1,0:T(8,128)(2,1)S(1)}, bf16[2,8,64,128]{3,2,1,0:T(8,128)(2,1)S(1)}, u32[]{:S(2)}, u32[]{:S(2)}) collective-permute-start(bf16[2,8,64,128]{3,2,1,0:T(8,128)(2,1)S(1)} %get-tuple-element.46), channel_id=1, source_target_pairs={{0,4},{1,5},{2,6},{3,7},{4,0},{5,1},{6,2},{7,3},{8,12},{9,13},{10,... | collective-permute-start | bytes 786440 | tf_op jit(solution)/shard_map/ppermute | solution.py:26
  8.4 26.4 %collective-permute-start.1 = (bf16[2,8,64,128]{3,2,1,0:T(8,128)(2,1)S(1)}, bf16[2,8,64,128]{3,2,1,0:T(8,128)(2,1)S(1)}, u32[]{:S(2)}, u32[]{:S(2)}) collective-permute-start(bf16[2,8,64,128]{3,2,1,0:T(8,128)(2,1)S(1)} %get-tuple-element.47), channel_id=1, source_target_pairs={{0,5},{1,4},{2,7},{3,6},{4,1},{5,0},{6,3},{7,2},{8,13},{9,12},{10,... | collective-permute-start | bytes 786440 | tf_op jit(solution)/shard_map/ppermute | solution.py:26
  9.7 34.2 %collective-permute-start.2 = (bf16[2,8,64,128]{3,2,1,0:T(8,128)(2,1)S(1)}, bf16[2,8,64,128]{3,2,1,0:T(8,128)(2,1)S(1)}, u32[]{:S(2)}, u32[]{:S(2)}) collective-permute-start(bf16[2,8,64,128]{3,2,1,0:T(8,128)(2,1)S(1)} %get-tuple-element.48), channel_id=1, source_target_pairs={{0,1},{1,0},{2,3},{3,2},{4,5},{5,4},{6,7},{7,6},{8,9},{9,8},{10,11... | collective-permute-start | bytes 786440 | tf_op jit(solution)/shard_map/ppermute | solution.py:26
  9.9 35.3 %collective-permute-start.3 = (bf16[2,8,64,128]{3,2,1,0:T(8,128)(2,1)S(1)}, bf16[2,8,64,128]{3,2,1,0:T(8,128)(2,1)S(1)}, u32[]{:S(2)}, u32[]{:S(2)}) collective-permute-start(bf16[2,8,64,128]{3,2,1,0:T(8,128)(2,1)S(1)} %get-tuple-element.49), channel_id=1, source_target_pairs={{0,2},{1,3},{2,0},{3,1},{4,6},{5,7},{6,4},{7,5},{8,10},{9,11},{10,... | collective-permute-start | bytes 786440 | tf_op jit(solution)/shard_map/ppermute | solution.py:26
  11.7 37.0 %collective-permute-start.4 = (bf16[2,8,64,128]{3,2,1,0:T(8,128)(2,1)S(1)}, bf16[2,8,64,128]{3,2,1,0:T(8,128)(2,1)S(1)}, u32[]{:S(2)}, u32[]{:S(2)}) collective-permute-start(bf16[2,8,64,128]{3,2,1,0:T(8,128)(2,1)S(1)} %get-tuple-element.50), channel_id=1, source_target_pairs={{0,3},{1,2},{2,1},{3,0},{4,7},{5,6},{6,5},{7,4},{8,11},{9,10},{10,... | collective-permute-start | bytes 786440 | tf_op jit(solution)/shard_map/ppermute | solution.py:26
  13.9 77.1 %copy-start.35 = (s32[8]{0:T(128)}, s32[8]{0:T(128)S(1)}, u32[]{:S(2)}) copy-start(s32[8]{0:T(128)S(1)} %dynamic_slice.7.lengths_ref) | copy-start | bytes 100
  26.8 22.6 %collective-permute-start.5 = (bf16[2,8,64,128]{3,2,1,0:T(8,128)(2,1)S(1)}, bf16[2,8,64,128]{3,2,1,0:T(8,128)(2,1)S(1)}, u32[]{:S(2)}, u32[]{:S(2)}) collective-permute-start(bf16[2,8,64,128]{3,2,1,0:T(8,128)(2,1)S(1)} %get-tuple-element.51), channel_id=1, source_target_pairs={{0,6},{1,7},{2,4},{3,5},{4,2},{5,3},{6,0},{7,1},{8,14},{9,15},{10,... | collective-permute-start | bytes 786440 | tf_op jit(solution)/shard_map/ppermute | solution.py:26
  34.8 14.6 %collective-permute-start.6 = (bf16[2,8,64,128]{3,2,1,0:T(8,128)(2,1)S(1)}, bf16[2,8,64,128]{3,2,1,0:T(8,128)(2,1)S(1)}, u32[]{:S(2)}, u32[]{:S(2)}) collective-permute-start(bf16[2,8,64,128]{3,2,1,0:T(8,128)(2,1)S(1)} %get-tuple-element.52), channel_id=1, source_target_pairs={{0,7},{1,6},{2,5},{3,4},{4,3},{5,2},{6,1},{7,0},{8,15},{9,14},{10,... | collective-permute-start | bytes 786440 | tf_op jit(solution)/shard_map/ppermute | solution.py:26
  44.6 14.7 %collective-permute-start.7 = (bf16[8,128]{1,0:T(8,128)(2,1)S(1)}, bf16[8,128]{1,0:T(8,128)(2,1)S(1)}, u32[]{:S(2)}, u32[]{:S(2)}) collective-permute-start(bf16[8,128]{1,0:T(8,128)(2,1)S(1)} %get-tuple-element.58), channel_id=1, source_target_pairs={{0,0},{1,2},{2,4},{3,6},{4,1},{5,3},{6,5},{7,7},{8,8},{9,10},{10,1... | collective-permute-start | bytes 6152 | tf_op jit(solution)/shard_map/ppermute | solution.py:293
  46.0 13.3 %collective-permute-start.8 = (bf16[8,128]{1,0:T(8,128)(2,1)S(1)}, bf16[8,128]{1,0:T(8,128)(2,1)S(1)}, u32[]{:S(2)}, u32[]{:S(2)}) collective-permute-start(bf16[8,128]{1,0:T(8,128)(2,1)S(1)} %get-tuple-element.59), channel_id=1, source_target_pairs={{0,1},{1,3},{2,5},{3,7},{4,0},{5,2},{6,4},{7,6},{8,9},{9,11},{10,1... | collective-permute-start | bytes 6152 | tf_op jit(solution)/shard_map/ppermute | solution.py:296
  49.5 41.5 %copy-start.17 = (bf16[2,8,64,128]{3,2,1,0:T(8,128)(2,1)}, bf16[2,8,64,128]{3,2,1,0:T(8,128)(2,1)S(1)}, u32[]{:S(2)}) copy-start(bf16[2,8,64,128]{3,2,1,0:T(8,128)(2,1)S(1)} %collective-permute-done.5.rest_5_) | copy-start | bytes 786436
  49.5 41.5 %copy-start.19 = (bf16[2,8,64,128]{3,2,1,0:T(8,128)(2,1)}, bf16[2,8,64,128]{3,2,1,0:T(8,128)(2,1)S(1)}, u32[]{:S(2)}) copy-start(bf16[2,8,64,128]{3,2,1,0:T(8,128)(2,1)S(1)} %collective-permute-done.6.rest_6_) | copy-start | bytes 786436
  49.5 4.2 %copy-start = (bf16[5120,1024]{1,0:T(8,128)(2,1)S(1)}, bf16[5120,1024]{1,0:T(8,128)(2,1)}, u32[]{:S(2)}) copy-start(bf16[5120,1024]{1,0:T(8,128)(2,1)} %w_ref.22) | copy-start | bytes 31457284
  56.5 28.5 %copy-start.5 = (bf16[5120,256]{1,0:T(8,128)(2,1)S(1)}, bf16[5120,256]{1,0:T(8,128)(2,1)}, u32[]{:S(2)}) copy-start(bf16[5120,256]{1,0:T(8,128)(2,1)} %w_ref.21) | copy-start | bytes 7864324
  56.5 28.5 %copy-start.24 = (f32[5120]{0:T(1024)S(1)}, f32[5120]{0:T(1024)}, u32[]{:S(2)}) copy-start(f32[5120]{0:T(1024)} %param.12) | copy-start | bytes 61444
  56.5 28.5 %copy-start.26 = (bf16[8,5120]{1,0:T(8,128)(2,1)S(1)}, bf16[8,5120]{1,0:T(8,128)(2,1)}, u32[]{:S(2)}) copy-start(bf16[8,5120]{1,0:T(8,128)(2,1)} %refs_0_.3) | copy-start | bytes 245764
  56.5 34.5 %slice-start = ((s8[10485760]{0:T(1024)(128)(4,1)}), s8[4194304]{0:T(1024)(128)(4,1)S(1)}, s32[]{:S(2)}) async-start(s8[10485760]{0:T(1024)(128)(4,1)} %bitcast.25), calls=%async_computation | async-start | bytes 8388608
  56.5 34.5 %slice-start.1 = ((s8[10485760]{0:T(1024)(128)(4,1)}), s8[4194304]{0:T(1024)(128)(4,1)S(1)}, s32[]{:S(2)}) async-start(s8[10485760]{0:T(1024)(128)(4,1)} %bitcast.25), calls=%async_computation.1 | async-start | bytes 8388608
  56.5 34.5 %copy-start.8 = (bf16[2,8,64,128]{3,2,1,0:T(8,128)(2,1)S(1)}, bf16[2,8,64,128]{3,2,1,0:T(8,128)(2,1)}, u32[]{:S(2)}) copy-start(bf16[2,8,64,128]{3,2,1,0:T(8,128)(2,1)} %copy-done.6) | copy-start | bytes 786436
  59.3 35.6 %copy-start.29 = (bf16[8,128]{1,0:T(8,128)(2,1)}, bf16[8,128]{1,0:T(8,128)(2,1)S(1)}, u32[]{:S(2)}) copy-start(bf16[8,128]{1,0:T(8,128)(2,1)S(1)} %collective-permute-done.8.rest_1_) | copy-start | bytes 6148
  59.3 4.4 %copy-start.2 = (bf16[1024,5120]{1,0:T(8,128)(2,1)S(1)}, bf16[1024,5120]{1,0:T(8,128)(2,1)}, u32[]{:S(2)}) copy-start(bf16[1024,5120]{1,0:T(8,128)(2,1)} %w_ref.23) | copy-start | bytes 31457284
  63.8 27.2 %slice-start.2 = ((s8[10485760]{0:T(1024)(128)(4,1)}), s8[2097152]{0:T(1024)(128)(4,1)S(1)}, s32[]{:S(2)}) async-start(s8[10485760]{0:T(1024)(128)(4,1)} %bitcast.25), calls=%async_computation.2 | async-start | bytes 4194304
  63.8 31.1 %slice-start.6 = ((s8[10485760]{0:T(1024)(128)(4,1)}), s8[4194304]{0:T(1024)(128)(4,1)S(1)}, s32[]{:S(2)}) async-start(s8[10485760]{0:T(1024)(128)(4,1)} %bitcast.29), calls=%async_computation.6 | async-start | bytes 8388608
  63.8 31.1 %slice-start.7 = ((s8[10485760]{0:T(1024)(128)(4,1)}), s8[4194304]{0:T(1024)(128)(4,1)S(1)}, s32[]{:S(2)}) async-start(s8[10485760]{0:T(1024)(128)(4,1)} %bitcast.29), calls=%async_computation.7 | async-start | bytes 8388608
  65.8 8.6 %collective-permute-start.10 = (bf16[8,5120]{1,0:T(8,128)(2,1)S(1)}, bf16[8,5120]{1,0:T(8,128)(2,1)S(1)}, u32[]{:S(2)}, u32[]{:S(2)}) collective-permute-start(bf16[8,5120]{1,0:T(8,128)(2,1)S(1)} %shard_map.125), channel_id=1, source_target_pairs={{0,2},{1,3},{2,0},{3,1},{4,6},{5,7},{6,4},{7,5},{8,10},{9,11},{10,... | collective-permute-start | bytes 245768 | tf_op jit(solution)/shard_map/ppermute | solution.py:26
  72.0 5.4 %collective-permute-start.11 = (bf16[8,5120]{1,0:T(8,128)(2,1)S(1)}, bf16[8,5120]{1,0:T(8,128)(2,1)S(1)}, u32[]{:S(2)}, u32[]{:S(2)}) collective-permute-start(bf16[8,5120]{1,0:T(8,128)(2,1)S(1)} %shard_map.125), channel_id=1, source_target_pairs={{0,3},{1,2},{2,1},{3,0},{4,7},{5,6},{6,5},{7,4},{8,11},{9,10},{10,... | collective-permute-start | bytes 245768 | tf_op jit(solution)/shard_map/ppermute | solution.py:26
  72.1 5.7 %collective-permute-start.9 = (bf16[8,5120]{1,0:T(8,128)(2,1)S(1)}, bf16[8,5120]{1,0:T(8,128)(2,1)S(1)}, u32[]{:S(2)}, u32[]{:S(2)}) collective-permute-start(bf16[8,5120]{1,0:T(8,128)(2,1)S(1)} %shard_map.125), channel_id=1, source_target_pairs={{0,1},{1,0},{2,3},{3,2},{4,5},{5,4},{6,7},{7,6},{8,9},{9,8},{10,11... | collective-permute-start | bytes 245768 | tf_op jit(solution)/shard_map/ppermute | solution.py:26
  77.9 7.1 %collective-permute-start.12 = (bf16[8,5120]{1,0:T(8,128)(2,1)S(1)}, bf16[8,5120]{1,0:T(8,128)(2,1)S(1)}, u32[]{:S(2)}, u32[]{:S(2)}) collective-permute-start(bf16[8,5120]{1,0:T(8,128)(2,1)S(1)} %add_convert_fusion.3.refs_1_), channel_id=1, source_target_pairs={{0,4},{1,5},{2,6},{3,7},{4,0},{5,1},{6,2},{7,3},{8,12},{9,13},{10,... | collective-permute-start | bytes 245768 | tf_op jit(solution)/shard_map/ppermute | solution.py:26
  87.6 6.2 %collective-permute-start.13 = (bf16[8,128]{1,0:T(8,128)(2,1)S(1)}, bf16[8,128]{1,0:T(8,128)(2,1)S(1)}, u32[]{:S(2)}, u32[]{:S(2)}) collective-permute-start(bf16[8,128]{1,0:T(8,128)(2,1)S(1)} %get-tuple-element.66), channel_id=1, source_target_pairs={{0,0},{1,2},{2,4},{3,6},{4,1},{5,3},{6,5},{7,7},{8,8},{9,10},{10,1... | collective-permute-start | bytes 6152 | tf_op jit(solution)/shard_map/ppermute | solution.py:293
  88.2 6.6 %collective-permute-start.14 = (bf16[8,128]{1,0:T(8,128)(2,1)S(1)}, bf16[8,128]{1,0:T(8,128)(2,1)S(1)}, u32[]{:S(2)}, u32[]{:S(2)}) collective-permute-start(bf16[8,128]{1,0:T(8,128)(2,1)S(1)} %get-tuple-element.67), channel_id=1, source_target_pairs={{0,1},{1,3},{2,5},{3,7},{4,0},{5,2},{6,4},{7,6},{8,9},{9,11},{10,1... | collective-permute-start | bytes 6152 | tf_op jit(solution)/shard_map/ppermute | solution.py:296
  93.8 4.6 %copy-start.31 = (bf16[8,128]{1,0:T(8,128)(2,1)}, bf16[8,128]{1,0:T(8,128)(2,1)S(1)}, u32[]{:S(2)}) copy-start(bf16[8,128]{1,0:T(8,128)(2,1)S(1)} %collective-permute-done.13.rest_2_) | copy-start | bytes 6148
  94.9 4.2 %copy-start.33 = (bf16[8,128]{1,0:T(8,128)(2,1)}, bf16[8,128]{1,0:T(8,128)(2,1)S(1)}, u32[]{:S(2)}) copy-start(bf16[8,128]{1,0:T(8,128)(2,1)S(1)} %collective-permute-done.14.rest_3_) | copy-start | bytes 6148
  97.0 5.0 %collective-permute-start.15 = (bf16[8,5120]{1,0:T(8,128)(2,1)S(1)}, bf16[8,5120]{1,0:T(8,128)(2,1)}, u32[]{:S(2)}, u32[]{:S(2)}) collective-permute-start(bf16[8,5120]{1,0:T(8,128)(2,1)S(1)} %shard_map.128), channel_id=1, source_target_pairs={{0,1},{1,0},{2,3},{3,2},{4,5},{5,4},{6,7},{7,6},{8,9},{9,8},{10,11... | collective-permute-start | bytes 245768 | tf_op jit(solution)/shard_map/ppermute | solution.py:26
  98.4 4.5 %collective-permute-start.16 = (bf16[8,5120]{1,0:T(8,128)(2,1)S(1)}, bf16[8,5120]{1,0:T(8,128)(2,1)}, u32[]{:S(2)}, u32[]{:S(2)}) collective-permute-start(bf16[8,5120]{1,0:T(8,128)(2,1)S(1)} %shard_map.128), channel_id=1, source_target_pairs={{0,2},{1,3},{2,0},{3,1},{4,6},{5,7},{6,4},{7,5},{8,10},{9,11},{10,... | collective-permute-start | bytes 245768 | tf_op jit(solution)/shard_map/ppermute | solution.py:26
  99.1 5.4 %collective-permute-start.17 = (bf16[8,5120]{1,0:T(8,128)(2,1)S(1)}, bf16[8,5120]{1,0:T(8,128)(2,1)}, u32[]{:S(2)}, u32[]{:S(2)}) collective-permute-start(bf16[8,5120]{1,0:T(8,128)(2,1)S(1)} %shard_map.128), channel_id=1, source_target_pairs={{0,3},{1,2},{2,1},{3,0},{4,7},{5,6},{6,5},{7,4},{8,11},{9,10},{10,... | collective-permute-start | bytes 245768 | tf_op jit(solution)/shard_map/ppermute | solution.py:26
  100.5 29.9 %copy-start.30 = (bf16[8,128]{1,0:T(8,128)(2,1)S(1)}, bf16[8,128]{1,0:T(8,128)(2,1)}, u32[]{:S(2)}) copy-start(bf16[8,128]{1,0:T(8,128)(2,1)} %copy-done.29) | copy-start | bytes 6148
  100.5 29.9 %copy-start.32 = (bf16[8,128]{1,0:T(8,128)(2,1)S(1)}, bf16[8,128]{1,0:T(8,128)(2,1)}, u32[]{:S(2)}) copy-start(bf16[8,128]{1,0:T(8,128)(2,1)} %copy-done.31) | copy-start | bytes 6148
  100.5 29.9 %copy-start.34 = (bf16[8,128]{1,0:T(8,128)(2,1)S(1)}, bf16[8,128]{1,0:T(8,128)(2,1)}, u32[]{:S(2)}) copy-start(bf16[8,128]{1,0:T(8,128)(2,1)} %copy-done.33) | copy-start | bytes 6148
  105.5 5.4 %collective-permute-start.18 = (bf16[8,5120]{1,0:T(8,128)(2,1)S(1)}, bf16[8,5120]{1,0:T(8,128)(2,1)S(1)}, u32[]{:S(2)}, u32[]{:S(2)}) collective-permute-start(bf16[8,5120]{1,0:T(8,128)(2,1)S(1)} %add_convert_fusion.2.refs_1_), channel_id=1, source_target_pairs={{0,4},{1,5},{2,6},{3,7},{4,0},{5,1},{6,2},{7,3},{8,12},{9,13},{10,... | collective-permute-start | bytes 245768 | tf_op jit(solution)/shard_map/ppermute | solution.py:26
  113.2 17.2 %collective-permute-start.19 = (bf16[8,128]{1,0:T(8,128)(2,1)S(1)}, bf16[8,128]{1,0:T(8,128)(2,1)S(1)}, u32[]{:S(2)}, u32[]{:S(2)}) collective-permute-start(bf16[8,128]{1,0:T(8,128)(2,1)S(1)} %get-tuple-element.74), channel_id=1, source_target_pairs={{0,0},{1,2},{2,4},{3,6},{4,1},{5,3},{6,5},{7,7},{8,8},{9,10},{10,1... | collective-permute-start | bytes 6152 | tf_op jit(solution)/shard_map/ppermute | solution.py:293
  113.8 16.6 %collective-permute-start.20 = (bf16[8,128]{1,0:T(8,128)(2,1)S(1)}, bf16[8,128]{1,0:T(8,128)(2,1)S(1)}, u32[]{:S(2)}, u32[]{:S(2)}) collective-permute-start(bf16[8,128]{1,0:T(8,128)(2,1)S(1)} %get-tuple-element.75), channel_id=1, source_target_pairs={{0,1},{1,3},{2,5},{3,7},{4,0},{5,2},{6,4},{7,6},{8,9},{9,11},{10,1... | collective-permute-start | bytes 6152 | tf_op jit(solution)/shard_map/ppermute | solution.py:296
  127.6 27.8 %slice-start.3 = ((s8[10485760]{0:T(1024)(128)(4,1)}), s8[4194304]{0:T(1024)(128)(4,1)S(1)}, s32[]{:S(2)}) async-start(s8[10485760]{0:T(1024)(128)(4,1)} %bitcast.27), calls=%async_computation.3 | async-start | bytes 8388608
  127.6 27.8 %slice-start.4 = ((s8[10485760]{0:T(1024)(128)(4,1)}), s8[4194304]{0:T(1024)(128)(4,1)S(1)}, s32[]{:S(2)}) async-start(s8[10485760]{0:T(1024)(128)(4,1)} %bitcast.27), calls=%async_computation.4 | async-start | bytes 8388608
  127.6 27.8 %copy-start.10 = (bf16[2,8,64,128]{3,2,1,0:T(8,128)(2,1)S(1)}, bf16[2,8,64,128]{3,2,1,0:T(8,128)(2,1)}, u32[]{:S(2)}) copy-start(bf16[2,8,64,128]{3,2,1,0:T(8,128)(2,1)} %copy-done.6) | copy-start | bytes 786436
  127.6 27.8 %copy-start.37 = (s32[8]{0:T(128)S(1)}, s32[8]{0:T(128)}, u32[]{:S(2)}) copy-start(s32[8]{0:T(128)} %copy-done.35) | copy-start | bytes 100
  130.5 4.0 %copy-start.3 = (bf16[1024,5120]{1,0:T(8,128)(2,1)S(1)}, bf16[1024,5120]{1,0:T(8,128)(2,1)}, u32[]{:S(2)}) copy-start(bf16[1024,5120]{1,0:T(8,128)(2,1)} %w_ref.23) | copy-start | bytes 31457284
  134.4 21.0 %slice-start.5 = ((s8[10485760]{0:T(1024)(128)(4,1)}), s8[2097152]{0:T(1024)(128)(4,1)S(1)}, s32[]{:S(2)}) async-start(s8[10485760]{0:T(1024)(128)(4,1)} %bitcast.27), calls=%async_computation.5 | async-start | bytes 4194304
  134.4 24.6 %slice-start.9 = ((s8[10485760]{0:T(1024)(128)(4,1)}), s8[4194304]{0:T(1024)(128)(4,1)S(1)}, s32[]{:S(2)}) async-start(s8[10485760]{0:T(1024)(128)(4,1)} %bitcast.31), calls=%async_computation.9 | async-start | bytes 8388608
  134.4 24.6 %slice-start.10 = ((s8[10485760]{0:T(1024)(128)(4,1)}), s8[4194304]{0:T(1024)(128)(4,1)S(1)}, s32[]{:S(2)}) async-start(s8[10485760]{0:T(1024)(128)(4,1)} %bitcast.31), calls=%async_computation.10 | async-start | bytes 8388608
  136.5 4.4 %collective-permute-start.21 = (bf16[8,5120]{1,0:T(8,128)(2,1)S(1)}, bf16[8,5120]{1,0:T(8,128)(2,1)S(1)}, u32[]{:S(2)}, u32[]{:S(2)}) collective-permute-start(bf16[8,5120]{1,0:T(8,128)(2,1)S(1)} %shard_map.131), channel_id=1, source_target_pairs={{0,1},{1,0},{2,3},{3,2},{4,5},{5,4},{6,7},{7,6},{8,9},{9,8},{10,11... | collective-permute-start | bytes 245768 | tf_op jit(solution)/shard_map/ppermute | solution.py:26
  137.9 5.3 %collective-permute-start.22 = (bf16[8,5120]{1,0:T(8,128)(2,1)S(1)}, bf16[8,5120]{1,0:T(8,128)(2,1)S(1)}, u32[]{:S(2)}, u32[]{:S(2)}) collective-permute-start(bf16[8,5120]{1,0:T(8,128)(2,1)S(1)} %shard_map.131), channel_id=1, source_target_pairs={{0,2},{1,3},{2,0},{3,1},{4,6},{5,7},{6,4},{7,5},{8,10},{9,11},{10,... | collective-permute-start | bytes 245768 | tf_op jit(solution)/shard_map/ppermute | solution.py:26
  137.9 5.8 %collective-permute-start.23 = (bf16[8,5120]{1,0:T(8,128)(2,1)S(1)}, bf16[8,5120]{1,0:T(8,128)(2,1)S(1)}, u32[]{:S(2)}, u32[]{:S(2)}) collective-permute-start(bf16[8,5120]{1,0:T(8,128)(2,1)S(1)} %shard_map.131), channel_id=1, source_target_pairs={{0,3},{1,2},{2,1},{3,0},{4,7},{5,6},{6,5},{7,4},{8,11},{9,10},{10,... | collective-permute-start | bytes 245768 | tf_op jit(solution)/shard_map/ppermute | solution.py:26
  143.7 5.4 %collective-permute-start.24 = (bf16[8,5120]{1,0:T(8,128)(2,1)S(1)}, bf16[8,5120]{1,0:T(8,128)(2,1)S(1)}, u32[]{:S(2)}, u32[]{:S(2)}) collective-permute-start(bf16[8,5120]{1,0:T(8,128)(2,1)S(1)} %add_convert_fusion.1.refs_1_), channel_id=1, source_target_pairs={{0,4},{1,5},{2,6},{3,7},{4,0},{5,1},{6,2},{7,3},{8,12},{9,13},{10,... | collective-permute-start | bytes 245768 | tf_op jit(solution)/shard_map/ppermute | solution.py:26
  150.4 7.9 %collective-permute-start.25 = (bf16[8,128]{1,0:T(8,128)(2,1)S(1)}, bf16[8,128]{1,0:T(8,128)(2,1)S(1)}, u32[]{:S(2)}, u32[]{:S(2)}) collective-permute-start(bf16[8,128]{1,0:T(8,128)(2,1)S(1)} %get-tuple-element.82), channel_id=1, source_target_pairs={{0,0},{1,2},{2,4},{3,6},{4,1},{5,3},{6,5},{7,7},{8,8},{9,10},{10,1... | collective-permute-start | bytes 6152 | tf_op jit(solution)/shard_map/ppermute | solution.py:293
  151.1 7.9 %collective-permute-start.26 = (bf16[8,128]{1,0:T(8,128)(2,1)S(1)}, bf16[8,128]{1,0:T(8,128)(2,1)S(1)}, u32[]{:S(2)}, u32[]{:S(2)}) collective-permute-start(bf16[8,128]{1,0:T(8,128)(2,1)S(1)} %get-tuple-element.83), channel_id=1, source_target_pairs={{0,1},{1,3},{2,5},{3,7},{4,0},{5,2},{6,4},{7,6},{8,9},{9,11},{10,1... | collective-permute-start | bytes 6152 | tf_op jit(solution)/shard_map/ppermute | solution.py:296
  155.5 15.2 %copy-start.39 = (bf16[8,256]{1,0:T(8,128)(2,1)S(1)}, bf16[8,256]{1,0:T(8,128)(2,1)}, u32[]{:S(2)}) copy-start(bf16[8,256]{1,0:T(8,128)(2,1)} %copy-done.38) | copy-start | bytes 12292
  155.5 15.1 %copy-start.41 = (bf16[8,256]{1,0:T(8,128)(2,1)S(1)}, bf16[8,256]{1,0:T(8,128)(2,1)}, u32[]{:S(2)}) copy-start(bf16[8,256]{1,0:T(8,128)(2,1)} %copy-done.40) | copy-start | bytes 12292
  155.5 20.4 %copy-start.42 = (pred[8]{0:T(512)(128)(4,1)S(1)}, pred[8]{0:T(512)(128)(4,1)}, u32[]{:S(2)}) copy-start(pred[8]{0:T(512)(128)(4,1)} %get-tuple-element.88) | copy-start | bytes 28
  161.2 4.8 %collective-permute-start.27 = (bf16[8,5120]{1,0:T(8,128)(2,1)S(1)}, bf16[8,5120]{1,0:T(8,128)(2,1)S(1)}, u32[]{:S(2)}, u32[]{:S(2)}) collective-permute-start(bf16[8,5120]{1,0:T(8,128)(2,1)S(1)} %shard_map.134), channel_id=1, source_target_pairs={{0,1},{1,0},{2,3},{3,2},{4,5},{5,4},{6,7},{7,6},{8,9},{9,8},{10,11... | collective-permute-start | bytes 245768 | tf_op jit(solution)/shard_map/ppermute | solution.py:26
  163.5 4.4 %collective-permute-start.28 = (bf16[8,5120]{1,0:T(8,128)(2,1)S(1)}, bf16[8,5120]{1,0:T(8,128)(2,1)S(1)}, u32[]{:S(2)}, u32[]{:S(2)}) collective-permute-start(bf16[8,5120]{1,0:T(8,128)(2,1)S(1)} %shard_map.134), channel_id=1, source_target_pairs={{0,2},{1,3},{2,0},{3,1},{4,6},{5,7},{6,4},{7,5},{8,10},{9,11},{10,... | collective-permute-start | bytes 245768 | tf_op jit(solution)/shard_map/ppermute | solution.py:26
  164.2 5.3 %collective-permute-start.29 = (bf16[8,5120]{1,0:T(8,128)(2,1)S(1)}, bf16[8,5120]{1,0:T(8,128)(2,1)S(1)}, u32[]{:S(2)}, u32[]{:S(2)}) collective-permute-start(bf16[8,5120]{1,0:T(8,128)(2,1)S(1)} %shard_map.134), channel_id=1, source_target_pairs={{0,3},{1,2},{2,1},{3,0},{4,7},{5,6},{6,5},{7,4},{8,11},{9,10},{10,... | collective-permute-start | bytes 245768 | tf_op jit(solution)/shard_map/ppermute | solution.py:26
  169.6 6.3 %collective-permute-start.30 = (bf16[8,5120]{1,0:T(8,128)(2,1)S(1)}, bf16[8,5120]{1,0:T(8,128)(2,1)S(1)}, u32[]{:S(2)}, u32[]{:S(2)}) collective-permute-start(bf16[8,5120]{1,0:T(8,128)(2,1)S(1)} %add_convert_fusion), channel_id=1, source_target_pairs={{0,4},{1,5},{2,6},{3,7},{4,0},{5,1},{6,2},{7,3},{8,12},{9,13},{10,... | collective-permute-start | bytes 245768 | tf_op jit(solution)/shard_map/ppermute | solution.py:26
  170.6 5.4 %collective-permute-start.32 = (bf16[4,8,256]{2,1,0:T(8,128)(2,1)S(1)}, bf16[4,8,256]{2,1,0:T(8,128)(2,1)S(1)}, u32[]{:S(2)}, u32[]{:S(2)}) collective-permute-start(bf16[4,8,256]{2,1,0:T(8,128)(2,1)S(1)} %pad_maximum_fusion.1), channel_id=1, source_target_pairs={{0,8},{8,0},{1,9},{9,1},{2,10},{10,2},{3,11},{11,3},{4,12},{12,4},... | collective-permute-start | bytes 49160 | tf_op jit(solution)/shard_map/ppermute | solution.py:26
  176.0 1.3 collective-permute-start.31
  (24 other events, 30.4 us)

commit v3 on v2

v3 whole, which is shorter than its diff:
```python
import functools
import math

import jax
import jax.numpy as jnp
from jax import lax
from jax.experimental import pallas as pl
from jax.experimental.pallas import tpu as pltpu
from jax.sharding import PartitionSpec as P

HD = 128
STEPS = 4
KERNEL_VMEM = 18 * 2**20


rope_base = 1000000.0
norm_eps = 1e-06

in_vmem = pl.BlockSpec(memory_space=pltpu.VMEM)
in_smem = pl.BlockSpec(memory_space=pltpu.SMEM)


def exchange(block, axis, mask):
    count = lax.axis_size(axis)
    return lax.ppermute(block, axis, [(low, low ^ mask) for low in range(count)])


def root_norm(values):
    return values * lax.rsqrt(jnp.mean(values * values, axis=-1, keepdims=True) + norm_eps)


def turn(values, cosine, sine):
    return values * cosine + pltpu.roll(values, values.shape[-1] // 2, 1) * sine


def prepare_kernel(block_len, one_head_each, flags_ref, lengths_ref, remaining_ref, from_ref, to_ref, tables_ref, tables_out, rows_out):
    me, group, count = flags_ref[0], flags_ref[1], flags_ref[2]
    seq_count = rows_out.shape[1]
    tables_out[...] = tables_ref[group]
    rows = lax.broadcasted_iota(jnp.int32, rows_out.shape[1:], 0)

    def fill(value):
        return jnp.full(rows.shape, value, jnp.int32)

    remaining, lengths = fill(0), fill(0)
    for seq in range(seq_count):
        remaining = jnp.where(rows == seq, remaining_ref[group * seq_count + seq], remaining)
        lengths = jnp.where(rows == seq, lengths_ref[group * seq_count + seq], lengths)
    rows_out[0] = remaining
    rows_out[1] = lengths
    rows_out[2] = fill((2 * me < count).astype(jnp.int32))
    rows_out[3] = fill(((me & 1) == 0).astype(jnp.int32) if one_head_each else 1)
    rows_out[4] = fill(me * block_len if one_head_each else 0)
    for move in range(from_ref.shape[0]):
        rows_out[5 + 2 * move] = fill(jnp.where(group == 0, from_ref[move], to_ref[move]))
        rows_out[6 + 2 * move] = fill(jnp.where(group == 0, to_ref[move], from_ref[move]))


def pack_kernel(masks, flags_ref, keys_ref, values_ref, *outs):
    me = flags_ref[0]
    for mask, out in zip(masks, outs):
        head = pl.multiple_of((me ^ mask) * HD, HD)
        out[0] = keys_ref[:, :, pl.ds(head, HD)]
        out[1] = values_ref[:, :, pl.ds(head, HD)]


def updated(step, rows_ref, hidden_ref, first_ref, second_ref):
    hidden = hidden_ref[...].astype(jnp.float32)
    update = first_ref[...].astype(jnp.float32) + second_ref[...].astype(jnp.float32)
    return jnp.where(rows_ref[0][:, :1] > step, hidden + update, hidden)


def add_kernel(*refs):
    terms = [ref[...].astype(jnp.float32) for ref in refs[:-1]]
    while len(terms) > 1:
        terms = [one + other for one, other in zip(terms[0::2], terms[1::2])]
    refs[-1][...] = terms[0].astype(jnp.bfloat16)


def norm_kernel(step, split_heads, rows_ref, tables_ref, gain_ref, w_ref, *refs):
    if step > 0:
        hidden_ref, first_ref, second_ref, hidden_out, *refs = refs
        hidden = updated(step - 1, rows_ref, hidden_ref, first_ref, second_ref).astype(jnp.bfloat16)
        hidden_out[...] = hidden
        hidden = hidden.astype(jnp.float32)
    else:
        hidden_ref, *refs = refs
        hidden = hidden_ref[...].astype(jnp.float32)
    normed = (root_norm(hidden) * gain_ref[...]).astype(jnp.bfloat16)
    normed_out, raw_out, *refs = refs
    normed_out[...] = normed
    raw = jnp.dot(normed, w_ref[...], preferred_element_type=jnp.float32).astype(jnp.bfloat16)
    if not split_heads:
        raw_out[...] = raw
        return
    is_key = rows_ref[2] > 0
    live = rows_ref[0] > step
    done = []
    for head in range(2):
        piece = raw[:, head * HD : (head + 1) * HD].astype(jnp.float32)
        turned = turn(root_norm(piece), tables_ref[step, 0], tables_ref[step, 1])
        done.append(jnp.where(live, jnp.where(is_key, turned, piece), 0.0))
        raw_out[:, head * HD : (head + 1) * HD] = done[head].astype(jnp.bfloat16)
    a_out, b_out = refs
    a_out[...] = jnp.where(is_key, done[0], done[1]).astype(jnp.bfloat16)
    b_out[...] = jnp.where(is_key, done[1], done[0]).astype(jnp.bfloat16)


def query_kernel(step, masks, rows_ref, tables_ref, normed_ref, w_ref, *rest):
    caches, rest = rest[: len(masks)], rest[len(masks) :]
    query_out, num_out, max_out, den_out = rest
    caches = [cache for _, cache in sorted(zip(masks, caches), key=lambda pair: pair[0])]
    seq_count = normed_ref.shape[0]
    heads = w_ref.shape[1] // HD
    projected = jnp.dot(normed_ref[...], w_ref[...], preferred_element_type=jnp.float32)
    for head in range(heads):
        piece = projected[:, head * HD : (head + 1) * HD]
        turned = turn(root_norm(piece), tables_ref[step, 0], tables_ref[step, 1])
        query_out[head] = turned.astype(jnp.bfloat16).astype(jnp.float32)

    def rows(which, seq):
        return jnp.concatenate(
            [
                ref[which, seq] if ref.ndim == 4 else ref[:, which, seq].reshape(-1, HD)
                for ref in caches
            ],
            axis=0,
        )

    scores = [
        lax.dot_general(
            query_out[:, seq, :].astype(jnp.bfloat16),
            rows(0, seq),
            (((1,), (1,)), ((), ())),
            preferred_element_type=jnp.float32,
        )
        * (1.0 / math.sqrt(HD))
        for seq in range(seq_count)
    ]
    places = lax.broadcasted_iota(jnp.int32, scores[0].shape, 1) ^ rows_ref[4][:1, :1]
    lengths = rows_ref[1]
    valids = [places < lengths[seq : seq + 1, :1] for seq in range(seq_count)]
    tops = [
        jnp.max(jnp.where(valid, score, -1e30), axis=-1, keepdims=True)
        for valid, score in zip(valids, scores)
    ]
    weights = [
        jnp.where(valid, jnp.exp(score - top), 0.0).astype(jnp.bfloat16)
        for valid, score, top in zip(valids, scores, tops)
    ]
    for seq in range(seq_count):
        num_out[:, seq, :] = jnp.dot(
            weights[seq], rows(1, seq), preferred_element_type=jnp.float32
        )
        mass = jnp.sum(weights[seq].astype(jnp.float32), axis=-1, keepdims=True)
        max_out[:, seq, :] = jnp.broadcast_to(tops[seq], (heads, HD))
        den_out[:, seq, :] = jnp.broadcast_to(mass, (heads, HD))


def output_kernel(rows_ref, query_ref, num_ref, max_ref, den_ref, w_ref, *rest):
    fresh, out_ref = rest[:-1], rest[-1]
    heads = query_ref.shape[0]
    key_first = rows_ref[3] > 0
    keys, values = [], []
    for one_ref, other_ref in zip(fresh[0::2], fresh[1::2]):
        one, other = one_ref[...].astype(jnp.float32), other_ref[...].astype(jnp.float32)
        keys.append(jnp.where(key_first, one, other))
        values.append(jnp.where(key_first, other, one))
    attended = []
    for head in range(heads):
        query = query_ref[head]
        scores = [
            jnp.sum(query * key, axis=-1, keepdims=True) * (1.0 / math.sqrt(HD)) for key in keys
        ]
        top_old = max_ref[head]
        top = functools.reduce(jnp.maximum, scores, top_old)
        scale = jnp.exp(top_old - top)
        num = scale * num_ref[head]
        den = scale * den_ref[head]
        for score, value in zip(scores, values):
            weight = jnp.exp(score - top).astype(jnp.bfloat16).astype(jnp.float32)
            num = num + weight * value
            den = den + weight
        attended.append((num / den).astype(jnp.bfloat16))
    out_ref[...] = jnp.dot(
        jnp.concatenate(attended, axis=1), w_ref[...], preferred_element_type=jnp.float32
    ).astype(jnp.bfloat16)


def final_kernel(step, rows_ref, hidden_ref, first_ref, second_ref, *refs):
    *raws, out_ref = refs
    width = hidden_ref.shape[1]
    out_ref[:, :width] = updated(step, rows_ref, hidden_ref, first_ref, second_ref).astype(
        jnp.bfloat16
    )
    for at, raw in enumerate(raws):
        columns = raw.shape[1]
        out_ref[:, width + at * columns : width + (at + 1) * columns] = raw[...]


def trade_kernel(moves, rows_ref, own_ref, other_ref, hidden_out, kv_out):
    rows = own_ref[...].astype(jnp.float32)
    other = other_ref[...].astype(jnp.float32)
    index = lax.broadcasted_iota(jnp.int32, rows.shape, 0)
    own = rows
    for move in range(moves):
        here, there = rows_ref[5 + 2 * move][:1, :1], rows_ref[6 + 2 * move][:1, :1]
        picked = jnp.sum(jnp.where(index == there, other, 0.0), axis=0, keepdims=True)
        own = jnp.where(index == here, picked, own)
    own = own.astype(jnp.bfloat16)
    width = hidden_out.shape[1]
    hidden_out[...] = own[:, :width]
    for step in range(kv_out.shape[0]):
        columns = kv_out.shape[2]
        kv_out[step] = own[:, width + step * columns : width + (step + 1) * columns]


def run(kernel, outs, *args, scalars=0, vmem=6 * 2**20, flops=0, moved=0):
    return pl.pallas_call(
        kernel,
        out_shape=outs,
        in_specs=[in_smem] * scalars + [in_vmem] * (len(args) - scalars),
        out_specs=jax.tree.map(lambda _: in_vmem, outs),
        cost_estimate=pl.CostEstimate(flops=flops, bytes_accessed=moved, transcendentals=0),
        compiler_params=pltpu.CompilerParams(vmem_limit_bytes=vmem),
    )(*args)


def sum_rounds(part, axis):
    masks = [1 << bit for bit in range(lax.axis_size(axis).bit_length() - 1)]
    *masks, last = masks
    while masks:
        now, masks = masks[:2], masks[2:]
        if len(now) == 2:
            now = now + [now[0] | now[1]]
        others = [exchange(part, axis, mask) for mask in now]
        part = run(add_kernel, jax.ShapeDtypeStruct(part.shape, part.dtype), part, *others)
    return part, exchange(part, axis, last)


def per_device(
    hidden_in,
    norm_gain,
    w_query,
    w_key_value,
    w_output,
    cache_keys,
    cache_values,
    cache_lengths,
    remaining_steps,
    move_from,
    move_to,
):
    bf16, f32 = jnp.bfloat16, jnp.float32
    seq_count, width = hidden_in.shape
    model_size = lax.axis_size("mp")
    model_index = lax.axis_index("mp")
    group_index = lax.axis_index("dp")
    heads_here = w_query.shape[1] // HD
    kv_width = cache_keys.shape[2]
    kv_heads = kv_width // HD
    block_len = cache_keys.shape[1]
    col_width = w_key_value.shape[1]
    one_head_each = model_size == kv_heads and col_width == 2 * HD

    def struct(*shape, dtype=bf16):
        return jax.ShapeDtypeStruct(shape, dtype)

    half = HD // 2
    frequency = rope_base ** (-jnp.arange(half).astype(f32) * 2.0 / HD)
    positions = cache_lengths.reshape(-1, 1, seq_count) + jnp.arange(STEPS)[None, :, None]
    angles = positions.astype(f32)[..., None] * frequency
    cosine, sine = jnp.cos(angles), jnp.sin(angles)
    tables = jnp.stack(
        [
            jnp.concatenate([cosine, cosine], axis=-1),
            jnp.concatenate([-sine, sine], axis=-1),
        ],
        axis=2,
    )
    flags = jnp.stack([model_index, group_index, jnp.int32(model_size)])
    moves = move_from.shape[0]
    own_head = model_index * kv_heads // model_size

    if one_head_each:
        half_size = model_size // 2
        across = list(range(half_size, model_size))
        within = list(range(1, half_size))
        masks = across[:2] + within + across[2:] + [0]
        packed = run(
            functools.partial(pack_kernel, masks),
            [struct(2, seq_count, block_len, HD)] * model_size,
            flags,
            cache_keys,
            cache_values,
            scalars=1,
        )
        blocks = dict(zip(masks, packed))
        landed = {0: blocks[0]}
        for mask in across[:2] + within:
            landed[mask] = exchange(blocks[mask], "mp", mask)
        for mask, earlier in zip(across[2:], within):
            sent, landed[earlier] = lax.optimization_barrier((blocks[mask], landed[earlier]))
            landed[mask] = exchange(sent, "mp", mask)
        caches = [landed[mask] for mask in masks]
    else:
        masks = [0]
        both = jnp.stack([cache_keys, cache_values]).reshape(
            2, seq_count, block_len, kv_heads, HD
        )
        to_all = jnp.repeat(jnp.moveaxis(both, 3, 0), model_size // kv_heads, axis=0)
        caches = [lax.all_to_all(to_all, "mp", 0, 0, tiled=True)]

    tables, rows = run(
        functools.partial(prepare_kernel, block_len, one_head_each),
        [struct(*tables.shape[1:], dtype=f32), struct(5 + 2 * moves, seq_count, HD, dtype=jnp.int32)],
        flags,
        cache_lengths,
        remaining_steps,
        move_from,
        move_to,
        tables,
        scalars=5,
    )
    gain = norm_gain.reshape(1, width)
    hidden = hidden_in
    terms = ()
    fresh, kv_outputs = [], []
    for step in range(STEPS):
        made = run(
            functools.partial(norm_kernel, step, one_head_each),
            [struct(seq_count, width)] * (1 + (step > 0))
            + [struct(seq_count, col_width)]
            + [struct(seq_count, HD)] * (2 * one_head_each),
            rows,
            tables,
            gain,
            w_key_value,
            hidden,
            *terms,
        )
        if step > 0:
            hidden, *made = made
        normed, raw, *sent = made
        if one_head_each:
            kv_outputs.append(raw)
            pairs = model_size // 2
            to_even = [(low, 2 * low) for low in range(pairs)]
            to_odd = [(low, 2 * low + 1) for low in range(pairs)]
            fresh.append(
                lax.ppermute(sent[0], "mp", to_even + [(pairs + a, b) for a, b in to_odd])
            )
            fresh.append(
                lax.ppermute(sent[1], "mp", to_odd + [(pairs + a, b) for a, b in to_even])
            )
        else:
            raw_full = lax.all_gather(raw, "mp", axis=1, tiled=True)
            key_part = raw_full[:, :kv_width].astype(f32).reshape(seq_count, kv_heads, HD)
            key_part = root_norm(key_part)
            swapped = jnp.concatenate([key_part[..., half:], key_part[..., :half]], axis=-1)
            new_keys = (
                key_part * tables[step, 0][:, None, :] + swapped * tables[step, 1][:, None, :]
            ).astype(bf16)
            new_values = raw_full[:, kv_width:].reshape(seq_count, kv_heads, HD)
            live = (rows[0] > step)[:, None, :]
            new_kv = jnp.where(live, jnp.concatenate([new_keys, new_values], axis=1), 0)
            kv_outputs.append(
                lax.dynamic_slice_in_dim(
                    new_kv.reshape(seq_count, 2 * kv_width), model_index * col_width, col_width, 1
                )
            )
            fresh.append(lax.dynamic_index_in_dim(new_kv, own_head, 1, False))
            fresh.append(lax.dynamic_index_in_dim(new_kv, kv_heads + own_head, 1, False))
        attention = run(
            functools.partial(query_kernel, step, masks),
            [struct(heads_here, seq_count, HD, dtype=f32)] * 4,
            rows,
            tables,
            normed,
            w_query,
            *caches,
            vmem=KERNEL_VMEM,
            flops=2 * seq_count * width * heads_here * HD,
            moved=2 * width * heads_here * HD,
        )
        part = run(
            output_kernel,
            struct(seq_count, width),
            rows,
            *attention,
            w_output,
            *fresh,
            vmem=KERNEL_VMEM,
        )
        terms = sum_rounds(part, "mp")

    own = run(
        functools.partial(final_kernel, STEPS - 1),
        struct(seq_count, width + STEPS * col_width),
        rows,
        hidden,
        *terms,
        *kv_outputs,
    )
    return tuple(
        run(
            functools.partial(trade_kernel, moves),
            [struct(seq_count, width), struct(STEPS, seq_count, col_width)],
            rows,
            own,
            exchange(own, "dp", 1),
        )
    )


def solution(mesh):
    placed = (
        P(("parts", "dp"), None),
        P(),
        P(None, "mp"),
        P(None, "mp"),
        P("mp", None),
        P(("parts", "dp"), "mp", None),
        P(("parts", "dp"), "mp", None),
        P("parts"),
        P("parts"),
        P("parts"),
        P("parts"),
    )
    return jax.shard_map(
        per_device,
        mesh=mesh,
        in_specs=placed,
        out_specs=(P(("parts", "dp"), None), P(None, ("parts", "dp"), "mp")),
        check_vma=False,
    )
```

time: 179 us -> 152 us (0.85)
  local copies, waits for them, and re-layouts: 36.4 us -> 17.1 us
  Pallas kernels: 25.7 us -> 20.8 us
  other arithmetic: 3.7 us -> 0.38 us
  waiting for transfers between devices: 51.1 us -> 52.9 us
    unnamed x110 -> x40, local copies, waits for them, and re-layouts: 35.6 us -> 16.4 us
    pallas_call x13 -> x20, Pallas kernels: 25.7 us -> 20.8 us  [run(): pl.pallas_call(kernel, out_shape=outs, in_specs=[in_smem] * scalars + [in...]
    ppermute x4, waiting for transfers between devices: 1.83 us -> 6.16 us  [per_device(): lax.ppermute(sent[1], 'mp', to_odd + [(pairs + a, b) for a, b in to_even])]
    ppermute x25 -> x24, waiting for transfers between devices: 49.2 us -> 46.7 us  [exchange(): lax.ppermute(block, axis, [(low, low ^ mask) for low in range(count)])]
    ppermute x25 -> x24, starting transfers between devices: 41.8 us -> 43.7 us  [exchange(): lax.ppermute(block, axis, [(low, low ^ mask) for low in range(count)])]
  transfers between devices with their start and end apart: 33 -> 32, of which waited for: 21 -> 22; matrix products, arithmetic and copies ran while one was open for 2% -> 1% of each run, Pallas kernels for 7% -> 7%
where the time goes in v3:
time: 152 us; the launch traced here: 151 us
  starting transfers between devices  59.1 us (39%)
  waiting for transfers between devices  52.9 us (35%)
  Pallas kernels  20.8 us (14%)
  local copies, waits for them, and re-layouts  17.1 us (11%)
    ppermute x24, waiting for transfers between devices, exchange(): lax.ppermute(block, axis, [(low, low ^ mask) for low in range(count)])  46.7 us
    ppermute x24, starting transfers between devices, exchange(): lax.ppermute(block, axis, [(low, low ^ mask) for low in range(count)])  43.7 us
    pallas_call x20, Pallas kernels, run(): pl.pallas_call(kernel, out_shape=outs, in_specs=[in_smem] * scalars + [in...  20.8 us
    unnamed x40, local copies, waits for them, and re-layouts  16.4 us
    ppermute x4, starting transfers between devices, per_device(): lax.ppermute(sent[1], 'mp', to_odd + [(pairs + a, b) for a, b in to_even])  12.7 us
    ppermute x4, waiting for transfers between devices, per_device(): lax.ppermute(sent[1], 'mp', to_odd + [(pairs + a, b) for a, b in to_even])  6.16 us
  transfers between devices with their start and end apart: 32, of which 22 were waited for; matrix products, arithmetic and copies ran while one was open for 1% of the time, Pallas kernels for 7%

profile of v3, /device:TPU:0, one launch (start us, length us, event | category | flops | bytes accessed | tf_op | source)
XLA Modules:
  0.0 151.2 jit_solution(17627393301660985439)
XLA Ops:
  0.7 1.2 copy-done.4
  1.9 1.2 copy-done.5
  3.2 1.1 shard_map.124
  4.3 4.1 %collective-permute-start = (bf16[2,8,64,128]{3,2,1,0:T(8,128)(2,1)S(1)}, bf16[2,8,64,128]{3,2,1,0:T(8,128)(2,1)S(1)}, u32[]{:S(2)}, u32[]{:S(2)}) collective-permute-start(bf16[2,8,64,128]{3,2,1,0:T(8,128)(2,1)S(1)} %get-tuple-element.54), channel_id=1, source_target_pairs={{0,4},{1,5},{2,6},{3,7},{4,0},{5,1},{6,2},{7,3},{8,12},{9,13},{10,... | collective-permute-start | bytes 786440 | tf_op jit(solution)/shard_map/ppermute | solution.py:25
  8.4 1.3 collective-permute-start.1
  9.9 1.8 %collective-permute-start.3 = (bf16[2,8,64,128]{3,2,1,0:T(8,128)(2,1)S(1)}, bf16[2,8,64,128]{3,2,1,0:T(8,128)(2,1)S(1)}, u32[]{:S(2)}, u32[]{:S(2)}) collective-permute-start(bf16[2,8,64,128]{3,2,1,0:T(8,128)(2,1)S(1)} %get-tuple-element.60), channel_id=1, source_target_pairs={{0,2},{1,3},{2,0},{3,1},{4,6},{5,7},{6,4},{7,5},{8,10},{9,11},{10,... | collective-permute-start | bytes 786440 | tf_op jit(solution)/shard_map/ppermute | solution.py:25
  11.7 1.4 collective-permute-start.4
  13.9 4.1 %collective-permute-done.2.rest_2_ = bf16[2,8,64,128]{3,2,1,0:T(8,128)(2,1)S(1)} collective-permute-done((bf16[2,8,64,128]{3,2,1,0:T(8,128)(2,1)S(1)}, bf16[2,8,64,128]{3,2,1,0:T(8,128)(2,1)S(1)}, u32[]{:S(2)}, u32[]{:S(2)}) %collective-permute-start.2) | collective-permute-done | bytes 262176 | tf_op jit(solution)/shard_map/ppermute | solution.py:25
  18.0 3.6 %collective-permute-start.5 = (bf16[2,8,64,128]{3,2,1,0:T(8,128)(2,1)S(1)}, bf16[2,8,64,128]{3,2,1,0:T(8,128)(2,1)S(1)}, u32[]{:S(2)}, u32[]{:S(2)}) collective-permute-start(bf16[2,8,64,128]{3,2,1,0:T(8,128)(2,1)S(1)} %get-tuple-element.63), channel_id=1, source_target_pairs={{0,6},{1,7},{2,4},{3,5},{4,2},{5,3},{6,0},{7,1},{8,14},{9,15},{10,... | collective-permute-start | bytes 786440 | tf_op jit(solution)/shard_map/ppermute | solution.py:25
  21.5 4.9 %collective-permute-done.3.rest_3_ = bf16[2,8,64,128]{3,2,1,0:T(8,128)(2,1)S(1)} collective-permute-done((bf16[2,8,64,128]{3,2,1,0:T(8,128)(2,1)S(1)}, bf16[2,8,64,128]{3,2,1,0:T(8,128)(2,1)S(1)}, u32[]{:S(2)}, u32[]{:S(2)}) %collective-permute-start.3) | collective-permute-done | bytes 262176 | tf_op jit(solution)/shard_map/ppermute | solution.py:25
  26.4 2.3 %collective-permute-start.6 = (bf16[2,8,64,128]{3,2,1,0:T(8,128)(2,1)S(1)}, bf16[2,8,64,128]{3,2,1,0:T(8,128)(2,1)S(1)}, u32[]{:S(2)}, u32[]{:S(2)}) collective-permute-start(bf16[2,8,64,128]{3,2,1,0:T(8,128)(2,1)S(1)} %get-tuple-element.64), channel_id=1, source_target_pairs={{0,7},{1,6},{2,5},{3,4},{4,3},{5,2},{6,1},{7,0},{8,15},{9,14},{10,... | collective-permute-start | bytes 786440 | tf_op jit(solution)/shard_map/ppermute | solution.py:25
  32.2 1.7 %copy-done.2 = bf16[5120,256]{1,0:T(8,128)(2,1)S(1)} copy-done((bf16[5120,256]{1,0:T(8,128)(2,1)S(1)}, bf16[5120,256]{1,0:T(8,128)(2,1)}, u32[]{:S(2)}) %copy-start.2) | copy-done | bytes 2621464
  34.7 0.9 copy-done.8
  36.9 4.3 %collective-permute-start.8 = (bf16[8,128]{1,0:T(8,128)(2,1)S(1)}, bf16[8,128]{1,0:T(8,128)(2,1)S(1)}, u32[]{:S(2)}, u32[]{:S(2)}) collective-permute-start(bf16[8,128]{1,0:T(8,128)(2,1)S(1)} %get-tuple-element.71), channel_id=1, source_target_pairs={{0,1},{1,3},{2,5},{3,7},{4,0},{5,2},{6,4},{7,6},{8,9},{9,11},{10,1... | collective-permute-start | bytes 6152 | tf_op jit(solution)/shard_map/ppermute | solution.py:354
  41.3 4.0 %collective-permute-done.4.rest_4_ = bf16[2,8,64,128]{3,2,1,0:T(8,128)(2,1)S(1)} collective-permute-done((bf16[2,8,64,128]{3,2,1,0:T(8,128)(2,1)S(1)}, bf16[2,8,64,128]{3,2,1,0:T(8,128)(2,1)S(1)}, u32[]{:S(2)}, u32[]{:S(2)}) %collective-permute-start.4) | collective-permute-done | bytes 262176 | tf_op jit(solution)/shard_map/ppermute | solution.py:25
  45.3 4.0 %copy-done = bf16[5120,1024]{1,0:T(8,128)(2,1)S(1)} copy-done((bf16[5120,1024]{1,0:T(8,128)(2,1)S(1)}, bf16[5120,1024]{1,0:T(8,128)(2,1)}, u32[]{:S(2)}) %copy-start) | copy-done | bytes 10485784
  49.3 2.2 %shard_map.125 = (f32[8,8,128]{2,1,0:T(8,128)S(1)}, f32[8,8,128]{2,1,0:T(8,128)S(1)}, f32[8,8,128]{2,1,0:T(8,128)S(1)}, f32[8,8,128]{2,1,0:T(8,128)S(1)}) custom-call(s32[9,8,128]{2,1,0:T(8,128)S(1)} %get-tuple-element.51.rows_ref, f32[4,2,8,128]{3,2,1,0:T(8,128)S(1)} %get-tuple-element.52.tables_ref, bf16[8,5120]{1,0:T(8,128)(2,1)S(1)} %get-tuple-element.53.normed_ref, ...), custom_call_target="tpu_custom_call" | custom-call | flops 83886080 | bytes 10485760 | tf_op jit(solution)/shard_map/pallas_call | solution.py:219
  51.6 2.6 %collective-permute-done.8.rest_1_ = bf16[8,128]{1,0:T(8,128)(2,1)S(1)} collective-permute-done((bf16[8,128]{1,0:T(8,128)(2,1)S(1)}, bf16[8,128]{1,0:T(8,128)(2,1)S(1)}, u32[]{:S(2)}, u32[]{:S(2)}) %collective-permute-start.8) | collective-permute-done | bytes 2080 | tf_op jit(solution)/shard_map/ppermute | solution.py:354
  54.1 4.0 %copy-done.1 = bf16[1024,5120]{1,0:T(8,128)(2,1)S(1)} copy-done((bf16[1024,5120]{1,0:T(8,128)(2,1)S(1)}, bf16[1024,5120]{1,0:T(8,128)(2,1)}, u32[]{:S(2)}) %copy-start.1) | copy-done | bytes 10485784
  58.1 1.5 %shard_map.126.refs_0_ = bf16[8,5120]{1,0:T(8,128)(2,1)S(1)} custom-call(s32[9,8,128]{2,1,0:T(8,128)S(1)} %get-tuple-element.51.rows_ref, f32[8,8,128]{2,1,0:T(8,128)S(1)} %get-tuple-element.66.query_ref, f32[8,8,128]{2,1,0:T(8,128)S(1)} %get-tuple-element.67.num_ref, f32[8,8,128]{2,1,0:T(8,128)S(1)} %get-tuple-element.68.max_ref, ...), custom_call_target="tpu_custom_call" | custom-call | tf_op jit(solution)/shard_map/pallas_call | solution.py:219
  59.6 8.7 %collective-permute-start.11 = (bf16[8,5120]{1,0:T(8,128)(2,1)S(1)}, bf16[8,5120]{1,0:T(8,128)(2,1)S(1)}, u32[]{:S(2)}, u32[]{:S(2)}) collective-permute-start(bf16[8,5120]{1,0:T(8,128)(2,1)S(1)} %shard_map.126.refs_0_), channel_id=1, source_target_pairs={{0,3},{1,2},{2,1},{3,0},{4,7},{5,6},{6,5},{7,4},{8,11},{9,10},{10,... | collective-permute-start | bytes 245768 | tf_op jit(solution)/shard_map/ppermute | solution.py:25
  68.3 1.3 collective-permute-start.9
  69.6 1.6 %collective-permute-done.11.refs_3_ = bf16[8,5120]{1,0:T(8,128)(2,1)S(1)} collective-permute-done((bf16[8,5120]{1,0:T(8,128)(2,1)S(1)}, bf16[8,5120]{1,0:T(8,128)(2,1)S(1)}, u32[]{:S(2)}, u32[]{:S(2)}) %collective-permute-start.11) | collective-permute-done | bytes 81952 | tf_op jit(solution)/shard_map/ppermute | solution.py:25
  71.3 1.5 collective-permute-done.10.refs_2_
  72.8 4.5 %collective-permute-start.12 = (bf16[8,5120]{1,0:T(8,128)(2,1)S(1)}, bf16[8,5120]{1,0:T(8,128)(2,1)S(1)}, u32[]{:S(2)}, u32[]{:S(2)}) collective-permute-start(bf16[8,5120]{1,0:T(8,128)(2,1)S(1)} %shard_map.127.refs_1_), channel_id=1, source_target_pairs={{0,4},{1,5},{2,6},{3,7},{4,0},{5,1},{6,2},{7,3},{8,12},{9,13},{10,... | collective-permute-start | bytes 245768 | tf_op jit(solution)/shard_map/ppermute | solution.py:25
  77.3 3.5 %collective-permute-done.12.refs_2_ = bf16[8,5120]{1,0:T(8,128)(2,1)S(1)} collective-permute-done((bf16[8,5120]{1,0:T(8,128)(2,1)S(1)}, bf16[8,5120]{1,0:T(8,128)(2,1)S(1)}, u32[]{:S(2)}, u32[]{:S(2)}) %collective-permute-start.12) | collective-permute-done | bytes 81952 | tf_op jit(solution)/shard_map/ppermute | solution.py:25
  80.8 0.8 shard_map.128
  82.3 2.4 %collective-permute-start.14 = (bf16[8,128]{1,0:T(8,128)(2,1)S(1)}, bf16[8,128]{1,0:T(8,128)(2,1)S(1)}, u32[]{:S(2)}, u32[]{:S(2)}) collective-permute-start(bf16[8,128]{1,0:T(8,128)(2,1)S(1)} %get-tuple-element.79), channel_id=1, source_target_pairs={{0,1},{1,3},{2,5},{3,7},{4,0},{5,2},{6,4},{7,6},{8,9},{9,11},{10,1... | collective-permute-start | bytes 6152 | tf_op jit(solution)/shard_map/ppermute | solution.py:354
  84.8 2.2 %shard_map.129 = (f32[8,8,128]{2,1,0:T(8,128)S(1)}, f32[8,8,128]{2,1,0:T(8,128)S(1)}, f32[8,8,128]{2,1,0:T(8,128)S(1)}, f32[8,8,128]{2,1,0:T(8,128)S(1)}) custom-call(s32[9,8,128]{2,1,0:T(8,128)S(1)} %get-tuple-element.51.rows_ref, f32[4,2,8,128]{3,2,1,0:T(8,128)S(1)} %get-tuple-element.52.tables_ref, bf16[8,5120]{1,0:T(8,128)(2,1)S(1)} %get-tuple-element.73.normed_ref, ...), custom_call_target="tpu_custom_call" | custom-call | flops 83886080 | bytes 10485760 | tf_op jit(solution)/shard_map/pallas_call | solution.py:219
  87.0 1.3 collective-permute-done.14.rest_3_
  88.3 1.5 %shard_map.130.refs_0_ = bf16[8,5120]{1,0:T(8,128)(2,1)S(1)} custom-call(s32[9,8,128]{2,1,0:T(8,128)S(1)} %get-tuple-element.51.rows_ref, f32[8,8,128]{2,1,0:T(8,128)S(1)} %get-tuple-element.74.query_ref, f32[8,8,128]{2,1,0:T(8,128)S(1)} %get-tuple-element.75.num_ref, f32[8,8,128]{2,1,0:T(8,128)S(1)} %get-tuple-element.76.max_ref, ...), custom_call_target="tpu_custom_call" | custom-call | tf_op jit(solution)/shard_map/pallas_call | solution.py:219
  89.8 2.1 %collective-permute-start.17 = (bf16[8,5120]{1,0:T(8,128)(2,1)S(1)}, bf16[8,5120]{1,0:T(8,128)(2,1)S(1)}, u32[]{:S(2)}, u32[]{:S(2)}) collective-permute-start(bf16[8,5120]{1,0:T(8,128)(2,1)S(1)} %shard_map.130.refs_0_), channel_id=1, source_target_pairs={{0,3},{1,2},{2,1},{3,0},{4,7},{5,6},{6,5},{7,4},{8,11},{9,10},{10,... | collective-permute-start | bytes 245768 | tf_op jit(solution)/shard_map/ppermute | solution.py:25
  91.9 0.8 collective-permute-start.16
  92.7 0.8 collective-permute-start.15
  93.5 1.7 %collective-permute-done.17.refs_3_ = bf16[8,5120]{1,0:T(8,128)(2,1)S(1)} collective-permute-done((bf16[8,5120]{1,0:T(8,128)(2,1)S(1)}, bf16[8,5120]{1,0:T(8,128)(2,1)S(1)}, u32[]{:S(2)}, u32[]{:S(2)}) %collective-permute-start.17) | collective-permute-done | bytes 81952 | tf_op jit(solution)/shard_map/ppermute | solution.py:25
  95.2 2.0 %collective-permute-done.16.refs_2_ = bf16[8,5120]{1,0:T(8,128)(2,1)S(1)} collective-permute-done((bf16[8,5120]{1,0:T(8,128)(2,1)S(1)}, bf16[8,5120]{1,0:T(8,128)(2,1)S(1)}, u32[]{:S(2)}, u32[]{:S(2)}) %collective-permute-start.16) | collective-permute-done | bytes 81952 | tf_op jit(solution)/shard_map/ppermute | solution.py:25
  97.2 1.5 %collective-permute-start.18 = (bf16[8,5120]{1,0:T(8,128)(2,1)S(1)}, bf16[8,5120]{1,0:T(8,128)(2,1)S(1)}, u32[]{:S(2)}, u32[]{:S(2)}) collective-permute-start(bf16[8,5120]{1,0:T(8,128)(2,1)S(1)} %shard_map.131.refs_1_), channel_id=1, source_target_pairs={{0,4},{1,5},{2,6},{3,7},{4,0},{5,1},{6,2},{7,3},{8,12},{9,13},{10,... | collective-permute-start | bytes 245768 | tf_op jit(solution)/shard_map/ppermute | solution.py:25
  98.8 4.8 %collective-permute-done.18.refs_2_ = bf16[8,5120]{1,0:T(8,128)(2,1)S(1)} collective-permute-done((bf16[8,5120]{1,0:T(8,128)(2,1)S(1)}, bf16[8,5120]{1,0:T(8,128)(2,1)S(1)}, u32[]{:S(2)}, u32[]{:S(2)}) %collective-permute-start.18) | collective-permute-done | bytes 81952 | tf_op jit(solution)/shard_map/ppermute | solution.py:25
  103.5 0.8 shard_map.132
  105.0 3.3 %collective-permute-start.20 = (bf16[8,128]{1,0:T(8,128)(2,1)S(1)}, bf16[8,128]{1,0:T(8,128)(2,1)S(1)}, u32[]{:S(2)}, u32[]{:S(2)}) collective-permute-start(bf16[8,128]{1,0:T(8,128)(2,1)S(1)} %get-tuple-element.87), channel_id=1, source_target_pairs={{0,1},{1,3},{2,5},{3,7},{4,0},{5,2},{6,4},{7,6},{8,9},{9,11},{10,1... | collective-permute-start | bytes 6152 | tf_op jit(solution)/shard_map/ppermute | solution.py:354
  108.3 2.2 %shard_map.133 = (f32[8,8,128]{2,1,0:T(8,128)S(1)}, f32[8,8,128]{2,1,0:T(8,128)S(1)}, f32[8,8,128]{2,1,0:T(8,128)S(1)}, f32[8,8,128]{2,1,0:T(8,128)S(1)}) custom-call(s32[9,8,128]{2,1,0:T(8,128)S(1)} %get-tuple-element.51.rows_ref, f32[4,2,8,128]{3,2,1,0:T(8,128)S(1)} %get-tuple-element.52.tables_ref, bf16[8,5120]{1,0:T(8,128)(2,1)S(1)} %get-tuple-element.81.normed_ref, ...), custom_call_target="tpu_custom_call" | custom-call | flops 83886080 | bytes 10485760 | tf_op jit(solution)/shard_map/pallas_call | solution.py:219
  110.5 1.5 collective-permute-done.20.rest_5_
  112.0 1.5 %shard_map.134.refs_0_ = bf16[8,5120]{1,0:T(8,128)(2,1)S(1)} custom-call(s32[9,8,128]{2,1,0:T(8,128)S(1)} %get-tuple-element.51.rows_ref, f32[8,8,128]{2,1,0:T(8,128)S(1)} %get-tuple-element.82.query_ref, f32[8,8,128]{2,1,0:T(8,128)S(1)} %get-tuple-element.83.num_ref, f32[8,8,128]{2,1,0:T(8,128)S(1)} %get-tuple-element.84.max_ref, ...), custom_call_target="tpu_custom_call" | custom-call | tf_op jit(solution)/shard_map/pallas_call | solution.py:219
  113.5 1.4 collective-permute-start.23
  114.9 1.3 collective-permute-start.22
  116.2 0.8 collective-permute-start.21
  117.0 1.9 %collective-permute-done.23.refs_3_ = bf16[8,5120]{1,0:T(8,128)(2,1)S(1)} collective-permute-done((bf16[8,5120]{1,0:T(8,128)(2,1)S(1)}, bf16[8,5120]{1,0:T(8,128)(2,1)S(1)}, u32[]{:S(2)}, u32[]{:S(2)}) %collective-permute-start.23) | collective-permute-done | bytes 81952 | tf_op jit(solution)/shard_map/ppermute | solution.py:25
  119.5 1.1 collective-permute-done.21.refs_1_
  120.7 1.3 collective-permute-start.24
  122.0 5.0 %collective-permute-done.24.refs_2_ = bf16[8,5120]{1,0:T(8,128)(2,1)S(1)} collective-permute-done((bf16[8,5120]{1,0:T(8,128)(2,1)S(1)}, bf16[8,5120]{1,0:T(8,128)(2,1)S(1)}, u32[]{:S(2)}, u32[]{:S(2)}) %collective-permute-start.24) | collective-permute-done | bytes 81952 | tf_op jit(solution)/shard_map/ppermute | solution.py:25
  127.0 0.8 shard_map.136
  128.4 2.7 %collective-permute-start.26 = (bf16[8,128]{1,0:T(8,128)(2,1)S(1)}, bf16[8,128]{1,0:T(8,128)(2,1)S(1)}, u32[]{:S(2)}, u32[]{:S(2)}) collective-permute-start(bf16[8,128]{1,0:T(8,128)(2,1)S(1)} %get-tuple-element.95), channel_id=1, source_target_pairs={{0,1},{1,3},{2,5},{3,7},{4,0},{5,2},{6,4},{7,6},{8,9},{9,11},{10,1... | collective-permute-start | bytes 6152 | tf_op jit(solution)/shard_map/ppermute | solution.py:354
  131.1 2.2 %shard_map.137 = (f32[8,8,128]{2,1,0:T(8,128)S(1)}, f32[8,8,128]{2,1,0:T(8,128)S(1)}, f32[8,8,128]{2,1,0:T(8,128)S(1)}, f32[8,8,128]{2,1,0:T(8,128)S(1)}) custom-call(s32[9,8,128]{2,1,0:T(8,128)S(1)} %get-tuple-element.51.rows_ref, f32[4,2,8,128]{3,2,1,0:T(8,128)S(1)} %get-tuple-element.52.tables_ref, bf16[8,5120]{1,0:T(8,128)(2,1)S(1)} %get-tuple-element.89.normed_ref, ...), custom_call_target="tpu_custom_call" | custom-call | flops 83886080 | bytes 10485760 | tf_op jit(solution)/shard_map/pallas_call | solution.py:219
  133.4 0.8 collective-permute-done.26.rest_7_
  134.2 1.6 %shard_map.138.refs_0_ = bf16[8,5120]{1,0:T(8,128)(2,1)S(1)} custom-call(s32[9,8,128]{2,1,0:T(8,128)S(1)} %get-tuple-element.51.rows_ref, f32[8,8,128]{2,1,0:T(8,128)S(1)} %get-tuple-element.90.query_ref, f32[8,8,128]{2,1,0:T(8,128)S(1)} %get-tuple-element.91.num_ref, f32[8,8,128]{2,1,0:T(8,128)S(1)} %get-tuple-element.92.max_ref, ...), custom_call_target="tpu_custom_call" | custom-call | tf_op jit(solution)/shard_map/pallas_call | solution.py:219
  135.8 1.0 collective-permute-start.29
  136.7 1.9 %collective-permute-start.28 = (bf16[8,5120]{1,0:T(8,128)(2,1)S(1)}, bf16[8,5120]{1,0:T(8,128)(2,1)S(1)}, u32[]{:S(2)}, u32[]{:S(2)}) collective-permute-start(bf16[8,5120]{1,0:T(8,128)(2,1)S(1)} %shard_map.138.refs_0_), channel_id=1, source_target_pairs={{0,2},{1,3},{2,0},{3,1},{4,6},{5,7},{6,4},{7,5},{8,10},{9,11},{10,... | collective-permute-start | bytes 245768 | tf_op jit(solution)/shard_map/ppermute | solution.py:25
  139.3 1.9 %collective-permute-done.29.refs_3_ = bf16[8,5120]{1,0:T(8,128)(2,1)S(1)} collective-permute-done((bf16[8,5120]{1,0:T(8,128)(2,1)S(1)}, bf16[8,5120]{1,0:T(8,128)(2,1)S(1)}, u32[]{:S(2)}, u32[]{:S(2)}) %collective-permute-start.29) | collective-permute-done | bytes 81952 | tf_op jit(solution)/shard_map/ppermute | solution.py:25
  141.1 0.8 collective-permute-done.28.refs_2_
  141.9 1.1 collective-permute-done.27.refs_1_
  143.1 1.0 collective-permute-start.30
  144.1 4.9 %collective-permute-done.30.second_ref = bf16[8,5120]{1,0:T(8,128)(2,1)S(1)} collective-permute-done((bf16[8,5120]{1,0:T(8,128)(2,1)S(1)}, bf16[8,5120]{1,0:T(8,128)(2,1)S(1)}, u32[]{:S(2)}, u32[]{:S(2)}) %collective-permute-start.30) | collective-permute-done | bytes 81952 | tf_op jit(solution)/shard_map/ppermute | solution.py:25
  149.1 1.3 collective-permute-done.31.other_ref
  150.4 0.8 shard_map.141
  (69 shorter events, 10.3 us)
Async XLA Ops:
  0.7 1.2 copy-start.4
  1.9 1.2 copy-start.5
  4.3 32.0 %collective-permute-start = (bf16[2,8,64,128]{3,2,1,0:T(8,128)(2,1)S(1)}, bf16[2,8,64,128]{3,2,1,0:T(8,128)(2,1)S(1)}, u32[]{:S(2)}, u32[]{:S(2)}) collective-permute-start(bf16[2,8,64,128]{3,2,1,0:T(8,128)(2,1)S(1)} %get-tuple-element.54), channel_id=1, source_target_pairs={{0,4},{1,5},{2,6},{3,7},{4,0},{5,1},{6,2},{7,3},{8,12},{9,13},{10,... | collective-permute-start | bytes 786440 | tf_op jit(solution)/shard_map/ppermute | solution.py:25
  8.4 28.6 %collective-permute-start.1 = (bf16[2,8,64,128]{3,2,1,0:T(8,128)(2,1)S(1)}, bf16[2,8,64,128]{3,2,1,0:T(8,128)(2,1)S(1)}, u32[]{:S(2)}, u32[]{:S(2)}) collective-permute-start(bf16[2,8,64,128]{3,2,1,0:T(8,128)(2,1)S(1)} %get-tuple-element.55), channel_id=1, source_target_pairs={{0,5},{1,4},{2,7},{3,6},{4,1},{5,0},{6,3},{7,2},{8,13},{9,12},{10,... | collective-permute-start | bytes 786440 | tf_op jit(solution)/shard_map/ppermute | solution.py:25
  9.6 8.3 %collective-permute-start.2 = (bf16[2,8,64,128]{3,2,1,0:T(8,128)(2,1)S(1)}, bf16[2,8,64,128]{3,2,1,0:T(8,128)(2,1)S(1)}, u32[]{:S(2)}, u32[]{:S(2)}) collective-permute-start(bf16[2,8,64,128]{3,2,1,0:T(8,128)(2,1)S(1)} %get-tuple-element.57), channel_id=1, source_target_pairs={{0,1},{1,0},{2,3},{3,2},{4,5},{5,4},{6,7},{7,6},{8,9},{9,8},{10,11... | collective-permute-start | bytes 786440 | tf_op jit(solution)/shard_map/ppermute | solution.py:25
  9.9 16.5 %collective-permute-start.3 = (bf16[2,8,64,128]{3,2,1,0:T(8,128)(2,1)S(1)}, bf16[2,8,64,128]{3,2,1,0:T(8,128)(2,1)S(1)}, u32[]{:S(2)}, u32[]{:S(2)}) collective-permute-start(bf16[2,8,64,128]{3,2,1,0:T(8,128)(2,1)S(1)} %get-tuple-element.60), channel_id=1, source_target_pairs={{0,2},{1,3},{2,0},{3,1},{4,6},{5,7},{6,4},{7,5},{8,10},{9,11},{10,... | collective-permute-start | bytes 786440 | tf_op jit(solution)/shard_map/ppermute | solution.py:25
  11.7 33.6 %collective-permute-start.4 = (bf16[2,8,64,128]{3,2,1,0:T(8,128)(2,1)S(1)}, bf16[2,8,64,128]{3,2,1,0:T(8,128)(2,1)S(1)}, u32[]{:S(2)}, u32[]{:S(2)}) collective-permute-start(bf16[2,8,64,128]{3,2,1,0:T(8,128)(2,1)S(1)} %get-tuple-element.62), channel_id=1, source_target_pairs={{0,3},{1,2},{2,1},{3,0},{4,7},{5,6},{6,5},{7,4},{8,11},{9,10},{10,... | collective-permute-start | bytes 786440 | tf_op jit(solution)/shard_map/ppermute | solution.py:25
  18.0 27.3 %collective-permute-start.5 = (bf16[2,8,64,128]{3,2,1,0:T(8,128)(2,1)S(1)}, bf16[2,8,64,128]{3,2,1,0:T(8,128)(2,1)S(1)}, u32[]{:S(2)}, u32[]{:S(2)}) collective-permute-start(bf16[2,8,64,128]{3,2,1,0:T(8,128)(2,1)S(1)} %get-tuple-element.63), channel_id=1, source_target_pairs={{0,6},{1,7},{2,4},{3,5},{4,2},{5,3},{6,0},{7,1},{8,14},{9,15},{10,... | collective-permute-start | bytes 786440 | tf_op jit(solution)/shard_map/ppermute | solution.py:25
  26.4 18.9 %collective-permute-start.6 = (bf16[2,8,64,128]{3,2,1,0:T(8,128)(2,1)S(1)}, bf16[2,8,64,128]{3,2,1,0:T(8,128)(2,1)S(1)}, u32[]{:S(2)}, u32[]{:S(2)}) collective-permute-start(bf16[2,8,64,128]{3,2,1,0:T(8,128)(2,1)S(1)} %get-tuple-element.64), channel_id=1, source_target_pairs={{0,7},{1,6},{2,5},{3,4},{4,3},{5,2},{6,1},{7,0},{8,15},{9,14},{10,... | collective-permute-start | bytes 786440 | tf_op jit(solution)/shard_map/ppermute | solution.py:25
  29.0 0.7 copy-start.10
  29.6 0.7 copy-start.11
  30.3 0.7 copy-start.12
  30.9 0.7 copy-start.13
  32.2 1.7 %copy-start.2 = (bf16[5120,256]{1,0:T(8,128)(2,1)S(1)}, bf16[5120,256]{1,0:T(8,128)(2,1)}, u32[]{:S(2)}) copy-start(bf16[5120,256]{1,0:T(8,128)(2,1)} %w_ref.21) | copy-start | bytes 7864324
  33.9 0.7 copy-start.6
  34.7 0.9 copy-start.8
  36.3 15.3 %collective-permute-start.7 = (bf16[8,128]{1,0:T(8,128)(2,1)S(1)}, bf16[8,128]{1,0:T(8,128)(2,1)S(1)}, u32[]{:S(2)}, u32[]{:S(2)}) collective-permute-start(bf16[8,128]{1,0:T(8,128)(2,1)S(1)} %get-tuple-element.70), channel_id=1, source_target_pairs={{0,0},{1,2},{2,4},{3,6},{4,1},{5,3},{6,5},{7,7},{8,8},{9,10},{10,1... | collective-permute-start | bytes 6152 | tf_op jit(solution)/shard_map/ppermute | solution.py:351
  36.9 17.2 %collective-permute-start.8 = (bf16[8,128]{1,0:T(8,128)(2,1)S(1)}, bf16[8,128]{1,0:T(8,128)(2,1)S(1)}, u32[]{:S(2)}, u32[]{:S(2)}) collective-permute-start(bf16[8,128]{1,0:T(8,128)(2,1)S(1)} %get-tuple-element.71), channel_id=1, source_target_pairs={{0,1},{1,3},{2,5},{3,7},{4,0},{5,2},{6,4},{7,6},{8,9},{9,11},{10,1... | collective-permute-start | bytes 6152 | tf_op jit(solution)/shard_map/ppermute | solution.py:354
  45.3 4.0 %copy-start = (bf16[5120,1024]{1,0:T(8,128)(2,1)S(1)}, bf16[5120,1024]{1,0:T(8,128)(2,1)}, u32[]{:S(2)}) copy-start(bf16[5120,1024]{1,0:T(8,128)(2,1)} %w_ref.22) | copy-start | bytes 31457284
  49.3 31.5 %copy-start.3 = (bf16[5120,256]{1,0:T(8,128)(2,1)S(1)}, bf16[5120,256]{1,0:T(8,128)(2,1)}, u32[]{:S(2)}) copy-start(bf16[5120,256]{1,0:T(8,128)(2,1)} %w_ref.21) | copy-start | bytes 7864324
  49.3 31.5 %copy-start.7 = (f32[5120]{0:T(1024)S(1)}, f32[5120]{0:T(1024)}, u32[]{:S(2)}) copy-start(f32[5120]{0:T(1024)} %param.12) | copy-start | bytes 61444
  49.3 31.5 %copy-start.9 = (bf16[8,5120]{1,0:T(8,128)(2,1)S(1)}, bf16[8,5120]{1,0:T(8,128)(2,1)}, u32[]{:S(2)}) copy-start(bf16[8,5120]{1,0:T(8,128)(2,1)} %refs_0_.3) | copy-start | bytes 245764
  49.3 35.4 %slice-start = ((s8[10485760]{0:T(1024)(128)(4,1)}), s8[4194304]{0:T(1024)(128)(4,1)S(1)}, s32[]{:S(2)}) async-start(s8[10485760]{0:T(1024)(128)(4,1)} %bitcast.9), calls=%async_computation | async-start | bytes 8388608
  49.3 35.4 %slice-start.1 = ((s8[10485760]{0:T(1024)(128)(4,1)}), s8[4194304]{0:T(1024)(128)(4,1)S(1)}, s32[]{:S(2)}) async-start(s8[10485760]{0:T(1024)(128)(4,1)} %bitcast.9), calls=%async_computation.1 | async-start | bytes 8388608
  54.1 4.0 %copy-start.1 = (bf16[1024,5120]{1,0:T(8,128)(2,1)S(1)}, bf16[1024,5120]{1,0:T(8,128)(2,1)}, u32[]{:S(2)}) copy-start(bf16[1024,5120]{1,0:T(8,128)(2,1)} %w_ref.23) | copy-start | bytes 31457284
  58.1 26.6 %slice-start.2 = ((s8[10485760]{0:T(1024)(128)(4,1)}), s8[2097152]{0:T(1024)(128)(4,1)S(1)}, s32[]{:S(2)}) async-start(s8[10485760]{0:T(1024)(128)(4,1)} %bitcast.9), calls=%async_computation.2 | async-start | bytes 4194304
  58.1 30.1 %slice-start.3 = ((s8[10485760]{0:T(1024)(128)(4,1)}), s8[4194304]{0:T(1024)(128)(4,1)S(1)}, s32[]{:S(2)}) async-start(s8[10485760]{0:T(1024)(128)(4,1)} %bitcast.11), calls=%async_computation.3 | async-start | bytes 8388608
  58.1 30.1 %slice-start.4 = ((s8[10485760]{0:T(1024)(128)(4,1)}), s8[4194304]{0:T(1024)(128)(4,1)S(1)}, s32[]{:S(2)}) async-start(s8[10485760]{0:T(1024)(128)(4,1)} %bitcast.11), calls=%async_computation.4 | async-start | bytes 8388608
  59.6 11.6 %collective-permute-start.11 = (bf16[8,5120]{1,0:T(8,128)(2,1)S(1)}, bf16[8,5120]{1,0:T(8,128)(2,1)S(1)}, u32[]{:S(2)}, u32[]{:S(2)}) collective-permute-start(bf16[8,5120]{1,0:T(8,128)(2,1)S(1)} %shard_map.126.refs_0_), channel_id=1, source_target_pairs={{0,3},{1,2},{2,1},{3,0},{4,7},{5,6},{6,5},{7,4},{8,11},{9,10},{10,... | collective-permute-start | bytes 245768 | tf_op jit(solution)/shard_map/ppermute | solution.py:25
  68.3 4.4 %collective-permute-start.10 = (bf16[8,5120]{1,0:T(8,128)(2,1)S(1)}, bf16[8,5120]{1,0:T(8,128)(2,1)S(1)}, u32[]{:S(2)}, u32[]{:S(2)}) collective-permute-start(bf16[8,5120]{1,0:T(8,128)(2,1)S(1)} %shard_map.126.refs_0_), channel_id=1, source_target_pairs={{0,2},{1,3},{2,0},{3,1},{4,6},{5,7},{6,4},{7,5},{8,10},{9,11},{10,... | collective-permute-start | bytes 245768 | tf_op jit(solution)/shard_map/ppermute | solution.py:25
  68.3 4.4 %collective-permute-start.9 = (bf16[8,5120]{1,0:T(8,128)(2,1)S(1)}, bf16[8,5120]{1,0:T(8,128)(2,1)S(1)}, u32[]{:S(2)}, u32[]{:S(2)}) collective-permute-start(bf16[8,5120]{1,0:T(8,128)(2,1)S(1)} %shard_map.126.refs_0_), channel_id=1, source_target_pairs={{0,1},{1,0},{2,3},{3,2},{4,5},{5,4},{6,7},{7,6},{8,9},{9,8},{10,11... | collective-permute-start | bytes 245768 | tf_op jit(solution)/shard_map/ppermute | solution.py:25
  72.8 8.0 %collective-permute-start.12 = (bf16[8,5120]{1,0:T(8,128)(2,1)S(1)}, bf16[8,5120]{1,0:T(8,128)(2,1)S(1)}, u32[]{:S(2)}, u32[]{:S(2)}) collective-permute-start(bf16[8,5120]{1,0:T(8,128)(2,1)S(1)} %shard_map.127.refs_1_), channel_id=1, source_target_pairs={{0,4},{1,5},{2,6},{3,7},{4,0},{5,1},{6,2},{7,3},{8,12},{9,13},{10,... | collective-permute-start | bytes 245768 | tf_op jit(solution)/shard_map/ppermute | solution.py:25
  81.6 5.3 %collective-permute-start.13 = (bf16[8,128]{1,0:T(8,128)(2,1)S(1)}, bf16[8,128]{1,0:T(8,128)(2,1)S(1)}, u32[]{:S(2)}, u32[]{:S(2)}) collective-permute-start(bf16[8,128]{1,0:T(8,128)(2,1)S(1)} %get-tuple-element.78), channel_id=1, source_target_pairs={{0,0},{1,2},{2,4},{3,6},{4,1},{5,3},{6,5},{7,7},{8,8},{9,10},{10,1... | collective-permute-start | bytes 6152 | tf_op jit(solution)/shard_map/ppermute | solution.py:351
  82.3 5.9 %collective-permute-start.14 = (bf16[8,128]{1,0:T(8,128)(2,1)S(1)}, bf16[8,128]{1,0:T(8,128)(2,1)S(1)}, u32[]{:S(2)}, u32[]{:S(2)}) collective-permute-start(bf16[8,128]{1,0:T(8,128)(2,1)S(1)} %get-tuple-element.79), channel_id=1, source_target_pairs={{0,1},{1,3},{2,5},{3,7},{4,0},{5,2},{6,4},{7,6},{8,9},{9,11},{10,1... | collective-permute-start | bytes 6152 | tf_op jit(solution)/shard_map/ppermute | solution.py:354
  84.7 3.5 %slice-start.5 = ((s8[10485760]{0:T(1024)(128)(4,1)}), s8[2097152]{0:T(1024)(128)(4,1)S(1)}, s32[]{:S(2)}) async-start(s8[10485760]{0:T(1024)(128)(4,1)} %bitcast.11), calls=%async_computation.5 | async-start | bytes 4194304
  89.8 5.3 %collective-permute-start.17 = (bf16[8,5120]{1,0:T(8,128)(2,1)S(1)}, bf16[8,5120]{1,0:T(8,128)(2,1)S(1)}, u32[]{:S(2)}, u32[]{:S(2)}) collective-permute-start(bf16[8,5120]{1,0:T(8,128)(2,1)S(1)} %shard_map.130.refs_0_), channel_id=1, source_target_pairs={{0,3},{1,2},{2,1},{3,0},{4,7},{5,6},{6,5},{7,4},{8,11},{9,10},{10,... | collective-permute-start | bytes 245768 | tf_op jit(solution)/shard_map/ppermute | solution.py:25
  91.9 5.3 %collective-permute-start.16 = (bf16[8,5120]{1,0:T(8,128)(2,1)S(1)}, bf16[8,5120]{1,0:T(8,128)(2,1)S(1)}, u32[]{:S(2)}, u32[]{:S(2)}) collective-permute-start(bf16[8,5120]{1,0:T(8,128)(2,1)S(1)} %shard_map.130.refs_0_), channel_id=1, source_target_pairs={{0,2},{1,3},{2,0},{3,1},{4,6},{5,7},{6,4},{7,5},{8,10},{9,11},{10,... | collective-permute-start | bytes 245768 | tf_op jit(solution)/shard_map/ppermute | solution.py:25
  92.7 4.5 %collective-permute-start.15 = (bf16[8,5120]{1,0:T(8,128)(2,1)S(1)}, bf16[8,5120]{1,0:T(8,128)(2,1)S(1)}, u32[]{:S(2)}, u32[]{:S(2)}) collective-permute-start(bf16[8,5120]{1,0:T(8,128)(2,1)S(1)} %shard_map.130.refs_0_), channel_id=1, source_target_pairs={{0,1},{1,0},{2,3},{3,2},{4,5},{5,4},{6,7},{7,6},{8,9},{9,8},{10,11... | collective-permute-start | bytes 245768 | tf_op jit(solution)/shard_map/ppermute | solution.py:25
  97.2 6.3 %collective-permute-start.18 = (bf16[8,5120]{1,0:T(8,128)(2,1)S(1)}, bf16[8,5120]{1,0:T(8,128)(2,1)S(1)}, u32[]{:S(2)}, u32[]{:S(2)}) collective-permute-start(bf16[8,5120]{1,0:T(8,128)(2,1)S(1)} %shard_map.131.refs_1_), channel_id=1, source_target_pairs={{0,4},{1,5},{2,6},{3,7},{4,0},{5,1},{6,2},{7,3},{8,12},{9,13},{10,... | collective-permute-start | bytes 245768 | tf_op jit(solution)/shard_map/ppermute | solution.py:25
  104.3 6.2 %collective-permute-start.19 = (bf16[8,128]{1,0:T(8,128)(2,1)S(1)}, bf16[8,128]{1,0:T(8,128)(2,1)S(1)}, u32[]{:S(2)}, u32[]{:S(2)}) collective-permute-start(bf16[8,128]{1,0:T(8,128)(2,1)S(1)} %get-tuple-element.86), channel_id=1, source_target_pairs={{0,0},{1,2},{2,4},{3,6},{4,1},{5,3},{6,5},{7,7},{8,8},{9,10},{10,1... | collective-permute-start | bytes 6152 | tf_op jit(solution)/shard_map/ppermute | solution.py:351
  105.0 7.0 %collective-permute-start.20 = (bf16[8,128]{1,0:T(8,128)(2,1)S(1)}, bf16[8,128]{1,0:T(8,128)(2,1)S(1)}, u32[]{:S(2)}, u32[]{:S(2)}) collective-permute-start(bf16[8,128]{1,0:T(8,128)(2,1)S(1)} %get-tuple-element.87), channel_id=1, source_target_pairs={{0,1},{1,3},{2,5},{3,7},{4,0},{5,2},{6,4},{7,6},{8,9},{9,11},{10,1... | collective-permute-start | bytes 6152 | tf_op jit(solution)/shard_map/ppermute | solution.py:354
  113.5 5.3 %collective-permute-start.23 = (bf16[8,5120]{1,0:T(8,128)(2,1)S(1)}, bf16[8,5120]{1,0:T(8,128)(2,1)S(1)}, u32[]{:S(2)}, u32[]{:S(2)}) collective-permute-start(bf16[8,5120]{1,0:T(8,128)(2,1)S(1)} %shard_map.134.refs_0_), channel_id=1, source_target_pairs={{0,3},{1,2},{2,1},{3,0},{4,7},{5,6},{6,5},{7,4},{8,11},{9,10},{10,... | collective-permute-start | bytes 245768 | tf_op jit(solution)/shard_map/ppermute | solution.py:25
  114.9 4.6 %collective-permute-start.22 = (bf16[8,5120]{1,0:T(8,128)(2,1)S(1)}, bf16[8,5120]{1,0:T(8,128)(2,1)S(1)}, u32[]{:S(2)}, u32[]{:S(2)}) collective-permute-start(bf16[8,5120]{1,0:T(8,128)(2,1)S(1)} %shard_map.134.refs_0_), channel_id=1, source_target_pairs={{0,2},{1,3},{2,0},{3,1},{4,6},{5,7},{6,4},{7,5},{8,10},{9,11},{10,... | collective-permute-start | bytes 245768 | tf_op jit(solution)/shard_map/ppermute | solution.py:25
  116.2 4.4 %collective-permute-start.21 = (bf16[8,5120]{1,0:T(8,128)(2,1)S(1)}, bf16[8,5120]{1,0:T(8,128)(2,1)S(1)}, u32[]{:S(2)}, u32[]{:S(2)}) collective-permute-start(bf16[8,5120]{1,0:T(8,128)(2,1)S(1)} %shard_map.134.refs_0_), channel_id=1, source_target_pairs={{0,1},{1,0},{2,3},{3,2},{4,5},{5,4},{6,7},{7,6},{8,9},{9,8},{10,11... | collective-permute-start | bytes 245768 | tf_op jit(solution)/shard_map/ppermute | solution.py:25
  120.7 6.3 %collective-permute-start.24 = (bf16[8,5120]{1,0:T(8,128)(2,1)S(1)}, bf16[8,5120]{1,0:T(8,128)(2,1)S(1)}, u32[]{:S(2)}, u32[]{:S(2)}) collective-permute-start(bf16[8,5120]{1,0:T(8,128)(2,1)S(1)} %shard_map.135.refs_1_), channel_id=1, source_target_pairs={{0,4},{1,5},{2,6},{3,7},{4,0},{5,1},{6,2},{7,3},{8,12},{9,13},{10,... | collective-permute-start | bytes 245768 | tf_op jit(solution)/shard_map/ppermute | solution.py:25
  127.8 5.6 %collective-permute-start.25 = (bf16[8,128]{1,0:T(8,128)(2,1)S(1)}, bf16[8,128]{1,0:T(8,128)(2,1)S(1)}, u32[]{:S(2)}, u32[]{:S(2)}) collective-permute-start(bf16[8,128]{1,0:T(8,128)(2,1)S(1)} %get-tuple-element.94), channel_id=1, source_target_pairs={{0,0},{1,2},{2,4},{3,6},{4,1},{5,3},{6,5},{7,7},{8,8},{9,10},{10,1... | collective-permute-start | bytes 6152 | tf_op jit(solution)/shard_map/ppermute | solution.py:351
  128.4 5.8 %collective-permute-start.26 = (bf16[8,128]{1,0:T(8,128)(2,1)S(1)}, bf16[8,128]{1,0:T(8,128)(2,1)S(1)}, u32[]{:S(2)}, u32[]{:S(2)}) collective-permute-start(bf16[8,128]{1,0:T(8,128)(2,1)S(1)} %get-tuple-element.95), channel_id=1, source_target_pairs={{0,1},{1,3},{2,5},{3,7},{4,0},{5,2},{6,4},{7,6},{8,9},{9,11},{10,1... | collective-permute-start | bytes 6152 | tf_op jit(solution)/shard_map/ppermute | solution.py:354
  135.8 5.3 %collective-permute-start.29 = (bf16[8,5120]{1,0:T(8,128)(2,1)S(1)}, bf16[8,5120]{1,0:T(8,128)(2,1)S(1)}, u32[]{:S(2)}, u32[]{:S(2)}) collective-permute-start(bf16[8,5120]{1,0:T(8,128)(2,1)S(1)} %shard_map.138.refs_0_), channel_id=1, source_target_pairs={{0,3},{1,2},{2,1},{3,0},{4,7},{5,6},{6,5},{7,4},{8,11},{9,10},{10,... | collective-permute-start | bytes 245768 | tf_op jit(solution)/shard_map/ppermute | solution.py:25
  136.7 5.2 %collective-permute-start.28 = (bf16[8,5120]{1,0:T(8,128)(2,1)S(1)}, bf16[8,5120]{1,0:T(8,128)(2,1)S(1)}, u32[]{:S(2)}, u32[]{:S(2)}) collective-permute-start(bf16[8,5120]{1,0:T(8,128)(2,1)S(1)} %shard_map.138.refs_0_), channel_id=1, source_target_pairs={{0,2},{1,3},{2,0},{3,1},{4,6},{5,7},{6,4},{7,5},{8,10},{9,11},{10,... | collective-permute-start | bytes 245768 | tf_op jit(solution)/shard_map/ppermute | solution.py:25
  138.6 4.4 %collective-permute-start.27 = (bf16[8,5120]{1,0:T(8,128)(2,1)S(1)}, bf16[8,5120]{1,0:T(8,128)(2,1)S(1)}, u32[]{:S(2)}, u32[]{:S(2)}) collective-permute-start(bf16[8,5120]{1,0:T(8,128)(2,1)S(1)} %shard_map.138.refs_0_), channel_id=1, source_target_pairs={{0,1},{1,0},{2,3},{3,2},{4,5},{5,4},{6,7},{7,6},{8,9},{9,8},{10,11... | collective-permute-start | bytes 245768 | tf_op jit(solution)/shard_map/ppermute | solution.py:25
  143.1 5.9 %collective-permute-start.30 = (bf16[8,5120]{1,0:T(8,128)(2,1)S(1)}, bf16[8,5120]{1,0:T(8,128)(2,1)S(1)}, u32[]{:S(2)}, u32[]{:S(2)}) collective-permute-start(bf16[8,5120]{1,0:T(8,128)(2,1)S(1)} %shard_map.139.first_ref), channel_id=1, source_target_pairs={{0,4},{1,5},{2,6},{3,7},{4,0},{5,1},{6,2},{7,3},{8,12},{9,13},{10,... | collective-permute-start | bytes 245768 | tf_op jit(solution)/shard_map/ppermute | solution.py:25
  149.1 1.4 collective-permute-start.31

commit v4 on v3

--- a/solution.py
+++ b/solution.py
@@ -11,6 +11,8 @@
 HD = 128
 STEPS = 4
 KERNEL_VMEM = 18 * 2**20
+LOAD_VMEM = 28 * 2**20
+COPY_VMEM = 8 * 2**20
 
 
 rope_base = 1000000.0
@@ -18,6 +20,7 @@
 
 in_vmem = pl.BlockSpec(memory_space=pltpu.VMEM)
 in_smem = pl.BlockSpec(memory_space=pltpu.SMEM)
+in_place = pl.BlockSpec(memory_space=pltpu.HBM)
 
 
 def exchange(block, axis, mask):
@@ -33,10 +36,11 @@
     return values * cosine + pltpu.roll(values, values.shape[-1] // 2, 1) * sine
 
 
-def prepare_kernel(block_len, one_head_each, flags_ref, lengths_ref, remaining_ref, from_ref, to_ref, tables_ref, tables_out, rows_out):
-    me, group, count = flags_ref[0], flags_ref[1], flags_ref[2]
+def prepare_kernel(block_len, one_head_each, total, moves, scalars_ref, tables_ref, tables_out, rows_out):
+    me, group, count = scalars_ref[0], scalars_ref[1], scalars_ref[2]
     seq_count = rows_out.shape[1]
-    tables_out[...] = tables_ref[group]
+    first = pl.multiple_of(group * seq_count, seq_count)
+    tables_out[...] = tables_ref[:, :, pl.ds(first, seq_count), :]
     rows = lax.broadcasted_iota(jnp.int32, rows_out.shape[1:], 0)
 
     def fill(value):
@@ -44,24 +48,30 @@
 
     remaining, lengths = fill(0), fill(0)
     for seq in range(seq_count):
-        remaining = jnp.where(rows == seq, remaining_ref[group * seq_count + seq], remaining)
-        lengths = jnp.where(rows == seq, lengths_ref[group * seq_count + seq], lengths)
+        lengths = jnp.where(rows == seq, scalars_ref[3 + first + seq], lengths)
+        remaining = jnp.where(rows == seq, scalars_ref[3 + total + first + seq], remaining)
     rows_out[0] = remaining
     rows_out[1] = lengths
     rows_out[2] = fill((2 * me < count).astype(jnp.int32))
     rows_out[3] = fill(((me & 1) == 0).astype(jnp.int32) if one_head_each else 1)
     rows_out[4] = fill(me * block_len if one_head_each else 0)
-    for move in range(from_ref.shape[0]):
-        rows_out[5 + 2 * move] = fill(jnp.where(group == 0, from_ref[move], to_ref[move]))
-        rows_out[6 + 2 * move] = fill(jnp.where(group == 0, to_ref[move], from_ref[move]))
-
-
-def pack_kernel(masks, flags_ref, keys_ref, values_ref, *outs):
-    me = flags_ref[0]
-    for mask, out in zip(masks, outs):
-        head = pl.multiple_of((me ^ mask) * HD, HD)
-        out[0] = keys_ref[:, :, pl.ds(head, HD)]
-        out[1] = values_ref[:, :, pl.ds(head, HD)]
+    for move in range(moves):
+        slots = [scalars_ref[3 + 2 * total + moves * side + move] for side in range(2)]
+        rows_out[5 + 2 * move] = fill(jnp.where(group == 0, slots[0], slots[1]))
+        rows_out[6 + 2 * move] = fill(jnp.where(group == 0, slots[1], slots[0]))
+
+
+def load_kernel(*refs):
+    *refs, sems = refs
+    count = len(refs) // 2
+    copies = [
+        pltpu.make_async_copy(source, target, sems.at[at])
+        for at, (source, target) in enumerate(zip(refs[:count], refs[count:]))
+    ]
+    for copy in copies:
+        copy.start()
+    for copy in copies:
+        copy.wait()
 
 
 def updated(step, rows_ref, hidden_ref, first_ref, second_ref):
@@ -106,17 +116,24 @@
     b_out[...] = jnp.where(is_key, done[1], done[0]).astype(jnp.bfloat16)
 
 
-def query_kernel(step, masks, rows_ref, tables_ref, normed_ref, w_ref, *rest):
-    caches, rest = rest[: len(masks)], rest[len(masks) :]
-    query_out, num_out, max_out, den_out = rest
-    caches = [cache for _, cache in sorted(zip(masks, caches), key=lambda pair: pair[0])]
-    seq_count = normed_ref.shape[0]
-    heads = w_ref.shape[1] // HD
+def project_kernel(step, tables_ref, normed_ref, w_ref, query_out):
     projected = jnp.dot(normed_ref[...], w_ref[...], preferred_element_type=jnp.float32)
-    for head in range(heads):
+    for head in range(query_out.shape[0]):
         piece = projected[:, head * HD : (head + 1) * HD]
         turned = turn(root_norm(piece), tables_ref[step, 0], tables_ref[step, 1])
         query_out[head] = turned.astype(jnp.bfloat16).astype(jnp.float32)
+
+
+def query_kernel(step, masks, rows_ref, tables_ref, normed_ref, w_ref, *rest):
+    *caches, query_out, num_out, max_out, den_out = rest
+    project_kernel(step, tables_ref, normed_ref, w_ref, query_out)
+    attend_kernel(masks, rows_ref, query_out, *caches, num_out, max_out, den_out)
+
+
+def attend_kernel(masks, rows_ref, query_ref, *rest):
+    *caches, num_out, max_out, den_out = rest
+    caches = [cache for _, cache in sorted(zip(masks, caches), key=lambda pair: pair[0])]
+    heads, seq_count = query_ref.shape[:2]
 
     def rows(which, seq):
         return jnp.concatenate(
@@ -129,7 +146,7 @@
 
     scores = [
         lax.dot_general(
-            query_out[:, seq, :].astype(jnp.bfloat16),
+            query_ref[:, seq, :].astype(jnp.bfloat16),
             rows(0, seq),
             (((1,), (1,)), ((), ())),
             preferred_element_type=jnp.float32,
@@ -188,25 +205,25 @@
 
 
 def final_kernel(step, rows_ref, hidden_ref, first_ref, second_ref, *refs):
-    *raws, out_ref = refs
-    width = hidden_ref.shape[1]
-    out_ref[:, :width] = updated(step, rows_ref, hidden_ref, first_ref, second_ref).astype(
-        jnp.bfloat16
-    )
-    for at, raw in enumerate(raws):
-        columns = raw.shape[1]
-        out_ref[:, width + at * columns : width + (at + 1) * columns] = raw[...]
-
-
-def trade_kernel(moves, rows_ref, own_ref, other_ref, hidden_out, kv_out):
-    rows = own_ref[...].astype(jnp.float32)
-    other = other_ref[...].astype(jnp.float32)
-    index = lax.broadcasted_iota(jnp.int32, rows.shape, 0)
-    own = rows
-    for move in range(moves):
-        here, there = rows_ref[5 + 2 * move][:1, :1], rows_ref[6 + 2 * move][:1, :1]
-        picked = jnp.sum(jnp.where(index == there, other, 0.0), axis=0, keepdims=True)
-        own = jnp.where(index == here, picked, own)
+    *raws, out_ref, sent_ref = refs
+    last = updated(step, rows_ref, hidden_ref, first_ref, second_ref).astype(jnp.bfloat16)
+    own = jnp.concatenate([last] + [raw[...] for raw in raws], axis=1)
+    out_ref[...] = own
+    own = own.astype(jnp.float32)
+    index = lax.broadcasted_iota(jnp.int32, own.shape, 0)
+    moved = [
+        jnp.sum(jnp.where(index == rows_ref[5 + 2 * move][:1, :1], own, 0.0), axis=0, keepdims=True)
+        for move in range(sent_ref.shape[0])
+    ]
+    sent_ref[...] = jnp.concatenate(moved, axis=0).astype(jnp.bfloat16)
+
+
+def trade_kernel(rows_ref, own_ref, got_ref, hidden_out, kv_out):
+    own = own_ref[...].astype(jnp.float32)
+    got = got_ref[...].astype(jnp.float32)
+    index = lax.broadcasted_iota(jnp.int32, own.shape, 0)
+    for move in range(got.shape[0]):
+        own = jnp.where(index == rows_ref[5 + 2 * move][:1, :1], got[move : move + 1], own)
     own = own.astype(jnp.bfloat16)
     width = hidden_out.shape[1]
     hidden_out[...] = own[:, :width]
@@ -215,12 +232,17 @@
         kv_out[step] = own[:, width + step * columns : width + (step + 1) * columns]
 
 
-def run(kernel, outs, *args, scalars=0, vmem=6 * 2**20, flops=0, moved=0):
+def after(one, *others):
+    return lax.optimization_barrier((one, *others))[0] if others else one
+
+
+def run(kernel, outs, *args, scalars=0, copies=0, vmem=6 * 2**20, flops=0, moved=0):
     return pl.pallas_call(
         kernel,
         out_shape=outs,
-        in_specs=[in_smem] * scalars + [in_vmem] * (len(args) - scalars),
+        in_specs=[in_smem] * scalars + [in_place if copies else in_vmem] * (len(args) - scalars),
         out_specs=jax.tree.map(lambda _: in_vmem, outs),
+        scratch_shapes=[pltpu.SemaphoreType.DMA((copies,))] if copies else [],
         cost_estimate=pl.CostEstimate(flops=flops, bytes_accessed=moved, transcendentals=0),
         compiler_params=pltpu.CompilerParams(vmem_limit_bytes=vmem),
     )(*args)
@@ -267,19 +289,14 @@
         return jax.ShapeDtypeStruct(shape, dtype)
 
     half = HD // 2
-    frequency = rope_base ** (-jnp.arange(half).astype(f32) * 2.0 / HD)
-    positions = cache_lengths.reshape(-1, 1, seq_count) + jnp.arange(STEPS)[None, :, None]
+    frequency = rope_base ** (-(jnp.arange(HD) % half).astype(f32) * 2.0 / HD)
+    positions = cache_lengths[None, :] + jnp.arange(STEPS)[:, None]
     angles = positions.astype(f32)[..., None] * frequency
-    cosine, sine = jnp.cos(angles), jnp.sin(angles)
-    tables = jnp.stack(
-        [
-            jnp.concatenate([cosine, cosine], axis=-1),
-            jnp.concatenate([-sine, sine], axis=-1),
-        ],
-        axis=2,
-    )
-    flags = jnp.stack([model_index, group_index, jnp.int32(model_size)])
-    moves = move_from.shape[0]
+    sign = jnp.where(jnp.arange(HD) < half, -1.0, 1.0)
+    tables = jnp.stack([jnp.cos(angles), jnp.sin(angles) * sign], axis=1)
+    total, moves = cache_lengths.shape[0], move_from.shape[0]
+    place = jnp.stack([model_index, group_index, jnp.int32(model_size)])
+    scalars = jnp.concatenate([place, cache_lengths, remaining_steps, move_from, move_to])
     own_head = model_index * kv_heads // model_size
 
     if one_head_each:
@@ -287,21 +304,18 @@
         across = list(range(half_size, model_size))
         within = list(range(1, half_size))
         masks = across[:2] + within + across[2:] + [0]
-        packed = run(
-            functools.partial(pack_kernel, masks),
-            [struct(2, seq_count, block_len, HD)] * model_size,
-            flags,
-            cache_keys,
-            cache_values,
-            scalars=1,
-        )
-        blocks = dict(zip(masks, packed))
-        landed = {0: blocks[0]}
-        for mask in across[:2] + within:
-            landed[mask] = exchange(blocks[mask], "mp", mask)
-        for mask, earlier in zip(across[2:], within):
-            sent, landed[earlier] = lax.optimization_barrier((blocks[mask], landed[earlier]))
-            landed[mask] = exchange(sent, "mp", mask)
+        landed = {}
+        for mask in masks:
+            head = (model_index ^ mask) * HD
+            block = jnp.stack(
+                [
+                    lax.dynamic_slice_in_dim(cache, head, HD, 2)
+                    for cache in (cache_keys, cache_values)
+                ]
+            )
+            if mask in across[2:]:
+                block = after(block, landed[within[mask - across[2]]])
+            landed[mask] = exchange(block, "mp", mask) if mask else block
         caches = [landed[mask] for mask in masks]
     else:
         masks = [0]
@@ -312,18 +326,28 @@
         caches = [lax.all_to_all(to_all, "mp", 0, 0, tiled=True)]
 
     tables, rows = run(
-        functools.partial(prepare_kernel, block_len, one_head_each),
-        [struct(*tables.shape[1:], dtype=f32), struct(5 + 2 * moves, seq_count, HD, dtype=jnp.int32)],
-        flags,
-        cache_lengths,
-        remaining_steps,
-        move_from,
-        move_to,
+        functools.partial(prepare_kernel, block_len, one_head_each, total, moves),
+        [
+            struct(STEPS, 2, seq_count, HD, dtype=f32),
+            struct(5 + 2 * moves, seq_count, HD, dtype=jnp.int32),
+        ],
+        scalars,
         tables,
-        scalars=5,
+        scalars=1,
     )
+
+    def load(*arrays, vmem):
+        return run(
+            load_kernel,
+            [struct(*array.shape, dtype=array.dtype) for array in arrays],
+            *arrays,
+            copies=len(arrays),
+            vmem=vmem,
+            moved=sum(array.size * array.dtype.itemsize for array in arrays),
+        )
+
     gain = norm_gain.reshape(1, width)
-    hidden = hidden_in
+    w_key_value, hidden, gain = load(w_key_value, hidden_in, gain, vmem=COPY_VMEM)
     terms = ()
     fresh, kv_outputs = [], []
     for step in range(STEPS):
@@ -371,18 +395,34 @@
             )
             fresh.append(lax.dynamic_index_in_dim(new_kv, own_head, 1, False))
             fresh.append(lax.dynamic_index_in_dim(new_kv, kv_heads + own_head, 1, False))
-        attention = run(
-            functools.partial(query_kernel, step, masks),
-            [struct(heads_here, seq_count, HD, dtype=f32)] * 4,
-            rows,
-            tables,
-            normed,
-            w_query,
-            *caches,
-            vmem=KERNEL_VMEM,
-            flops=2 * seq_count * width * heads_here * HD,
-            moved=2 * width * heads_here * HD,
-        )
+        if step == 0:
+            w_query, w_output = load(w_query, w_output, vmem=LOAD_VMEM)
+        sums = [struct(heads_here, seq_count, HD, dtype=f32)] * 4
+        cost = {"flops": 2 * seq_count * width * heads_here * HD, "moved": 2 * width * heads_here * HD}
+        if step > 0:
+            attention = run(
+                functools.partial(query_kernel, step, masks),
+                sums,
+                rows,
+                tables,
+                normed,
+                w_query,
+                *caches,
+                vmem=KERNEL_VMEM,
+                **cost,
+            )
+        else:
+            queries = run(
+                functools.partial(project_kernel, step),
+                sums[0],
+                tables,
+                normed,
+                w_query,
+                vmem=KERNEL_VMEM,
+                **cost,
+            )
+            attention = run(functools.partial(attend_kernel, masks), sums[1:], rows, queries, *caches)
+            attention = [queries, *attention]
         part = run(
             output_kernel,
             struct(seq_count, width),
@@ -394,9 +434,9 @@
         )
         terms = sum_rounds(part, "mp")
 
-    own = run(
+    own, sent = run(
         functools.partial(final_kernel, STEPS - 1),
-        struct(seq_count, width + STEPS * col_width),
+        [struct(seq_count, width + STEPS * col_width), struct(moves, width + STEPS * col_width)],
         rows,
         hidden,
         *terms,
@@ -404,11 +444,11 @@
     )
     return tuple(
         run(
-            functools.partial(trade_kernel, moves),
+            trade_kernel,
             [struct(seq_count, width), struct(STEPS, seq_count, col_width)],
             rows,
             own,
-            exchange(own, "dp", 1),
+            exchange(sent, "dp", 1),
         )
     )
 

time: 152 us -> 139 us (0.914)
  local copies, waits for them, and re-layouts: 17.1 us -> 3.26 us
  Pallas kernels: 20.8 us -> 27.2 us
  starting transfers between devices: 59.1 us -> 53.4 us
    unnamed x40 -> x6, local copies, waits for them, and re-layouts: 16.4 us -> 0.55 us
    ppermute x24, starting transfers between devices: 43.7 us -> 36.5 us  [exchange(): lax.ppermute(block, axis, [(low, low ^ mask) for low in range(count)])]
    pallas_call x20 -> x22, Pallas kernels: 20.8 us -> 27.2 us  [run(): pl.pallas_call(kernel, out_shape=outs, in_specs=[in_smem] * scalars + [in...]
    ppermute x4, waiting for transfers between devices: 6.16 us -> 9.98 us  [per_device(): lax.ppermute(sent[1], 'mp', to_odd + [(pairs + a, b) for a, b in to_even])]
    ppermute x24, waiting for transfers between devices: 46.7 us -> 43.2 us  [exchange(): lax.ppermute(block, axis, [(low, low ^ mask) for low in range(count)])]
    another operation x0 -> x1, local copies, waits for them, and re-layouts: none -> 1.93 us  [per_device(): jnp.stack([lax.dynamic_slice_in_dim(cache, head, HD, 2) for cache in (cac...]
  transfers between devices with their start and end apart: 32 -> 32, of which waited for: 22 -> 22; matrix products, arithmetic and copies ran while one was open for 1% -> 1% of each run, Pallas kernels for 7% -> 13%
where the time goes in v4:
time: 139 us
  starting transfers between devices  53.4 us (38%)
  waiting for transfers between devices  53.2 us (38%)
  Pallas kernels  27.2 us (20%)
  local copies, waits for them, and re-layouts  3.26 us (2%)
    ppermute x24, waiting for transfers between devices, exchange(): lax.ppermute(block, axis, [(low, low ^ mask) for low in range(count)])  43.2 us
    ppermute x24, starting transfers between devices, exchange(): lax.ppermute(block, axis, [(low, low ^ mask) for low in range(count)])  36.5 us
    pallas_call x22, Pallas kernels, run(): pl.pallas_call(kernel, out_shape=outs, in_specs=[in_smem] * scalars + [in...  27.2 us
    ppermute x4, starting transfers between devices, per_device(): lax.ppermute(sent[1], 'mp', to_odd + [(pairs + a, b) for a, b in to_even])  14.3 us
    ppermute x4, waiting for transfers between devices, per_device(): lax.ppermute(sent[1], 'mp', to_odd + [(pairs + a, b) for a, b in to_even])  9.98 us
  transfers between devices with their start and end apart: 32, of which 22 were waited for; matrix products, arithmetic and copies ran while one was open for 1% of the time, Pallas kernels for 13%

profile of v4, /device:TPU:0, one launch (start us, length us, event | category | flops | bytes accessed | tf_op | source)
XLA Modules:
  0.0 139.1 jit_solution(11043353047775474027)
XLA Ops:
  0.7 1.9 %dynamic-slice_bitcast_fusion = (bf16[1,8,64,128]{3,2,1,0:T(8,128)(2,1)S(1)}, bf16[1,8,64,128]{3,2,1,0:T(8,128)(2,1)S(1)}, bf16[1,8,64,128]{3,2,1,0:T(8,128)(2,1...) fusion(bf16[8,64,1024]{2,1,0:T(8,128)(2,1)} %param.17, ...), kind=kLoop, calls=%fused_computation.8 | loop fusion | bytes 4194336 | tf_op jit(solution)/shard_map/stack | solution.py:310
  2.7 4.1 %collective-permute-start = (bf16[2,8,64,128]{3,2,1,0:T(8,128)(2,1)S(1)}, bf16[2,8,64,128]{3,2,1,0:T(8,128)(2,1)S(1)}, u32[]{:S(2)}, u32[]{:S(2)}) collective-permute-start(bf16[2,8,64,128]{3,2,1,0:T(8,128)(2,1)S(1)} %pad_maximum_fusion), channel_id=1, source_target_pairs={{0,4},{1,5},{2,6},{3,7},{4,0},{5,1},{6,2},{7,3},{8,12},{9,13},{10,... | collective-permute-start | bytes 786440 | tf_op jit(solution)/shard_map/ppermute | solution.py:28
  6.8 1.4 collective-permute-start.1
  8.5 1.9 %collective-permute-start.3 = (bf16[2,8,64,128]{3,2,1,0:T(8,128)(2,1)S(1)}, bf16[2,8,64,128]{3,2,1,0:T(8,128)(2,1)S(1)}, u32[]{:S(2)}, u32[]{:S(2)}) collective-permute-start(bf16[2,8,64,128]{3,2,1,0:T(8,128)(2,1)S(1)} %pad_maximum_fusion.3), channel_id=1, source_target_pairs={{0,2},{1,3},{2,0},{3,1},{4,6},{5,7},{6,4},{7,5},{8,10},{9,11},{10,... | collective-permute-start | bytes 786440 | tf_op jit(solution)/shard_map/ppermute | solution.py:28
  10.4 1.5 %collective-permute-start.4 = (bf16[2,8,64,128]{3,2,1,0:T(8,128)(2,1)S(1)}, bf16[2,8,64,128]{3,2,1,0:T(8,128)(2,1)S(1)}, u32[]{:S(2)}, u32[]{:S(2)}) collective-permute-start(bf16[2,8,64,128]{3,2,1,0:T(8,128)(2,1)S(1)} %pad_maximum_fusion.4), channel_id=1, source_target_pairs={{0,3},{1,2},{2,1},{3,0},{4,7},{5,6},{6,5},{7,4},{8,11},{9,10},{10,... | collective-permute-start | bytes 786440 | tf_op jit(solution)/shard_map/ppermute | solution.py:28
  12.0 0.7 add_convert_fusion
  12.7 3.8 %collective-permute-done.2.rest_2_ = bf16[2,8,64,128]{3,2,1,0:T(8,128)(2,1)S(1)} collective-permute-done((bf16[2,8,64,128]{3,2,1,0:T(8,128)(2,1)S(1)}, bf16[2,8,64,128]{3,2,1,0:T(8,128)(2,1)S(1)}, u32[]{:S(2)}, u32[]{:S(2)}) %collective-permute-start.2) | collective-permute-done | bytes 262176 | tf_op jit(solution)/shard_map/ppermute | solution.py:28
  16.5 3.6 %collective-permute-start.5 = (bf16[2,8,64,128]{3,2,1,0:T(8,128)(2,1)S(1)}, bf16[2,8,64,128]{3,2,1,0:T(8,128)(2,1)S(1)}, u32[]{:S(2)}, u32[]{:S(2)}) collective-permute-start(bf16[2,8,64,128]{3,2,1,0:T(8,128)(2,1)S(1)} %pad_maximum_fusion.5), channel_id=1, source_target_pairs={{0,6},{1,7},{2,4},{3,5},{4,2},{5,3},{6,0},{7,1},{8,14},{9,15},{10,... | collective-permute-start | bytes 786440 | tf_op jit(solution)/shard_map/ppermute | solution.py:28
  20.0 4.8 %collective-permute-done.3.rest_3_ = bf16[2,8,64,128]{3,2,1,0:T(8,128)(2,1)S(1)} collective-permute-done((bf16[2,8,64,128]{3,2,1,0:T(8,128)(2,1)S(1)}, bf16[2,8,64,128]{3,2,1,0:T(8,128)(2,1)S(1)}, u32[]{:S(2)}, u32[]{:S(2)}) %collective-permute-start.3) | collective-permute-done | bytes 262176 | tf_op jit(solution)/shard_map/ppermute | solution.py:28
  24.8 2.3 %collective-permute-start.6 = (bf16[2,8,64,128]{3,2,1,0:T(8,128)(2,1)S(1)}, bf16[2,8,64,128]{3,2,1,0:T(8,128)(2,1)S(1)}, u32[]{:S(2)}, u32[]{:S(2)}) collective-permute-start(bf16[2,8,64,128]{3,2,1,0:T(8,128)(2,1)S(1)} %pad_maximum_fusion.6), channel_id=1, source_target_pairs={{0,7},{1,6},{2,5},{3,4},{4,3},{5,2},{6,1},{7,0},{8,15},{9,14},{10,... | collective-permute-start | bytes 786440 | tf_op jit(solution)/shard_map/ppermute | solution.py:28
  27.3 0.8 concatenate.3.scalars_ref
  28.7 7.1 %shard_map.125 = (bf16[5120,1024]{1,0:T(8,128)(2,1)S(1)}, bf16[1024,5120]{1,0:T(8,128)(2,1)S(1)}) custom-call(bf16[5120,1024]{1,0:T(8,128)(2,1)} %refs_0_.3, bf16[1024,5120]{1,0:T(8,128)(2,1)} %refs_1_.3), custom_call_target="tpu_custom_call" | custom-call | bytes 20971520 | tf_op jit(solution)/shard_map/pallas_call | solution.py:240
  36.7 0.7 shard_map.124
  37.4 0.7 collective-permute-start.7
  38.1 4.3 %collective-permute-start.8 = (bf16[8,128]{1,0:T(8,128)(2,1)S(1)}, bf16[8,128]{1,0:T(8,128)(2,1)S(1)}, u32[]{:S(2)}, u32[]{:S(2)}) collective-permute-start(bf16[8,128]{1,0:T(8,128)(2,1)S(1)} %get-tuple-element.61), channel_id=1, source_target_pairs={{0,1},{1,3},{2,5},{3,7},{4,0},{5,2},{6,4},{7,6},{8,9},{9,11},{10,1... | collective-permute-start | bytes 6152 | tf_op jit(solution)/shard_map/ppermute | solution.py:378
  42.5 1.6 %shard_map.126.query_ref = f32[8,8,128]{2,1,0:T(8,128)S(1)} custom-call(f32[4,2,8,128]{3,2,1,0:T(8,128)S(1)} %get-tuple-element.48.tables_ref, bf16[8,5120]{1,0:T(8,128)(2,1)S(1)} %get-tuple-element.52.normed_ref, bf16[5120,1024]{1,0:T(8,128)(2,1)S(1)} %get-tuple-element.53.w_ref), custom_call_target="tpu_custom_call" | custom-call | flops 83886080 | bytes 10485760 | tf_op jit(solution)/shard_map/pallas_call | solution.py:240
  44.7 7.8 %collective-permute-done.8.rest_1_ = bf16[8,128]{1,0:T(8,128)(2,1)S(1)} collective-permute-done((bf16[8,128]{1,0:T(8,128)(2,1)S(1)}, bf16[8,128]{1,0:T(8,128)(2,1)S(1)}, u32[]{:S(2)}, u32[]{:S(2)}) %collective-permute-start.8) | collective-permute-done | bytes 2080 | tf_op jit(solution)/shard_map/ppermute | solution.py:378
  52.5 1.5 %shard_map.128.refs_0_ = bf16[8,5120]{1,0:T(8,128)(2,1)S(1)} custom-call(s32[9,8,128]{2,1,0:T(8,128)S(1)} %get-tuple-element.47.rows_ref, f32[8,8,128]{2,1,0:T(8,128)S(1)} %shard_map.126.query_ref, f32[8,8,128]{2,1,0:T(8,128)S(1)} %get-tuple-element.56.num_ref, f32[8,8,128]{2,1,0:T(8,128)S(1)} %get-tuple-element.57.max_ref, ...), custom_call_target="tpu_custom_call" | custom-call | tf_op jit(solution)/shard_map/pallas_call | solution.py:240
  54.1 2.3 %collective-permute-start.11 = (bf16[8,5120]{1,0:T(8,128)(2,1)S(1)}, bf16[8,5120]{1,0:T(8,128)(2,1)S(1)}, u32[]{:S(2)}, u32[]{:S(2)}) collective-permute-start(bf16[8,5120]{1,0:T(8,128)(2,1)S(1)} %shard_map.128.refs_0_), channel_id=1, source_target_pairs={{0,3},{1,2},{2,1},{3,0},{4,7},{5,6},{6,5},{7,4},{8,11},{9,10},{10,... | collective-permute-start | bytes 245768 | tf_op jit(solution)/shard_map/ppermute | solution.py:28
  57.0 0.7 collective-permute-start.9
  57.7 2.5 %collective-permute-done.11.refs_3_ = bf16[8,5120]{1,0:T(8,128)(2,1)S(1)} collective-permute-done((bf16[8,5120]{1,0:T(8,128)(2,1)S(1)}, bf16[8,5120]{1,0:T(8,128)(2,1)S(1)}, u32[]{:S(2)}, u32[]{:S(2)}) %collective-permute-start.11) | collective-permute-done | bytes 81952 | tf_op jit(solution)/shard_map/ppermute | solution.py:28
  60.2 0.9 collective-permute-done.10.refs_2_
  61.5 3.9 %collective-permute-start.12 = (bf16[8,5120]{1,0:T(8,128)(2,1)S(1)}, bf16[8,5120]{1,0:T(8,128)(2,1)S(1)}, u32[]{:S(2)}, u32[]{:S(2)}) collective-permute-start(bf16[8,5120]{1,0:T(8,128)(2,1)S(1)} %shard_map.129.refs_1_), channel_id=1, source_target_pairs={{0,4},{1,5},{2,6},{3,7},{4,0},{5,1},{6,2},{7,3},{8,12},{9,13},{10,... | collective-permute-start | bytes 245768 | tf_op jit(solution)/shard_map/ppermute | solution.py:28
  65.3 3.5 %collective-permute-done.12.refs_2_ = bf16[8,5120]{1,0:T(8,128)(2,1)S(1)} collective-permute-done((bf16[8,5120]{1,0:T(8,128)(2,1)S(1)}, bf16[8,5120]{1,0:T(8,128)(2,1)S(1)}, u32[]{:S(2)}, u32[]{:S(2)}) %collective-permute-start.12) | collective-permute-done | bytes 81952 | tf_op jit(solution)/shard_map/ppermute | solution.py:28
  68.9 0.8 shard_map.130
  69.7 0.7 collective-permute-start.13
  70.4 2.4 %collective-permute-start.14 = (bf16[8,128]{1,0:T(8,128)(2,1)S(1)}, bf16[8,128]{1,0:T(8,128)(2,1)S(1)}, u32[]{:S(2)}, u32[]{:S(2)}) collective-permute-start(bf16[8,128]{1,0:T(8,128)(2,1)S(1)} %get-tuple-element.69), channel_id=1, source_target_pairs={{0,1},{1,3},{2,5},{3,7},{4,0},{5,2},{6,4},{7,6},{8,9},{9,11},{10,1... | collective-permute-start | bytes 6152 | tf_op jit(solution)/shard_map/ppermute | solution.py:378
  72.8 2.2 %shard_map.131 = (f32[8,8,128]{2,1,0:T(8,128)S(1)}, f32[8,8,128]{2,1,0:T(8,128)S(1)}, f32[8,8,128]{2,1,0:T(8,128)S(1)}, f32[8,8,128]{2,1,0:T(8,128)S(1)}) custom-call(s32[9,8,128]{2,1,0:T(8,128)S(1)} %get-tuple-element.47.rows_ref, f32[4,2,8,128]{3,2,1,0:T(8,128)S(1)} %get-tuple-element.48.tables_ref, bf16[8,5120]{1,0:T(8,128)(2,1)S(1)} %get-tuple-element.63.normed_ref, ...), custom_call_target="tpu_custom_call" | custom-call | flops 83886080 | bytes 10485760 | tf_op jit(solution)/shard_map/pallas_call | solution.py:240
  75.0 1.5 %collective-permute-done.14.rest_3_ = bf16[8,128]{1,0:T(8,128)(2,1)S(1)} collective-permute-done((bf16[8,128]{1,0:T(8,128)(2,1)S(1)}, bf16[8,128]{1,0:T(8,128)(2,1)S(1)}, u32[]{:S(2)}, u32[]{:S(2)}) %collective-permute-start.14) | collective-permute-done | bytes 2080 | tf_op jit(solution)/shard_map/ppermute | solution.py:378
  76.5 1.5 %shard_map.132.refs_0_ = bf16[8,5120]{1,0:T(8,128)(2,1)S(1)} custom-call(s32[9,8,128]{2,1,0:T(8,128)S(1)} %get-tuple-element.47.rows_ref, f32[8,8,128]{2,1,0:T(8,128)S(1)} %get-tuple-element.64.query_ref, f32[8,8,128]{2,1,0:T(8,128)S(1)} %get-tuple-element.65.num_ref, f32[8,8,128]{2,1,0:T(8,128)S(1)} %get-tuple-element.66.max_ref, ...), custom_call_target="tpu_custom_call" | custom-call | tf_op jit(solution)/shard_map/pallas_call | solution.py:240
  78.1 3.1 %collective-permute-start.17 = (bf16[8,5120]{1,0:T(8,128)(2,1)S(1)}, bf16[8,5120]{1,0:T(8,128)(2,1)S(1)}, u32[]{:S(2)}, u32[]{:S(2)}) collective-permute-start(bf16[8,5120]{1,0:T(8,128)(2,1)S(1)} %shard_map.132.refs_0_), channel_id=1, source_target_pairs={{0,3},{1,2},{2,1},{3,0},{4,7},{5,6},{6,5},{7,4},{8,11},{9,10},{10,... | collective-permute-start | bytes 245768 | tf_op jit(solution)/shard_map/ppermute | solution.py:28
  81.1 0.7 collective-permute-start.16
  81.8 1.7 %collective-permute-done.17.refs_3_ = bf16[8,5120]{1,0:T(8,128)(2,1)S(1)} collective-permute-done((bf16[8,5120]{1,0:T(8,128)(2,1)S(1)}, bf16[8,5120]{1,0:T(8,128)(2,1)S(1)}, u32[]{:S(2)}, u32[]{:S(2)}) %collective-permute-start.17) | collective-permute-done | bytes 81952 | tf_op jit(solution)/shard_map/ppermute | solution.py:28
  83.5 2.9 %collective-permute-done.16.refs_2_ = bf16[8,5120]{1,0:T(8,128)(2,1)S(1)} collective-permute-done((bf16[8,5120]{1,0:T(8,128)(2,1)S(1)}, bf16[8,5120]{1,0:T(8,128)(2,1)S(1)}, u32[]{:S(2)}, u32[]{:S(2)}) %collective-permute-start.16) | collective-permute-done | bytes 81952 | tf_op jit(solution)/shard_map/ppermute | solution.py:28
  86.5 0.9 collective-permute-start.18
  87.4 5.4 %collective-permute-done.18.refs_2_ = bf16[8,5120]{1,0:T(8,128)(2,1)S(1)} collective-permute-done((bf16[8,5120]{1,0:T(8,128)(2,1)S(1)}, bf16[8,5120]{1,0:T(8,128)(2,1)S(1)}, u32[]{:S(2)}, u32[]{:S(2)}) %collective-permute-start.18) | collective-permute-done | bytes 81952 | tf_op jit(solution)/shard_map/ppermute | solution.py:28
  92.8 0.8 shard_map.134
  93.6 0.7 collective-permute-start.19
  94.2 3.3 %collective-permute-start.20 = (bf16[8,128]{1,0:T(8,128)(2,1)S(1)}, bf16[8,128]{1,0:T(8,128)(2,1)S(1)}, u32[]{:S(2)}, u32[]{:S(2)}) collective-permute-start(bf16[8,128]{1,0:T(8,128)(2,1)S(1)} %get-tuple-element.77), channel_id=1, source_target_pairs={{0,1},{1,3},{2,5},{3,7},{4,0},{5,2},{6,4},{7,6},{8,9},{9,11},{10,1... | collective-permute-start | bytes 6152 | tf_op jit(solution)/shard_map/ppermute | solution.py:378
  97.5 2.2 %shard_map.135 = (f32[8,8,128]{2,1,0:T(8,128)S(1)}, f32[8,8,128]{2,1,0:T(8,128)S(1)}, f32[8,8,128]{2,1,0:T(8,128)S(1)}, f32[8,8,128]{2,1,0:T(8,128)S(1)}) custom-call(s32[9,8,128]{2,1,0:T(8,128)S(1)} %get-tuple-element.47.rows_ref, f32[4,2,8,128]{3,2,1,0:T(8,128)S(1)} %get-tuple-element.48.tables_ref, bf16[8,5120]{1,0:T(8,128)(2,1)S(1)} %get-tuple-element.71.normed_ref, ...), custom_call_target="tpu_custom_call" | custom-call | flops 83886080 | bytes 10485760 | tf_op jit(solution)/shard_map/pallas_call | solution.py:240
  100.1 1.5 %shard_map.136.refs_0_ = bf16[8,5120]{1,0:T(8,128)(2,1)S(1)} custom-call(s32[9,8,128]{2,1,0:T(8,128)S(1)} %get-tuple-element.47.rows_ref, f32[8,8,128]{2,1,0:T(8,128)S(1)} %get-tuple-element.72.query_ref, f32[8,8,128]{2,1,0:T(8,128)S(1)} %get-tuple-element.73.num_ref, f32[8,8,128]{2,1,0:T(8,128)S(1)} %get-tuple-element.74.max_ref, ...), custom_call_target="tpu_custom_call" | custom-call | tf_op jit(solution)/shard_map/pallas_call | solution.py:240
  101.6 2.2 %collective-permute-start.23 = (bf16[8,5120]{1,0:T(8,128)(2,1)S(1)}, bf16[8,5120]{1,0:T(8,128)(2,1)S(1)}, u32[]{:S(2)}, u32[]{:S(2)}) collective-permute-start(bf16[8,5120]{1,0:T(8,128)(2,1)S(1)} %shard_map.136.refs_0_), channel_id=1, source_target_pairs={{0,3},{1,2},{2,1},{3,0},{4,7},{5,6},{6,5},{7,4},{8,11},{9,10},{10,... | collective-permute-start | bytes 245768 | tf_op jit(solution)/shard_map/ppermute | solution.py:28
  103.8 0.7 collective-permute-start.22
  104.5 0.6 collective-permute-start.21
  105.1 2.0 %collective-permute-done.23.refs_3_ = bf16[8,5120]{1,0:T(8,128)(2,1)S(1)} collective-permute-done((bf16[8,5120]{1,0:T(8,128)(2,1)S(1)}, bf16[8,5120]{1,0:T(8,128)(2,1)S(1)}, u32[]{:S(2)}, u32[]{:S(2)}) %collective-permute-start.23) | collective-permute-done | bytes 81952 | tf_op jit(solution)/shard_map/ppermute | solution.py:28
  107.2 1.1 collective-permute-done.22.refs_2_
  108.3 0.7 collective-permute-done.21.refs_1_
  109.0 1.3 collective-permute-start.24
  110.2 4.2 %collective-permute-done.24.refs_2_ = bf16[8,5120]{1,0:T(8,128)(2,1)S(1)} collective-permute-done((bf16[8,5120]{1,0:T(8,128)(2,1)S(1)}, bf16[8,5120]{1,0:T(8,128)(2,1)S(1)}, u32[]{:S(2)}, u32[]{:S(2)}) %collective-permute-start.24) | collective-permute-done | bytes 81952 | tf_op jit(solution)/shard_map/ppermute | solution.py:28
  114.4 0.8 shard_map.138
  115.2 0.7 collective-permute-start.25
  115.9 4.2 %collective-permute-start.26 = (bf16[8,128]{1,0:T(8,128)(2,1)S(1)}, bf16[8,128]{1,0:T(8,128)(2,1)S(1)}, u32[]{:S(2)}, u32[]{:S(2)}) collective-permute-start(bf16[8,128]{1,0:T(8,128)(2,1)S(1)} %get-tuple-element.85), channel_id=1, source_target_pairs={{0,1},{1,3},{2,5},{3,7},{4,0},{5,2},{6,4},{7,6},{8,9},{9,11},{10,1... | collective-permute-start | bytes 6152 | tf_op jit(solution)/shard_map/ppermute | solution.py:378
  120.0 2.2 %shard_map.139 = (f32[8,8,128]{2,1,0:T(8,128)S(1)}, f32[8,8,128]{2,1,0:T(8,128)S(1)}, f32[8,8,128]{2,1,0:T(8,128)S(1)}, f32[8,8,128]{2,1,0:T(8,128)S(1)}) custom-call(s32[9,8,128]{2,1,0:T(8,128)S(1)} %get-tuple-element.47.rows_ref, f32[4,2,8,128]{3,2,1,0:T(8,128)S(1)} %get-tuple-element.48.tables_ref, bf16[8,5120]{1,0:T(8,128)(2,1)S(1)} %get-tuple-element.79.normed_ref, ...), custom_call_target="tpu_custom_call" | custom-call | flops 83886080 | bytes 10485760 | tf_op jit(solution)/shard_map/pallas_call | solution.py:240
  122.6 1.6 %shard_map.140.refs_0_ = bf16[8,5120]{1,0:T(8,128)(2,1)S(1)} custom-call(s32[9,8,128]{2,1,0:T(8,128)S(1)} %get-tuple-element.47.rows_ref, f32[8,8,128]{2,1,0:T(8,128)S(1)} %get-tuple-element.80.query_ref, f32[8,8,128]{2,1,0:T(8,128)S(1)} %get-tuple-element.81.num_ref, f32[8,8,128]{2,1,0:T(8,128)S(1)} %get-tuple-element.82.max_ref, ...), custom_call_target="tpu_custom_call" | custom-call | tf_op jit(solution)/shard_map/pallas_call | solution.py:240
  124.2 2.2 %collective-permute-start.29 = (bf16[8,5120]{1,0:T(8,128)(2,1)S(1)}, bf16[8,5120]{1,0:T(8,128)(2,1)S(1)}, u32[]{:S(2)}, u32[]{:S(2)}) collective-permute-start(bf16[8,5120]{1,0:T(8,128)(2,1)S(1)} %shard_map.140.refs_0_), channel_id=1, source_target_pairs={{0,3},{1,2},{2,1},{3,0},{4,7},{5,6},{6,5},{7,4},{8,11},{9,10},{10,... | collective-permute-start | bytes 245768 | tf_op jit(solution)/shard_map/ppermute | solution.py:28
  126.3 0.7 collective-permute-start.28
  127.0 0.6 collective-permute-start.27
  127.6 1.9 %collective-permute-done.29.refs_3_ = bf16[8,5120]{1,0:T(8,128)(2,1)S(1)} collective-permute-done((bf16[8,5120]{1,0:T(8,128)(2,1)S(1)}, bf16[8,5120]{1,0:T(8,128)(2,1)S(1)}, u32[]{:S(2)}, u32[]{:S(2)}) %collective-permute-start.29) | collective-permute-done | bytes 81952 | tf_op jit(solution)/shard_map/ppermute | solution.py:28
  129.5 1.3 collective-permute-done.28.refs_2_
  130.8 0.7 collective-permute-done.27.refs_1_
  131.5 1.0 collective-permute-start.30
  132.5 4.4 %collective-permute-done.30.second_ref = bf16[8,5120]{1,0:T(8,128)(2,1)S(1)} collective-permute-done((bf16[8,5120]{1,0:T(8,128)(2,1)S(1)}, bf16[8,5120]{1,0:T(8,128)(2,1)S(1)}, u32[]{:S(2)}, u32[]{:S(2)}) %collective-permute-start.30) | collective-permute-done | bytes 81952 | tf_op jit(solution)/shard_map/ppermute | solution.py:28
  137.2 1.2 collective-permute-done.31.got_ref
  138.4 0.7 shard_map.143
  (42 shorter events, 4.8 us)
Async XLA Ops:
  2.7 34.8 %collective-permute-start = (bf16[2,8,64,128]{3,2,1,0:T(8,128)(2,1)S(1)}, bf16[2,8,64,128]{3,2,1,0:T(8,128)(2,1)S(1)}, u32[]{:S(2)}, u32[]{:S(2)}) collective-permute-start(bf16[2,8,64,128]{3,2,1,0:T(8,128)(2,1)S(1)} %pad_maximum_fusion), channel_id=1, source_target_pairs={{0,4},{1,5},{2,6},{3,7},{4,0},{5,1},{6,2},{7,3},{8,12},{9,13},{10,... | collective-permute-start | bytes 786440 | tf_op jit(solution)/shard_map/ppermute | solution.py:28
  6.8 31.3 %collective-permute-start.1 = (bf16[2,8,64,128]{3,2,1,0:T(8,128)(2,1)S(1)}, bf16[2,8,64,128]{3,2,1,0:T(8,128)(2,1)S(1)}, u32[]{:S(2)}, u32[]{:S(2)}) collective-permute-start(bf16[2,8,64,128]{3,2,1,0:T(8,128)(2,1)S(1)} %pad_maximum_fusion.1), channel_id=1, source_target_pairs={{0,5},{1,4},{2,7},{3,6},{4,1},{5,0},{6,3},{7,2},{8,13},{9,12},{10,... | collective-permute-start | bytes 786440 | tf_op jit(solution)/shard_map/ppermute | solution.py:28
  8.2 8.3 %collective-permute-start.2 = (bf16[2,8,64,128]{3,2,1,0:T(8,128)(2,1)S(1)}, bf16[2,8,64,128]{3,2,1,0:T(8,128)(2,1)S(1)}, u32[]{:S(2)}, u32[]{:S(2)}) collective-permute-start(bf16[2,8,64,128]{3,2,1,0:T(8,128)(2,1)S(1)} %pad_maximum_fusion.2), channel_id=1, source_target_pairs={{0,1},{1,0},{2,3},{3,2},{4,5},{5,4},{6,7},{7,6},{8,9},{9,8},{10,11... | collective-permute-start | bytes 786440 | tf_op jit(solution)/shard_map/ppermute | solution.py:28
  8.5 16.3 %collective-permute-start.3 = (bf16[2,8,64,128]{3,2,1,0:T(8,128)(2,1)S(1)}, bf16[2,8,64,128]{3,2,1,0:T(8,128)(2,1)S(1)}, u32[]{:S(2)}, u32[]{:S(2)}) collective-permute-start(bf16[2,8,64,128]{3,2,1,0:T(8,128)(2,1)S(1)} %pad_maximum_fusion.3), channel_id=1, source_target_pairs={{0,2},{1,3},{2,0},{3,1},{4,6},{5,7},{6,4},{7,5},{8,10},{9,11},{10,... | collective-permute-start | bytes 786440 | tf_op jit(solution)/shard_map/ppermute | solution.py:28
  10.4 33.6 %collective-permute-start.4 = (bf16[2,8,64,128]{3,2,1,0:T(8,128)(2,1)S(1)}, bf16[2,8,64,128]{3,2,1,0:T(8,128)(2,1)S(1)}, u32[]{:S(2)}, u32[]{:S(2)}) collective-permute-start(bf16[2,8,64,128]{3,2,1,0:T(8,128)(2,1)S(1)} %pad_maximum_fusion.4), channel_id=1, source_target_pairs={{0,3},{1,2},{2,1},{3,0},{4,7},{5,6},{6,5},{7,4},{8,11},{9,10},{10,... | collective-permute-start | bytes 786440 | tf_op jit(solution)/shard_map/ppermute | solution.py:28
  16.5 27.6 %collective-permute-start.5 = (bf16[2,8,64,128]{3,2,1,0:T(8,128)(2,1)S(1)}, bf16[2,8,64,128]{3,2,1,0:T(8,128)(2,1)S(1)}, u32[]{:S(2)}, u32[]{:S(2)}) collective-permute-start(bf16[2,8,64,128]{3,2,1,0:T(8,128)(2,1)S(1)} %pad_maximum_fusion.5), channel_id=1, source_target_pairs={{0,6},{1,7},{2,4},{3,5},{4,2},{5,3},{6,0},{7,1},{8,14},{9,15},{10,... | collective-permute-start | bytes 786440 | tf_op jit(solution)/shard_map/ppermute | solution.py:28
  24.8 19.3 %collective-permute-start.6 = (bf16[2,8,64,128]{3,2,1,0:T(8,128)(2,1)S(1)}, bf16[2,8,64,128]{3,2,1,0:T(8,128)(2,1)S(1)}, u32[]{:S(2)}, u32[]{:S(2)}) collective-permute-start(bf16[2,8,64,128]{3,2,1,0:T(8,128)(2,1)S(1)} %pad_maximum_fusion.6), channel_id=1, source_target_pairs={{0,7},{1,6},{2,5},{3,4},{4,3},{5,2},{6,1},{7,0},{8,15},{9,14},{10,... | collective-permute-start | bytes 786440 | tf_op jit(solution)/shard_map/ppermute | solution.py:28
  28.6 7.7 %copy-start = (bf16[5120,256]{1,0:T(8,128)(2,1)S(1)}, bf16[5120,256]{1,0:T(8,128)(2,1)}, u32[]{:S(2)}) copy-start(bf16[5120,256]{1,0:T(8,128)(2,1)} %refs_0_.2) | copy-start | bytes 7864324
  28.6 7.7 %copy-start.1 = (bf16[8,5120]{1,0:T(8,128)(2,1)S(1)}, bf16[8,5120]{1,0:T(8,128)(2,1)}, u32[]{:S(2)}) copy-start(bf16[8,5120]{1,0:T(8,128)(2,1)} %refs_1_.2) | copy-start | bytes 245764
  28.6 7.7 %copy-start.2 = (f32[5120]{0:T(1024)S(1)}, f32[5120]{0:T(1024)}, u32[]{:S(2)}) copy-start(f32[5120]{0:T(1024)} %param.12) | copy-start | bytes 61444
  37.4 7.3 %collective-permute-start.7 = (bf16[8,128]{1,0:T(8,128)(2,1)S(1)}, bf16[8,128]{1,0:T(8,128)(2,1)S(1)}, u32[]{:S(2)}, u32[]{:S(2)}) collective-permute-start(bf16[8,128]{1,0:T(8,128)(2,1)S(1)} %get-tuple-element.60), channel_id=1, source_target_pairs={{0,0},{1,2},{2,4},{3,6},{4,1},{5,3},{6,5},{7,7},{8,8},{9,10},{10,1... | collective-permute-start | bytes 6152 | tf_op jit(solution)/shard_map/ppermute | solution.py:375
  38.1 14.4 %collective-permute-start.8 = (bf16[8,128]{1,0:T(8,128)(2,1)S(1)}, bf16[8,128]{1,0:T(8,128)(2,1)S(1)}, u32[]{:S(2)}, u32[]{:S(2)}) collective-permute-start(bf16[8,128]{1,0:T(8,128)(2,1)S(1)} %get-tuple-element.61), channel_id=1, source_target_pairs={{0,1},{1,3},{2,5},{3,7},{4,0},{5,2},{6,4},{7,6},{8,9},{9,11},{10,1... | collective-permute-start | bytes 6152 | tf_op jit(solution)/shard_map/ppermute | solution.py:378
  54.1 6.2 %collective-permute-start.11 = (bf16[8,5120]{1,0:T(8,128)(2,1)S(1)}, bf16[8,5120]{1,0:T(8,128)(2,1)S(1)}, u32[]{:S(2)}, u32[]{:S(2)}) collective-permute-start(bf16[8,5120]{1,0:T(8,128)(2,1)S(1)} %shard_map.128.refs_0_), channel_id=1, source_target_pairs={{0,3},{1,2},{2,1},{3,0},{4,7},{5,6},{6,5},{7,4},{8,11},{9,10},{10,... | collective-permute-start | bytes 245768 | tf_op jit(solution)/shard_map/ppermute | solution.py:28
  56.4 4.8 %collective-permute-start.10 = (bf16[8,5120]{1,0:T(8,128)(2,1)S(1)}, bf16[8,5120]{1,0:T(8,128)(2,1)S(1)}, u32[]{:S(2)}, u32[]{:S(2)}) collective-permute-start(bf16[8,5120]{1,0:T(8,128)(2,1)S(1)} %shard_map.128.refs_0_), channel_id=1, source_target_pairs={{0,2},{1,3},{2,0},{3,1},{4,6},{5,7},{6,4},{7,5},{8,10},{9,11},{10,... | collective-permute-start | bytes 245768 | tf_op jit(solution)/shard_map/ppermute | solution.py:28
  57.0 4.4 %collective-permute-start.9 = (bf16[8,5120]{1,0:T(8,128)(2,1)S(1)}, bf16[8,5120]{1,0:T(8,128)(2,1)S(1)}, u32[]{:S(2)}, u32[]{:S(2)}) collective-permute-start(bf16[8,5120]{1,0:T(8,128)(2,1)S(1)} %shard_map.128.refs_0_), channel_id=1, source_target_pairs={{0,1},{1,0},{2,3},{3,2},{4,5},{5,4},{6,7},{7,6},{8,9},{9,8},{10,11... | collective-permute-start | bytes 245768 | tf_op jit(solution)/shard_map/ppermute | solution.py:28
  61.5 7.4 %collective-permute-start.12 = (bf16[8,5120]{1,0:T(8,128)(2,1)S(1)}, bf16[8,5120]{1,0:T(8,128)(2,1)S(1)}, u32[]{:S(2)}, u32[]{:S(2)}) collective-permute-start(bf16[8,5120]{1,0:T(8,128)(2,1)S(1)} %shard_map.129.refs_1_), channel_id=1, source_target_pairs={{0,4},{1,5},{2,6},{3,7},{4,0},{5,1},{6,2},{7,3},{8,12},{9,13},{10,... | collective-permute-start | bytes 245768 | tf_op jit(solution)/shard_map/ppermute | solution.py:28
  69.7 5.3 %collective-permute-start.13 = (bf16[8,128]{1,0:T(8,128)(2,1)S(1)}, bf16[8,128]{1,0:T(8,128)(2,1)S(1)}, u32[]{:S(2)}, u32[]{:S(2)}) collective-permute-start(bf16[8,128]{1,0:T(8,128)(2,1)S(1)} %get-tuple-element.68), channel_id=1, source_target_pairs={{0,0},{1,2},{2,4},{3,6},{4,1},{5,3},{6,5},{7,7},{8,8},{9,10},{10,1... | collective-permute-start | bytes 6152 | tf_op jit(solution)/shard_map/ppermute | solution.py:375
  70.4 6.2 %collective-permute-start.14 = (bf16[8,128]{1,0:T(8,128)(2,1)S(1)}, bf16[8,128]{1,0:T(8,128)(2,1)S(1)}, u32[]{:S(2)}, u32[]{:S(2)}) collective-permute-start(bf16[8,128]{1,0:T(8,128)(2,1)S(1)} %get-tuple-element.69), channel_id=1, source_target_pairs={{0,1},{1,3},{2,5},{3,7},{4,0},{5,2},{6,4},{7,6},{8,9},{9,11},{10,1... | collective-permute-start | bytes 6152 | tf_op jit(solution)/shard_map/ppermute | solution.py:378
  78.1 5.5 %collective-permute-start.17 = (bf16[8,5120]{1,0:T(8,128)(2,1)S(1)}, bf16[8,5120]{1,0:T(8,128)(2,1)S(1)}, u32[]{:S(2)}, u32[]{:S(2)}) collective-permute-start(bf16[8,5120]{1,0:T(8,128)(2,1)S(1)} %shard_map.132.refs_0_), channel_id=1, source_target_pairs={{0,3},{1,2},{2,1},{3,0},{4,7},{5,6},{6,5},{7,4},{8,11},{9,10},{10,... | collective-permute-start | bytes 245768 | tf_op jit(solution)/shard_map/ppermute | solution.py:28
  81.1 5.3 %collective-permute-start.16 = (bf16[8,5120]{1,0:T(8,128)(2,1)S(1)}, bf16[8,5120]{1,0:T(8,128)(2,1)S(1)}, u32[]{:S(2)}, u32[]{:S(2)}) collective-permute-start(bf16[8,5120]{1,0:T(8,128)(2,1)S(1)} %shard_map.132.refs_0_), channel_id=1, source_target_pairs={{0,2},{1,3},{2,0},{3,1},{4,6},{5,7},{6,4},{7,5},{8,10},{9,11},{10,... | collective-permute-start | bytes 245768 | tf_op jit(solution)/shard_map/ppermute | solution.py:28
  81.8 4.6 %collective-permute-start.15 = (bf16[8,5120]{1,0:T(8,128)(2,1)S(1)}, bf16[8,5120]{1,0:T(8,128)(2,1)S(1)}, u32[]{:S(2)}, u32[]{:S(2)}) collective-permute-start(bf16[8,5120]{1,0:T(8,128)(2,1)S(1)} %shard_map.132.refs_0_), channel_id=1, source_target_pairs={{0,1},{1,0},{2,3},{3,2},{4,5},{5,4},{6,7},{7,6},{8,9},{9,8},{10,11... | collective-permute-start | bytes 245768 | tf_op jit(solution)/shard_map/ppermute | solution.py:28
  86.5 6.3 %collective-permute-start.18 = (bf16[8,5120]{1,0:T(8,128)(2,1)S(1)}, bf16[8,5120]{1,0:T(8,128)(2,1)S(1)}, u32[]{:S(2)}, u32[]{:S(2)}) collective-permute-start(bf16[8,5120]{1,0:T(8,128)(2,1)S(1)} %shard_map.133.refs_1_), channel_id=1, source_target_pairs={{0,4},{1,5},{2,6},{3,7},{4,0},{5,1},{6,2},{7,3},{8,12},{9,13},{10,... | collective-permute-start | bytes 245768 | tf_op jit(solution)/shard_map/ppermute | solution.py:28
  93.6 6.2 %collective-permute-start.19 = (bf16[8,128]{1,0:T(8,128)(2,1)S(1)}, bf16[8,128]{1,0:T(8,128)(2,1)S(1)}, u32[]{:S(2)}, u32[]{:S(2)}) collective-permute-start(bf16[8,128]{1,0:T(8,128)(2,1)S(1)} %get-tuple-element.76), channel_id=1, source_target_pairs={{0,0},{1,2},{2,4},{3,6},{4,1},{5,3},{6,5},{7,7},{8,8},{9,10},{10,1... | collective-permute-start | bytes 6152 | tf_op jit(solution)/shard_map/ppermute | solution.py:375
  94.2 5.9 %collective-permute-start.20 = (bf16[8,128]{1,0:T(8,128)(2,1)S(1)}, bf16[8,128]{1,0:T(8,128)(2,1)S(1)}, u32[]{:S(2)}, u32[]{:S(2)}) collective-permute-start(bf16[8,128]{1,0:T(8,128)(2,1)S(1)} %get-tuple-element.77), channel_id=1, source_target_pairs={{0,1},{1,3},{2,5},{3,7},{4,0},{5,2},{6,4},{7,6},{8,9},{9,11},{10,1... | collective-permute-start | bytes 6152 | tf_op jit(solution)/shard_map/ppermute | solution.py:378
  101.6 5.5 %collective-permute-start.23 = (bf16[8,5120]{1,0:T(8,128)(2,1)S(1)}, bf16[8,5120]{1,0:T(8,128)(2,1)S(1)}, u32[]{:S(2)}, u32[]{:S(2)}) collective-permute-start(bf16[8,5120]{1,0:T(8,128)(2,1)S(1)} %shard_map.136.refs_0_), channel_id=1, source_target_pairs={{0,3},{1,2},{2,1},{3,0},{4,7},{5,6},{6,5},{7,4},{8,11},{9,10},{10,... | collective-permute-start | bytes 245768 | tf_op jit(solution)/shard_map/ppermute | solution.py:28
  103.8 4.4 %collective-permute-start.22 = (bf16[8,5120]{1,0:T(8,128)(2,1)S(1)}, bf16[8,5120]{1,0:T(8,128)(2,1)S(1)}, u32[]{:S(2)}, u32[]{:S(2)}) collective-permute-start(bf16[8,5120]{1,0:T(8,128)(2,1)S(1)} %shard_map.136.refs_0_), channel_id=1, source_target_pairs={{0,2},{1,3},{2,0},{3,1},{4,6},{5,7},{6,4},{7,5},{8,10},{9,11},{10,... | collective-permute-start | bytes 245768 | tf_op jit(solution)/shard_map/ppermute | solution.py:28
  104.5 4.4 %collective-permute-start.21 = (bf16[8,5120]{1,0:T(8,128)(2,1)S(1)}, bf16[8,5120]{1,0:T(8,128)(2,1)S(1)}, u32[]{:S(2)}, u32[]{:S(2)}) collective-permute-start(bf16[8,5120]{1,0:T(8,128)(2,1)S(1)} %shard_map.136.refs_0_), channel_id=1, source_target_pairs={{0,1},{1,0},{2,3},{3,2},{4,5},{5,4},{6,7},{7,6},{8,9},{9,8},{10,11... | collective-permute-start | bytes 245768 | tf_op jit(solution)/shard_map/ppermute | solution.py:28
  109.0 5.4 %collective-permute-start.24 = (bf16[8,5120]{1,0:T(8,128)(2,1)S(1)}, bf16[8,5120]{1,0:T(8,128)(2,1)S(1)}, u32[]{:S(2)}, u32[]{:S(2)}) collective-permute-start(bf16[8,5120]{1,0:T(8,128)(2,1)S(1)} %shard_map.137.refs_1_), channel_id=1, source_target_pairs={{0,4},{1,5},{2,6},{3,7},{4,0},{5,1},{6,2},{7,3},{8,12},{9,13},{10,... | collective-permute-start | bytes 245768 | tf_op jit(solution)/shard_map/ppermute | solution.py:28
  115.2 7.1 %collective-permute-start.25 = (bf16[8,128]{1,0:T(8,128)(2,1)S(1)}, bf16[8,128]{1,0:T(8,128)(2,1)S(1)}, u32[]{:S(2)}, u32[]{:S(2)}) collective-permute-start(bf16[8,128]{1,0:T(8,128)(2,1)S(1)} %get-tuple-element.84), channel_id=1, source_target_pairs={{0,0},{1,2},{2,4},{3,6},{4,1},{5,3},{6,5},{7,7},{8,8},{9,10},{10,1... | collective-permute-start | bytes 6152 | tf_op jit(solution)/shard_map/ppermute | solution.py:375
  115.9 6.7 %collective-permute-start.26 = (bf16[8,128]{1,0:T(8,128)(2,1)S(1)}, bf16[8,128]{1,0:T(8,128)(2,1)S(1)}, u32[]{:S(2)}, u32[]{:S(2)}) collective-permute-start(bf16[8,128]{1,0:T(8,128)(2,1)S(1)} %get-tuple-element.85), channel_id=1, source_target_pairs={{0,1},{1,3},{2,5},{3,7},{4,0},{5,2},{6,4},{7,6},{8,9},{9,11},{10,1... | collective-permute-start | bytes 6152 | tf_op jit(solution)/shard_map/ppermute | solution.py:378
  124.2 5.3 %collective-permute-start.29 = (bf16[8,5120]{1,0:T(8,128)(2,1)S(1)}, bf16[8,5120]{1,0:T(8,128)(2,1)S(1)}, u32[]{:S(2)}, u32[]{:S(2)}) collective-permute-start(bf16[8,5120]{1,0:T(8,128)(2,1)S(1)} %shard_map.140.refs_0_), channel_id=1, source_target_pairs={{0,3},{1,2},{2,1},{3,0},{4,7},{5,6},{6,5},{7,4},{8,11},{9,10},{10,... | collective-permute-start | bytes 245768 | tf_op jit(solution)/shard_map/ppermute | solution.py:28
  126.3 4.4 %collective-permute-start.28 = (bf16[8,5120]{1,0:T(8,128)(2,1)S(1)}, bf16[8,5120]{1,0:T(8,128)(2,1)S(1)}, u32[]{:S(2)}, u32[]{:S(2)}) collective-permute-start(bf16[8,5120]{1,0:T(8,128)(2,1)S(1)} %shard_map.140.refs_0_), channel_id=1, source_target_pairs={{0,2},{1,3},{2,0},{3,1},{4,6},{5,7},{6,4},{7,5},{8,10},{9,11},{10,... | collective-permute-start | bytes 245768 | tf_op jit(solution)/shard_map/ppermute | solution.py:28
  127.0 4.4 %collective-permute-start.27 = (bf16[8,5120]{1,0:T(8,128)(2,1)S(1)}, bf16[8,5120]{1,0:T(8,128)(2,1)S(1)}, u32[]{:S(2)}, u32[]{:S(2)}) collective-permute-start(bf16[8,5120]{1,0:T(8,128)(2,1)S(1)} %shard_map.140.refs_0_), channel_id=1, source_target_pairs={{0,1},{1,0},{2,3},{3,2},{4,5},{5,4},{6,7},{7,6},{8,9},{9,8},{10,11... | collective-permute-start | bytes 245768 | tf_op jit(solution)/shard_map/ppermute | solution.py:28
  131.5 5.4 %collective-permute-start.30 = (bf16[8,5120]{1,0:T(8,128)(2,1)S(1)}, bf16[8,5120]{1,0:T(8,128)(2,1)S(1)}, u32[]{:S(2)}, u32[]{:S(2)}) collective-permute-start(bf16[8,5120]{1,0:T(8,128)(2,1)S(1)} %shard_map.141.first_ref), channel_id=1, source_target_pairs={{0,4},{1,5},{2,6},{3,7},{4,0},{5,1},{6,2},{7,3},{8,12},{9,13},{10,... | collective-permute-start | bytes 245768 | tf_op jit(solution)/shard_map/ppermute | solution.py:28
  137.1 1.3 collective-permute-start.31

commit v5 on v4

--- a/solution.py
+++ b/solution.py
@@ -232,10 +232,6 @@
         kv_out[step] = own[:, width + step * columns : width + (step + 1) * columns]
 
 
-def after(one, *others):
-    return lax.optimization_barrier((one, *others))[0] if others else one
-
-
 def run(kernel, outs, *args, scalars=0, copies=0, vmem=6 * 2**20, flops=0, moved=0):
     return pl.pallas_call(
         kernel,
@@ -303,7 +299,7 @@
         half_size = model_size // 2
         across = list(range(half_size, model_size))
         within = list(range(1, half_size))
-        masks = across[:2] + within + across[2:] + [0]
+        masks = within + across + [0]
         landed = {}
         for mask in masks:
             head = (model_index ^ mask) * HD
@@ -313,8 +309,6 @@
                     for cache in (cache_keys, cache_values)
                 ]
             )
-            if mask in across[2:]:
-                block = after(block, landed[within[mask - across[2]]])
             landed[mask] = exchange(block, "mp", mask) if mask else block
         caches = [landed[mask] for mask in masks]
     else:

time: 139 us -> 138 us (level)
  starting transfers between devices: 53.4 us -> 52 us
    ppermute x24, waiting for transfers between devices: 43.2 us -> 46.8 us  [exchange(): lax.ppermute(block, axis, [(low, low ^ mask) for low in range(count)])]
    ppermute x4, waiting for transfers between devices: 9.98 us -> 6.68 us  [per_device(): lax.ppermute(sent[1], 'mp', to_odd + [(pairs + a, b) for a, b in to_even])]
    ppermute x4, starting transfers between devices: 14.3 us -> 11.5 us  [per_device(): lax.ppermute(sent[1], 'mp', to_odd + [(pairs + a, b) for a, b in to_even])]
  transfers between devices with their start and end apart: 32 -> 32, of which waited for: 22 -> 23; matrix products, arithmetic and copies ran while one was open for 1% -> 1% of each run, Pallas kernels for 13% -> 13%
where the time goes in v5:
time: 138 us
  waiting for transfers between devices  53.5 us (39%)
  starting transfers between devices  52 us (38%)
  Pallas kernels  27.2 us (20%)
  local copies, waits for them, and re-layouts  3.27 us (2%)
    ppermute x24, waiting for transfers between devices, exchange(): lax.ppermute(block, axis, [(low, low ^ mask) for low in range(count)])  46.8 us
    ppermute x24, starting transfers between devices, exchange(): lax.ppermute(block, axis, [(low, low ^ mask) for low in range(count)])  37.9 us
    pallas_call x22, Pallas kernels, run(): pl.pallas_call(kernel, out_shape=outs, in_specs=[in_smem] * scalars + [in...  27.2 us
    ppermute x4, starting transfers between devices, per_device(): lax.ppermute(sent[1], 'mp', to_odd + [(pairs + a, b) for a, b in to_even])  11.5 us
    ppermute x4, waiting for transfers between devices, per_device(): lax.ppermute(sent[1], 'mp', to_odd + [(pairs + a, b) for a, b in to_even])  6.68 us
  transfers between devices with their start and end apart: 32, of which 23 were waited for; matrix products, arithmetic and copies ran while one was open for 1% of the time, Pallas kernels for 13%

profile of v5, /device:TPU:0, one launch (start us, length us, event | category | flops | bytes accessed | tf_op | source)
XLA Modules:
  0.0 138.0 jit_solution(8778920847474358919)
XLA Ops:
  0.7 1.9 %dynamic-slice_bitcast_fusion = (bf16[1,8,64,128]{3,2,1,0:T(8,128)(2,1)S(1)}, bf16[1,8,64,128]{3,2,1,0:T(8,128)(2,1)S(1)}, bf16[1,8,64,128]{3,2,1,0:T(8,128)(2,1...) fusion(bf16[8,64,1024]{2,1,0:T(8,128)(2,1)} %param.17, ...), kind=kLoop, calls=%fused_computation.8 | loop fusion | bytes 4194336 | tf_op jit(solution)/shard_map/stack | solution.py:306
  2.7 6.1 %collective-permute-start.6 = (bf16[2,8,64,128]{3,2,1,0:T(8,128)(2,1)S(1)}, bf16[2,8,64,128]{3,2,1,0:T(8,128)(2,1)S(1)}, u32[]{:S(2)}, u32[]{:S(2)}) collective-permute-start(bf16[2,8,64,128]{3,2,1,0:T(8,128)(2,1)S(1)} %pad_maximum_fusion.6), channel_id=1, source_target_pairs={{0,7},{1,6},{2,5},{3,4},{4,3},{5,2},{6,1},{7,0},{8,15},{9,14},{10,... | collective-permute-start | bytes 786440 | tf_op jit(solution)/shard_map/ppermute | solution.py:28
  9.5 3.0 %collective-permute-start.2 = (bf16[2,8,64,128]{3,2,1,0:T(8,128)(2,1)S(1)}, bf16[2,8,64,128]{3,2,1,0:T(8,128)(2,1)S(1)}, u32[]{:S(2)}, u32[]{:S(2)}) collective-permute-start(bf16[2,8,64,128]{3,2,1,0:T(8,128)(2,1)S(1)} %pad_maximum_fusion.2), channel_id=1, source_target_pairs={{0,3},{1,2},{2,1},{3,0},{4,7},{5,6},{6,5},{7,4},{8,11},{9,10},{10,... | collective-permute-start | bytes 786440 | tf_op jit(solution)/shard_map/ppermute | solution.py:28
  12.7 0.7 add_convert_fusion
  13.4 2.6 %collective-permute-done.6.rest_6_ = bf16[2,8,64,128]{3,2,1,0:T(8,128)(2,1)S(1)} collective-permute-done((bf16[2,8,64,128]{3,2,1,0:T(8,128)(2,1)S(1)}, bf16[2,8,64,128]{3,2,1,0:T(8,128)(2,1)S(1)}, u32[]{:S(2)}, u32[]{:S(2)}) %collective-permute-start.6) | collective-permute-done | bytes 262176 | tf_op jit(solution)/shard_map/ppermute | solution.py:28
  15.9 7.7 %collective-permute-start.4 = (bf16[2,8,64,128]{3,2,1,0:T(8,128)(2,1)S(1)}, bf16[2,8,64,128]{3,2,1,0:T(8,128)(2,1)S(1)}, u32[]{:S(2)}, u32[]{:S(2)}) collective-permute-start(bf16[2,8,64,128]{3,2,1,0:T(8,128)(2,1)S(1)} %pad_maximum_fusion.4), channel_id=1, source_target_pairs={{0,5},{1,4},{2,7},{3,6},{4,1},{5,0},{6,3},{7,2},{8,13},{9,12},{10,... | collective-permute-start | bytes 786440 | tf_op jit(solution)/shard_map/ppermute | solution.py:28
  23.6 0.9 collective-permute-start.5
  24.7 0.8 concatenate.3.scalars_ref
  26.1 7.1 %shard_map.125 = (bf16[5120,1024]{1,0:T(8,128)(2,1)S(1)}, bf16[1024,5120]{1,0:T(8,128)(2,1)S(1)}) custom-call(bf16[5120,1024]{1,0:T(8,128)(2,1)} %refs_0_.3, bf16[1024,5120]{1,0:T(8,128)(2,1)} %refs_1_.3), custom_call_target="tpu_custom_call" | custom-call | bytes 20971520 | tf_op jit(solution)/shard_map/pallas_call | solution.py:236
  34.2 0.7 shard_map.124
  34.9 0.7 collective-permute-start.7
  35.6 2.0 %collective-permute-start.8 = (bf16[8,128]{1,0:T(8,128)(2,1)S(1)}, bf16[8,128]{1,0:T(8,128)(2,1)S(1)}, u32[]{:S(2)}, u32[]{:S(2)}) collective-permute-start(bf16[8,128]{1,0:T(8,128)(2,1)S(1)} %get-tuple-element.57), channel_id=1, source_target_pairs={{0,1},{1,3},{2,5},{3,7},{4,0},{5,2},{6,4},{7,6},{8,9},{9,11},{10,1... | collective-permute-start | bytes 6152 | tf_op jit(solution)/shard_map/ppermute | solution.py:372
  37.6 1.6 %shard_map.126.query_ref = f32[8,8,128]{2,1,0:T(8,128)S(1)} custom-call(f32[4,2,8,128]{3,2,1,0:T(8,128)S(1)} %get-tuple-element.46.tables_ref, bf16[8,5120]{1,0:T(8,128)(2,1)S(1)} %get-tuple-element.50.normed_ref, bf16[5120,1024]{1,0:T(8,128)(2,1)S(1)} %get-tuple-element.51.w_ref), custom_call_target="tpu_custom_call" | custom-call | flops 83886080 | bytes 10485760 | tf_op jit(solution)/shard_map/pallas_call | solution.py:236
  39.2 9.8 %collective-permute-done.4.rest_4_ = bf16[2,8,64,128]{3,2,1,0:T(8,128)(2,1)S(1)} collective-permute-done((bf16[2,8,64,128]{3,2,1,0:T(8,128)(2,1)S(1)}, bf16[2,8,64,128]{3,2,1,0:T(8,128)(2,1)S(1)}, u32[]{:S(2)}, u32[]{:S(2)}) %collective-permute-start.4) | collective-permute-done | bytes 262176 | tf_op jit(solution)/shard_map/ppermute | solution.py:28
  49.0 0.6 shard_map.127
  49.6 4.1 %collective-permute-done.8.rest_1_ = bf16[8,128]{1,0:T(8,128)(2,1)S(1)} collective-permute-done((bf16[8,128]{1,0:T(8,128)(2,1)S(1)}, bf16[8,128]{1,0:T(8,128)(2,1)S(1)}, u32[]{:S(2)}, u32[]{:S(2)}) %collective-permute-start.8) | collective-permute-done | bytes 2080 | tf_op jit(solution)/shard_map/ppermute | solution.py:372
  53.6 1.5 %shard_map.128.refs_0_ = bf16[8,5120]{1,0:T(8,128)(2,1)S(1)} custom-call(s32[9,8,128]{2,1,0:T(8,128)S(1)} %get-tuple-element.45.rows_ref, f32[8,8,128]{2,1,0:T(8,128)S(1)} %shard_map.126.query_ref, f32[8,8,128]{2,1,0:T(8,128)S(1)} %get-tuple-element.52.num_ref, f32[8,8,128]{2,1,0:T(8,128)S(1)} %get-tuple-element.53.max_ref, ...), custom_call_target="tpu_custom_call" | custom-call | tf_op jit(solution)/shard_map/pallas_call | solution.py:236
  55.2 1.2 collective-permute-start.11
  56.3 1.8 %collective-permute-start.10 = (bf16[8,5120]{1,0:T(8,128)(2,1)S(1)}, bf16[8,5120]{1,0:T(8,128)(2,1)S(1)}, u32[]{:S(2)}, u32[]{:S(2)}) collective-permute-start(bf16[8,5120]{1,0:T(8,128)(2,1)S(1)} %shard_map.128.refs_0_), channel_id=1, source_target_pairs={{0,2},{1,3},{2,0},{3,1},{4,6},{5,7},{6,4},{7,5},{8,10},{9,11},{10,... | collective-permute-start | bytes 245768 | tf_op jit(solution)/shard_map/ppermute | solution.py:28
  58.1 0.6 collective-permute-start.9
  58.7 2.0 %collective-permute-done.11.refs_3_ = bf16[8,5120]{1,0:T(8,128)(2,1)S(1)} collective-permute-done((bf16[8,5120]{1,0:T(8,128)(2,1)S(1)}, bf16[8,5120]{1,0:T(8,128)(2,1)S(1)}, u32[]{:S(2)}, u32[]{:S(2)}) %collective-permute-start.11) | collective-permute-done | bytes 81952 | tf_op jit(solution)/shard_map/ppermute | solution.py:28
  60.6 0.8 collective-permute-done.10.refs_2_
  61.4 1.1 collective-permute-done.9.refs_1_
  62.6 1.7 %collective-permute-start.12 = (bf16[8,5120]{1,0:T(8,128)(2,1)S(1)}, bf16[8,5120]{1,0:T(8,128)(2,1)S(1)}, u32[]{:S(2)}, u32[]{:S(2)}) collective-permute-start(bf16[8,5120]{1,0:T(8,128)(2,1)S(1)} %shard_map.129.refs_1_), channel_id=1, source_target_pairs={{0,4},{1,5},{2,6},{3,7},{4,0},{5,1},{6,2},{7,3},{8,12},{9,13},{10,... | collective-permute-start | bytes 245768 | tf_op jit(solution)/shard_map/ppermute | solution.py:28
  64.3 4.3 %collective-permute-done.12.refs_2_ = bf16[8,5120]{1,0:T(8,128)(2,1)S(1)} collective-permute-done((bf16[8,5120]{1,0:T(8,128)(2,1)S(1)}, bf16[8,5120]{1,0:T(8,128)(2,1)S(1)}, u32[]{:S(2)}, u32[]{:S(2)}) %collective-permute-start.12) | collective-permute-done | bytes 81952 | tf_op jit(solution)/shard_map/ppermute | solution.py:28
  68.6 0.8 shard_map.130
  69.4 0.7 collective-permute-start.13
  70.0 2.5 %collective-permute-start.14 = (bf16[8,128]{1,0:T(8,128)(2,1)S(1)}, bf16[8,128]{1,0:T(8,128)(2,1)S(1)}, u32[]{:S(2)}, u32[]{:S(2)}) collective-permute-start(bf16[8,128]{1,0:T(8,128)(2,1)S(1)} %get-tuple-element.65), channel_id=1, source_target_pairs={{0,1},{1,3},{2,5},{3,7},{4,0},{5,2},{6,4},{7,6},{8,9},{9,11},{10,1... | collective-permute-start | bytes 6152 | tf_op jit(solution)/shard_map/ppermute | solution.py:372
  72.5 2.2 %shard_map.131 = (f32[8,8,128]{2,1,0:T(8,128)S(1)}, f32[8,8,128]{2,1,0:T(8,128)S(1)}, f32[8,8,128]{2,1,0:T(8,128)S(1)}, f32[8,8,128]{2,1,0:T(8,128)S(1)}) custom-call(s32[9,8,128]{2,1,0:T(8,128)S(1)} %get-tuple-element.45.rows_ref, f32[4,2,8,128]{3,2,1,0:T(8,128)S(1)} %get-tuple-element.46.tables_ref, bf16[8,5120]{1,0:T(8,128)(2,1)S(1)} %get-tuple-element.59.normed_ref, ...), custom_call_target="tpu_custom_call" | custom-call | flops 83886080 | bytes 10485760 | tf_op jit(solution)/shard_map/pallas_call | solution.py:236
  74.8 1.4 %collective-permute-done.14.rest_3_ = bf16[8,128]{1,0:T(8,128)(2,1)S(1)} collective-permute-done((bf16[8,128]{1,0:T(8,128)(2,1)S(1)}, bf16[8,128]{1,0:T(8,128)(2,1)S(1)}, u32[]{:S(2)}, u32[]{:S(2)}) %collective-permute-start.14) | collective-permute-done | bytes 2080 | tf_op jit(solution)/shard_map/ppermute | solution.py:372
  76.2 1.5 %shard_map.132.refs_0_ = bf16[8,5120]{1,0:T(8,128)(2,1)S(1)} custom-call(s32[9,8,128]{2,1,0:T(8,128)S(1)} %get-tuple-element.45.rows_ref, f32[8,8,128]{2,1,0:T(8,128)S(1)} %get-tuple-element.60.query_ref, f32[8,8,128]{2,1,0:T(8,128)S(1)} %get-tuple-element.61.num_ref, f32[8,8,128]{2,1,0:T(8,128)S(1)} %get-tuple-element.62.max_ref, ...), custom_call_target="tpu_custom_call" | custom-call | tf_op jit(solution)/shard_map/pallas_call | solution.py:236
  77.7 1.2 collective-permute-start.17
  78.9 1.7 %collective-permute-start.16 = (bf16[8,5120]{1,0:T(8,128)(2,1)S(1)}, bf16[8,5120]{1,0:T(8,128)(2,1)S(1)}, u32[]{:S(2)}, u32[]{:S(2)}) collective-permute-start(bf16[8,5120]{1,0:T(8,128)(2,1)S(1)} %shard_map.132.refs_0_), channel_id=1, source_target_pairs={{0,2},{1,3},{2,0},{3,1},{4,6},{5,7},{6,4},{7,5},{8,10},{9,11},{10,... | collective-permute-start | bytes 245768 | tf_op jit(solution)/shard_map/ppermute | solution.py:28
  81.2 2.7 %collective-permute-done.17.refs_3_ = bf16[8,5120]{1,0:T(8,128)(2,1)S(1)} collective-permute-done((bf16[8,5120]{1,0:T(8,128)(2,1)S(1)}, bf16[8,5120]{1,0:T(8,128)(2,1)S(1)}, u32[]{:S(2)}, u32[]{:S(2)}) %collective-permute-start.17) | collective-permute-done | bytes 81952 | tf_op jit(solution)/shard_map/ppermute | solution.py:28
  84.1 1.0 collective-permute-done.15.refs_1_
  85.1 1.4 %collective-permute-start.18 = (bf16[8,5120]{1,0:T(8,128)(2,1)S(1)}, bf16[8,5120]{1,0:T(8,128)(2,1)S(1)}, u32[]{:S(2)}, u32[]{:S(2)}) collective-permute-start(bf16[8,5120]{1,0:T(8,128)(2,1)S(1)} %shard_map.133.refs_1_), channel_id=1, source_target_pairs={{0,4},{1,5},{2,6},{3,7},{4,0},{5,1},{6,2},{7,3},{8,12},{9,13},{10,... | collective-permute-start | bytes 245768 | tf_op jit(solution)/shard_map/ppermute | solution.py:28
  86.5 4.9 %collective-permute-done.18.refs_2_ = bf16[8,5120]{1,0:T(8,128)(2,1)S(1)} collective-permute-done((bf16[8,5120]{1,0:T(8,128)(2,1)S(1)}, bf16[8,5120]{1,0:T(8,128)(2,1)S(1)}, u32[]{:S(2)}, u32[]{:S(2)}) %collective-permute-start.18) | collective-permute-done | bytes 81952 | tf_op jit(solution)/shard_map/ppermute | solution.py:28
  91.4 0.8 shard_map.134
  92.2 0.7 collective-permute-start.19
  92.9 2.8 %collective-permute-start.20 = (bf16[8,128]{1,0:T(8,128)(2,1)S(1)}, bf16[8,128]{1,0:T(8,128)(2,1)S(1)}, u32[]{:S(2)}, u32[]{:S(2)}) collective-permute-start(bf16[8,128]{1,0:T(8,128)(2,1)S(1)} %get-tuple-element.73), channel_id=1, source_target_pairs={{0,1},{1,3},{2,5},{3,7},{4,0},{5,2},{6,4},{7,6},{8,9},{9,11},{10,1... | collective-permute-start | bytes 6152 | tf_op jit(solution)/shard_map/ppermute | solution.py:372
  95.7 2.2 %shard_map.135 = (f32[8,8,128]{2,1,0:T(8,128)S(1)}, f32[8,8,128]{2,1,0:T(8,128)S(1)}, f32[8,8,128]{2,1,0:T(8,128)S(1)}, f32[8,8,128]{2,1,0:T(8,128)S(1)}) custom-call(s32[9,8,128]{2,1,0:T(8,128)S(1)} %get-tuple-element.45.rows_ref, f32[4,2,8,128]{3,2,1,0:T(8,128)S(1)} %get-tuple-element.46.tables_ref, bf16[8,5120]{1,0:T(8,128)(2,1)S(1)} %get-tuple-element.67.normed_ref, ...), custom_call_target="tpu_custom_call" | custom-call | flops 83886080 | bytes 10485760 | tf_op jit(solution)/shard_map/pallas_call | solution.py:236
  97.9 1.0 collective-permute-done.20.rest_5_
  98.9 1.5 %shard_map.136.refs_0_ = bf16[8,5120]{1,0:T(8,128)(2,1)S(1)} custom-call(s32[9,8,128]{2,1,0:T(8,128)S(1)} %get-tuple-element.45.rows_ref, f32[8,8,128]{2,1,0:T(8,128)S(1)} %get-tuple-element.68.query_ref, f32[8,8,128]{2,1,0:T(8,128)S(1)} %get-tuple-element.69.num_ref, f32[8,8,128]{2,1,0:T(8,128)S(1)} %get-tuple-element.70.max_ref, ...), custom_call_target="tpu_custom_call" | custom-call | tf_op jit(solution)/shard_map/pallas_call | solution.py:236
  100.4 2.3 %collective-permute-start.23 = (bf16[8,5120]{1,0:T(8,128)(2,1)S(1)}, bf16[8,5120]{1,0:T(8,128)(2,1)S(1)}, u32[]{:S(2)}, u32[]{:S(2)}) collective-permute-start(bf16[8,5120]{1,0:T(8,128)(2,1)S(1)} %shard_map.136.refs_0_), channel_id=1, source_target_pairs={{0,3},{1,2},{2,1},{3,0},{4,7},{5,6},{6,5},{7,4},{8,11},{9,10},{10,... | collective-permute-start | bytes 245768 | tf_op jit(solution)/shard_map/ppermute | solution.py:28
  102.8 0.7 collective-permute-start.22
  103.9 1.9 %collective-permute-done.23.refs_3_ = bf16[8,5120]{1,0:T(8,128)(2,1)S(1)} collective-permute-done((bf16[8,5120]{1,0:T(8,128)(2,1)S(1)}, bf16[8,5120]{1,0:T(8,128)(2,1)S(1)}, u32[]{:S(2)}, u32[]{:S(2)}) %collective-permute-start.23) | collective-permute-done | bytes 81952 | tf_op jit(solution)/shard_map/ppermute | solution.py:28
  105.8 1.4 %collective-permute-done.22.refs_2_ = bf16[8,5120]{1,0:T(8,128)(2,1)S(1)} collective-permute-done((bf16[8,5120]{1,0:T(8,128)(2,1)S(1)}, bf16[8,5120]{1,0:T(8,128)(2,1)S(1)}, u32[]{:S(2)}, u32[]{:S(2)}) %collective-permute-start.22) | collective-permute-done | bytes 81952 | tf_op jit(solution)/shard_map/ppermute | solution.py:28
  107.2 0.7 collective-permute-done.21.refs_1_
  107.9 1.0 collective-permute-start.24
  108.9 4.4 %collective-permute-done.24.refs_2_ = bf16[8,5120]{1,0:T(8,128)(2,1)S(1)} collective-permute-done((bf16[8,5120]{1,0:T(8,128)(2,1)S(1)}, bf16[8,5120]{1,0:T(8,128)(2,1)S(1)}, u32[]{:S(2)}, u32[]{:S(2)}) %collective-permute-start.24) | collective-permute-done | bytes 81952 | tf_op jit(solution)/shard_map/ppermute | solution.py:28
  113.3 0.8 shard_map.138
  114.1 0.7 collective-permute-start.25
  114.8 4.2 %collective-permute-start.26 = (bf16[8,128]{1,0:T(8,128)(2,1)S(1)}, bf16[8,128]{1,0:T(8,128)(2,1)S(1)}, u32[]{:S(2)}, u32[]{:S(2)}) collective-permute-start(bf16[8,128]{1,0:T(8,128)(2,1)S(1)} %get-tuple-element.81), channel_id=1, source_target_pairs={{0,1},{1,3},{2,5},{3,7},{4,0},{5,2},{6,4},{7,6},{8,9},{9,11},{10,1... | collective-permute-start | bytes 6152 | tf_op jit(solution)/shard_map/ppermute | solution.py:372
  119.0 2.2 %shard_map.139 = (f32[8,8,128]{2,1,0:T(8,128)S(1)}, f32[8,8,128]{2,1,0:T(8,128)S(1)}, f32[8,8,128]{2,1,0:T(8,128)S(1)}, f32[8,8,128]{2,1,0:T(8,128)S(1)}) custom-call(s32[9,8,128]{2,1,0:T(8,128)S(1)} %get-tuple-element.45.rows_ref, f32[4,2,8,128]{3,2,1,0:T(8,128)S(1)} %get-tuple-element.46.tables_ref, bf16[8,5120]{1,0:T(8,128)(2,1)S(1)} %get-tuple-element.75.normed_ref, ...), custom_call_target="tpu_custom_call" | custom-call | flops 83886080 | bytes 10485760 | tf_op jit(solution)/shard_map/pallas_call | solution.py:236
  121.4 1.6 %shard_map.140.refs_0_ = bf16[8,5120]{1,0:T(8,128)(2,1)S(1)} custom-call(s32[9,8,128]{2,1,0:T(8,128)S(1)} %get-tuple-element.45.rows_ref, f32[8,8,128]{2,1,0:T(8,128)S(1)} %get-tuple-element.76.query_ref, f32[8,8,128]{2,1,0:T(8,128)S(1)} %get-tuple-element.77.num_ref, f32[8,8,128]{2,1,0:T(8,128)S(1)} %get-tuple-element.78.max_ref, ...), custom_call_target="tpu_custom_call" | custom-call | tf_op jit(solution)/shard_map/pallas_call | solution.py:236
  123.0 2.3 %collective-permute-start.29 = (bf16[8,5120]{1,0:T(8,128)(2,1)S(1)}, bf16[8,5120]{1,0:T(8,128)(2,1)S(1)}, u32[]{:S(2)}, u32[]{:S(2)}) collective-permute-start(bf16[8,5120]{1,0:T(8,128)(2,1)S(1)} %shard_map.140.refs_0_), channel_id=1, source_target_pairs={{0,3},{1,2},{2,1},{3,0},{4,7},{5,6},{6,5},{7,4},{8,11},{9,10},{10,... | collective-permute-start | bytes 245768 | tf_op jit(solution)/shard_map/ppermute | solution.py:28
  125.3 0.7 collective-permute-start.28
  126.5 1.9 %collective-permute-done.29.refs_3_ = bf16[8,5120]{1,0:T(8,128)(2,1)S(1)} collective-permute-done((bf16[8,5120]{1,0:T(8,128)(2,1)S(1)}, bf16[8,5120]{1,0:T(8,128)(2,1)S(1)}, u32[]{:S(2)}, u32[]{:S(2)}) %collective-permute-start.29) | collective-permute-done | bytes 81952 | tf_op jit(solution)/shard_map/ppermute | solution.py:28
  128.3 1.4 collective-permute-done.28.refs_2_
  129.7 0.7 collective-permute-done.27.refs_1_
  130.4 1.3 collective-permute-start.30
  131.7 4.2 %collective-permute-done.30.second_ref = bf16[8,5120]{1,0:T(8,128)(2,1)S(1)} collective-permute-done((bf16[8,5120]{1,0:T(8,128)(2,1)S(1)}, bf16[8,5120]{1,0:T(8,128)(2,1)S(1)}, u32[]{:S(2)}, u32[]{:S(2)}) %collective-permute-start.30) | collective-permute-done | bytes 81952 | tf_op jit(solution)/shard_map/ppermute | solution.py:28
  136.1 1.2 collective-permute-done.31.got_ref
  137.3 0.7 shard_map.143
  (42 shorter events, 5.0 us)
Async XLA Ops:
  2.7 13.3 %collective-permute-start.6 = (bf16[2,8,64,128]{3,2,1,0:T(8,128)(2,1)S(1)}, bf16[2,8,64,128]{3,2,1,0:T(8,128)(2,1)S(1)}, u32[]{:S(2)}, u32[]{:S(2)}) collective-permute-start(bf16[2,8,64,128]{3,2,1,0:T(8,128)(2,1)S(1)} %pad_maximum_fusion.6), channel_id=1, source_target_pairs={{0,7},{1,6},{2,5},{3,4},{4,3},{5,2},{6,1},{7,0},{8,15},{9,14},{10,... | collective-permute-start | bytes 786440 | tf_op jit(solution)/shard_map/ppermute | solution.py:28
  8.8 14.9 %collective-permute-start = (bf16[2,8,64,128]{3,2,1,0:T(8,128)(2,1)S(1)}, bf16[2,8,64,128]{3,2,1,0:T(8,128)(2,1)S(1)}, u32[]{:S(2)}, u32[]{:S(2)}) collective-permute-start(bf16[2,8,64,128]{3,2,1,0:T(8,128)(2,1)S(1)} %pad_maximum_fusion), channel_id=1, source_target_pairs={{0,1},{1,0},{2,3},{3,2},{4,5},{5,4},{6,7},{7,6},{8,9},{9,8},{10,11... | collective-permute-start | bytes 786440 | tf_op jit(solution)/shard_map/ppermute | solution.py:28
  9.4 25.5 %collective-permute-start.1 = (bf16[2,8,64,128]{3,2,1,0:T(8,128)(2,1)S(1)}, bf16[2,8,64,128]{3,2,1,0:T(8,128)(2,1)S(1)}, u32[]{:S(2)}, u32[]{:S(2)}) collective-permute-start(bf16[2,8,64,128]{3,2,1,0:T(8,128)(2,1)S(1)} %pad_maximum_fusion.1), channel_id=1, source_target_pairs={{0,2},{1,3},{2,0},{3,1},{4,6},{5,7},{6,4},{7,5},{8,10},{9,11},{10,... | collective-permute-start | bytes 786440 | tf_op jit(solution)/shard_map/ppermute | solution.py:28
  9.5 26.1 %collective-permute-start.2 = (bf16[2,8,64,128]{3,2,1,0:T(8,128)(2,1)S(1)}, bf16[2,8,64,128]{3,2,1,0:T(8,128)(2,1)S(1)}, u32[]{:S(2)}, u32[]{:S(2)}) collective-permute-start(bf16[2,8,64,128]{3,2,1,0:T(8,128)(2,1)S(1)} %pad_maximum_fusion.2), channel_id=1, source_target_pairs={{0,3},{1,2},{2,1},{3,0},{4,7},{5,6},{6,5},{7,4},{8,11},{9,10},{10,... | collective-permute-start | bytes 786440 | tf_op jit(solution)/shard_map/ppermute | solution.py:28
  12.5 26.7 %collective-permute-start.3 = (bf16[2,8,64,128]{3,2,1,0:T(8,128)(2,1)S(1)}, bf16[2,8,64,128]{3,2,1,0:T(8,128)(2,1)S(1)}, u32[]{:S(2)}, u32[]{:S(2)}) collective-permute-start(bf16[2,8,64,128]{3,2,1,0:T(8,128)(2,1)S(1)} %pad_maximum_fusion.3), channel_id=1, source_target_pairs={{0,4},{1,5},{2,6},{3,7},{4,0},{5,1},{6,2},{7,3},{8,12},{9,13},{10,... | collective-permute-start | bytes 786440 | tf_op jit(solution)/shard_map/ppermute | solution.py:28
  15.9 33.0 %collective-permute-start.4 = (bf16[2,8,64,128]{3,2,1,0:T(8,128)(2,1)S(1)}, bf16[2,8,64,128]{3,2,1,0:T(8,128)(2,1)S(1)}, u32[]{:S(2)}, u32[]{:S(2)}) collective-permute-start(bf16[2,8,64,128]{3,2,1,0:T(8,128)(2,1)S(1)} %pad_maximum_fusion.4), channel_id=1, source_target_pairs={{0,5},{1,4},{2,7},{3,6},{4,1},{5,0},{6,3},{7,2},{8,13},{9,12},{10,... | collective-permute-start | bytes 786440 | tf_op jit(solution)/shard_map/ppermute | solution.py:28
  23.6 25.3 %collective-permute-start.5 = (bf16[2,8,64,128]{3,2,1,0:T(8,128)(2,1)S(1)}, bf16[2,8,64,128]{3,2,1,0:T(8,128)(2,1)S(1)}, u32[]{:S(2)}, u32[]{:S(2)}) collective-permute-start(bf16[2,8,64,128]{3,2,1,0:T(8,128)(2,1)S(1)} %pad_maximum_fusion.5), channel_id=1, source_target_pairs={{0,6},{1,7},{2,4},{3,5},{4,2},{5,3},{6,0},{7,1},{8,14},{9,15},{10,... | collective-permute-start | bytes 786440 | tf_op jit(solution)/shard_map/ppermute | solution.py:28
  26.1 7.7 %copy-start = (bf16[5120,256]{1,0:T(8,128)(2,1)S(1)}, bf16[5120,256]{1,0:T(8,128)(2,1)}, u32[]{:S(2)}) copy-start(bf16[5120,256]{1,0:T(8,128)(2,1)} %refs_0_.2) | copy-start | bytes 7864324
  26.1 7.7 %copy-start.1 = (bf16[8,5120]{1,0:T(8,128)(2,1)S(1)}, bf16[8,5120]{1,0:T(8,128)(2,1)}, u32[]{:S(2)}) copy-start(bf16[8,5120]{1,0:T(8,128)(2,1)} %refs_1_.2) | copy-start | bytes 245764
  26.1 7.7 %copy-start.2 = (f32[5120]{0:T(1024)S(1)}, f32[5120]{0:T(1024)}, u32[]{:S(2)}) copy-start(f32[5120]{0:T(1024)} %param.12) | copy-start | bytes 61444
  34.9 14.7 %collective-permute-start.7 = (bf16[8,128]{1,0:T(8,128)(2,1)S(1)}, bf16[8,128]{1,0:T(8,128)(2,1)S(1)}, u32[]{:S(2)}, u32[]{:S(2)}) collective-permute-start(bf16[8,128]{1,0:T(8,128)(2,1)S(1)} %get-tuple-element.56), channel_id=1, source_target_pairs={{0,0},{1,2},{2,4},{3,6},{4,1},{5,3},{6,5},{7,7},{8,8},{9,10},{10,1... | collective-permute-start | bytes 6152 | tf_op jit(solution)/shard_map/ppermute | solution.py:369
  35.6 18.1 %collective-permute-start.8 = (bf16[8,128]{1,0:T(8,128)(2,1)S(1)}, bf16[8,128]{1,0:T(8,128)(2,1)S(1)}, u32[]{:S(2)}, u32[]{:S(2)}) collective-permute-start(bf16[8,128]{1,0:T(8,128)(2,1)S(1)} %get-tuple-element.57), channel_id=1, source_target_pairs={{0,1},{1,3},{2,5},{3,7},{4,0},{5,2},{6,4},{7,6},{8,9},{9,11},{10,1... | collective-permute-start | bytes 6152 | tf_op jit(solution)/shard_map/ppermute | solution.py:372
  55.2 5.5 %collective-permute-start.11 = (bf16[8,5120]{1,0:T(8,128)(2,1)S(1)}, bf16[8,5120]{1,0:T(8,128)(2,1)S(1)}, u32[]{:S(2)}, u32[]{:S(2)}) collective-permute-start(bf16[8,5120]{1,0:T(8,128)(2,1)S(1)} %shard_map.128.refs_0_), channel_id=1, source_target_pairs={{0,3},{1,2},{2,1},{3,0},{4,7},{5,6},{6,5},{7,4},{8,11},{9,10},{10,... | collective-permute-start | bytes 245768 | tf_op jit(solution)/shard_map/ppermute | solution.py:28
  56.3 5.0 %collective-permute-start.10 = (bf16[8,5120]{1,0:T(8,128)(2,1)S(1)}, bf16[8,5120]{1,0:T(8,128)(2,1)S(1)}, u32[]{:S(2)}, u32[]{:S(2)}) collective-permute-start(bf16[8,5120]{1,0:T(8,128)(2,1)S(1)} %shard_map.128.refs_0_), channel_id=1, source_target_pairs={{0,2},{1,3},{2,0},{3,1},{4,6},{5,7},{6,4},{7,5},{8,10},{9,11},{10,... | collective-permute-start | bytes 245768 | tf_op jit(solution)/shard_map/ppermute | solution.py:28
  58.1 4.4 %collective-permute-start.9 = (bf16[8,5120]{1,0:T(8,128)(2,1)S(1)}, bf16[8,5120]{1,0:T(8,128)(2,1)S(1)}, u32[]{:S(2)}, u32[]{:S(2)}) collective-permute-start(bf16[8,5120]{1,0:T(8,128)(2,1)S(1)} %shard_map.128.refs_0_), channel_id=1, source_target_pairs={{0,1},{1,0},{2,3},{3,2},{4,5},{5,4},{6,7},{7,6},{8,9},{9,8},{10,11... | collective-permute-start | bytes 245768 | tf_op jit(solution)/shard_map/ppermute | solution.py:28
  62.6 6.0 %collective-permute-start.12 = (bf16[8,5120]{1,0:T(8,128)(2,1)S(1)}, bf16[8,5120]{1,0:T(8,128)(2,1)S(1)}, u32[]{:S(2)}, u32[]{:S(2)}) collective-permute-start(bf16[8,5120]{1,0:T(8,128)(2,1)S(1)} %shard_map.129.refs_1_), channel_id=1, source_target_pairs={{0,4},{1,5},{2,6},{3,7},{4,0},{5,1},{6,2},{7,3},{8,12},{9,13},{10,... | collective-permute-start | bytes 245768 | tf_op jit(solution)/shard_map/ppermute | solution.py:28
  69.4 5.4 %collective-permute-start.13 = (bf16[8,128]{1,0:T(8,128)(2,1)S(1)}, bf16[8,128]{1,0:T(8,128)(2,1)S(1)}, u32[]{:S(2)}, u32[]{:S(2)}) collective-permute-start(bf16[8,128]{1,0:T(8,128)(2,1)S(1)} %get-tuple-element.64), channel_id=1, source_target_pairs={{0,0},{1,2},{2,4},{3,6},{4,1},{5,3},{6,5},{7,7},{8,8},{9,10},{10,1... | collective-permute-start | bytes 6152 | tf_op jit(solution)/shard_map/ppermute | solution.py:369
  70.0 6.1 %collective-permute-start.14 = (bf16[8,128]{1,0:T(8,128)(2,1)S(1)}, bf16[8,128]{1,0:T(8,128)(2,1)S(1)}, u32[]{:S(2)}, u32[]{:S(2)}) collective-permute-start(bf16[8,128]{1,0:T(8,128)(2,1)S(1)} %get-tuple-element.65), channel_id=1, source_target_pairs={{0,1},{1,3},{2,5},{3,7},{4,0},{5,2},{6,4},{7,6},{8,9},{9,11},{10,1... | collective-permute-start | bytes 6152 | tf_op jit(solution)/shard_map/ppermute | solution.py:372
  77.7 6.2 %collective-permute-start.17 = (bf16[8,5120]{1,0:T(8,128)(2,1)S(1)}, bf16[8,5120]{1,0:T(8,128)(2,1)S(1)}, u32[]{:S(2)}, u32[]{:S(2)}) collective-permute-start(bf16[8,5120]{1,0:T(8,128)(2,1)S(1)} %shard_map.132.refs_0_), channel_id=1, source_target_pairs={{0,3},{1,2},{2,1},{3,0},{4,7},{5,6},{6,5},{7,4},{8,11},{9,10},{10,... | collective-permute-start | bytes 245768 | tf_op jit(solution)/shard_map/ppermute | solution.py:28
  78.9 5.2 %collective-permute-start.16 = (bf16[8,5120]{1,0:T(8,128)(2,1)S(1)}, bf16[8,5120]{1,0:T(8,128)(2,1)S(1)}, u32[]{:S(2)}, u32[]{:S(2)}) collective-permute-start(bf16[8,5120]{1,0:T(8,128)(2,1)S(1)} %shard_map.132.refs_0_), channel_id=1, source_target_pairs={{0,2},{1,3},{2,0},{3,1},{4,6},{5,7},{6,4},{7,5},{8,10},{9,11},{10,... | collective-permute-start | bytes 245768 | tf_op jit(solution)/shard_map/ppermute | solution.py:28
  80.6 4.4 %collective-permute-start.15 = (bf16[8,5120]{1,0:T(8,128)(2,1)S(1)}, bf16[8,5120]{1,0:T(8,128)(2,1)S(1)}, u32[]{:S(2)}, u32[]{:S(2)}) collective-permute-start(bf16[8,5120]{1,0:T(8,128)(2,1)S(1)} %shard_map.132.refs_0_), channel_id=1, source_target_pairs={{0,1},{1,0},{2,3},{3,2},{4,5},{5,4},{6,7},{7,6},{8,9},{9,8},{10,11... | collective-permute-start | bytes 245768 | tf_op jit(solution)/shard_map/ppermute | solution.py:28
  85.1 6.3 %collective-permute-start.18 = (bf16[8,5120]{1,0:T(8,128)(2,1)S(1)}, bf16[8,5120]{1,0:T(8,128)(2,1)S(1)}, u32[]{:S(2)}, u32[]{:S(2)}) collective-permute-start(bf16[8,5120]{1,0:T(8,128)(2,1)S(1)} %shard_map.133.refs_1_), channel_id=1, source_target_pairs={{0,4},{1,5},{2,6},{3,7},{4,0},{5,1},{6,2},{7,3},{8,12},{9,13},{10,... | collective-permute-start | bytes 245768 | tf_op jit(solution)/shard_map/ppermute | solution.py:28
  92.2 5.7 %collective-permute-start.19 = (bf16[8,128]{1,0:T(8,128)(2,1)S(1)}, bf16[8,128]{1,0:T(8,128)(2,1)S(1)}, u32[]{:S(2)}, u32[]{:S(2)}) collective-permute-start(bf16[8,128]{1,0:T(8,128)(2,1)S(1)} %get-tuple-element.72), channel_id=1, source_target_pairs={{0,0},{1,2},{2,4},{3,6},{4,1},{5,3},{6,5},{7,7},{8,8},{9,10},{10,1... | collective-permute-start | bytes 6152 | tf_op jit(solution)/shard_map/ppermute | solution.py:369
  92.9 6.0 %collective-permute-start.20 = (bf16[8,128]{1,0:T(8,128)(2,1)S(1)}, bf16[8,128]{1,0:T(8,128)(2,1)S(1)}, u32[]{:S(2)}, u32[]{:S(2)}) collective-permute-start(bf16[8,128]{1,0:T(8,128)(2,1)S(1)} %get-tuple-element.73), channel_id=1, source_target_pairs={{0,1},{1,3},{2,5},{3,7},{4,0},{5,2},{6,4},{7,6},{8,9},{9,11},{10,1... | collective-permute-start | bytes 6152 | tf_op jit(solution)/shard_map/ppermute | solution.py:372
  100.4 5.3 %collective-permute-start.23 = (bf16[8,5120]{1,0:T(8,128)(2,1)S(1)}, bf16[8,5120]{1,0:T(8,128)(2,1)S(1)}, u32[]{:S(2)}, u32[]{:S(2)}) collective-permute-start(bf16[8,5120]{1,0:T(8,128)(2,1)S(1)} %shard_map.136.refs_0_), channel_id=1, source_target_pairs={{0,3},{1,2},{2,1},{3,0},{4,7},{5,6},{6,5},{7,4},{8,11},{9,10},{10,... | collective-permute-start | bytes 245768 | tf_op jit(solution)/shard_map/ppermute | solution.py:28
  102.8 4.4 %collective-permute-start.22 = (bf16[8,5120]{1,0:T(8,128)(2,1)S(1)}, bf16[8,5120]{1,0:T(8,128)(2,1)S(1)}, u32[]{:S(2)}, u32[]{:S(2)}) collective-permute-start(bf16[8,5120]{1,0:T(8,128)(2,1)S(1)} %shard_map.136.refs_0_), channel_id=1, source_target_pairs={{0,2},{1,3},{2,0},{3,1},{4,6},{5,7},{6,4},{7,5},{8,10},{9,11},{10,... | collective-permute-start | bytes 245768 | tf_op jit(solution)/shard_map/ppermute | solution.py:28
  103.4 4.4 %collective-permute-start.21 = (bf16[8,5120]{1,0:T(8,128)(2,1)S(1)}, bf16[8,5120]{1,0:T(8,128)(2,1)S(1)}, u32[]{:S(2)}, u32[]{:S(2)}) collective-permute-start(bf16[8,5120]{1,0:T(8,128)(2,1)S(1)} %shard_map.136.refs_0_), channel_id=1, source_target_pairs={{0,1},{1,0},{2,3},{3,2},{4,5},{5,4},{6,7},{7,6},{8,9},{9,8},{10,11... | collective-permute-start | bytes 245768 | tf_op jit(solution)/shard_map/ppermute | solution.py:28
  107.9 5.4 %collective-permute-start.24 = (bf16[8,5120]{1,0:T(8,128)(2,1)S(1)}, bf16[8,5120]{1,0:T(8,128)(2,1)S(1)}, u32[]{:S(2)}, u32[]{:S(2)}) collective-permute-start(bf16[8,5120]{1,0:T(8,128)(2,1)S(1)} %shard_map.137.refs_1_), channel_id=1, source_target_pairs={{0,4},{1,5},{2,6},{3,7},{4,0},{5,1},{6,2},{7,3},{8,12},{9,13},{10,... | collective-permute-start | bytes 245768 | tf_op jit(solution)/shard_map/ppermute | solution.py:28
  114.1 7.1 %collective-permute-start.25 = (bf16[8,128]{1,0:T(8,128)(2,1)S(1)}, bf16[8,128]{1,0:T(8,128)(2,1)S(1)}, u32[]{:S(2)}, u32[]{:S(2)}) collective-permute-start(bf16[8,128]{1,0:T(8,128)(2,1)S(1)} %get-tuple-element.80), channel_id=1, source_target_pairs={{0,0},{1,2},{2,4},{3,6},{4,1},{5,3},{6,5},{7,7},{8,8},{9,10},{10,1... | collective-permute-start | bytes 6152 | tf_op jit(solution)/shard_map/ppermute | solution.py:369
  114.8 6.6 %collective-permute-start.26 = (bf16[8,128]{1,0:T(8,128)(2,1)S(1)}, bf16[8,128]{1,0:T(8,128)(2,1)S(1)}, u32[]{:S(2)}, u32[]{:S(2)}) collective-permute-start(bf16[8,128]{1,0:T(8,128)(2,1)S(1)} %get-tuple-element.81), channel_id=1, source_target_pairs={{0,1},{1,3},{2,5},{3,7},{4,0},{5,2},{6,4},{7,6},{8,9},{9,11},{10,1... | collective-permute-start | bytes 6152 | tf_op jit(solution)/shard_map/ppermute | solution.py:372
  123.0 5.3 %collective-permute-start.29 = (bf16[8,5120]{1,0:T(8,128)(2,1)S(1)}, bf16[8,5120]{1,0:T(8,128)(2,1)S(1)}, u32[]{:S(2)}, u32[]{:S(2)}) collective-permute-start(bf16[8,5120]{1,0:T(8,128)(2,1)S(1)} %shard_map.140.refs_0_), channel_id=1, source_target_pairs={{0,3},{1,2},{2,1},{3,0},{4,7},{5,6},{6,5},{7,4},{8,11},{9,10},{10,... | collective-permute-start | bytes 245768 | tf_op jit(solution)/shard_map/ppermute | solution.py:28
  125.3 4.4 %collective-permute-start.28 = (bf16[8,5120]{1,0:T(8,128)(2,1)S(1)}, bf16[8,5120]{1,0:T(8,128)(2,1)S(1)}, u32[]{:S(2)}, u32[]{:S(2)}) collective-permute-start(bf16[8,5120]{1,0:T(8,128)(2,1)S(1)} %shard_map.140.refs_0_), channel_id=1, source_target_pairs={{0,2},{1,3},{2,0},{3,1},{4,6},{5,7},{6,4},{7,5},{8,10},{9,11},{10,... | collective-permute-start | bytes 245768 | tf_op jit(solution)/shard_map/ppermute | solution.py:28
  125.9 4.4 %collective-permute-start.27 = (bf16[8,5120]{1,0:T(8,128)(2,1)S(1)}, bf16[8,5120]{1,0:T(8,128)(2,1)S(1)}, u32[]{:S(2)}, u32[]{:S(2)}) collective-permute-start(bf16[8,5120]{1,0:T(8,128)(2,1)S(1)} %shard_map.140.refs_0_), channel_id=1, source_target_pairs={{0,1},{1,0},{2,3},{3,2},{4,5},{5,4},{6,7},{7,6},{8,9},{9,8},{10,11... | collective-permute-start | bytes 245768 | tf_op jit(solution)/shard_map/ppermute | solution.py:28
  130.4 5.4 %collective-permute-start.30 = (bf16[8,5120]{1,0:T(8,128)(2,1)S(1)}, bf16[8,5120]{1,0:T(8,128)(2,1)S(1)}, u32[]{:S(2)}, u32[]{:S(2)}) collective-permute-start(bf16[8,5120]{1,0:T(8,128)(2,1)S(1)} %shard_map.141.first_ref), channel_id=1, source_target_pairs={{0,4},{1,5},{2,6},{3,7},{4,0},{5,1},{6,2},{7,3},{8,12},{9,13},{10,... | collective-permute-start | bytes 245768 | tf_op jit(solution)/shard_map/ppermute | solution.py:28
  136.0 1.3 collective-permute-start.31

commit v6 on v5

--- a/solution.py
+++ b/solution.py
@@ -252,7 +252,9 @@
         if len(now) == 2:
             now = now + [now[0] | now[1]]
         others = [exchange(part, axis, mask) for mask in now]
-        part = run(add_kernel, jax.ShapeDtypeStruct(part.shape, part.dtype), part, *others)
+        part = run(
+            add_kernel, jax.ShapeDtypeStruct(part.shape, part.dtype), *reversed(others), part
+        )
     return part, exchange(part, axis, last)
 
 

time: 138 us -> 141 us (1.022)
  waiting for transfers between devices: 53.5 us -> 56.5 us
    ppermute x24, waiting for transfers between devices: 46.8 us -> 49.8 us  [exchange(): lax.ppermute(block, axis, [(low, low ^ mask) for low in range(count)])]
  transfers between devices with their start and end apart: 32 -> 32, of which waited for: 23 -> 23; matrix products, arithmetic and copies ran while one was open for 1% -> 1% of each run, Pallas kernels for 13% -> 12%
where the time goes in v6:
time: 141 us
  waiting for transfers between devices  56.5 us (40%)
  starting transfers between devices  52 us (37%)
  Pallas kernels  27.2 us (19%)
  local copies, waits for them, and re-layouts  3.27 us (2%)
    ppermute x24, waiting for transfers between devices, exchange(): lax.ppermute(block, axis, [(low, low ^ mask) for low in range(count)])  49.8 us
    ppermute x24, starting transfers between devices, exchange(): lax.ppermute(block, axis, [(low, low ^ mask) for low in range(count)])  37.4 us
    pallas_call x22, Pallas kernels, run(): pl.pallas_call(kernel, out_shape=outs, in_specs=[in_smem] * scalars + [in...  27.2 us
    ppermute x4, starting transfers between devices, per_device(): lax.ppermute(sent[1], 'mp', to_odd + [(pairs + a, b) for a, b in to_even])  12 us
    ppermute x4, waiting for transfers between devices, per_device(): lax.ppermute(sent[1], 'mp', to_odd + [(pairs + a, b) for a, b in to_even])  6.64 us
  transfers between devices with their start and end apart: 32, of which 23 were waited for; matrix products, arithmetic and copies ran while one was open for 1% of the time, Pallas kernels for 12%

profile of v6, /device:TPU:0, one launch (start us, length us, event | category | flops | bytes accessed | tf_op | source)
XLA Modules:
  0.0 141.0 jit_solution(17824229122227894189)
XLA Ops:
  0.7 1.9 %dynamic-slice_bitcast_fusion = (bf16[1,8,64,128]{3,2,1,0:T(8,128)(2,1)S(1)}, bf16[1,8,64,128]{3,2,1,0:T(8,128)(2,1)S(1)}, bf16[1,8,64,128]{3,2,1,0:T(8,128)(2,1...) fusion(bf16[8,64,1024]{2,1,0:T(8,128)(2,1)} %param.17, ...), kind=kLoop, calls=%fused_computation.8 | loop fusion | bytes 4194336 | tf_op jit(solution)/shard_map/stack | solution.py:308
  2.7 6.1 %collective-permute-start.6 = (bf16[2,8,64,128]{3,2,1,0:T(8,128)(2,1)S(1)}, bf16[2,8,64,128]{3,2,1,0:T(8,128)(2,1)S(1)}, u32[]{:S(2)}, u32[]{:S(2)}) collective-permute-start(bf16[2,8,64,128]{3,2,1,0:T(8,128)(2,1)S(1)} %pad_maximum_fusion.6), channel_id=1, source_target_pairs={{0,7},{1,6},{2,5},{3,4},{4,3},{5,2},{6,1},{7,0},{8,15},{9,14},{10,... | collective-permute-start | bytes 786440 | tf_op jit(solution)/shard_map/ppermute | solution.py:28
  9.5 3.0 %collective-permute-start.2 = (bf16[2,8,64,128]{3,2,1,0:T(8,128)(2,1)S(1)}, bf16[2,8,64,128]{3,2,1,0:T(8,128)(2,1)S(1)}, u32[]{:S(2)}, u32[]{:S(2)}) collective-permute-start(bf16[2,8,64,128]{3,2,1,0:T(8,128)(2,1)S(1)} %pad_maximum_fusion.2), channel_id=1, source_target_pairs={{0,3},{1,2},{2,1},{3,0},{4,7},{5,6},{6,5},{7,4},{8,11},{9,10},{10,... | collective-permute-start | bytes 786440 | tf_op jit(solution)/shard_map/ppermute | solution.py:28
  12.7 0.7 add_convert_fusion
  13.4 2.6 %collective-permute-done.6.rest_6_ = bf16[2,8,64,128]{3,2,1,0:T(8,128)(2,1)S(1)} collective-permute-done((bf16[2,8,64,128]{3,2,1,0:T(8,128)(2,1)S(1)}, bf16[2,8,64,128]{3,2,1,0:T(8,128)(2,1)S(1)}, u32[]{:S(2)}, u32[]{:S(2)}) %collective-permute-start.6) | collective-permute-done | bytes 262176 | tf_op jit(solution)/shard_map/ppermute | solution.py:28
  15.9 7.7 %collective-permute-start.4 = (bf16[2,8,64,128]{3,2,1,0:T(8,128)(2,1)S(1)}, bf16[2,8,64,128]{3,2,1,0:T(8,128)(2,1)S(1)}, u32[]{:S(2)}, u32[]{:S(2)}) collective-permute-start(bf16[2,8,64,128]{3,2,1,0:T(8,128)(2,1)S(1)} %pad_maximum_fusion.4), channel_id=1, source_target_pairs={{0,5},{1,4},{2,7},{3,6},{4,1},{5,0},{6,3},{7,2},{8,13},{9,12},{10,... | collective-permute-start | bytes 786440 | tf_op jit(solution)/shard_map/ppermute | solution.py:28
  23.6 0.9 collective-permute-start.5
  24.7 0.8 concatenate.3.scalars_ref
  26.1 7.1 %shard_map.125 = (bf16[5120,1024]{1,0:T(8,128)(2,1)S(1)}, bf16[1024,5120]{1,0:T(8,128)(2,1)S(1)}) custom-call(bf16[5120,1024]{1,0:T(8,128)(2,1)} %refs_0_.3, bf16[1024,5120]{1,0:T(8,128)(2,1)} %refs_1_.3), custom_call_target="tpu_custom_call" | custom-call | bytes 20971520 | tf_op jit(solution)/shard_map/pallas_call | solution.py:236
  34.2 0.7 shard_map.124
  35.6 2.0 %collective-permute-start.8 = (bf16[8,128]{1,0:T(8,128)(2,1)S(1)}, bf16[8,128]{1,0:T(8,128)(2,1)S(1)}, u32[]{:S(2)}, u32[]{:S(2)}) collective-permute-start(bf16[8,128]{1,0:T(8,128)(2,1)S(1)} %get-tuple-element.57), channel_id=1, source_target_pairs={{0,1},{1,3},{2,5},{3,7},{4,0},{5,2},{6,4},{7,6},{8,9},{9,11},{10,1... | collective-permute-start | bytes 6152 | tf_op jit(solution)/shard_map/ppermute | solution.py:374
  37.6 1.6 %shard_map.126.query_ref = f32[8,8,128]{2,1,0:T(8,128)S(1)} custom-call(f32[4,2,8,128]{3,2,1,0:T(8,128)S(1)} %get-tuple-element.46.tables_ref, bf16[8,5120]{1,0:T(8,128)(2,1)S(1)} %get-tuple-element.50.normed_ref, bf16[5120,1024]{1,0:T(8,128)(2,1)S(1)} %get-tuple-element.51.w_ref), custom_call_target="tpu_custom_call" | custom-call | flops 83886080 | bytes 10485760 | tf_op jit(solution)/shard_map/pallas_call | solution.py:236
  39.2 9.8 %collective-permute-done.4.rest_4_ = bf16[2,8,64,128]{3,2,1,0:T(8,128)(2,1)S(1)} collective-permute-done((bf16[2,8,64,128]{3,2,1,0:T(8,128)(2,1)S(1)}, bf16[2,8,64,128]{3,2,1,0:T(8,128)(2,1)S(1)}, u32[]{:S(2)}, u32[]{:S(2)}) %collective-permute-start.4) | collective-permute-done | bytes 262176 | tf_op jit(solution)/shard_map/ppermute | solution.py:28
  49.6 4.1 %collective-permute-done.8.rest_1_ = bf16[8,128]{1,0:T(8,128)(2,1)S(1)} collective-permute-done((bf16[8,128]{1,0:T(8,128)(2,1)S(1)}, bf16[8,128]{1,0:T(8,128)(2,1)S(1)}, u32[]{:S(2)}, u32[]{:S(2)}) %collective-permute-start.8) | collective-permute-done | bytes 2080 | tf_op jit(solution)/shard_map/ppermute | solution.py:374
  53.6 1.5 %shard_map.128.refs_3_ = bf16[8,5120]{1,0:T(8,128)(2,1)S(1)} custom-call(s32[9,8,128]{2,1,0:T(8,128)S(1)} %get-tuple-element.45.rows_ref, f32[8,8,128]{2,1,0:T(8,128)S(1)} %shard_map.126.query_ref, f32[8,8,128]{2,1,0:T(8,128)S(1)} %get-tuple-element.52.num_ref, f32[8,8,128]{2,1,0:T(8,128)S(1)} %get-tuple-element.53.max_ref, ...), custom_call_target="tpu_custom_call" | custom-call | tf_op jit(solution)/shard_map/pallas_call | solution.py:236
  55.2 1.5 %collective-permute-start.11 = (bf16[8,5120]{1,0:T(8,128)(2,1)S(1)}, bf16[8,5120]{1,0:T(8,128)(2,1)S(1)}, u32[]{:S(2)}, u32[]{:S(2)}) collective-permute-start(bf16[8,5120]{1,0:T(8,128)(2,1)S(1)} %shard_map.128.refs_3_), channel_id=1, source_target_pairs={{0,1},{1,0},{2,3},{3,2},{4,5},{5,4},{6,7},{7,6},{8,9},{9,8},{10,11... | collective-permute-start | bytes 245768 | tf_op jit(solution)/shard_map/ppermute | solution.py:28
  56.9 1.8 %collective-permute-start.9 = (bf16[8,5120]{1,0:T(8,128)(2,1)S(1)}, bf16[8,5120]{1,0:T(8,128)(2,1)S(1)}, u32[]{:S(2)}, u32[]{:S(2)}) collective-permute-start(bf16[8,5120]{1,0:T(8,128)(2,1)S(1)} %shard_map.128.refs_3_), channel_id=1, source_target_pairs={{0,3},{1,2},{2,1},{3,0},{4,7},{5,6},{6,5},{7,4},{8,11},{9,10},{10,... | collective-permute-start | bytes 245768 | tf_op jit(solution)/shard_map/ppermute | solution.py:28
  58.7 1.8 %collective-permute-done.11.refs_2_ = bf16[8,5120]{1,0:T(8,128)(2,1)S(1)} collective-permute-done((bf16[8,5120]{1,0:T(8,128)(2,1)S(1)}, bf16[8,5120]{1,0:T(8,128)(2,1)S(1)}, u32[]{:S(2)}, u32[]{:S(2)}) %collective-permute-start.11) | collective-permute-done | bytes 81952 | tf_op jit(solution)/shard_map/ppermute | solution.py:28
  61.1 1.2 collective-permute-done.9.refs_0_
  62.3 2.0 %collective-permute-start.12 = (bf16[8,5120]{1,0:T(8,128)(2,1)S(1)}, bf16[8,5120]{1,0:T(8,128)(2,1)S(1)}, u32[]{:S(2)}, u32[]{:S(2)}) collective-permute-start(bf16[8,5120]{1,0:T(8,128)(2,1)S(1)} %shard_map.129.refs_1_), channel_id=1, source_target_pairs={{0,4},{1,5},{2,6},{3,7},{4,0},{5,1},{6,2},{7,3},{8,12},{9,13},{10,... | collective-permute-start | bytes 245768 | tf_op jit(solution)/shard_map/ppermute | solution.py:28
  64.3 3.4 %collective-permute-done.12.refs_2_ = bf16[8,5120]{1,0:T(8,128)(2,1)S(1)} collective-permute-done((bf16[8,5120]{1,0:T(8,128)(2,1)S(1)}, bf16[8,5120]{1,0:T(8,128)(2,1)S(1)}, u32[]{:S(2)}, u32[]{:S(2)}) %collective-permute-start.12) | collective-permute-done | bytes 81952 | tf_op jit(solution)/shard_map/ppermute | solution.py:28
  67.7 0.8 shard_map.130
  68.5 0.7 collective-permute-start.13
  69.2 4.5 %collective-permute-start.14 = (bf16[8,128]{1,0:T(8,128)(2,1)S(1)}, bf16[8,128]{1,0:T(8,128)(2,1)S(1)}, u32[]{:S(2)}, u32[]{:S(2)}) collective-permute-start(bf16[8,128]{1,0:T(8,128)(2,1)S(1)} %get-tuple-element.65), channel_id=1, source_target_pairs={{0,1},{1,3},{2,5},{3,7},{4,0},{5,2},{6,4},{7,6},{8,9},{9,11},{10,1... | collective-permute-start | bytes 6152 | tf_op jit(solution)/shard_map/ppermute | solution.py:374
  73.7 2.2 %shard_map.131 = (f32[8,8,128]{2,1,0:T(8,128)S(1)}, f32[8,8,128]{2,1,0:T(8,128)S(1)}, f32[8,8,128]{2,1,0:T(8,128)S(1)}, f32[8,8,128]{2,1,0:T(8,128)S(1)}) custom-call(s32[9,8,128]{2,1,0:T(8,128)S(1)} %get-tuple-element.45.rows_ref, f32[4,2,8,128]{3,2,1,0:T(8,128)S(1)} %get-tuple-element.46.tables_ref, bf16[8,5120]{1,0:T(8,128)(2,1)S(1)} %get-tuple-element.59.normed_ref, ...), custom_call_target="tpu_custom_call" | custom-call | flops 83886080 | bytes 10485760 | tf_op jit(solution)/shard_map/pallas_call | solution.py:236
  75.9 0.8 collective-permute-done.14.rest_3_
  76.7 1.5 %shard_map.132.refs_3_ = bf16[8,5120]{1,0:T(8,128)(2,1)S(1)} custom-call(s32[9,8,128]{2,1,0:T(8,128)S(1)} %get-tuple-element.45.rows_ref, f32[8,8,128]{2,1,0:T(8,128)S(1)} %get-tuple-element.60.query_ref, f32[8,8,128]{2,1,0:T(8,128)S(1)} %get-tuple-element.61.num_ref, f32[8,8,128]{2,1,0:T(8,128)S(1)} %get-tuple-element.62.max_ref, ...), custom_call_target="tpu_custom_call" | custom-call | tf_op jit(solution)/shard_map/pallas_call | solution.py:236
  78.3 1.7 %collective-permute-start.17 = (bf16[8,5120]{1,0:T(8,128)(2,1)S(1)}, bf16[8,5120]{1,0:T(8,128)(2,1)S(1)}, u32[]{:S(2)}, u32[]{:S(2)}) collective-permute-start(bf16[8,5120]{1,0:T(8,128)(2,1)S(1)} %shard_map.132.refs_3_), channel_id=1, source_target_pairs={{0,1},{1,0},{2,3},{3,2},{4,5},{5,4},{6,7},{7,6},{8,9},{9,8},{10,11... | collective-permute-start | bytes 245768 | tf_op jit(solution)/shard_map/ppermute | solution.py:28
  80.0 1.4 collective-permute-start.16
  81.8 1.0 collective-permute-done.17.refs_2_
  82.7 2.1 %collective-permute-done.16.refs_1_ = bf16[8,5120]{1,0:T(8,128)(2,1)S(1)} collective-permute-done((bf16[8,5120]{1,0:T(8,128)(2,1)S(1)}, bf16[8,5120]{1,0:T(8,128)(2,1)S(1)}, u32[]{:S(2)}, u32[]{:S(2)}) %collective-permute-start.16) | collective-permute-done | bytes 81952 | tf_op jit(solution)/shard_map/ppermute | solution.py:28
  84.9 1.8 %collective-permute-done.15.refs_0_ = bf16[8,5120]{1,0:T(8,128)(2,1)S(1)} collective-permute-done((bf16[8,5120]{1,0:T(8,128)(2,1)S(1)}, bf16[8,5120]{1,0:T(8,128)(2,1)S(1)}, u32[]{:S(2)}, u32[]{:S(2)}) %collective-permute-start.15) | collective-permute-done | bytes 81952 | tf_op jit(solution)/shard_map/ppermute | solution.py:28
  86.7 1.0 collective-permute-start.18
  87.7 5.4 %collective-permute-done.18.refs_2_ = bf16[8,5120]{1,0:T(8,128)(2,1)S(1)} collective-permute-done((bf16[8,5120]{1,0:T(8,128)(2,1)S(1)}, bf16[8,5120]{1,0:T(8,128)(2,1)S(1)}, u32[]{:S(2)}, u32[]{:S(2)}) %collective-permute-start.18) | collective-permute-done | bytes 81952 | tf_op jit(solution)/shard_map/ppermute | solution.py:28
  93.1 0.8 shard_map.134
  93.8 0.7 collective-permute-start.19
  94.5 2.8 %collective-permute-start.20 = (bf16[8,128]{1,0:T(8,128)(2,1)S(1)}, bf16[8,128]{1,0:T(8,128)(2,1)S(1)}, u32[]{:S(2)}, u32[]{:S(2)}) collective-permute-start(bf16[8,128]{1,0:T(8,128)(2,1)S(1)} %get-tuple-element.73), channel_id=1, source_target_pairs={{0,1},{1,3},{2,5},{3,7},{4,0},{5,2},{6,4},{7,6},{8,9},{9,11},{10,1... | collective-permute-start | bytes 6152 | tf_op jit(solution)/shard_map/ppermute | solution.py:374
  97.3 2.2 %shard_map.135 = (f32[8,8,128]{2,1,0:T(8,128)S(1)}, f32[8,8,128]{2,1,0:T(8,128)S(1)}, f32[8,8,128]{2,1,0:T(8,128)S(1)}, f32[8,8,128]{2,1,0:T(8,128)S(1)}) custom-call(s32[9,8,128]{2,1,0:T(8,128)S(1)} %get-tuple-element.45.rows_ref, f32[4,2,8,128]{3,2,1,0:T(8,128)S(1)} %get-tuple-element.46.tables_ref, bf16[8,5120]{1,0:T(8,128)(2,1)S(1)} %get-tuple-element.67.normed_ref, ...), custom_call_target="tpu_custom_call" | custom-call | flops 83886080 | bytes 10485760 | tf_op jit(solution)/shard_map/pallas_call | solution.py:236
  99.5 0.9 collective-permute-done.20.rest_5_
  100.4 1.5 %shard_map.136.refs_3_ = bf16[8,5120]{1,0:T(8,128)(2,1)S(1)} custom-call(s32[9,8,128]{2,1,0:T(8,128)S(1)} %get-tuple-element.45.rows_ref, f32[8,8,128]{2,1,0:T(8,128)S(1)} %get-tuple-element.68.query_ref, f32[8,8,128]{2,1,0:T(8,128)S(1)} %get-tuple-element.69.num_ref, f32[8,8,128]{2,1,0:T(8,128)S(1)} %get-tuple-element.70.max_ref, ...), custom_call_target="tpu_custom_call" | custom-call | tf_op jit(solution)/shard_map/pallas_call | solution.py:236
  102.0 1.2 collective-permute-start.23
  103.2 1.4 collective-permute-start.22
  104.5 0.9 collective-permute-start.21
  105.5 1.0 collective-permute-done.23.refs_2_
  106.4 1.2 collective-permute-done.22.refs_1_
  107.6 2.2 %collective-permute-done.21.refs_0_ = bf16[8,5120]{1,0:T(8,128)(2,1)S(1)} collective-permute-done((bf16[8,5120]{1,0:T(8,128)(2,1)S(1)}, bf16[8,5120]{1,0:T(8,128)(2,1)S(1)}, u32[]{:S(2)}, u32[]{:S(2)}) %collective-permute-start.21) | collective-permute-done | bytes 81952 | tf_op jit(solution)/shard_map/ppermute | solution.py:28
  109.9 1.0 collective-permute-start.24
  110.9 5.3 %collective-permute-done.24.refs_2_ = bf16[8,5120]{1,0:T(8,128)(2,1)S(1)} collective-permute-done((bf16[8,5120]{1,0:T(8,128)(2,1)S(1)}, bf16[8,5120]{1,0:T(8,128)(2,1)S(1)}, u32[]{:S(2)}, u32[]{:S(2)}) %collective-permute-start.24) | collective-permute-done | bytes 81952 | tf_op jit(solution)/shard_map/ppermute | solution.py:28
  116.2 0.8 shard_map.138
  117.0 0.7 collective-permute-start.25
  117.7 2.7 %collective-permute-start.26 = (bf16[8,128]{1,0:T(8,128)(2,1)S(1)}, bf16[8,128]{1,0:T(8,128)(2,1)S(1)}, u32[]{:S(2)}, u32[]{:S(2)}) collective-permute-start(bf16[8,128]{1,0:T(8,128)(2,1)S(1)} %get-tuple-element.81), channel_id=1, source_target_pairs={{0,1},{1,3},{2,5},{3,7},{4,0},{5,2},{6,4},{7,6},{8,9},{9,11},{10,1... | collective-permute-start | bytes 6152 | tf_op jit(solution)/shard_map/ppermute | solution.py:374
  120.3 2.2 %shard_map.139 = (f32[8,8,128]{2,1,0:T(8,128)S(1)}, f32[8,8,128]{2,1,0:T(8,128)S(1)}, f32[8,8,128]{2,1,0:T(8,128)S(1)}, f32[8,8,128]{2,1,0:T(8,128)S(1)}) custom-call(s32[9,8,128]{2,1,0:T(8,128)S(1)} %get-tuple-element.45.rows_ref, f32[4,2,8,128]{3,2,1,0:T(8,128)S(1)} %get-tuple-element.46.tables_ref, bf16[8,5120]{1,0:T(8,128)(2,1)S(1)} %get-tuple-element.75.normed_ref, ...), custom_call_target="tpu_custom_call" | custom-call | flops 83886080 | bytes 10485760 | tf_op jit(solution)/shard_map/pallas_call | solution.py:236
  122.5 0.9 collective-permute-done.26.rest_7_
  123.4 1.6 %shard_map.140.refs_3_ = bf16[8,5120]{1,0:T(8,128)(2,1)S(1)} custom-call(s32[9,8,128]{2,1,0:T(8,128)S(1)} %get-tuple-element.45.rows_ref, f32[8,8,128]{2,1,0:T(8,128)S(1)} %get-tuple-element.76.query_ref, f32[8,8,128]{2,1,0:T(8,128)S(1)} %get-tuple-element.77.num_ref, f32[8,8,128]{2,1,0:T(8,128)S(1)} %get-tuple-element.78.max_ref, ...), custom_call_target="tpu_custom_call" | custom-call | tf_op jit(solution)/shard_map/pallas_call | solution.py:236
  125.0 1.3 collective-permute-start.29
  126.2 1.0 collective-permute-start.28
  127.2 1.3 collective-permute-start.27
  128.5 1.0 collective-permute-done.29.refs_2_
  129.4 1.2 collective-permute-done.28.refs_1_
  130.7 1.9 %collective-permute-done.27.refs_0_ = bf16[8,5120]{1,0:T(8,128)(2,1)S(1)} collective-permute-done((bf16[8,5120]{1,0:T(8,128)(2,1)S(1)}, bf16[8,5120]{1,0:T(8,128)(2,1)S(1)}, u32[]{:S(2)}, u32[]{:S(2)}) %collective-permute-start.27) | collective-permute-done | bytes 81952 | tf_op jit(solution)/shard_map/ppermute | solution.py:28
  132.6 1.0 collective-permute-start.30
  133.5 5.3 %collective-permute-done.30.second_ref = bf16[8,5120]{1,0:T(8,128)(2,1)S(1)} collective-permute-done((bf16[8,5120]{1,0:T(8,128)(2,1)S(1)}, bf16[8,5120]{1,0:T(8,128)(2,1)S(1)}, u32[]{:S(2)}, u32[]{:S(2)}) %collective-permute-start.30) | collective-permute-done | bytes 81952 | tf_op jit(solution)/shard_map/ppermute | solution.py:28
  139.1 1.2 collective-permute-done.31.got_ref
  140.3 0.7 shard_map.143
  (42 shorter events, 5.6 us)
Async XLA Ops:
  2.7 13.3 %collective-permute-start.6 = (bf16[2,8,64,128]{3,2,1,0:T(8,128)(2,1)S(1)}, bf16[2,8,64,128]{3,2,1,0:T(8,128)(2,1)S(1)}, u32[]{:S(2)}, u32[]{:S(2)}) collective-permute-start(bf16[2,8,64,128]{3,2,1,0:T(8,128)(2,1)S(1)} %pad_maximum_fusion.6), channel_id=1, source_target_pairs={{0,7},{1,6},{2,5},{3,4},{4,3},{5,2},{6,1},{7,0},{8,15},{9,14},{10,... | collective-permute-start | bytes 786440 | tf_op jit(solution)/shard_map/ppermute | solution.py:28
  8.8 14.9 %collective-permute-start = (bf16[2,8,64,128]{3,2,1,0:T(8,128)(2,1)S(1)}, bf16[2,8,64,128]{3,2,1,0:T(8,128)(2,1)S(1)}, u32[]{:S(2)}, u32[]{:S(2)}) collective-permute-start(bf16[2,8,64,128]{3,2,1,0:T(8,128)(2,1)S(1)} %pad_maximum_fusion), channel_id=1, source_target_pairs={{0,1},{1,0},{2,3},{3,2},{4,5},{5,4},{6,7},{7,6},{8,9},{9,8},{10,11... | collective-permute-start | bytes 786440 | tf_op jit(solution)/shard_map/ppermute | solution.py:28
  9.4 25.5 %collective-permute-start.1 = (bf16[2,8,64,128]{3,2,1,0:T(8,128)(2,1)S(1)}, bf16[2,8,64,128]{3,2,1,0:T(8,128)(2,1)S(1)}, u32[]{:S(2)}, u32[]{:S(2)}) collective-permute-start(bf16[2,8,64,128]{3,2,1,0:T(8,128)(2,1)S(1)} %pad_maximum_fusion.1), channel_id=1, source_target_pairs={{0,2},{1,3},{2,0},{3,1},{4,6},{5,7},{6,4},{7,5},{8,10},{9,11},{10,... | collective-permute-start | bytes 786440 | tf_op jit(solution)/shard_map/ppermute | solution.py:28
  9.5 26.1 %collective-permute-start.2 = (bf16[2,8,64,128]{3,2,1,0:T(8,128)(2,1)S(1)}, bf16[2,8,64,128]{3,2,1,0:T(8,128)(2,1)S(1)}, u32[]{:S(2)}, u32[]{:S(2)}) collective-permute-start(bf16[2,8,64,128]{3,2,1,0:T(8,128)(2,1)S(1)} %pad_maximum_fusion.2), channel_id=1, source_target_pairs={{0,3},{1,2},{2,1},{3,0},{4,7},{5,6},{6,5},{7,4},{8,11},{9,10},{10,... | collective-permute-start | bytes 786440 | tf_op jit(solution)/shard_map/ppermute | solution.py:28
  12.5 26.7 %collective-permute-start.3 = (bf16[2,8,64,128]{3,2,1,0:T(8,128)(2,1)S(1)}, bf16[2,8,64,128]{3,2,1,0:T(8,128)(2,1)S(1)}, u32[]{:S(2)}, u32[]{:S(2)}) collective-permute-start(bf16[2,8,64,128]{3,2,1,0:T(8,128)(2,1)S(1)} %pad_maximum_fusion.3), channel_id=1, source_target_pairs={{0,4},{1,5},{2,6},{3,7},{4,0},{5,1},{6,2},{7,3},{8,12},{9,13},{10,... | collective-permute-start | bytes 786440 | tf_op jit(solution)/shard_map/ppermute | solution.py:28
  15.9 33.0 %collective-permute-start.4 = (bf16[2,8,64,128]{3,2,1,0:T(8,128)(2,1)S(1)}, bf16[2,8,64,128]{3,2,1,0:T(8,128)(2,1)S(1)}, u32[]{:S(2)}, u32[]{:S(2)}) collective-permute-start(bf16[2,8,64,128]{3,2,1,0:T(8,128)(2,1)S(1)} %pad_maximum_fusion.4), channel_id=1, source_target_pairs={{0,5},{1,4},{2,7},{3,6},{4,1},{5,0},{6,3},{7,2},{8,13},{9,12},{10,... | collective-permute-start | bytes 786440 | tf_op jit(solution)/shard_map/ppermute | solution.py:28
  23.6 25.3 %collective-permute-start.5 = (bf16[2,8,64,128]{3,2,1,0:T(8,128)(2,1)S(1)}, bf16[2,8,64,128]{3,2,1,0:T(8,128)(2,1)S(1)}, u32[]{:S(2)}, u32[]{:S(2)}) collective-permute-start(bf16[2,8,64,128]{3,2,1,0:T(8,128)(2,1)S(1)} %pad_maximum_fusion.5), channel_id=1, source_target_pairs={{0,6},{1,7},{2,4},{3,5},{4,2},{5,3},{6,0},{7,1},{8,14},{9,15},{10,... | collective-permute-start | bytes 786440 | tf_op jit(solution)/shard_map/ppermute | solution.py:28
  26.1 7.7 %copy-start = (bf16[5120,256]{1,0:T(8,128)(2,1)S(1)}, bf16[5120,256]{1,0:T(8,128)(2,1)}, u32[]{:S(2)}) copy-start(bf16[5120,256]{1,0:T(8,128)(2,1)} %refs_0_.2) | copy-start | bytes 7864324
  26.1 7.7 %copy-start.1 = (bf16[8,5120]{1,0:T(8,128)(2,1)S(1)}, bf16[8,5120]{1,0:T(8,128)(2,1)}, u32[]{:S(2)}) copy-start(bf16[8,5120]{1,0:T(8,128)(2,1)} %refs_1_.2) | copy-start | bytes 245764
  26.1 7.7 %copy-start.2 = (f32[5120]{0:T(1024)S(1)}, f32[5120]{0:T(1024)}, u32[]{:S(2)}) copy-start(f32[5120]{0:T(1024)} %param.12) | copy-start | bytes 61444
  34.9 14.7 %collective-permute-start.7 = (bf16[8,128]{1,0:T(8,128)(2,1)S(1)}, bf16[8,128]{1,0:T(8,128)(2,1)S(1)}, u32[]{:S(2)}, u32[]{:S(2)}) collective-permute-start(bf16[8,128]{1,0:T(8,128)(2,1)S(1)} %get-tuple-element.56), channel_id=1, source_target_pairs={{0,0},{1,2},{2,4},{3,6},{4,1},{5,3},{6,5},{7,7},{8,8},{9,10},{10,1... | collective-permute-start | bytes 6152 | tf_op jit(solution)/shard_map/ppermute | solution.py:371
  35.6 18.1 %collective-permute-start.8 = (bf16[8,128]{1,0:T(8,128)(2,1)S(1)}, bf16[8,128]{1,0:T(8,128)(2,1)S(1)}, u32[]{:S(2)}, u32[]{:S(2)}) collective-permute-start(bf16[8,128]{1,0:T(8,128)(2,1)S(1)} %get-tuple-element.57), channel_id=1, source_target_pairs={{0,1},{1,3},{2,5},{3,7},{4,0},{5,2},{6,4},{7,6},{8,9},{9,11},{10,1... | collective-permute-start | bytes 6152 | tf_op jit(solution)/shard_map/ppermute | solution.py:374
  55.2 5.3 %collective-permute-start.11 = (bf16[8,5120]{1,0:T(8,128)(2,1)S(1)}, bf16[8,5120]{1,0:T(8,128)(2,1)S(1)}, u32[]{:S(2)}, u32[]{:S(2)}) collective-permute-start(bf16[8,5120]{1,0:T(8,128)(2,1)S(1)} %shard_map.128.refs_3_), channel_id=1, source_target_pairs={{0,1},{1,0},{2,3},{3,2},{4,5},{5,4},{6,7},{7,6},{8,9},{9,8},{10,11... | collective-permute-start | bytes 245768 | tf_op jit(solution)/shard_map/ppermute | solution.py:28
  56.6 4.4 %collective-permute-start.10 = (bf16[8,5120]{1,0:T(8,128)(2,1)S(1)}, bf16[8,5120]{1,0:T(8,128)(2,1)S(1)}, u32[]{:S(2)}, u32[]{:S(2)}) collective-permute-start(bf16[8,5120]{1,0:T(8,128)(2,1)S(1)} %shard_map.128.refs_3_), channel_id=1, source_target_pairs={{0,2},{1,3},{2,0},{3,1},{4,6},{5,7},{6,4},{7,5},{8,10},{9,11},{10,... | collective-permute-start | bytes 245768 | tf_op jit(solution)/shard_map/ppermute | solution.py:28
  56.9 5.3 %collective-permute-start.9 = (bf16[8,5120]{1,0:T(8,128)(2,1)S(1)}, bf16[8,5120]{1,0:T(8,128)(2,1)S(1)}, u32[]{:S(2)}, u32[]{:S(2)}) collective-permute-start(bf16[8,5120]{1,0:T(8,128)(2,1)S(1)} %shard_map.128.refs_3_), channel_id=1, source_target_pairs={{0,3},{1,2},{2,1},{3,0},{4,7},{5,6},{6,5},{7,4},{8,11},{9,10},{10,... | collective-permute-start | bytes 245768 | tf_op jit(solution)/shard_map/ppermute | solution.py:28
  62.3 5.4 %collective-permute-start.12 = (bf16[8,5120]{1,0:T(8,128)(2,1)S(1)}, bf16[8,5120]{1,0:T(8,128)(2,1)S(1)}, u32[]{:S(2)}, u32[]{:S(2)}) collective-permute-start(bf16[8,5120]{1,0:T(8,128)(2,1)S(1)} %shard_map.129.refs_1_), channel_id=1, source_target_pairs={{0,4},{1,5},{2,6},{3,7},{4,0},{5,1},{6,2},{7,3},{8,12},{9,13},{10,... | collective-permute-start | bytes 245768 | tf_op jit(solution)/shard_map/ppermute | solution.py:28
  68.5 7.4 %collective-permute-start.13 = (bf16[8,128]{1,0:T(8,128)(2,1)S(1)}, bf16[8,128]{1,0:T(8,128)(2,1)S(1)}, u32[]{:S(2)}, u32[]{:S(2)}) collective-permute-start(bf16[8,128]{1,0:T(8,128)(2,1)S(1)} %get-tuple-element.64), channel_id=1, source_target_pairs={{0,0},{1,2},{2,4},{3,6},{4,1},{5,3},{6,5},{7,7},{8,8},{9,10},{10,1... | collective-permute-start | bytes 6152 | tf_op jit(solution)/shard_map/ppermute | solution.py:371
  69.2 7.6 %collective-permute-start.14 = (bf16[8,128]{1,0:T(8,128)(2,1)S(1)}, bf16[8,128]{1,0:T(8,128)(2,1)S(1)}, u32[]{:S(2)}, u32[]{:S(2)}) collective-permute-start(bf16[8,128]{1,0:T(8,128)(2,1)S(1)} %get-tuple-element.65), channel_id=1, source_target_pairs={{0,1},{1,3},{2,5},{3,7},{4,0},{5,2},{6,4},{7,6},{8,9},{9,11},{10,1... | collective-permute-start | bytes 6152 | tf_op jit(solution)/shard_map/ppermute | solution.py:374
  78.3 4.4 %collective-permute-start.17 = (bf16[8,5120]{1,0:T(8,128)(2,1)S(1)}, bf16[8,5120]{1,0:T(8,128)(2,1)S(1)}, u32[]{:S(2)}, u32[]{:S(2)}) collective-permute-start(bf16[8,5120]{1,0:T(8,128)(2,1)S(1)} %shard_map.132.refs_3_), channel_id=1, source_target_pairs={{0,1},{1,0},{2,3},{3,2},{4,5},{5,4},{6,7},{7,6},{8,9},{9,8},{10,11... | collective-permute-start | bytes 245768 | tf_op jit(solution)/shard_map/ppermute | solution.py:28
  80.0 4.9 %collective-permute-start.16 = (bf16[8,5120]{1,0:T(8,128)(2,1)S(1)}, bf16[8,5120]{1,0:T(8,128)(2,1)S(1)}, u32[]{:S(2)}, u32[]{:S(2)}) collective-permute-start(bf16[8,5120]{1,0:T(8,128)(2,1)S(1)} %shard_map.132.refs_3_), channel_id=1, source_target_pairs={{0,2},{1,3},{2,0},{3,1},{4,6},{5,7},{6,4},{7,5},{8,10},{9,11},{10,... | collective-permute-start | bytes 245768 | tf_op jit(solution)/shard_map/ppermute | solution.py:28
  81.3 5.3 %collective-permute-start.15 = (bf16[8,5120]{1,0:T(8,128)(2,1)S(1)}, bf16[8,5120]{1,0:T(8,128)(2,1)S(1)}, u32[]{:S(2)}, u32[]{:S(2)}) collective-permute-start(bf16[8,5120]{1,0:T(8,128)(2,1)S(1)} %shard_map.132.refs_3_), channel_id=1, source_target_pairs={{0,3},{1,2},{2,1},{3,0},{4,7},{5,6},{6,5},{7,4},{8,11},{9,10},{10,... | collective-permute-start | bytes 245768 | tf_op jit(solution)/shard_map/ppermute | solution.py:28
  86.7 6.3 %collective-permute-start.18 = (bf16[8,5120]{1,0:T(8,128)(2,1)S(1)}, bf16[8,5120]{1,0:T(8,128)(2,1)S(1)}, u32[]{:S(2)}, u32[]{:S(2)}) collective-permute-start(bf16[8,5120]{1,0:T(8,128)(2,1)S(1)} %shard_map.133.refs_1_), channel_id=1, source_target_pairs={{0,4},{1,5},{2,6},{3,7},{4,0},{5,1},{6,2},{7,3},{8,12},{9,13},{10,... | collective-permute-start | bytes 245768 | tf_op jit(solution)/shard_map/ppermute | solution.py:28
  93.8 5.7 %collective-permute-start.19 = (bf16[8,128]{1,0:T(8,128)(2,1)S(1)}, bf16[8,128]{1,0:T(8,128)(2,1)S(1)}, u32[]{:S(2)}, u32[]{:S(2)}) collective-permute-start(bf16[8,128]{1,0:T(8,128)(2,1)S(1)} %get-tuple-element.72), channel_id=1, source_target_pairs={{0,0},{1,2},{2,4},{3,6},{4,1},{5,3},{6,5},{7,7},{8,8},{9,10},{10,1... | collective-permute-start | bytes 6152 | tf_op jit(solution)/shard_map/ppermute | solution.py:371
  94.5 5.9 %collective-permute-start.20 = (bf16[8,128]{1,0:T(8,128)(2,1)S(1)}, bf16[8,128]{1,0:T(8,128)(2,1)S(1)}, u32[]{:S(2)}, u32[]{:S(2)}) collective-permute-start(bf16[8,128]{1,0:T(8,128)(2,1)S(1)} %get-tuple-element.73), channel_id=1, source_target_pairs={{0,1},{1,3},{2,5},{3,7},{4,0},{5,2},{6,4},{7,6},{8,9},{9,11},{10,1... | collective-permute-start | bytes 6152 | tf_op jit(solution)/shard_map/ppermute | solution.py:374
  102.0 4.4 %collective-permute-start.23 = (bf16[8,5120]{1,0:T(8,128)(2,1)S(1)}, bf16[8,5120]{1,0:T(8,128)(2,1)S(1)}, u32[]{:S(2)}, u32[]{:S(2)}) collective-permute-start(bf16[8,5120]{1,0:T(8,128)(2,1)S(1)} %shard_map.136.refs_3_), channel_id=1, source_target_pairs={{0,1},{1,0},{2,3},{3,2},{4,5},{5,4},{6,7},{7,6},{8,9},{9,8},{10,11... | collective-permute-start | bytes 245768 | tf_op jit(solution)/shard_map/ppermute | solution.py:28
  103.2 4.4 %collective-permute-start.22 = (bf16[8,5120]{1,0:T(8,128)(2,1)S(1)}, bf16[8,5120]{1,0:T(8,128)(2,1)S(1)}, u32[]{:S(2)}, u32[]{:S(2)}) collective-permute-start(bf16[8,5120]{1,0:T(8,128)(2,1)S(1)} %shard_map.136.refs_3_), channel_id=1, source_target_pairs={{0,2},{1,3},{2,0},{3,1},{4,6},{5,7},{6,4},{7,5},{8,10},{9,11},{10,... | collective-permute-start | bytes 245768 | tf_op jit(solution)/shard_map/ppermute | solution.py:28
  104.5 5.3 %collective-permute-start.21 = (bf16[8,5120]{1,0:T(8,128)(2,1)S(1)}, bf16[8,5120]{1,0:T(8,128)(2,1)S(1)}, u32[]{:S(2)}, u32[]{:S(2)}) collective-permute-start(bf16[8,5120]{1,0:T(8,128)(2,1)S(1)} %shard_map.136.refs_3_), channel_id=1, source_target_pairs={{0,3},{1,2},{2,1},{3,0},{4,7},{5,6},{6,5},{7,4},{8,11},{9,10},{10,... | collective-permute-start | bytes 245768 | tf_op jit(solution)/shard_map/ppermute | solution.py:28
  109.9 6.3 %collective-permute-start.24 = (bf16[8,5120]{1,0:T(8,128)(2,1)S(1)}, bf16[8,5120]{1,0:T(8,128)(2,1)S(1)}, u32[]{:S(2)}, u32[]{:S(2)}) collective-permute-start(bf16[8,5120]{1,0:T(8,128)(2,1)S(1)} %shard_map.137.refs_1_), channel_id=1, source_target_pairs={{0,4},{1,5},{2,6},{3,7},{4,0},{5,1},{6,2},{7,3},{8,12},{9,13},{10,... | collective-permute-start | bytes 245768 | tf_op jit(solution)/shard_map/ppermute | solution.py:28
  117.0 5.5 %collective-permute-start.25 = (bf16[8,128]{1,0:T(8,128)(2,1)S(1)}, bf16[8,128]{1,0:T(8,128)(2,1)S(1)}, u32[]{:S(2)}, u32[]{:S(2)}) collective-permute-start(bf16[8,128]{1,0:T(8,128)(2,1)S(1)} %get-tuple-element.80), channel_id=1, source_target_pairs={{0,0},{1,2},{2,4},{3,6},{4,1},{5,3},{6,5},{7,7},{8,8},{9,10},{10,1... | collective-permute-start | bytes 6152 | tf_op jit(solution)/shard_map/ppermute | solution.py:371
  117.7 5.7 %collective-permute-start.26 = (bf16[8,128]{1,0:T(8,128)(2,1)S(1)}, bf16[8,128]{1,0:T(8,128)(2,1)S(1)}, u32[]{:S(2)}, u32[]{:S(2)}) collective-permute-start(bf16[8,128]{1,0:T(8,128)(2,1)S(1)} %get-tuple-element.81), channel_id=1, source_target_pairs={{0,1},{1,3},{2,5},{3,7},{4,0},{5,2},{6,4},{7,6},{8,9},{9,11},{10,1... | collective-permute-start | bytes 6152 | tf_op jit(solution)/shard_map/ppermute | solution.py:374
  125.0 4.4 %collective-permute-start.29 = (bf16[8,5120]{1,0:T(8,128)(2,1)S(1)}, bf16[8,5120]{1,0:T(8,128)(2,1)S(1)}, u32[]{:S(2)}, u32[]{:S(2)}) collective-permute-start(bf16[8,5120]{1,0:T(8,128)(2,1)S(1)} %shard_map.140.refs_3_), channel_id=1, source_target_pairs={{0,1},{1,0},{2,3},{3,2},{4,5},{5,4},{6,7},{7,6},{8,9},{9,8},{10,11... | collective-permute-start | bytes 245768 | tf_op jit(solution)/shard_map/ppermute | solution.py:28
  126.2 4.4 %collective-permute-start.28 = (bf16[8,5120]{1,0:T(8,128)(2,1)S(1)}, bf16[8,5120]{1,0:T(8,128)(2,1)S(1)}, u32[]{:S(2)}, u32[]{:S(2)}) collective-permute-start(bf16[8,5120]{1,0:T(8,128)(2,1)S(1)} %shard_map.140.refs_3_), channel_id=1, source_target_pairs={{0,2},{1,3},{2,0},{3,1},{4,6},{5,7},{6,4},{7,5},{8,10},{9,11},{10,... | collective-permute-start | bytes 245768 | tf_op jit(solution)/shard_map/ppermute | solution.py:28
  127.2 5.3 %collective-permute-start.27 = (bf16[8,5120]{1,0:T(8,128)(2,1)S(1)}, bf16[8,5120]{1,0:T(8,128)(2,1)S(1)}, u32[]{:S(2)}, u32[]{:S(2)}) collective-permute-start(bf16[8,5120]{1,0:T(8,128)(2,1)S(1)} %shard_map.140.refs_3_), channel_id=1, source_target_pairs={{0,3},{1,2},{2,1},{3,0},{4,7},{5,6},{6,5},{7,4},{8,11},{9,10},{10,... | collective-permute-start | bytes 245768 | tf_op jit(solution)/shard_map/ppermute | solution.py:28
  132.6 6.3 %collective-permute-start.30 = (bf16[8,5120]{1,0:T(8,128)(2,1)S(1)}, bf16[8,5120]{1,0:T(8,128)(2,1)S(1)}, u32[]{:S(2)}, u32[]{:S(2)}) collective-permute-start(bf16[8,5120]{1,0:T(8,128)(2,1)S(1)} %shard_map.141.first_ref), channel_id=1, source_target_pairs={{0,4},{1,5},{2,6},{3,7},{4,0},{5,1},{6,2},{7,3},{8,12},{9,13},{10,... | collective-permute-start | bytes 245768 | tf_op jit(solution)/shard_map/ppermute | solution.py:28
  139.1 1.3 collective-permute-start.31
